TPU v7x, 32 devices: a whole 2x2x4 slice. The times are simulated.
32 devices in a mesh: groups: 2 (over x), expert: 16 (over z, y, core).
Axes of the slice: x: 2, y: 2, z: 4, core: 2. Of those that a mesh axis runs over, the one named last changes fastest.
Arguments:
- tokens: bfloat16 [4096, 4096], P(('groups', 'expert')), parts along dimension 0, may hold values from -6 to 6
- w_in: bfloat16 [16, 4096, 2048], P('expert'), may hold values from -0.09375 to 0.09375
- w_out: bfloat16 [16, 2048, 4096], P('expert'), may hold values from -0.09375 to 0.09375
- w_bcd: bfloat16 [4096, 160], replicated, may hold values from -0.09375 to 0.09375
- dt_bias: float32 [32], replicated, may hold values from -1 to 1
- decay_rate: float32 [32], replicated, may hold values from 0.00048828125 to 0.05
- skip_gain: float32 [32], replicated, may hold values from 0.5 to 1.5
- norm_gain: float32 [4096], replicated, may hold values from 0.5 to 1.5
- expert_ids: int32 [4096, 1], P(('groups', 'expert')), parts along dimension 0, may hold values from 0 to 7; in each aligned block of 128 rows (0 to 127, 128 to 255, ...) at most 24 rows name the same one
- decode_heads: int32 [16], P('expert'), may hold values from 0 to 15, as said below
Outputs:
- mixed: bfloat16 [4096, 4096], P(('groups', 'expert')), parts along dimension 0
- decode_state: float32 [32, 8192], P(('groups', 'expert')), parts along dimension 0
There are 2 independent parts, one for each index of `groups`. A program takes and returns all parts, laid end to end along the dimension named above; an argument that names none is the same for every part. Nothing has to cross between parts.
Inputs may be any that keep to these rules, and one draw needn't show every extreme that they name: `expert_ids`: in each aligned block of 128 rows (the rows of one device) no expert is named more than 24 times. `decode_heads`: the entries are the device numbers modulo 32, shuffled.
All inputs are finite; a program needn't handle non-finite values.
Results may differ from a plain program's by a relative error of at most 0.0065.
Values may be sent and summed in bfloat16 or wider, within the bound.
No kernel may reach another device: no remote copies, remote signals or barrier semaphores. Data moves between devices by JAX's collectives and lax.ppermute only.
A program may use at most 192 MiB of HBM per device.

v0:
```python
import jax
import jax.numpy as jnp
from jax import lax
from jax.sharding import PartitionSpec as P

INNER = 4096
HEADDIM = 128
NS = 64
EXPERTS = 8
SPAN = 128


def carried_in(part, axis, combine, identity):
    place = lax.axis_index(axis)
    gathered = jax.tree.map(lambda a: lax.all_gather(a, axis), part)
    state = jax.tree.map(lambda a, e: jnp.zeros_like(a) + jnp.asarray(e, a.dtype), part, identity)

    def one(lap, state):
        return combine(
            state, jax.tree.map(lambda a: lax.dynamic_index_in_dim(a, lap, 0, False), gathered)
        )

    return lax.fori_loop(0, place, one, state)


def broadcast(block, axis, owner):
    block = jnp.where(lax.axis_index(axis) == owner, block, jnp.zeros_like(block))
    return lax.psum(block, axis)


def ssd_pass(x_heads, steps_dt, b_proj, c_proj, decay_rate):
    span_count = x_heads.shape[0] // SPAN
    head_count = x_heads.shape[1]
    best = lax.Precision.HIGHEST

    def span_step(carry_pair, pieces):
        carry_state, offset = carry_pair
        span_x, span_dt, span_b, span_c = pieces
        log_decay = -span_dt * decay_rate[None, :]
        running = jnp.cumsum(log_decay, axis=0)
        places = jnp.arange(SPAN)
        causal = (places[:, None] >= places[None, :])[:, :, None]
        log_gap = jnp.where(causal, running[:, None, :] - running[None, :, :], 0.0)
        scores = jnp.dot(span_c, span_b.T, precision=best)
        weights = (
            jnp.where(causal, jnp.exp(log_gap), 0.0) * scores[:, :, None] * span_dt[None, :, :]
        )
        within = jnp.einsum("tuh,uhp->thp", weights, span_x, precision=best)
        carried = jnp.exp(running)[:, :, None] * jnp.einsum(
            "tn,hpn->thp", span_c, carry_state, precision=best
        )
        tail_weight = jnp.exp(running[-1][None, :] - running) * span_dt
        new_state = jnp.exp(running[-1])[:, None, None] * carry_state + jnp.einsum(
            "uh,uhp,un->hpn", tail_weight, span_x, span_b, precision=best
        )
        return ((new_state, offset + running[-1]), (within + carried, offset[None, :] + running))

    init_state = jnp.zeros((head_count, HEADDIM, NS), jnp.float32)
    init_offset = jnp.zeros((head_count,), jnp.float32)
    pieces = (
        x_heads.reshape(span_count, SPAN, head_count, HEADDIM),
        steps_dt.reshape(span_count, SPAN, head_count),
        b_proj.reshape(span_count, SPAN, NS),
        c_proj.reshape(span_count, SPAN, NS),
    )
    (final_state, log_total), (y_blocks, log_rows) = lax.scan(
        span_step, (init_state, init_offset), pieces
    )
    return (
        y_blocks.reshape(-1, head_count, HEADDIM),
        final_state,
        log_rows.reshape(-1, head_count),
        log_total,
    )


def chain_combine(earlier_pair, later_pair):
    return (
        earlier_pair[0] * later_pair[0],
        later_pair[0][:, None, None] * earlier_pair[1] + later_pair[1],
    )


def send_inner(inner_rows):
    return lax.all_to_all(inner_rows, "expert", split_axis=0, concat_axis=0, tiled=True)


def shards(
    tokens, w_in, w_out, w_bcd, dt_bias, decay_rate, skip_gain, norm_gain, expert_ids, decode_heads
):
    dev_count = lax.axis_size("expert")
    slices = dev_count // EXPERTS
    tok_rows = tokens.shape[0]
    cap_slots = slices * ((tok_rows * 3 // 16 + slices - 1) // slices)
    row_width = tokens.shape[1]
    in_dev = w_in.shape[2]
    head_count = INNER // HEADDIM
    routed = expert_ids[:, 0]
    onehot = (routed[:, None] == jnp.arange(EXPERTS, dtype=jnp.int32)[None, :]).astype(jnp.int32)
    slot_ids = jnp.sum((jnp.cumsum(onehot, axis=0) - onehot) * onehot, axis=1)
    sectioned = (
        jnp.zeros((EXPERTS, cap_slots, row_width), jnp.bfloat16).at[routed, slot_ids].set(tokens)
    )
    weight_in = w_in[0]
    weight_out = w_out[0]
    outgoing = jnp.broadcast_to(
        sectioned[:, None], (EXPERTS, slices, cap_slots, row_width)
    ).reshape(dev_count, cap_slots, row_width)
    inner_rows = jnp.einsum(
        "sid,de->sie",
        lax.all_to_all(outgoing, "expert", split_axis=0, concat_axis=0, tiled=True),
        weight_in,
        preferred_element_type=jnp.float32,
    ).astype(jnp.bfloat16)
    returned = send_inner(inner_rows)
    x_inner = returned.reshape(EXPERTS, slices, cap_slots, in_dev)[routed, :, slot_ids, :].reshape(
        tok_rows, INNER
    )
    mixing = jnp.dot(tokens, w_bcd, preferred_element_type=jnp.float32)
    b_proj = mixing[:, :NS]
    c_proj = mixing[:, NS : 2 * NS]
    steps_dt = jax.nn.softplus(mixing[:, 2 * NS :] + dt_bias[None, :])
    x_heads = x_inner.astype(jnp.float32).reshape(tok_rows, head_count, HEADDIM)
    y_local, state_end, log_rows, log_total = ssd_pass(
        x_heads, steps_dt, b_proj, c_proj, decay_rate
    )
    block_decay = jnp.exp(log_total)
    identity = (jnp.ones_like(block_decay), jnp.zeros_like(state_end))
    prefix_decay, prefix_state = carried_in(
        (block_decay, state_end), "expert", chain_combine, identity
    )
    incoming = jnp.einsum("tn,hpn->thp", c_proj, prefix_state, precision=lax.Precision.HIGHEST)
    y_full = y_local + jnp.exp(log_rows)[:, :, None] * incoming + skip_gain[None, :, None] * x_heads
    y_flat = y_full.reshape(tok_rows, INNER)
    normed = (
        y_flat
        * lax.rsqrt(jnp.mean(y_flat * y_flat, axis=1, keepdims=True) + 1e-05)
        * norm_gain[None, :]
    ).astype(jnp.bfloat16)
    returning = (
        jnp.zeros((EXPERTS, slices, cap_slots, in_dev), jnp.bfloat16)
        .at[routed, :, slot_ids, :]
        .set(normed.reshape(tok_rows, slices, in_dev))
        .reshape(dev_count, cap_slots, in_dev)
    )
    partial_value = jnp.einsum(
        "sie,ed->sid",
        lax.all_to_all(returning, "expert", split_axis=0, concat_axis=0, tiled=True),
        weight_out,
        preferred_element_type=jnp.float32,
    ).astype(jnp.bfloat16)
    gathered = lax.all_to_all(partial_value, "expert", split_axis=0, concat_axis=0, tiled=True)
    mixed_rows = jnp.sum(
        gathered.reshape(EXPERTS, slices, cap_slots, row_width)[routed, :, slot_ids, :].astype(
            jnp.float32
        ),
        axis=1,
    ).astype(jnp.bfloat16)
    final_here = block_decay[:, None, None] * prefix_state + state_end
    all_heads = broadcast(final_here, "expert", dev_count - 1)
    chosen = all_heads[decode_heads[0]].reshape(1, HEADDIM * NS)
    return (mixed_rows, chosen)


def solution(mesh):
    in_specs = (
        P(("groups", "expert"), None),
        P("expert", None, None),
        P("expert", None, None),
        P(),
        P(),
        P(),
        P(),
        P(),
        P(("groups", "expert"), None),
        P("expert"),
    )
    out_specs = (P(("groups", "expert"), None), P(("groups", "expert"), None))
    return jax.shard_map(shards, mesh=mesh, in_specs=in_specs, out_specs=out_specs, check_vma=False)
```

profile of v0, /device:TPU:0, one launch (start us, length us, event | category | flops | bytes accessed | tf_op | source)
XLA Modules:
  0.0 625.5 jit_solution(9336413367514208867)
XLA Ops:
  7.2 0.8 fusion.30
  8.2 0.8 select_reduce_fusion
  9.9 24.9 %scatter_fusion = bf16[8,24,4096]{2,1,0:T(8,128)(2,1)S(1)} fusion(bf16[8,24,4096]{2,1,0:T(8,128)(2,1)S(1)} %broadcast_in_dim.58, s32[128]{0:T(128)S(1)} %get-tuple-element.114, bf16[128,4096]{1,0:T(8,128)(2,1)} %param.12), kind=kCustom, calls=%fused_computation.2 | custom fusion | bytes 3146752 | tf_op jit(solution)/shard_map/scatter | solution.py:102
  35.2 77.0 %all_to_all.20 = bf16[16,24,4096]{2,1,0:T(8,128)(2,1)S(1)} all-to-all(bf16[16,24,4096]{2,1,0:T(8,128)(2,1)S(1)} %bitcast.73), channel_id=1, replica_groups=mesh['groups'=2,'expert'=16] {'expert'}, dimensions={0} | all-to-all | bytes 6291456 | tf_op jit(solution)/shard_map/all_to_all | solution.py:111
  112.2 11.6 %fusion.7 = bf16[16,24,2048]{2,1,0:T(8,128)(2,1)} fusion(bf16[16,24,4096]{2,1,0:T(8,128)(2,1)S(1)} %all_to_all.20, bf16[1,4096,2048]{2,1,0:T(8,128)(2,1)} %param.13), kind=kOutput, calls=%fused_computation.12 | convolution fusion | flops 6443237376 | bytes 21495808 | tf_op jit(solution)/shard_map/sid,de->sie/dot_general | solution.py:109
  123.9 5.3 all-to-all-start.1
  129.4 1.7 fusion.44
  131.7 29.4 %all-to-all-done.1 = bf16[16,24,2048]{2,1,0:T(8,128)(2,1)S(1)} async-done(((bf16[16,24,2048]{2,1,0:T(8,128)(2,1)}), bf16[16,24,2048]{2,1,0:T(8,128)(2,1)S(1)}, u32[]{:S(2)}, u32[]{:S(2)}) %all-to-all-start.1) | async-done | bytes 1572896 | tf_op jit(solution)/shard_map/all_to_all | solution.py:85
  161.2 2.8 copy.73
  164.0 4.2 gather_fusion
  168.2 1.0 copy.74
  169.3 3.1 convolution_add_fusion
  172.6 24.9 %all-gather.1 = f32[16,1,32]{2,1,0:T(1,128)S(1)} all-gather(f32[1,1,32]{2,1,0:T(1,128)S(1)} %get-tuple-element.119), channel_id=1, replica_groups=mesh['groups'=2,'expert'=16] {'expert'}, dimensions={0}, use_global_device_ids=true | all-gather | bytes 2176 | tf_op jit(solution)/shard_map/all_gather | solution.py:15
  197.8 3.1 fusion.28
  200.9 3.8 fusion.12
  204.8 99.1 %all-gather.4.cloned.1.call-done = f32[512,128,64]{1,2,0:T(8,128)} async-done(((f32[32,128,64]{1,2,0:T(8,128)}), f32[512,128,64]{1,2,0:T(8,128)}) %all-gather.4.cloned.1.call-update) | async-done | bytes 16777232 | tf_op jit(solution)/shard_map/all_gather | solution.py:15
  303.9 1.6 broadcast.80.clone
  306.1 5.6 multiply_reduce_fusion
  311.7 1.9 copy.84
  313.5 1.9 multiply_convert_fusion
  315.4 1.1 copy.85
  316.5 1.1 broadcast_in_dim.57
  317.6 5.7 scatter_fusion.1
  323.9 116.0 %all_to_all.21 = bf16[16,24,2048]{2,1,0:T(8,128)(2,1)S(1)} all-to-all(bf16[16,24,2048]{2,1,0:T(8,128)(2,1)S(1)} %bitcast.79), channel_id=1, replica_groups=mesh['groups'=2,'expert'=16] {'expert'}, dimensions={0} | all-to-all | bytes 3145728 | tf_op jit(solution)/shard_map/all_to_all | solution.py:148
  439.9 11.4 %fusion.4 = bf16[16,24,4096]{2,1,0:T(8,128)(2,1)} fusion(bf16[16,24,2048]{2,1,0:T(8,128)(2,1)S(1)} %all_to_all.21, bf16[1,2048,4096]{2,1,0:T(8,128)(2,1)} %param.14), kind=kOutput, calls=%fused_computation.11 | convolution fusion | flops 6444023808 | bytes 21495808 | tf_op jit(solution)/shard_map/sie,ed->sid/dot_general | solution.py:146
  451.4 5.2 all-to-all-start.3
  456.7 1.6 copy.88
  458.2 2.4 add_select_fusion
  461.3 130.4 %all-reduce.2.cloned.1.call-done = f32[32,128,64]{1,2,0:T(8,128)} async-done(((f32[32,128,64]{1,2,0:T(8,128)}), f32[32,128,64]{1,2,0:T(8,128)}) %all-reduce.2.cloned.1.call-update) | async-done | bytes 1048592 | tf_op jit(solution)/shard_map/psum | solution.py:28
  593.2 6.8 %copy.87 = bf16[8,2,24,4096]{3,1,2,0:T(2,128)(2,1)} copy(bf16[8,2,24,4096]{3,2,1,0:T(8,128)(2,1)} %bitcast.21) | data formatting | bytes 6291456 | tf_op jit(solution)/shard_map/reshape | solution.py:154
  600.1 10.7 %gather_fusion.1 = bf16[128,2,4096]{2,1,0:T(2,128)(2,1)S(1)} fusion(bf16[8,2,24,4096]{3,1,2,0:T(2,128)(2,1)} %copy.87, s32[128]{0:T(128)S(1)} %bitcast.72), kind=kCustom, calls=%fused_computation.1 | custom fusion | bytes 4195328 | tf_op jit(solution)/shard_map/gather | solution.py:154
  610.8 7.4 %reduce_sum.35 = bf16[128,4096]{1,0:T(8,128)(2,1)} reduce(bf16[128,2,4096]{2,1,0:T(2,128)(2,1)S(1)} %gather_fusion.1, bf16[]{:T(256)} %constant.38.clone.1), dimensions={1}, to_apply=%region_8.9 | reduce | flops 524288 | bytes 3145730 | tf_op jit(solution)/shard_map/reduce_sum | solution.py:153
  (46 shorter events, 5.6 us)
Async XLA Ops:
  7.2 122.3 %copy-start = (bf16[4096,160]{0,1:T(8,128)(2,1)S(1)}, bf16[4096,160]{0,1:T(8,128)(2,1)}, u32[]{:S(2)}) copy-start(bf16[4096,160]{0,1:T(8,128)(2,1)} %param.15) | copy-start | bytes 3932164
  123.9 7.3 %copy-start.6 = (f32[32]{0:T(128)S(1)}, f32[32]{0:T(128)}, u32[]{:S(2)}) copy-start(f32[32]{0:T(128)} %param.17) | copy-start | bytes 388
  123.9 7.3 %copy-start.7 = (f32[32]{0:T(128)S(1)}, f32[32]{0:T(128)}, u32[]{:S(2)}) copy-start(f32[32]{0:T(128)} %param.16) | copy-start | bytes 388
  123.9 37.3 %all-to-all-start.1 = ((bf16[16,24,2048]{2,1,0:T(8,128)(2,1)}), bf16[16,24,2048]{2,1,0:T(8,128)(2,1)S(1)}, u32[]{:S(2)}, u32[]{:S(2)}) async-start(bf16[16,24,2048]{2,1,0:T(8,128)(2,1)} %fusion.7), calls=%async_computation.1 | async-start | bytes 3145728 | tf_op jit(solution)/shard_map/all_to_all | solution.py:85
  129.2 174.7 %all-gather.4.cloned.1.call-start = ((), (), s32[]{:S(2)}) async-start(), calls=%async_computation.5 | async-start | bytes 17825792 | tf_op jit(solution)/shard_map/all_gather | solution.py:15
  169.2 31.7 %copy-start.4 = (bf16[128,2,2048]{0,2,1:T(8,128)(2,1)}, bf16[128,2,2048]{0,2,1:T(8,128)(2,1)S(1)}, u32[]{:S(2)}) copy-start(bf16[128,2,2048]{0,2,1:T(8,128)(2,1)S(1)} %copy.74) | copy-start | bytes 3145732
  169.2 3.3 copy-start.5
  305.5 0.7 copy-start.8
  451.4 5.3 copy-start.2
  451.4 141.9 %all-to-all-start.3 = ((bf16[16,24,4096]{2,1,0:T(8,128)(2,1)}), bf16[16,24,4096]{2,1,0:T(8,128)(2,1)}, u32[]{:S(2)}, u32[]{:S(2)}) async-start(bf16[16,24,4096]{2,1,0:T(8,128)(2,1)} %fusion.4), calls=%async_computation.3 | async-start | bytes 6291456 | tf_op jit(solution)/shard_map/all_to_all | solution.py:152
  456.6 1.6 copy-start.3
  456.6 135.1 %all-reduce.2.cloned.1.call-start = ((), (), s32[]{:S(2)}) async-start(), calls=%async_computation.4 | async-start | bytes 2097152 | tf_op jit(solution)/shard_map/psum | solution.py:28
  600.1 18.1 %copy-start.1 = (bf16[4096,160]{0,1:T(8,128)(2,1)S(1)}, bf16[4096,160]{0,1:T(8,128)(2,1)}, u32[]{:S(2)}) copy-start(bf16[4096,160]{0,1:T(8,128)(2,1)} %param.15) | copy-start | bytes 3932164
Sparse Core Ops, SparseCore 0:
  172.5 131.3 all-gather.3
  461.5 130.1 all-reduce.1
where the time goes:
time: 632 us; the launch traced here: 625 us
  waiting for transfers between devices  259 us (41%)
  blocking collectives  218 us (34%)
  local copies, waits for them, and re-layouts  66.8 us (11%)
  matrix products  40.8 us (6%)
  between operations  15.4 us (2%)
  other arithmetic  14.6 us (2%)
  starting transfers between devices  10.8 us (2%)
    psum x1, waiting for transfers between devices, broadcast(): return lax.psum(block, axis)  130 us
    all_to_all x1, blocking collectives, shards(): lax.all_to_all(returning, 'expert', split_axis=0, concat_axis=0, tiled=True)  116 us
    all_gather x1, waiting for transfers between devices, carried_in(): gathered = jax.tree.map(lambda a: lax.all_gather(a, axis), part)  99.1 us
    all_to_all x1, blocking collectives, shards(): lax.all_to_all(outgoing, 'expert', split_axis=0, concat_axis=0, tiled=True)  77 us
    all_to_all x1, waiting for transfers between devices, send_inner(): lax.all_to_all(inner_rows, 'expert', split_axis=0, concat_axis=0, tiled=T...  29.4 us
    all_gather x1, blocking collectives, carried_in(): gathered = jax.tree.map(lambda a: lax.all_gather(a, axis), part)  24.9 us
    scatter x1, local copies, waits for them, and re-layouts, shards(): jnp.zeros((EXPERTS, cap_slots, row_width), jnp.bfloat16)  24.9 us
  transfers between devices with their start and end apart: 4, of which 3 were waited for; matrix products, arithmetic and copies ran while one was open for 2% of the time, Pallas kernels for 0%

commit v1 on v0

v1 whole, which is shorter than its diff:
```python
import functools

import jax
import jax.numpy as jnp
from jax import lax
from jax.experimental import pallas as pl
from jax.experimental.pallas import tpu as pltpu
from jax.sharding import PartitionSpec as P

INNER = 4096
HEADDIM = 128
HEADS = 32
NS = 64
EXPERTS = 8
CAP = 24
PAIR = 256
PACK = 256
VMEM_BYTES = 48 * 1024 * 1024

f32 = jnp.float32
bf16 = jnp.bfloat16


def params(**extra):
    return pltpu.CompilerParams(vmem_limit_bytes=VMEM_BYTES, **extra)


def route_column(ids):
    rows = ids.shape[0]
    onehot = (ids == lax.broadcasted_iota(jnp.int32, (rows, 128), 1)).astype(f32)
    later = lax.broadcasted_iota(jnp.int32, (rows, rows), 0)
    earlier = lax.broadcasted_iota(jnp.int32, (rows, rows), 1)
    lower = (earlier < later).astype(f32).astype(bf16)
    before = jnp.dot(lower, onehot.astype(bf16), preferred_element_type=f32)
    return jnp.sum(before * onehot, axis=1, keepdims=True).astype(jnp.int32)


def dispatch_kernel(slices, ids_ref, tok_ref, out_ref, slot_ref):
    ids = ids_ref[...]
    rows, width = tok_ref.shape
    depth = width // slices
    step = min(512, depth)
    slot = route_column(ids)
    slot_ref[...] = slot
    pick = (
        (ids * CAP + slot == lax.broadcasted_iota(jnp.int32, (rows, EXPERTS * CAP), 1))
        .astype(f32)
        .astype(bf16)
    )
    for c in range(0, depth, step):
        got = [
            lax.dot_general(
                pick,
                tok_ref[:, s * depth + c : s * depth + c + step],
                (((0,), (0,)), ((), ())),
                preferred_element_type=f32,
            )
            for s in range(slices)
        ]
        for e in range(EXPERTS):
            piece = jnp.concatenate([g[e * CAP : (e + 1) * CAP] for g in got], axis=0)
            out_ref[e * slices * CAP : (e + 1) * slices * CAP, c : c + step] = piece.astype(bf16)


def dispatch(ids, tokens, slices):
    rows, width = tokens.shape
    return pl.pallas_call(
        functools.partial(dispatch_kernel, slices),
        out_shape=(
            jax.ShapeDtypeStruct((EXPERTS * slices * CAP, width // slices), bf16),
            jax.ShapeDtypeStruct((rows, 1), jnp.int32),
        ),
        compiler_params=params(),
        name="dispatch",
    )(ids, tokens)


def in_kernel(slices, units, place_ref, *refs):
    rows_refs, w_refs, out_ref = refs[:slices], refs[slices : 2 * slices], refs[-1]
    total = None
    for r in range(slices):
        part = jnp.dot(rows_refs[r][...], w_refs[r][...], preferred_element_type=f32)
        total = part if total is None else total + part
    for j in range(out_ref.shape[0]):
        out_ref[j] = total[:, j * units : (j + 1) * units].astype(bf16)


def in_projection(place, pieces, w_in, units):
    slices = len(pieces)
    rows, depth = pieces[0].shape
    in_dev = w_in.shape[1]
    tile = min(256, in_dev)

    def w_spec(r):
        return pl.BlockSpec(
            (depth, tile), lambda n, place_ref: ((place_ref[0] - r + slices) % slices, n)
        )

    return pl.pallas_call(
        functools.partial(in_kernel, slices, units),
        out_shape=jax.ShapeDtypeStruct((in_dev // units, rows, units), bf16),
        grid_spec=pltpu.PrefetchScalarGridSpec(
            num_scalar_prefetch=1,
            grid=(in_dev // tile,),
            in_specs=[pl.BlockSpec((rows, depth), lambda n, place_ref: (0, 0))] * slices
            + [w_spec(r) for r in range(slices)],
            out_specs=pl.BlockSpec(
                (tile // units, rows, units), lambda n, place_ref: (n, 0, 0)
            ),
        ),
        compiler_params=params(),
        cost_estimate=pl.CostEstimate(
            flops=2 * rows * slices * depth * in_dev,
            bytes_accessed=2 * slices * depth * (in_dev + rows) + 2 * rows * in_dev,
            transcendentals=0,
        ),
        name="in_projection",
    )(place, *pieces, *([w_in] * slices))


def prep_kernel(heads, head_ref, rate_ref, skip_ref, pack_ref, w_ref, c_ref, b_ref, a_ref):
    first = head_ref[0]
    pack = pack_ref[...]
    row = lax.broadcasted_iota(jnp.int32, (128, PACK), 0)
    lane = lax.broadcasted_iota(jnp.int32, (128, PACK), 1)
    at = lane - 2 * NS - first
    choose = ((row < heads) & ((at == row) | (at == row + HEADS))).astype(f32)
    route = jnp.where(lane == 2 * NS + 2 * HEADS, 2.0 * CAP, 0.0) + jnp.where(
        lane == 2 * NS + 2 * HEADS + 1, 1.0, 0.0
    )
    choose = choose + jnp.where(row == heads, route, 0.0)
    across = lax.dot_general(
        choose.astype(bf16), pack, (((1,), (1,)), ((), ())), preferred_element_type=f32
    )
    rate = jnp.zeros((128, PAIR), f32)
    row = lax.broadcasted_iota(jnp.int32, (128, PAIR), 0)
    for h in range(heads):
        rate = jnp.where(row == h, rate_ref[first + h], rate)
    upto = lax.broadcasted_iota(jnp.int32, (PAIR, PAIR), 0)
    now = lax.broadcasted_iota(jnp.int32, (PAIR, PAIR), 1)
    running = jnp.dot(
        -across * rate,
        (upto <= now).astype(f32),
        precision=lax.Precision.HIGHEST,
        preferred_element_type=f32,
    )
    second = lax.broadcasted_iota(jnp.int32, (1, PAIR), 1) >= PAIR // 2
    column = across[heads : heads + 1] + jnp.where(second, float(CAP), 0.0)
    slots = 2 * CAP * EXPERTS
    place_t = (
        (lax.broadcasted_iota(jnp.int32, (slots, PAIR), 0).astype(f32) == column)
        .astype(f32)
        .astype(bf16)
    )
    down = running.T
    b_rows = pack[:, :NS]
    c_rows = pack[:, NS : 2 * NS]
    scores = lax.dot_general(
        c_rows, b_rows, (((1,), (1,)), ((), ())), preferred_element_type=f32
    )
    causal = upto >= now
    diagonal = upto == now
    b_cols = b_rows.astype(f32).T
    c_wide = c_rows.astype(f32)
    for h in range(heads):
        run_row = running[h : h + 1]
        run_col = down[:, h : h + 1]
        dt_row = across[h : h + 1]
        last = run_row[:, PAIR - 1 : PAIR]
        gap = jnp.where(causal, run_col - run_row, 0.0)
        weights = jnp.where(causal, jnp.exp(gap) * scores * dt_row, 0.0)
        weights = weights + jnp.where(diagonal, skip_ref[first + h], 0.0)
        half = jnp.dot(place_t, weights.astype(bf16), preferred_element_type=f32).astype(bf16)
        w_ref[h, 0] = lax.dot_general(
            half, place_t, (((1,), (1,)), ((), ())), preferred_element_type=f32
        ).astype(bf16)
        c_now = (c_wide * jnp.exp(run_col)).astype(bf16)
        c_ref[h, 0] = jnp.dot(place_t, c_now, preferred_element_type=f32).astype(bf16)
        b_now = (b_cols * (jnp.exp(last - run_row) * dt_row)).astype(bf16)
        b_ref[h, 0] = lax.dot_general(
            b_now, place_t, (((1,), (1,)), ((), ())), preferred_element_type=f32
        ).astype(bf16)
        a_ref[h, 0] = jnp.broadcast_to(jnp.exp(last), (8, 128))


def prepare(first, rate, skip, pack, heads):
    pairs = pack.shape[0] // PAIR
    slots = 2 * CAP * EXPERTS
    smem = pl.BlockSpec(memory_space=pltpu.SMEM)
    return pl.pallas_call(
        functools.partial(prep_kernel, heads),
        out_shape=(
            jax.ShapeDtypeStruct((heads, pairs, slots, slots), bf16),
            jax.ShapeDtypeStruct((heads, pairs, slots, NS), bf16),
            jax.ShapeDtypeStruct((heads, pairs, NS, slots), bf16),
            jax.ShapeDtypeStruct((heads, pairs, 8, 128), f32),
        ),
        grid=(pairs,),
        in_specs=[smem, smem, smem, pl.BlockSpec((PAIR, PACK), lambda p: (p, 0))],
        out_specs=(
            pl.BlockSpec((heads, 1, slots, slots), lambda p: (0, p, 0, 0)),
            pl.BlockSpec((heads, 1, slots, NS), lambda p: (0, p, 0, 0)),
            pl.BlockSpec((heads, 1, NS, slots), lambda p: (0, p, 0, 0)),
            pl.BlockSpec((heads, 1, 8, 128), lambda p: (0, p, 0, 0)),
        ),
        compiler_params=params(),
        cost_estimate=pl.CostEstimate(
            flops=4 * heads * pairs * slots * slots * PAIR,
            bytes_accessed=2 * heads * pairs * slots * slots,
            transcendentals=heads * pairs * PAIR * PAIR,
        ),
        name="scan_weights",
    )(first, rate, skip, pack)


def scan_kernel(heads, x_ref, w_ref, c_ref, b_ref, a_ref, gain_ref, out_ref, last_ref, state):
    pair = pl.program_id(0)

    @pl.when(pair == 0)
    def _():
        state[...] = jnp.zeros_like(state)

    experts, rows, units = x_ref.shape
    width = units // heads
    x = x_ref[...].reshape(experts * rows, units)
    y = []
    for h in range(heads):
        x_head = x[:, h * width : (h + 1) * width]
        before = state[h]
        y.append(
            jnp.dot(w_ref[h, 0], x_head, preferred_element_type=f32)
            + jnp.dot(c_ref[h, 0], before.astype(bf16), preferred_element_type=f32)
        )
        after = before * a_ref[h, 0, 0:1, 0:1] + jnp.dot(
            b_ref[h, 0], x_head, preferred_element_type=f32
        )
        state[h] = after
        last_ref[h] = after
    z = y[0] if heads == 1 else jnp.concatenate(y, axis=1)
    out_ref[...] = (z * gain_ref[...]).astype(bf16).reshape(experts, rows, units)


def scan(x, weights, gain, heads):
    experts, rows, units = x.shape
    pairs = rows // (2 * CAP)
    slots = 2 * CAP * EXPERTS
    width = units // heads
    return pl.pallas_call(
        functools.partial(scan_kernel, heads),
        out_shape=(
            jax.ShapeDtypeStruct(x.shape, bf16),
            jax.ShapeDtypeStruct((heads, NS, width), f32),
        ),
        grid=(pairs,),
        in_specs=[
            pl.BlockSpec((experts, 2 * CAP, units), lambda p: (0, p, 0)),
            pl.BlockSpec((heads, 1, slots, slots), lambda p: (0, p, 0, 0)),
            pl.BlockSpec((heads, 1, slots, NS), lambda p: (0, p, 0, 0)),
            pl.BlockSpec((heads, 1, NS, slots), lambda p: (0, p, 0, 0)),
            pl.BlockSpec((heads, 1, 8, 128), lambda p: (0, p, 0, 0)),
            pl.BlockSpec((1, units), lambda p: (0, 0)),
        ],
        out_specs=(
            pl.BlockSpec((experts, 2 * CAP, units), lambda p: (0, p, 0)),
            pl.BlockSpec((heads, NS, width), lambda p: (0, 0, 0)),
        ),
        scratch_shapes=[pltpu.VMEM((heads, NS, width), f32)],
        compiler_params=params(),
        cost_estimate=pl.CostEstimate(
            flops=2 * heads * pairs * slots * (slots + 2 * NS) * width,
            bytes_accessed=2 * heads * pairs * slots * slots,
            transcendentals=0,
        ),
        name="scan",
    )(x, *weights, gain)


def out_kernel(z_ref, inverse_ref, w_ref, out_ref, square_ref):
    chunks, rows, units = z_ref.shape

    def squares():
        total = jnp.zeros((rows, 1), f32)
        for j in range(chunks):
            z = z_ref[j].astype(f32) * inverse_ref[:, j * units : (j + 1) * units]
            total = total + jnp.sum(z * z, axis=1, keepdims=True)
        square_ref[...] = total

    pl.when(pl.program_id(0) == 0)(squares)
    total = None
    for j in range(chunks):
        part = jnp.dot(
            z_ref[j], w_ref[j * units : (j + 1) * units, :], preferred_element_type=f32
        )
        total = part if total is None else total + part
    out_ref[0] = total.astype(bf16)


def out_projection(place, z, inverse, w_out, slices):
    chunks, rows, units = z.shape
    in_dev, width = w_out.shape
    depth = width // slices
    tile = min(512, depth)
    tiles = depth // tile

    def kernel(place_ref, *refs):
        out_kernel(*refs)

    return pl.pallas_call(
        kernel,
        out_shape=(
            jax.ShapeDtypeStruct((slices, rows, depth), bf16),
            jax.ShapeDtypeStruct((rows, 1), f32),
        ),
        grid_spec=pltpu.PrefetchScalarGridSpec(
            num_scalar_prefetch=1,
            grid=(slices * tiles,),
            in_specs=[
                pl.BlockSpec((chunks, rows, units), lambda n, place_ref: (0, 0, 0)),
                pl.BlockSpec((1, in_dev), lambda n, place_ref: (0, 0)),
                pl.BlockSpec(
                    (in_dev, tile),
                    lambda n, place_ref: (
                        0,
                        (place_ref[0] + 1 + n // tiles) % slices * tiles + n % tiles,
                    ),
                ),
            ],
            out_specs=(
                pl.BlockSpec(
                    (1, rows, tile), lambda n, place_ref: (n // tiles, 0, n % tiles)
                ),
                pl.BlockSpec((rows, 1), lambda n, place_ref: (0, 0)),
            ),
        ),
        compiler_params=params(),
        cost_estimate=pl.CostEstimate(
            flops=2 * rows * in_dev * width,
            bytes_accessed=2 * in_dev * width + 2 * rows * (in_dev + width),
            transcendentals=0,
        ),
        name="out_projection",
    )(place, z, inverse, w_out)


def collect_kernel(slices, ids_ref, slot_ref, rows_ref, out_ref):
    rows = ids_ref.shape[0]
    count, depth = rows_ref.shape
    step = min(512, depth)
    at = ids_ref[...] * (slices * CAP) + slot_ref[...]
    lane = lax.broadcasted_iota(jnp.int32, (rows, count), 1)
    for s in range(slices):
        pick = (at + s * CAP == lane).astype(f32).astype(bf16)
        for c in range(0, depth, step):
            out_ref[:, s * depth + c : s * depth + c + step] = jnp.dot(
                pick, rows_ref[:, c : c + step], preferred_element_type=f32
            ).astype(bf16)


def collect(ids, slot, rows, slices):
    return pl.pallas_call(
        functools.partial(collect_kernel, slices),
        out_shape=jax.ShapeDtypeStruct((ids.shape[0], rows.shape[1] * slices), bf16),
        compiler_params=params(),
        name="collect",
    )(ids, slot, rows)


def turn(a, n, slices, r):
    return lax.ppermute(
        a, "expert", [(d, d // slices * slices + (d + r) % slices) for d in range(n)]
    )


def shards(
    tokens, w_in, w_out, w_bcd, dt_bias, decay_rate, skip_gain, norm_gain, expert_ids, decode_heads
):
    n = lax.axis_size("expert")
    slices = n // EXPERTS
    in_dev = w_in.shape[2]
    units = in_dev // EXPERTS
    heads = max(1, units // HEADDIM)
    width = tokens.shape[1]
    me = lax.axis_index("expert")
    place = (me % slices).astype(jnp.int32)
    place_arr = place.reshape(1)
    own_units = place * in_dev + me // slices * units
    same_slice = [[j * slices + s for j in range(EXPERTS)] for s in range(slices)]

    outgoing, slot = dispatch(expert_ids, tokens, slices)
    landed = lax.all_to_all(outgoing, "expert", split_axis=0, concat_axis=0, tiled=True)

    mixing = jnp.dot(tokens, w_bcd, preferred_element_type=f32)
    steps_dt = jax.nn.softplus(mixing[:, 2 * NS :] + dt_bias[None, :])
    coarse = lax.reduce_precision(steps_dt, 8, 7)
    pack = jnp.concatenate(
        [
            mixing[:, : 2 * NS],
            coarse,
            steps_dt - coarse,
            expert_ids.astype(f32),
            slot.astype(f32),
            jnp.zeros((tokens.shape[0], PACK - 2 * NS - 2 * HEADS - 2), f32),
        ],
        axis=1,
    ).astype(bf16)
    pack = lax.all_gather(pack, "expert", axis=0, tiled=True)
    first_head = (own_units // HEADDIM).astype(jnp.int32).reshape(1)
    weights = prepare(first_head, decay_rate, skip_gain, pack, heads)

    pieces = [landed] + [turn(landed, n, slices, r) for r in range(1, slices)]
    inner = in_projection(place_arr, pieces, w_in[0], units)
    rows = inner.shape[1]
    x = lax.all_to_all(
        inner, "expert", split_axis=0, concat_axis=0, axis_index_groups=same_slice, tiled=True
    )
    gain = lax.dynamic_slice(norm_gain, (own_units,), (units,)).reshape(1, units)
    z, state = scan(x, weights, gain, heads)
    z = lax.all_to_all(
        z, "expert", split_axis=0, concat_axis=0, axis_index_groups=same_slice, tiled=True
    )
    inverse = (1.0 / lax.dynamic_slice(norm_gain, (place * in_dev,), (in_dev,))).reshape(1, in_dev)
    partial, squares = out_projection(place_arr, z, inverse, w_out[0], slices)
    summed = partial[slices - 1].astype(f32)
    whole_squares = squares
    for r in range(1, slices):
        summed = summed + turn(partial[r - 1], n, slices, r).astype(f32)
        whole_squares = whole_squares + turn(squares, n, slices, r)
    factor = lax.rsqrt(whole_squares / INNER + 1e-05)
    back = lax.all_to_all(
        (summed * factor).astype(bf16), "expert", split_axis=0, concat_axis=0, tiled=True
    )
    mixed = collect(expert_ids, slot, back, slices)

    states = lax.all_gather(state.astype(bf16), "expert", axis=0, tiled=False)
    per_head = HEADDIM * heads // units
    want = decode_heads[0]
    states = (
        states.reshape(EXPERTS, slices, heads, NS, units // heads)
        .transpose(1, 0, 2, 3, 4)
        .reshape(HEADS, per_head, NS, units // heads)
    )
    chosen = lax.dynamic_index_in_dim(states, want, 0, False).astype(f32)
    chosen = chosen.transpose(0, 2, 1).reshape(1, HEADDIM * NS)
    return (mixed, chosen)


def solution(mesh):
    in_specs = (
        P(("groups", "expert"), None),
        P("expert", None, None),
        P("expert", None, None),
        P(),
        P(),
        P(),
        P(),
        P(),
        P(("groups", "expert"), None),
        P("expert"),
    )
    out_specs = (P(("groups", "expert"), None), P(("groups", "expert"), None))
    return jax.shard_map(shards, mesh=mesh, in_specs=in_specs, out_specs=out_specs, check_vma=False)
```

time: 632 us -> 276 us (0.44)
  waiting for transfers between devices: 259 us -> 93.3 us
  blocking collectives: 218 us -> 88.4 us
  local copies, waits for them, and re-layouts: 66.8 us -> 11.2 us
  Pallas kernels: 0 us -> 48.6 us
  matrix products: 40.8 us -> 1.72 us
  other arithmetic: 14.6 us -> 1.93 us
    psum x1 -> x0, waiting for transfers between devices: 130 us -> none  [broadcast(): return lax.psum(block, axis)]
    all_to_all x1 -> x0, blocking collectives: 116 us -> none  [shards(): lax.all_to_all(returning, 'expert', split_axis=0, concat_axis=0, tiled=True)]
    pallas_call x0 -> x6, Pallas kernels: none -> 48.6 us  [the longest x1 14 us: prepare(): pl.pallas_call(functools.partial(prep_kernel, heads), out_shape=(jax.Shap...]
    all_gather x1, waiting for transfers between devices: 99.1 us -> 51 us  [shards(): pack = lax.all_gather(pack, 'expert', axis=0, tiled=True)]
    dot_general x8 -> x1, matrix products: 40.8 us -> 1.72 us  [shards(): mixing = jnp.dot(tokens, w_bcd, preferred_element_type=f32)]
    all_to_all x1, blocking collectives: 77 us -> 43.3 us  [shards(): lax.all_to_all(outgoing, 'expert', split_axis=0, concat_axis=0, tiled=True)]
    scatter x3 -> x0, local copies, waits for them, and re-layouts: 31.2 us -> none  [the longest x1 24.9 us: shards(): jnp.zeros((EXPERTS, cap_slots, row_width), jnp.bfloat16)]
    all_gather x1, blocking collectives: 24.9 us -> 45.1 us  [shards(): states = lax.all_gather(state.astype(bf16), 'expert', axis=0, tiled=False)]
  transfers between devices with their start and end apart: 4 -> 7, of which waited for: 3 -> 4; matrix products, arithmetic and copies ran while one was open for 2% -> 1% of each run, Pallas kernels for 0% -> 5%
where the time goes in v1:
time: 276 us; the launch traced here: 273 us
  waiting for transfers between devices  93.3 us (34%)
  blocking collectives  88.4 us (32%)
  Pallas kernels  48.6 us (18%)
  between operations  15 us (5%)
  starting transfers between devices  13.4 us (5%)
  local copies, waits for them, and re-layouts  11.2 us (4%)
    all_gather x1, waiting for transfers between devices, shards(): pack = lax.all_gather(pack, 'expert', axis=0, tiled=True)  51 us
    all_gather x1, blocking collectives, shards(): states = lax.all_gather(state.astype(bf16), 'expert', axis=0, tiled=False)  45.1 us
    all_to_all x1, blocking collectives, shards(): lax.all_to_all(outgoing, 'expert', split_axis=0, concat_axis=0, tiled=True)  43.3 us
    all_to_all x1, waiting for transfers between devices, shards(): lax.all_to_all(z, 'expert', split_axis=0, concat_axis=0, axis_index_group...  37.6 us
    pallas_call x1, Pallas kernels, prepare(): pl.pallas_call(functools.partial(prep_kernel, heads), out_shape=(jax.Shap...  14 us
    pallas_call x1, Pallas kernels, in_projection(): pl.pallas_call(functools.partial(in_kernel, slices, units), out_shape=jax...  13 us
    pallas_call x1, Pallas kernels, out_projection(): pl.pallas_call(kernel, out_shape=(jax.ShapeDtypeStruct((slices, rows, dep...  12.4 us
    unnamed x31, local copies, waits for them, and re-layouts  9.3 us
  transfers between devices with their start and end apart: 7, of which 4 were waited for; matrix products, arithmetic and copies ran while one was open for 1% of the time, Pallas kernels for 5%

profile of v1, /device:TPU:0, one launch (start us, length us, event | category | flops | bytes accessed | tf_op | source)
XLA Modules:
  0.0 273.5 jit_solution(2306792981824412434)
XLA Ops:
  7.2 0.9 copy.41.ids_ref
  8.1 1.2 copy-done.2
  9.3 0.9 dispatch.1
  10.2 43.3 %all_to_all.32 = bf16[16,24,2048]{2,1,0:T(8,128)(2,1)S(1)} all-to-all(bf16[16,24,2048]{2,1,0:T(8,128)(2,1)S(1)} %bitcast.33), channel_id=1, replica_groups=mesh['groups'=2,'expert'=16] {'expert'}, dimensions={0} | all-to-all | bytes 3145728 | tf_op jit(solution)/shard_map/all_to_all | solution.py:390
  53.5 0.8 collective-permute-start
  54.3 1.7 fusion.3
  56.0 1.4 collective-permute-done.refs_1_
  57.4 13.0 %in_projection.1 = bf16[8,384,256]{2,1,0:T(8,128)(2,1)} custom-call(s32[1]{0:T(128)} %bitcast.place_ref, bf16[384,2048]{1,0:T(8,128)(2,1)S(1)} %bitcast.31, bf16[384,2048]{1,0:T(8,128)(2,1)} %collective-permute-done.refs_1_, bf16[4096,2048]{1,0:T(8,128)(2,1)} %bitcast.36, bf16[4096,2048]{1,0:T(8,128)(2,1)} %bitcast.37), custom_call_target="tpu_custom_call" | custom-call | flops 6442450944 | bytes 21495808 | tf_op jit(solution)/shard_map/in_projection/pallas_call | solution.py:99
  70.5 4.7 %all-to-all-start.1 = ((bf16[8,384,256]{2,1,0:T(8,128)(2,1)}), bf16[8,384,256]{2,1,0:T(8,128)(2,1)S(1)}, u32[]{:S(2)}, u32[]{:S(2)}) async-start(bf16[8,384,256]{2,1,0:T(8,128)(2,1)} %in_projection.1), calls=%async_computation.1 | async-start | bytes 3145728 | tf_op jit(solution)/shard_map/all_to_all | solution.py:413
  75.2 0.1 copy.44
  75.5 0.1 copy.40
  75.7 0.8 concatenate.4
  76.6 51.0 %all-gather.3.cloned.1.call-done.pack_ref = bf16[2048,256]{1,0:T(8,128)(2,1)} async-done(((bf16[128,256]{1,0:T(8,128)(2,1)}), bf16[2048,256]{1,0:T(8,128)(2,1)}) %all-gather.3.cloned.1.call-update) | async-done | bytes 1048592 | tf_op jit(solution)/shard_map/all_gather | solution.py:406
  127.6 1.2 copy-done.8
  128.9 14.0 %scan_weights.1 = (bf16[2,8,384,384]{3,2,1,0:T(8,128)(2,1)}, bf16[2,8,384,64]{3,2,1,0:T(8,128)(2,1)S(1)}, bf16[2,8,64,384]{3,2,1,0:T(8,128)(2,1)S(1)}, f32[2,8,8,128]{3,2,1,0:T(8,128)S(1)}) custom-call(s32[1]{0:T(128)} %bitcast.4.head_ref, f32[32]{0:T(128)S(1)} %copy-done.9, f32[32]{0:T(128)S(1)} %copy-done.10, bf16[2048,256]{1,0:T(8,128)(2,1)S(1)} %copy-done.8), custom_call_target="tpu_custom_call" | custom-call | flops 2415919104 | bytes 4718592 | tf_op jit(solution)/shard_map/scan_weights/pallas_call | solution.py:190
  142.8 1.2 copy-done.3
  144.0 0.9 copy-done.6
  144.9 1.4 copy-done.4
  146.3 1.1 copy-done.7
  147.4 6.6 %scan.1 = (bf16[8,384,256]{2,1,0:T(8,128)(2,1)S(1)}, f32[2,64,128]{2,1,0:T(8,128)S(1)}) custom-call(bf16[8,384,256]{2,1,0:T(8,128)(2,1)S(1)} %all-to-all-done.1.x_ref, bf16[2,8,384,384]{3,2,1,0:T(8,128)(2,1)} %get-tuple-element.14.w_ref, bf16[2,8,384,64]{3,2,1,0:T(8,128)(2,1)S(1)} %copy-done.4, bf16[2,8,64,384]{3,2,1,0:T(8,128)(2,1)S(1)} %copy-done.7, ...), custom_call_target="tpu_custom_call" | custom-call | flops 805306368 | bytes 4718592 | tf_op jit(solution)/shard_map/scan/pallas_call | solution.py:248
  154.0 1.2 copy-done.5
  155.2 3.6 %all-to-all-start.2 = ((bf16[8,384,256]{2,1,0:T(8,128)(2,1)}), bf16[8,384,256]{2,1,0:T(8,128)(2,1)S(1)}, u32[]{:S(2)}, u32[]{:S(2)}) async-start(bf16[8,384,256]{2,1,0:T(8,128)(2,1)} %copy-done.5), calls=%async_computation.2 | async-start | bytes 3145728 | tf_op jit(solution)/shard_map/all_to_all | solution.py:418
  158.8 37.6 %all-to-all-done.2.refs_0_ = bf16[8,384,256]{2,1,0:T(8,128)(2,1)S(1)} async-done(((bf16[8,384,256]{2,1,0:T(8,128)(2,1)}), bf16[8,384,256]{2,1,0:T(8,128)(2,1)S(1)}, u32[]{:S(2)}, u32[]{:S(2)}) %all-to-all-start.2) | async-done | bytes 1572896 | tf_op jit(solution)/shard_map/all_to_all | solution.py:418
  196.4 12.4 %out_projection.1 = (bf16[2,384,2048]{2,1,0:T(8,128)(2,1)S(1)}, f32[384,1]{1,0:T(8,128)S(1)}) custom-call(s32[1]{0:T(128)} %bitcast.place_ref, bf16[8,384,256]{2,1,0:T(8,128)(2,1)S(1)} %all-to-all-done.2.refs_0_, f32[1,2048]{1,0:T(1,128)S(1)} %bitcast.34, bf16[2048,4096]{1,0:T(8,128)(2,1)} %bitcast.41), custom_call_target="tpu_custom_call" | custom-call | flops 6442450944 | bytes 21495808 | tf_op jit(solution)/shard_map/out_projection/pallas_call | solution.py:308
  209.0 0.5 collective-permute-start.2
  209.5 3.2 %collective-permute-done.2 = f32[384,1]{1,0:T(8,128)S(1)} collective-permute-done((f32[384,1]{1,0:T(8,128)S(1)}, f32[384,1]{1,0:T(8,128)S(1)}, u32[]{:S(2)}, u32[]{:S(2)}) %collective-permute-start.2) | collective-permute-done | bytes 1568 | tf_op jit(solution)/shard_map/ppermute | solution.py:369
  212.7 0.2 rsqrt_reduce_fusion
  212.8 1.7 fusion.1
  214.5 3.7 %all-to-all-start.3 = ((bf16[16,24,2048]{2,1,0:T(8,128)(2,1)}), bf16[16,24,2048]{2,1,0:T(8,128)(2,1)S(1)}, u32[]{:S(2)}, u32[]{:S(2)}) async-start(bf16[16,24,2048]{2,1,0:T(8,128)(2,1)} %bitcast.38), calls=%async_computation.3 | async-start | bytes 3145728 | tf_op jit(solution)/shard_map/all_to_all | solution.py:429
  218.9 45.1 %all-gather = bf16[32,64,128]{2,1,0:T(8,128)(2,1)S(1)} all-gather(bf16[2,64,128]{2,1,0:T(8,128)(2,1)S(1)} %convert_element_type.40), channel_id=2, replica_groups=mesh['groups'=2,'expert'=16] {'expert'}, dimensions={0}, use_global_device_ids=true | all-gather | bytes 557056 | tf_op jit(solution)/shard_map/all_gather | solution.py:434
  264.2 0.7 reshape.59
  264.9 1.7 collect.1
  (41 shorter events, 0.7 us)
Async XLA Ops:
  7.2 47.1 %copy-start = (bf16[4096,160]{0,1:T(8,128)(2,1)S(1)}, bf16[4096,160]{0,1:T(8,128)(2,1)}, u32[]{:S(2)}) copy-start(bf16[4096,160]{0,1:T(8,128)(2,1)} %param.13) | copy-start | bytes 3932164
  8.0 1.2 copy-start.2
  53.5 3.9 %collective-permute-start = (bf16[384,2048]{1,0:T(8,128)(2,1)S(1)}, bf16[384,2048]{1,0:T(8,128)(2,1)}, u32[]{:S(2)}, u32[]{:S(2)}) collective-permute-start(bf16[384,2048]{1,0:T(8,128)(2,1)S(1)} %bitcast.30), channel_id=1, source_target_pairs={{0,1},{1,0},{2,3},{3,2},{4,5},{5,4},{6,7},{7,6},{8,9},{9,8},{10,11... | collective-permute-start | bytes 4718600 | tf_op jit(solution)/shard_map/ppermute | solution.py:369
  70.4 4.8 %copy-start.12 = (s32[128,1]{0,1:T(1,128)S(1)}, s32[128,1]{0,1:T(1,128)}, u32[]{:S(2)}) copy-start(s32[128,1]{0,1:T(1,128)} %param.18) | copy-start | bytes 1540
  70.4 5.2 %copy-start.13 = (f32[32]{0:T(128)S(1)}, f32[32]{0:T(128)}, u32[]{:S(2)}) copy-start(f32[32]{0:T(128)} %param.14) | copy-start | bytes 388
  70.4 6.1 %copy-start.11 = (f32[4096]{0:T(1024)S(1)}, f32[4096]{0:T(1024)}, u32[]{:S(2)}) copy-start(f32[4096]{0:T(1024)} %param.17) | copy-start | bytes 49156
  70.5 57.2 %copy-start.9 = (f32[32]{0:T(128)S(1)}, f32[32]{0:T(128)}, u32[]{:S(2)}) copy-start(f32[32]{0:T(128)} %rate_ref.1) | copy-start | bytes 388
  70.5 57.2 %copy-start.10 = (f32[32]{0:T(128)S(1)}, f32[32]{0:T(128)}, u32[]{:S(2)}) copy-start(f32[32]{0:T(128)} %skip_ref.1) | copy-start | bytes 388
  70.5 74.4 %all-to-all-start.1 = ((bf16[8,384,256]{2,1,0:T(8,128)(2,1)}), bf16[8,384,256]{2,1,0:T(8,128)(2,1)S(1)}, u32[]{:S(2)}, u32[]{:S(2)}) async-start(bf16[8,384,256]{2,1,0:T(8,128)(2,1)} %in_projection.1), calls=%async_computation.1 | async-start | bytes 3145728 | tf_op jit(solution)/shard_map/all_to_all | solution.py:413
  75.2 52.5 %all-gather.3.cloned.1.call-start = ((), (), s32[]{:S(2)}) async-start(), calls=%async_computation.4 | async-start | bytes 1114112 | tf_op jit(solution)/shard_map/all_gather | solution.py:406
  127.6 1.2 copy-start.8
  142.8 1.2 copy-start.3
  144.0 0.9 copy-start.6
  144.9 1.4 copy-start.4
  146.3 1.1 copy-start.7
  154.0 1.2 copy-start.5
  155.2 41.2 %all-to-all-start.2 = ((bf16[8,384,256]{2,1,0:T(8,128)(2,1)}), bf16[8,384,256]{2,1,0:T(8,128)(2,1)S(1)}, u32[]{:S(2)}, u32[]{:S(2)}) async-start(bf16[8,384,256]{2,1,0:T(8,128)(2,1)} %copy-done.5), calls=%async_computation.2 | async-start | bytes 3145728 | tf_op jit(solution)/shard_map/all_to_all | solution.py:418
  208.9 3.9 %collective-permute-start.1 = (bf16[384,2048]{1,0:T(8,128)(2,1)S(1)}, bf16[384,2048]{1,0:T(8,128)(2,1)S(1)}, u32[]{:S(2)}, u32[]{:S(2)}) collective-permute-start(bf16[384,2048]{1,0:T(8,128)(2,1)S(1)} %slice_bitcast_fusion), channel_id=1, source_target_pairs={{0,1},{1,0},{2,3},{3,2},{4,5},{5,4},{6,7},{7,6},{8,9},{9,8},{10,11... | collective-permute-start | bytes 4718600 | tf_op jit(solution)/shard_map/ppermute | solution.py:369
  209.0 3.7 %collective-permute-start.2 = (f32[384,1]{1,0:T(8,128)S(1)}, f32[384,1]{1,0:T(8,128)S(1)}, u32[]{:S(2)}, u32[]{:S(2)}) collective-permute-start(f32[384,1]{1,0:T(8,128)S(1)} %get-tuple-element.20), channel_id=1, source_target_pairs={{0,1},{1,0},{2,3},{3,2},{4,5},{5,4},{6,7},{7,6},{8,9},{9,8},{10,11... | collective-permute-start | bytes 4616 | tf_op jit(solution)/shard_map/ppermute | solution.py:369
  214.5 50.4 %all-to-all-start.3 = ((bf16[16,24,2048]{2,1,0:T(8,128)(2,1)}), bf16[16,24,2048]{2,1,0:T(8,128)(2,1)S(1)}, u32[]{:S(2)}, u32[]{:S(2)}) async-start(bf16[16,24,2048]{2,1,0:T(8,128)(2,1)} %bitcast.38), calls=%async_computation.3 | async-start | bytes 3145728 | tf_op jit(solution)/shard_map/all_to_all | solution.py:429
  264.0 2.6 copy-start.1
Sparse Core Ops, SparseCore 0:
  78.7 48.8 all-gather.2

commit v2 on v1

v2 whole, which is shorter than its diff:
```python
import functools

import jax
import jax.numpy as jnp
from jax import lax
from jax.experimental import pallas as pl
from jax.experimental.pallas import tpu as pltpu
from jax.sharding import PartitionSpec as P

INNER = 4096
HEADDIM = 128
HEADS = 32
NS = 64
EXPERTS = 8
CAP = 24
PAIR = 256
PACK = 256
CHUNKS = 2
VMEM_BYTES = 40 * 1024 * 1024

f32 = jnp.float32
bf16 = jnp.bfloat16


def params():
    return pltpu.CompilerParams(vmem_limit_bytes=VMEM_BYTES)


def mask(condition):
    return condition.astype(f32).astype(bf16)


def iota(shape, dim):
    return lax.broadcasted_iota(jnp.int32, shape, dim)


def route(ids_row):
    rows = ids_row.shape[1]
    ids = jnp.broadcast_to(ids_row.astype(f32), (rows, rows)).T
    onehot = (ids == iota((rows, rows), 1).astype(f32)).astype(f32)
    lower = mask(iota((rows, rows), 1) < iota((rows, rows), 0))
    before = jnp.dot(lower, onehot.astype(bf16), preferred_element_type=f32)
    return ids, jnp.sum(before * onehot, axis=1, keepdims=True)


def dispatch_kernel(slices, bias_ref, ids_ref, tok_ref, bcd_ref, *outs):
    pack_ref, out_refs = outs[0], outs[1:]
    rows, width = tok_ref.shape
    depth = width // slices
    ids, slot = route(ids_ref[...])
    pick = mask(ids[:, :1] * CAP + slot == iota((rows, EXPERTS * CAP), 1).astype(f32))
    part = depth // CHUNKS
    step = min(512, part)
    for k in range(CHUNKS):
        for c in range(0, part, step):
            got = [
                lax.dot_general(
                    pick,
                    tok_ref[:, s * depth + k * part + c : s * depth + k * part + c + step],
                    (((0,), (0,)), ((), ())),
                    preferred_element_type=f32,
                )
                for s in range(slices)
            ]
            for e in range(EXPERTS):
                piece = jnp.concatenate([g[e * CAP : (e + 1) * CAP] for g in got], axis=0)
                out_refs[k][e * slices * CAP : (e + 1) * slices * CAP, c : c + step] = (
                    piece.astype(bf16)
                )

    across = (((1,), (1,)), ((), ()))
    tok = tok_ref[...]
    pack_ref[:, : 2 * NS] = lax.dot_general(
        tok, bcd_ref[: 2 * NS, :], across, preferred_element_type=f32
    ).astype(bf16)
    steps = bcd_ref[2 * NS : 2 * NS + HEADS, :]
    raw = lax.dot_general(
        tok, jnp.concatenate([steps] * 4, axis=0), across, preferred_element_type=f32
    )
    lane = iota((rows, 128), 1)
    for h in range(HEADS):
        raw = raw + jnp.where(lane % HEADS == h, bias_ref[h], 0.0)
    steps_dt = jnp.maximum(raw, 0.0) + jnp.log1p(jnp.exp(-jnp.abs(raw)))
    coarse = steps_dt.astype(bf16).astype(f32)
    side = jnp.where(lane < HEADS, coarse, steps_dt - coarse)
    side = jnp.where(lane == 2 * HEADS, ids, jnp.where(lane == 2 * HEADS + 1, slot, side))
    pack_ref[:, 2 * NS :] = jnp.where(lane < 2 * HEADS + 2, side, 0.0).astype(bf16)


def dispatch(bias, ids_row, tokens, bcd, slices):
    rows, width = tokens.shape
    vmem = pl.BlockSpec(memory_space=pltpu.VMEM)
    out = jax.ShapeDtypeStruct((EXPERTS * slices * CAP, width // slices // CHUNKS), bf16)
    return pl.pallas_call(
        functools.partial(dispatch_kernel, slices),
        out_shape=(jax.ShapeDtypeStruct((rows, PACK), bf16),) + (out,) * CHUNKS,
        in_specs=[pl.BlockSpec(memory_space=pltpu.SMEM), vmem, vmem, vmem],
        compiler_params=params(),
        name="dispatch",
    )(bias, ids_row, tokens, bcd)


def in_kernel(count, width, last, place_ref, *refs):
    rows_refs, w_refs, out_ref = refs[:count], refs[count : 2 * count], refs[-1]
    total = refs[2 * count][...] if last else None
    for r in range(count):
        part = jnp.dot(rows_refs[r][...], w_refs[r][...], preferred_element_type=f32)
        total = part if total is None else total + part
    if not last:
        out_ref[...] = total
        return
    for j in range(out_ref.shape[0]):
        out_ref[j] = total[:, j * width : (j + 1) * width].astype(bf16)


def in_projection(place, pieces, w_in, chunk, width=None, total=None, at=None):
    slices = len(pieces)
    rows, depth = pieces[0].shape
    in_dev = w_in.shape[1]
    last = total is not None
    span = EXPERTS * width if last else in_dev
    tile = min(256, span)
    first = at * (span // tile) if last else 0

    def w_spec(r):
        return pl.BlockSpec(
            (depth, tile),
            lambda n, place_ref: (
                (place_ref[0] - r + slices) % slices * CHUNKS + chunk,
                first + n,
            ),
        )

    in_specs = [pl.BlockSpec((rows, depth), lambda n, place_ref: (0, 0))] * slices
    in_specs += [w_spec(r) for r in range(slices)]
    operands = [*pieces, *([w_in] * slices)]
    if last:
        in_specs.append(pl.BlockSpec((rows, tile), lambda n, place_ref: (0, first + n)))
        operands.append(total)
        out_shape = jax.ShapeDtypeStruct((EXPERTS, rows, width), bf16)
        out_spec = pl.BlockSpec((tile // width, rows, width), lambda n, place_ref: (n, 0, 0))
    else:
        out_shape = jax.ShapeDtypeStruct((rows, in_dev), f32)
        out_spec = pl.BlockSpec((rows, tile), lambda n, place_ref: (0, n))
    return pl.pallas_call(
        functools.partial(in_kernel, slices, width, last),
        out_shape=out_shape,
        grid_spec=pltpu.PrefetchScalarGridSpec(
            num_scalar_prefetch=1,
            grid=(span // tile,),
            in_specs=in_specs,
            out_specs=out_spec,
        ),
        compiler_params=params(),
        cost_estimate=pl.CostEstimate(
            flops=2 * rows * slices * depth * span,
            bytes_accessed=2 * slices * depth * (span + rows) + 4 * rows * span,
            transcendentals=0,
        ),
        name="in_finish" if last else "in_begin",
    )(place, *operands)


def prep_kernel(heads, head_ref, rate_ref, skip_ref, pack_ref, w_ref, c_ref, b_ref, a_ref):
    pack = pack_ref[...]
    row = iota((128, PACK), 0)
    lane = iota((128, PACK), 1)
    choose = jnp.where(lane == 2 * NS + 2 * HEADS, 2.0 * CAP, 0.0)
    choose = choose + jnp.where(lane == 2 * NS + 2 * HEADS + 1, 1.0, 0.0)
    choose = jnp.where(row == heads, choose, 0.0)
    rate = jnp.zeros((128, PAIR), f32)
    for h in range(heads):
        at = lane - 2 * NS - head_ref[h]
        choose = jnp.where((row == h) & ((at == 0) | (at == HEADS)), 1.0, choose)
        rate = jnp.where(iota((128, PAIR), 0) == h, rate_ref[head_ref[h]], rate)
    across = lax.dot_general(
        choose.astype(bf16), pack, (((1,), (1,)), ((), ())), preferred_element_type=f32
    )
    upto = iota((PAIR, PAIR), 0)
    now = iota((PAIR, PAIR), 1)
    running = jnp.dot(
        -across * rate,
        (upto <= now).astype(f32),
        precision=lax.Precision.HIGHEST,
        preferred_element_type=f32,
    )
    second = iota((1, PAIR), 1) >= PAIR // 2
    column = across[heads : heads + 1] + jnp.where(second, float(CAP), 0.0)
    slots = 2 * CAP * EXPERTS
    place_t = mask(iota((slots, PAIR), 0).astype(f32) == column)
    down = running.T
    b_rows = pack[:, :NS]
    c_rows = pack[:, NS : 2 * NS]
    scores = lax.dot_general(
        c_rows, b_rows, (((1,), (1,)), ((), ())), preferred_element_type=f32
    )
    causal = upto >= now
    diagonal = upto == now
    b_cols = b_rows.astype(f32).T
    c_wide = c_rows.astype(f32)
    for h in range(heads):
        run_row = running[h : h + 1]
        run_col = down[:, h : h + 1]
        dt_row = across[h : h + 1]
        last = run_row[:, PAIR - 1 : PAIR]
        gap = jnp.where(causal, run_col - run_row, 0.0)
        weights = jnp.where(causal, jnp.exp(gap) * scores * dt_row, 0.0)
        weights = weights + jnp.where(diagonal, skip_ref[head_ref[h]], 0.0)
        half = jnp.dot(place_t, weights.astype(bf16), preferred_element_type=f32).astype(bf16)
        w_ref[h, 0] = lax.dot_general(
            half, place_t, (((1,), (1,)), ((), ())), preferred_element_type=f32
        ).astype(bf16)
        c_now = (c_wide * jnp.exp(run_col)).astype(bf16)
        c_ref[h, 0] = jnp.dot(place_t, c_now, preferred_element_type=f32).astype(bf16)
        b_now = (b_cols * (jnp.exp(last - run_row) * dt_row)).astype(bf16)
        b_ref[h, 0] = lax.dot_general(
            b_now, place_t, (((1,), (1,)), ((), ())), preferred_element_type=f32
        ).astype(bf16)
        a_ref[h, 0] = jnp.broadcast_to(jnp.exp(last), (8, 128))


def prepare(own_heads, rate, skip, pack):
    heads = own_heads.shape[0]
    pairs = pack.shape[0] // PAIR
    slots = 2 * CAP * EXPERTS
    smem = pl.BlockSpec(memory_space=pltpu.SMEM)

    def block(*dims):
        return pl.BlockSpec((heads, 1, *dims), lambda p: (0, p, 0, 0))

    return pl.pallas_call(
        functools.partial(prep_kernel, heads),
        out_shape=(
            jax.ShapeDtypeStruct((heads, pairs, slots, slots), bf16),
            jax.ShapeDtypeStruct((heads, pairs, slots, NS), bf16),
            jax.ShapeDtypeStruct((heads, pairs, NS, slots), bf16),
            jax.ShapeDtypeStruct((heads, pairs, 8, 128), f32),
        ),
        grid=(pairs,),
        in_specs=[smem, smem, smem, pl.BlockSpec((PAIR, PACK), lambda p: (p, 0))],
        out_specs=(block(slots, slots), block(slots, NS), block(NS, slots), block(8, 128)),
        compiler_params=params(),
        cost_estimate=pl.CostEstimate(
            flops=4 * heads * pairs * slots * slots * PAIR,
            bytes_accessed=2 * heads * pairs * slots * slots,
            transcendentals=heads * pairs * PAIR * PAIR,
        ),
        name="scan_weights",
    )(own_heads, rate, skip, pack)


def scan_kernel(x_ref, w_ref, c_ref, b_ref, a_ref, gain_ref, out_ref, last_ref, state):
    @pl.when(pl.program_id(0) == 0)
    def _():
        state[...] = jnp.zeros_like(state)

    experts, rows, width = x_ref.shape
    x = x_ref[...].reshape(experts * rows, width)
    before = state[...]
    y = jnp.dot(w_ref[0, 0], x, preferred_element_type=f32) + jnp.dot(
        c_ref[0, 0], before.astype(bf16), preferred_element_type=f32
    )
    after = before * a_ref[0, 0, 0:1, 0:1] + jnp.dot(
        b_ref[0, 0], x, preferred_element_type=f32
    )
    state[...] = after
    last_ref[...] = after
    out_ref[...] = (y * gain_ref[...]).astype(bf16).reshape(experts, rows, width)


def scan(x, weights, gain, h):
    experts, rows, width = x.shape
    pairs = rows // (2 * CAP)
    slots = 2 * CAP * EXPERTS

    def block(*dims):
        return pl.BlockSpec((1, 1, *dims), lambda p: (h, p, 0, 0))

    return pl.pallas_call(
        scan_kernel,
        out_shape=(
            jax.ShapeDtypeStruct(x.shape, bf16),
            jax.ShapeDtypeStruct((NS, width), f32),
        ),
        grid=(pairs,),
        in_specs=[
            pl.BlockSpec((experts, 2 * CAP, width), lambda p: (0, p, 0)),
            block(slots, slots),
            block(slots, NS),
            block(NS, slots),
            block(8, 128),
            pl.BlockSpec((1, width), lambda p: (0, 0)),
        ],
        out_specs=(
            pl.BlockSpec((experts, 2 * CAP, width), lambda p: (0, p, 0)),
            pl.BlockSpec((NS, width), lambda p: (0, 0)),
        ),
        scratch_shapes=[pltpu.VMEM((NS, width), f32)],
        compiler_params=params(),
        cost_estimate=pl.CostEstimate(
            flops=2 * pairs * slots * (slots + 2 * NS) * width,
            bytes_accessed=2 * pairs * slots * slots,
            transcendentals=0,
        ),
        name="scan",
    )(x, *weights, gain)


def chunk_product(z_ref, w_ref):
    owners, rows, width = z_ref.shape
    group = max(1, min(owners, 256 // width)) if width % 128 == 0 else 1
    total = None
    for j in range(0, owners, group):
        z = z_ref[j]
        if group > 1:
            z = jnp.concatenate([z_ref[j + i] for i in range(group)], axis=1)
        part = jnp.dot(
            z, w_ref[j * width : (j + group) * width, :], preferred_element_type=f32
        )
        total = part if total is None else total + part
    return total


def chunk_squares(z_ref, inverse_ref):
    owners, rows, width = z_ref.shape
    total = jnp.zeros((rows, 1), f32)
    for j in range(owners):
        z = z_ref[j].astype(f32) * inverse_ref[:, j * width : (j + 1) * width]
        total = total + jnp.sum(z * z, axis=1, keepdims=True)
    return total


def out_begin_kernel(place_ref, z_ref, w_ref, inverse_ref, out_ref, square_ref):
    @pl.when(pl.program_id(0) == 0)
    def _():
        square_ref[...] = chunk_squares(z_ref, inverse_ref)

    out_ref[0] = chunk_product(z_ref, w_ref)


def out_send_kernel(
    chunked, first, place_ref, z_ref, w_ref, inverse_ref, *refs
):
    refs = list(refs)
    total_ref, before_ref = (refs.pop(0), refs.pop(0)) if chunked else (None, None)
    out_ref = refs.pop(0)
    if first:
        square_ref = refs.pop(0)

        @pl.when(pl.program_id(0) == 0)
        def _():
            squares = chunk_squares(z_ref, inverse_ref)
            square_ref[...] = squares + before_ref[...] if chunked else squares

    total = chunk_product(z_ref, w_ref)
    if chunked:
        total = total + total_ref[0]
    out_ref[0] = total.astype(bf16)


def out_finish_kernel(chunked, others, place_ref, z_ref, w_ref, square_ref, *refs):
    refs = list(refs)
    total_ref = refs.pop(0) if chunked else None
    part_refs, square_refs, out_ref = refs[:others], refs[others : 2 * others], refs[-1]
    total = chunk_product(z_ref, w_ref)
    if chunked:
        total = total + total_ref[0]
    squares = square_ref[...]
    for part, square in zip(part_refs, square_refs):
        total = total + part[...].astype(f32)
        squares = squares + square[...]
    out_ref[...] = (total * lax.rsqrt(squares / INNER + 1e-05)).astype(bf16)


def out_call(kernel, place, operands, extra, row_block, span, shape, z, w_out, name):
    owners, rows, width = z.shape
    depth = owners * width
    slices, first, count, chunk = span
    slice_width = w_out.shape[1] // slices
    part = slice_width if chunk is None else slice_width // CHUNKS
    tile = min(512, part)
    tiles = part // tile
    offset = 0 if chunk is None else chunk * tiles
    whole = slice_width // tile

    def column(n, place_ref):
        return (place_ref[0] + first + n // tiles) % slices * whole + offset + n % tiles

    fixed = lambda *dims: pl.BlockSpec(dims, lambda n, place_ref: (0,) * len(dims))
    specs = [
        fixed(owners, rows, width),
        pl.BlockSpec((depth, tile), lambda n, place_ref: (row_block, column(n, place_ref))),
    ]
    for kind, _ in operands:
        if kind == "fixed":
            specs.append(fixed(*_.shape))
        elif kind == "total":
            specs.append(
                pl.BlockSpec(
                    (1, rows, tile),
                    lambda n, place_ref: (first - 1 + n // tiles, 0, offset + n % tiles),
                )
            )
        else:
            specs.append(pl.BlockSpec((rows, tile), lambda n, place_ref: (0, n)))
    if shape == 3:
        out_shape = [jax.ShapeDtypeStruct((count, rows, part), f32 if extra == "begin" else bf16)]
        out_specs = [
            pl.BlockSpec((1, rows, tile), lambda n, place_ref: (n // tiles, 0, n % tiles))
        ]
    else:
        out_shape = [jax.ShapeDtypeStruct((rows, part), bf16)]
        out_specs = [pl.BlockSpec((rows, tile), lambda n, place_ref: (0, n))]
    if extra is not None:
        out_shape.append(jax.ShapeDtypeStruct((rows, 1), f32))
        out_specs.append(fixed(rows, 1))
    return pl.pallas_call(
        kernel,
        out_shape=out_shape,
        grid_spec=pltpu.PrefetchScalarGridSpec(
            num_scalar_prefetch=1, grid=(count * tiles,), in_specs=specs, out_specs=out_specs
        ),
        compiler_params=params(),
        cost_estimate=pl.CostEstimate(
            flops=2 * rows * depth * count * part,
            bytes_accessed=2 * depth * count * part + 4 * rows * count * part,
            transcendentals=0,
        ),
        name=name,
    )(place, z, w_out, *[a for _, a in operands])


def collect_kernel(slices, ids_ref, *refs):
    chunk_refs, out_ref = refs[:-1], refs[-1]
    count, part = chunk_refs[0].shape
    rows = ids_ref.shape[1]
    depth = part * len(chunk_refs)
    step = min(512, part)
    ids, slot = route(ids_ref[...])
    at = ids[:, :1] * (slices * CAP) + slot
    lane = iota((rows, count), 1).astype(f32)
    for s in range(slices):
        pick = mask(at + s * CAP == lane)
        for k, rows_ref in enumerate(chunk_refs):
            for c in range(0, part, step):
                start = s * depth + k * part + c
                out_ref[:, start : start + step] = jnp.dot(
                    pick, rows_ref[:, c : c + step], preferred_element_type=f32
                ).astype(bf16)


def collect(ids_row, chunks, slices):
    width = sum(c.shape[1] for c in chunks) * slices
    return pl.pallas_call(
        functools.partial(collect_kernel, slices),
        out_shape=jax.ShapeDtypeStruct((ids_row.shape[1], width), bf16),
        compiler_params=params(),
        name="collect",
    )(ids_row, *chunks)


def turn(a, n, slices, r):
    return lax.ppermute(
        a, "expert", [(d, d // slices * slices + (d + r) % slices) for d in range(n)]
    )


def swap(a, groups=None):
    return lax.all_to_all(
        a, "expert", split_axis=0, concat_axis=0, axis_index_groups=groups, tiled=True
    )


def shards(
    tokens, w_in, w_out, w_bcd, dt_bias, decay_rate, skip_gain, norm_gain, expert_ids, decode_heads
):
    n = lax.axis_size("expert")
    slices = n // EXPERTS
    in_dev = w_in.shape[2]
    width = min(HEADDIM, in_dev // EXPERTS)
    heads = in_dev // EXPERTS // width
    span = EXPERTS * width
    me = lax.axis_index("expert")
    place = (me % slices).astype(jnp.int32)
    owner = (me // slices).astype(jnp.int32)
    place_arr = place.reshape(1)
    starts = [place * in_dev + h * span + owner * width for h in range(heads)]
    same_slice = [[j * slices + s for j in range(EXPERTS)] for s in range(slices)]
    ids_row = expert_ids.reshape(1, -1)
    w_in, w_out = w_in[0], w_out[0]

    pack, *outgoing = dispatch(dt_bias, ids_row, tokens, w_bcd.T, slices)
    pack = lax.all_gather(pack, "expert", axis=0, tiled=True)
    landed = [swap(o) for o in outgoing]

    def with_turned(a):
        return [a] + [turn(a, n, slices, r) for r in range(1, slices)]

    begun = in_projection(place_arr, with_turned(landed[0]), w_in, 0)
    landed[1], pack = lax.optimization_barrier((landed[1], pack))
    own_heads = jnp.stack(starts) // HEADDIM
    weights = prepare(own_heads.astype(jnp.int32), decay_rate, skip_gain, pack)
    pieces = with_turned(landed[1])
    x = [
        swap(in_projection(place_arr, pieces, w_in, 1, width, begun, h), same_slice)
        for h in range(heads)
    ]

    z, states = [], []
    for h in range(heads):
        gain = lax.dynamic_slice(norm_gain, (starts[h],), (width,)).reshape(1, width)
        rows, state = scan(x[h], weights, gain, h)
        z.append(swap(rows, same_slice))
        states.append(state)
    states = lax.all_gather(jnp.stack(states), "expert", axis=0, tiled=False)

    inverse = 1.0 / lax.dynamic_slice(norm_gain, (place * in_dev,), (in_dev,))
    inverse = [inverse[h * span : (h + 1) * span].reshape(1, span) for h in range(heads)]
    chunked = heads > 1
    total = squares = None
    for h in range(heads - 1):
        total, squares = out_call(
            out_begin_kernel,
            place_arr,
            [("fixed", inverse[h])],
            "begin",
            h,
            (slices, 1, slices, None),
            3,
            z[h],
            w_out,
            "out_begin",
        )
    h = heads - 1
    sent = []
    for k in range(CHUNKS):
        operands = [("fixed", inverse[h])]
        if chunked:
            operands += [("total", total), ("fixed", squares)]
        got = out_call(
            functools.partial(out_send_kernel, chunked, k == 0),
            place_arr,
            operands,
            "send" if k == 0 else None,
            h,
            (slices, 1, slices - 1, k),
            3,
            z[h],
            w_out,
            "out_send",
        )
        if k == 0:
            all_squares = got[1]
            others = [turn(all_squares, n, slices, r) for r in range(1, slices)]
        sent.append([turn(got[0][r - 1], n, slices, r) for r in range(1, slices)])
    back = []
    for k in range(CHUNKS):
        operands = [("fixed", all_squares)]
        if chunked:
            operands.append(("total", total))
        operands += [("part", a) for a in sent[k]] + [("fixed", a) for a in others]
        [done] = out_call(
            functools.partial(out_finish_kernel, chunked, slices - 1),
            place_arr,
            operands,
            None,
            h,
            (slices, slices, 1, k),
            2,
            z[h],
            w_out,
            "out_finish",
        )
        if k == CHUNKS - 1:
            done, states = lax.optimization_barrier((done, states))
        back.append(swap(done))
    mixed = collect(ids_row, back, slices)

    start = decode_heads[0] * HEADDIM
    within = start % in_dev // width
    states = states.reshape(EXPERTS, slices, heads, NS, width)
    chosen = lax.dynamic_slice(
        states,
        (within % EXPERTS, start // in_dev, within // EXPERTS, 0, 0),
        (HEADDIM // width, 1, 1, NS, width),
    )
    chosen = chosen.reshape(HEADDIM // width, NS, width).transpose(0, 2, 1)
    return (mixed, chosen.reshape(1, HEADDIM * NS))


def solution(mesh):
    in_specs = (
        P(("groups", "expert"), None),
        P("expert", None, None),
        P("expert", None, None),
        P(),
        P(),
        P(),
        P(),
        P(),
        P(("groups", "expert"), None),
        P("expert"),
    )
    out_specs = (P(("groups", "expert"), None), P(("groups", "expert"), None))
    return jax.shard_map(shards, mesh=mesh, in_specs=in_specs, out_specs=out_specs, check_vma=False)
```

time: 276 us -> 272 us (0.986)
  blocking collectives: 88.4 us -> 0 us
  starting transfers between devices: 13.4 us -> 41.4 us
  waiting for transfers between devices: 93.3 us -> 118 us
  local copies, waits for them, and re-layouts: 11.2 us -> 30.1 us
  Pallas kernels: 48.6 us -> 65.5 us
    all_to_all x3 -> x8, waiting for transfers between devices: 37.6 us -> 94.2 us  [swap(): lax.all_to_all(a, 'expert', split_axis=0, concat_axis=0, axis_index_group...]
    all_gather x1, waiting for transfers between devices: 51 us -> 0.01 us  [shards(): pack = lax.all_gather(pack, 'expert', axis=0, tiled=True)]
    all_gather x1 -> x0, blocking collectives: 45.1 us -> none  [shards(): states = lax.all_gather(state.astype(bf16), 'expert', axis=0, tiled=False)]
    all_to_all x1 -> x0, blocking collectives: 43.3 us -> none  [shards(): lax.all_to_all(outgoing, 'expert', split_axis=0, concat_axis=0, tiled=True)]
    all_to_all x3 -> x8, starting transfers between devices: 12 us -> 39.6 us  [swap(): lax.all_to_all(a, 'expert', split_axis=0, concat_axis=0, axis_index_group...]
    all_gather x0 -> x1, waiting for transfers between devices: none -> 19.4 us  [shards(): states = lax.all_gather(jnp.stack(states), 'expert', axis=0, tiled=False)]
    unnamed x31 -> x51, local copies, waits for them, and re-layouts: 9.3 us -> 28.5 us
    pallas_call x3 -> x10, Pallas kernels: 31.9 us -> 47 us  [the longest x5 21.5 us: out_call(): pl.pallas_call(kernel, out_shape=out_shape, grid_spec=pltpu.PrefetchScala...]
  transfers between devices with their start and end apart: 7 -> 15, of which waited for: 4 -> 9; matrix products, arithmetic and copies ran while one was open for 1% -> 1% of each run, Pallas kernels for 5% -> 19%
where the time goes in v2:
time: 272 us; the launch traced here: 270 us
  waiting for transfers between devices  118 us (43%)
  Pallas kernels  65.5 us (24%)
  starting transfers between devices  41.4 us (15%)
  local copies, waits for them, and re-layouts  30.1 us (11%)
  between operations  15 us (6%)
    all_to_all x8, waiting for transfers between devices, swap(): lax.all_to_all(a, 'expert', split_axis=0, concat_axis=0, axis_index_group...  94.2 us
    all_to_all x8, starting transfers between devices, swap(): lax.all_to_all(a, 'expert', split_axis=0, concat_axis=0, axis_index_group...  39.6 us
    unnamed x51, local copies, waits for them, and re-layouts  28.5 us
    pallas_call x5, Pallas kernels, out_call(): pl.pallas_call(kernel, out_shape=out_shape, grid_spec=pltpu.PrefetchScala...  21.5 us
    all_gather x1, waiting for transfers between devices, shards(): states = lax.all_gather(jnp.stack(states), 'expert', axis=0, tiled=False)  19.4 us
    pallas_call x3, Pallas kernels, in_projection(): pl.pallas_call(functools.partial(in_kernel, slices, width, last), out_sha...  17.9 us
    pallas_call x1, Pallas kernels, prepare(): pl.pallas_call(functools.partial(prep_kernel, heads), out_shape=(jax.Shap...  13.3 us
    pallas_call x2, Pallas kernels, scan(): pl.pallas_call(scan_kernel, out_shape=(jax.ShapeDtypeStruct(x.shape, bf16...  7.54 us
  transfers between devices with their start and end apart: 15, of which 9 were waited for; matrix products, arithmetic and copies ran while one was open for 1% of the time, Pallas kernels for 19%

profile of v2, /device:TPU:0, one launch (start us, length us, event | category | flops | bytes accessed | tf_op | source)
XLA Modules:
  0.0 270.3 jit_solution(2476160019128676539)
XLA Ops:
  11.0 3.2 %dispatch.1 = (bf16[128,256]{1,0:T(8,128)(2,1)}, bf16[384,1024]{1,0:T(8,128)(2,1)}, bf16[384,1024]{1,0:T(8,128)(2,1)}) custom-call(f32[32]{0:T(128)S(1)} %copy-done.20, s32[1,128]{1,0:T(1,128)S(1)} %bitcast.42, bf16[128,4096]{1,0:T(8,128)(2,1)S(1)} %copy-done.13, bf16[160,4096]{1,0:T(8,128)(2,1)S(1)} %bitcast.35), custom_call_target="tpu_custom_call" | custom-call | tf_op jit(solution)/shard_map/dispatch/pallas_call | solution.py:94
  14.2 7.4 %all-to-all-start.1 = ((bf16[16,24,1024]{2,1,0:T(8,128)(2,1)}), bf16[16,24,1024]{2,1,0:T(8,128)(2,1)S(1)}, u32[]{:S(2)}, u32[]{:S(2)}) async-start(bf16[16,24,1024]{2,1,0:T(8,128)(2,1)} %bitcast.6), calls=%async_computation.1 | async-start | bytes 1572864 | tf_op jit(solution)/shard_map/all_to_all | solution.py:469
  22.3 18.6 %all-to-all-done.1 = bf16[16,24,1024]{2,1,0:T(8,128)(2,1)S(1)} async-done(((bf16[16,24,1024]{2,1,0:T(8,128)(2,1)}), bf16[16,24,1024]{2,1,0:T(8,128)(2,1)S(1)}, u32[]{:S(2)}, u32[]{:S(2)}) %all-to-all-start.1) | async-done | bytes 786464 | tf_op jit(solution)/shard_map/all_to_all | solution.py:469
  40.9 6.4 %all-to-all-start = ((bf16[16,24,1024]{2,1,0:T(8,128)(2,1)}), bf16[16,24,1024]{2,1,0:T(8,128)(2,1)}, u32[]{:S(2)}, u32[]{:S(2)}) async-start(bf16[16,24,1024]{2,1,0:T(8,128)(2,1)} %bitcast.3), calls=%async_computation | async-start | bytes 1572864 | tf_op jit(solution)/shard_map/all_to_all | solution.py:469
  47.6 22.6 %all-to-all-done = bf16[16,24,1024]{2,1,0:T(8,128)(2,1)} async-done(((bf16[16,24,1024]{2,1,0:T(8,128)(2,1)}), bf16[16,24,1024]{2,1,0:T(8,128)(2,1)}, u32[]{:S(2)}, u32[]{:S(2)}) %all-to-all-start) | async-done | bytes 786464 | tf_op jit(solution)/shard_map/all_to_all | solution.py:469
  73.7 8.1 %in_begin.1.refs_4_ = f32[384,2048]{1,0:T(8,128)S(1)} custom-call(s32[1]{0:T(128)} %bitcast.1.place_ref, bf16[384,1024]{1,0:T(8,128)(2,1)S(1)} %bitcast.34, bf16[384,1024]{1,0:T(8,128)(2,1)S(1)} %copy-done.17, bf16[4096,2048]{1,0:T(8,128)(2,1)} %bitcast.44, bf16[4096,2048]{1,0:T(8,128)(2,1)} %bitcast.45), custom_call_target="tpu_custom_call" | custom-call | flops 3221225472 | bytes 13107200 | tf_op jit(solution)/shard_map/in_begin/pallas_call | solution.py:145
  81.8 4.9 %in_finish.3 = bf16[8,384,128]{2,1,0:T(8,128)(2,1)S(1)} custom-call(s32[1]{0:T(128)} %bitcast.1.place_ref, bf16[384,1024]{1,0:T(8,128)(2,1)} %bitcast.4.refs_0_, bf16[384,1024]{1,0:T(8,128)(2,1)} %collective-permute-done.refs_1_, bf16[4096,2048]{1,0:T(8,128)(2,1)} %bitcast.46, bf16[4096,2048]{1,0:T(8,128)(2,1)} %bitcast.47, f32[384,2048]{1,0:T(8,128)S(1)} %in_begin.1.refs_4_), custom_call_target="tpu_custom_call" | custom-call | flops 1610612736 | bytes 7340032 | tf_op jit(solution)/shard_map/in_finish/pallas_call | solution.py:145
  87.6 5.4 %all-to-all-start.4 = ((bf16[8,384,128]{2,1,0:T(8,128)(2,1)}), bf16[8,384,128]{2,1,0:T(8,128)(2,1)}, u32[]{:S(2)}, u32[]{:S(2)}) async-start(bf16[8,384,128]{2,1,0:T(8,128)(2,1)} %copy-done.11), calls=%async_computation.4 | async-start | bytes 1572864 | tf_op jit(solution)/shard_map/all_to_all | solution.py:469
  93.0 4.9 %in_finish.2 = bf16[8,384,128]{2,1,0:T(8,128)(2,1)S(1)} custom-call(s32[1]{0:T(128)} %bitcast.1.place_ref, bf16[384,1024]{1,0:T(8,128)(2,1)} %bitcast.4.refs_0_, bf16[384,1024]{1,0:T(8,128)(2,1)} %collective-permute-done.refs_1_, bf16[4096,2048]{1,0:T(8,128)(2,1)} %bitcast.48, bf16[4096,2048]{1,0:T(8,128)(2,1)} %bitcast.49, f32[384,2048]{1,0:T(8,128)S(1)} %in_begin.1.refs_4_), custom_call_target="tpu_custom_call" | custom-call | flops 1610612736 | bytes 7340032 | tf_op jit(solution)/shard_map/in_finish/pallas_call | solution.py:145
  98.8 14.9 %all-to-all-done.4.x_ref = bf16[8,384,128]{2,1,0:T(8,128)(2,1)} async-done(((bf16[8,384,128]{2,1,0:T(8,128)(2,1)}), bf16[8,384,128]{2,1,0:T(8,128)(2,1)}, u32[]{:S(2)}, u32[]{:S(2)}) %all-to-all-start.4) | async-done | bytes 786464 | tf_op jit(solution)/shard_map/all_to_all | solution.py:469
  113.6 3.6 %all-to-all-start.2 = ((bf16[8,384,128]{2,1,0:T(8,128)(2,1)}), bf16[8,384,128]{2,1,0:T(8,128)(2,1)S(1)}, u32[]{:S(2)}, u32[]{:S(2)}) async-start(bf16[8,384,128]{2,1,0:T(8,128)(2,1)} %copy-done.10), calls=%async_computation.2 | async-start | bytes 1572864 | tf_op jit(solution)/shard_map/all_to_all | solution.py:469
  118.6 13.3 %scan_weights.1 = (bf16[2,8,384,384]{3,2,1,0:T(8,128)(2,1)S(1)}, bf16[2,8,384,64]{3,2,1,0:T(8,128)(2,1)S(1)}, bf16[2,8,64,384]{3,2,1,0:T(8,128)(2,1)S(1)}, f32[2,8,8,128]{3,2,1,0:T(8,128)S(1)}) custom-call(s32[2]{0:T(128)S(1)} %and_select_fusion.head_ref, f32[32]{0:T(128)S(1)} %copy-done.22, f32[32]{0:T(128)S(1)} %copy-done.23, bf16[2048,256]{1,0:T(8,128)(2,1)S(1)} %copy-done.21), custom_call_target="tpu_custom_call" | custom-call | flops 2415919104 | bytes 4718592 | tf_op jit(solution)/shard_map/scan_weights/pallas_call | solution.py:231
  132.0 5.2 %scan.3 = (bf16[8,384,128]{2,1,0:T(8,128)(2,1)S(1)}, f32[64,128]{1,0:T(8,128)S(1)}) custom-call(bf16[8,384,128]{2,1,0:T(8,128)(2,1)} %all-to-all-done.4.x_ref, bf16[2,8,384,384]{3,2,1,0:T(8,128)(2,1)S(1)} %get-tuple-element.26.w_ref, bf16[2,8,384,64]{3,2,1,0:T(8,128)(2,1)S(1)} %get-tuple-element.27.c_ref, ...), custom_call_target="tpu_custom_call" | custom-call | flops 402653184 | bytes 2359296 | tf_op jit(solution)/shard_map/scan/pallas_call | solution.py:279
  140.3 6.0 %all-to-all-start.5 = ((bf16[8,384,128]{2,1,0:T(8,128)(2,1)}), bf16[8,384,128]{2,1,0:T(8,128)(2,1)S(1)}, u32[]{:S(2)}, u32[]{:S(2)}) async-start(bf16[8,384,128]{2,1,0:T(8,128)(2,1)} %copy-done.15), calls=%async_computation.5 | async-start | bytes 1572864 | tf_op jit(solution)/shard_map/all_to_all | solution.py:469
  146.3 2.3 copy-done.5
  149.7 2.4 scan.2
  153.0 13.1 %all-to-all-done.5.z_ref = bf16[8,384,128]{2,1,0:T(8,128)(2,1)S(1)} async-done(((bf16[8,384,128]{2,1,0:T(8,128)(2,1)}), bf16[8,384,128]{2,1,0:T(8,128)(2,1)S(1)}, u32[]{:S(2)}, u32[]{:S(2)}) %all-to-all-start.5) | async-done | bytes 786464 | tf_op jit(solution)/shard_map/all_to_all | solution.py:469
  166.1 3.5 %all-to-all-start.3 = ((bf16[8,384,128]{2,1,0:T(8,128)(2,1)}), bf16[8,384,128]{2,1,0:T(8,128)(2,1)S(1)}, u32[]{:S(2)}, u32[]{:S(2)}) async-start(bf16[8,384,128]{2,1,0:T(8,128)(2,1)} %copy-done.14), calls=%async_computation.3 | async-start | bytes 1572864 | tf_op jit(solution)/shard_map/all_to_all | solution.py:469
  169.8 8.9 %out_begin.1 = (f32[2,384,2048]{2,1,0:T(8,128)S(1)}, f32[384,1]{1,0:T(8,128)S(1)}) custom-call(s32[1]{0:T(128)} %bitcast.1.place_ref, bf16[8,384,128]{2,1,0:T(8,128)(2,1)S(1)} %all-to-all-done.5.z_ref, bf16[2048,4096]{1,0:T(8,128)(2,1)} %bitcast.50, f32[1,1024]{1,0:T(1,128)S(1)} %bitcast.41), custom_call_target="tpu_custom_call" | custom-call | flops 3221225472 | bytes 14680064 | tf_op jit(solution)/shard_map/out_begin/pallas_call | solution.py:417
  178.7 2.7 copy-done
  181.4 8.6 %all-to-all-done.3.z_ref = bf16[8,384,128]{2,1,0:T(8,128)(2,1)S(1)} async-done(((bf16[8,384,128]{2,1,0:T(8,128)(2,1)}), bf16[8,384,128]{2,1,0:T(8,128)(2,1)S(1)}, u32[]{:S(2)}, u32[]{:S(2)}) %all-to-all-start.3) | async-done | bytes 786464 | tf_op jit(solution)/shard_map/all_to_all | solution.py:469
  190.0 2.8 %copy-done.1 = f32[2,384,2048]{2,1,0:T(8,128)S(1)} copy-done((f32[2,384,2048]{2,1,0:T(8,128)S(1)}, f32[2,384,2048]{2,1,0:T(8,128)}, u32[]{:S(2)}) %copy-start.1) | copy-done | bytes 6291480
  192.8 3.6 %out_send.2 = (bf16[1,384,1024]{2,1,0:T(8,128)(2,1)}, f32[384,1]{1,0:T(8,128)S(1)}) custom-call(s32[1]{0:T(128)} %bitcast.1.place_ref, bf16[8,384,128]{2,1,0:T(8,128)(2,1)S(1)} %all-to-all-done.3.z_ref, bf16[2048,4096]{1,0:T(8,128)(2,1)} %bitcast.51, f32[1,1024]{1,0:T(1,128)S(1)} %bitcast.37, f32[2,384,2048]{2,1,0:T(8,128)S(1)} %copy-done.1, ...), custom_call_target="tpu_custom_call" | custom-call | flops 805306368 | bytes 3670016 | tf_op jit(solution)/shard_map/out_send/pallas_call | solution.py:417
  199.0 2.8 %copy-done.2 = f32[2,384,2048]{2,1,0:T(8,128)S(1)} copy-done((f32[2,384,2048]{2,1,0:T(8,128)S(1)}, f32[2,384,2048]{2,1,0:T(8,128)}, u32[]{:S(2)}) %copy-start.2) | copy-done | bytes 6291480
  201.8 3.2 %out_finish.2 = bf16[384,1024]{1,0:T(8,128)(2,1)} custom-call(s32[1]{0:T(128)} %bitcast.1.place_ref, bf16[8,384,128]{2,1,0:T(8,128)(2,1)S(1)} %all-to-all-done.3.z_ref, bf16[2048,4096]{1,0:T(8,128)(2,1)} %bitcast.52, f32[384,1]{1,0:T(8,128)S(1)} %get-tuple-element.34.square_ref, f32[2,384,2048]{2,1,0:T(8,128)S(1)} %copy-done.2, ...), custom_call_target="tpu_custom_call" | custom-call | flops 805306368 | bytes 3670016 | tf_op jit(solution)/shard_map/out_finish/pallas_call | solution.py:417
  205.0 3.6 %all-to-all-start.6 = ((bf16[16,24,1024]{2,1,0:T(8,128)(2,1)}), bf16[16,24,1024]{2,1,0:T(8,128)(2,1)S(1)}, u32[]{:S(2)}, u32[]{:S(2)}) async-start(bf16[16,24,1024]{2,1,0:T(8,128)(2,1)} %bitcast.16), calls=%async_computation.6 | async-start | bytes 1572864 | tf_op jit(solution)/shard_map/all_to_all | solution.py:469
  208.7 2.8 %copy-done.3 = f32[2,384,2048]{2,1,0:T(8,128)S(1)} copy-done((f32[2,384,2048]{2,1,0:T(8,128)S(1)}, f32[2,384,2048]{2,1,0:T(8,128)}, u32[]{:S(2)}) %copy-start.3) | copy-done | bytes 6291480
  211.5 2.5 out_send.3
  216.4 3.3 %out_finish.3 = bf16[384,1024]{1,0:T(8,128)(2,1)} custom-call(s32[1]{0:T(128)} %bitcast.1.place_ref, bf16[8,384,128]{2,1,0:T(8,128)(2,1)S(1)} %all-to-all-done.3.z_ref, bf16[2048,4096]{1,0:T(8,128)(2,1)} %bitcast.54, f32[384,1]{1,0:T(8,128)S(1)} %get-tuple-element.34.square_ref, f32[2,384,2048]{2,1,0:T(8,128)S(1)} %copy-done.3, ...), custom_call_target="tpu_custom_call" | custom-call | flops 805306368 | bytes 3670016 | tf_op jit(solution)/shard_map/out_finish/pallas_call | solution.py:417
  219.6 19.4 %all-gather.6.cloned.1.call-done = f32[32,64,128]{2,1,0:T(8,128)} async-done(((f32[2,64,128]{2,1,0:T(8,128)}), f32[32,64,128]{2,1,0:T(8,128)}) %all-gather.6.cloned.1.call-update) | async-done | bytes 1048592 | tf_op jit(solution)/shard_map/all_gather | solution.py:515
  239.1 3.7 %all-to-all-start.7 = ((bf16[16,24,1024]{2,1,0:T(8,128)(2,1)}), bf16[16,24,1024]{2,1,0:T(8,128)(2,1)S(1)}, u32[]{:S(2)}, u32[]{:S(2)}) async-start(bf16[16,24,1024]{2,1,0:T(8,128)(2,1)} %bitcast.22), calls=%async_computation.7 | async-start | bytes 1572864 | tf_op jit(solution)/shard_map/all_to_all | solution.py:469
  245.1 16.4 %all-to-all-done.7 = bf16[16,24,1024]{2,1,0:T(8,128)(2,1)S(1)} async-done(((bf16[16,24,1024]{2,1,0:T(8,128)(2,1)}), bf16[16,24,1024]{2,1,0:T(8,128)(2,1)S(1)}, u32[]{:S(2)}, u32[]{:S(2)}) %all-to-all-start.7) | async-done | bytes 786464 | tf_op jit(solution)/shard_map/all_to_all | solution.py:469
  (71 shorter events, 25.3 us)
Async XLA Ops:
  7.2 1.3 copy-start.12
  8.5 1.2 copy-start.13
  14.2 26.7 %all-to-all-start.1 = ((bf16[16,24,1024]{2,1,0:T(8,128)(2,1)}), bf16[16,24,1024]{2,1,0:T(8,128)(2,1)S(1)}, u32[]{:S(2)}, u32[]{:S(2)}) async-start(bf16[16,24,1024]{2,1,0:T(8,128)(2,1)} %bitcast.6), calls=%async_computation.1 | async-start | bytes 1572864 | tf_op jit(solution)/shard_map/all_to_all | solution.py:469
  21.6 48.6 %all-gather.4.cloned.1.call-start = ((), (), s32[]{:S(2)}) async-start(), calls=%async_computation.8 | async-start | bytes 1114112 | tf_op jit(solution)/shard_map/all_gather | solution.py:493
  40.9 30.5 %copy-start.6 = (bf16[16,24,1024]{2,1,0:T(8,128)(2,1)}, bf16[16,24,1024]{2,1,0:T(8,128)(2,1)S(1)}, u32[]{:S(2)}) copy-start(bf16[16,24,1024]{2,1,0:T(8,128)(2,1)S(1)} %all-to-all-done.1) | copy-start | bytes 2359300
  40.9 29.3 %all-to-all-start = ((bf16[16,24,1024]{2,1,0:T(8,128)(2,1)}), bf16[16,24,1024]{2,1,0:T(8,128)(2,1)}, u32[]{:S(2)}, u32[]{:S(2)}) async-start(bf16[16,24,1024]{2,1,0:T(8,128)(2,1)} %bitcast.3), calls=%async_computation | async-start | bytes 1572864 | tf_op jit(solution)/shard_map/all_to_all | solution.py:469
  47.3 23.2 %collective-permute-start.1 = (bf16[384,1024]{1,0:T(8,128)(2,1)S(1)}, bf16[384,1024]{1,0:T(8,128)(2,1)S(1)}, u32[]{:S(2)}, u32[]{:S(2)}) collective-permute-start(bf16[384,1024]{1,0:T(8,128)(2,1)S(1)} %bitcast.33), channel_id=1, source_target_pairs={{0,1},{1,0},{2,3},{3,2},{4,5},{5,4},{6,7},{7,6},{8,9},{9,8},{10,11... | collective-permute-start | bytes 2359304 | tf_op jit(solution)/shard_map/ppermute | solution.py:463
  70.2 11.6 %collective-permute-start = (bf16[384,1024]{1,0:T(8,128)(2,1)}, bf16[384,1024]{1,0:T(8,128)(2,1)}, u32[]{:S(2)}, u32[]{:S(2)}) collective-permute-start(bf16[384,1024]{1,0:T(8,128)(2,1)} %bitcast.4.refs_0_), channel_id=1, source_target_pairs={{0,1},{1,0},{2,3},{3,2},{4,5},{5,4},{6,7},{7,6},{8,9},{9,8},{10,11... | collective-permute-start | bytes 2359304 | tf_op jit(solution)/shard_map/ppermute | solution.py:463
  71.4 1.1 copy-start.7
  72.5 1.1 copy-start.17
  87.6 26.1 %all-to-all-start.4 = ((bf16[8,384,128]{2,1,0:T(8,128)(2,1)}), bf16[8,384,128]{2,1,0:T(8,128)(2,1)}, u32[]{:S(2)}, u32[]{:S(2)}) async-start(bf16[8,384,128]{2,1,0:T(8,128)(2,1)} %copy-done.11), calls=%async_computation.4 | async-start | bytes 1572864 | tf_op jit(solution)/shard_map/all_to_all | solution.py:469
  93.0 24.4 %copy-start.24 = (f32[4096]{0:T(1024)S(1)}, f32[4096]{0:T(1024)}, u32[]{:S(2)}) copy-start(f32[4096]{0:T(1024)} %param.17) | copy-start | bytes 49156
  93.0 24.4 %copy-start.22 = (f32[32]{0:T(128)S(1)}, f32[32]{0:T(128)}, u32[]{:S(2)}) copy-start(f32[32]{0:T(128)} %rate_ref.1) | copy-start | bytes 388
  93.0 24.4 %copy-start.23 = (f32[32]{0:T(128)S(1)}, f32[32]{0:T(128)}, u32[]{:S(2)}) copy-start(f32[32]{0:T(128)} %skip_ref.1) | copy-start | bytes 388
  113.6 26.6 %all-to-all-start.2 = ((bf16[8,384,128]{2,1,0:T(8,128)(2,1)}), bf16[8,384,128]{2,1,0:T(8,128)(2,1)S(1)}, u32[]{:S(2)}, u32[]{:S(2)}) async-start(bf16[8,384,128]{2,1,0:T(8,128)(2,1)} %copy-done.10), calls=%async_computation.2 | async-start | bytes 1572864 | tf_op jit(solution)/shard_map/all_to_all | solution.py:469
  117.4 1.2 copy-start.21
  132.0 8.3 %copy-start.8 = (bf16[2,8,64,384]{3,2,1,0:T(8,128)(2,1)}, bf16[2,8,64,384]{3,2,1,0:T(8,128)(2,1)S(1)}, u32[]{:S(2)}) copy-start(bf16[2,8,64,384]{3,2,1,0:T(8,128)(2,1)S(1)} %get-tuple-element.28.b_ref) | copy-start | bytes 2359300
  137.2 2.2 copy-start.4
  140.3 25.9 %all-to-all-start.5 = ((bf16[8,384,128]{2,1,0:T(8,128)(2,1)}), bf16[8,384,128]{2,1,0:T(8,128)(2,1)S(1)}, u32[]{:S(2)}, u32[]{:S(2)}) async-start(bf16[8,384,128]{2,1,0:T(8,128)(2,1)} %copy-done.15), calls=%async_computation.5 | async-start | bytes 1572864 | tf_op jit(solution)/shard_map/all_to_all | solution.py:469
  146.3 2.3 copy-start.5
  166.1 23.9 %all-to-all-start.3 = ((bf16[8,384,128]{2,1,0:T(8,128)(2,1)}), bf16[8,384,128]{2,1,0:T(8,128)(2,1)S(1)}, u32[]{:S(2)}, u32[]{:S(2)}) async-start(bf16[8,384,128]{2,1,0:T(8,128)(2,1)} %copy-done.14), calls=%async_computation.3 | async-start | bytes 1572864 | tf_op jit(solution)/shard_map/all_to_all | solution.py:469
  169.7 69.4 %all-gather.6.cloned.1.call-start = ((), (), s32[]{:S(2)}) async-start(), calls=%async_computation.9 | async-start | bytes 1114112 | tf_op jit(solution)/shard_map/all_gather | solution.py:515
  178.7 2.7 copy-start
  190.0 2.8 %copy-start.1 = (f32[2,384,2048]{2,1,0:T(8,128)S(1)}, f32[2,384,2048]{2,1,0:T(8,128)}, u32[]{:S(2)}) copy-start(f32[2,384,2048]{2,1,0:T(8,128)} %copy-done) | copy-start | bytes 18874372
  196.4 2.6 collective-permute-start.2
  197.1 1.9 collective-permute-start.3
  199.0 2.8 %copy-start.2 = (f32[2,384,2048]{2,1,0:T(8,128)S(1)}, f32[2,384,2048]{2,1,0:T(8,128)}, u32[]{:S(2)}) copy-start(f32[2,384,2048]{2,1,0:T(8,128)} %copy-done) | copy-start | bytes 18874372
  205.0 34.1 %all-to-all-start.6 = ((bf16[16,24,1024]{2,1,0:T(8,128)(2,1)}), bf16[16,24,1024]{2,1,0:T(8,128)(2,1)S(1)}, u32[]{:S(2)}, u32[]{:S(2)}) async-start(bf16[16,24,1024]{2,1,0:T(8,128)(2,1)} %bitcast.16), calls=%async_computation.6 | async-start | bytes 1572864 | tf_op jit(solution)/shard_map/all_to_all | solution.py:469
  208.7 2.8 %copy-start.3 = (f32[2,384,2048]{2,1,0:T(8,128)S(1)}, f32[2,384,2048]{2,1,0:T(8,128)}, u32[]{:S(2)}) copy-start(f32[2,384,2048]{2,1,0:T(8,128)} %copy-done) | copy-start | bytes 18874372
  214.0 47.5 %copy-start.19 = (s32[128,1]{0,1:T(1,128)S(1)}, s32[128,1]{0,1:T(1,128)}, u32[]{:S(2)}) copy-start(s32[128,1]{0,1:T(1,128)} %param.18) | copy-start | bytes 1540
  214.0 2.4 collective-permute-start.4
  239.1 22.4 %all-to-all-start.7 = ((bf16[16,24,1024]{2,1,0:T(8,128)(2,1)}), bf16[16,24,1024]{2,1,0:T(8,128)(2,1)S(1)}, u32[]{:S(2)}, u32[]{:S(2)}) async-start(bf16[16,24,1024]{2,1,0:T(8,128)(2,1)} %bitcast.22), calls=%async_computation.7 | async-start | bytes 1572864 | tf_op jit(solution)/shard_map/all_to_all | solution.py:469
  (8 other events, 6.9 us)
Sparse Core Ops, SparseCore 0:
  24.6 44.5 all-gather.3
  197.2 41.7 all-gather.5

commit v3 on v2

v3 whole, which is shorter than its diff:
```python
import functools

import jax
import jax.numpy as jnp
from jax import lax
from jax.experimental import pallas as pl
from jax.experimental.pallas import tpu as pltpu
from jax.sharding import PartitionSpec as P

INNER = 4096
HEADDIM = 128
HEADS = 32
NS = 64
EXPERTS = 8
CAP = 24
PAIR = 256
PACK = 256
CHUNKS = 2
VMEM_BYTES = 32 * 1024 * 1024

f32 = jnp.float32
bf16 = jnp.bfloat16


def params():
    return pltpu.CompilerParams(vmem_limit_bytes=VMEM_BYTES)


def mask(condition):
    return condition.astype(f32).astype(bf16)


def iota(shape, dim):
    return lax.broadcasted_iota(jnp.int32, shape, dim)


def route(ids_row):
    rows = ids_row.shape[1]
    ids = jnp.broadcast_to(ids_row.astype(f32), (rows, rows)).T
    onehot = (ids == iota((rows, rows), 1).astype(f32)).astype(f32)
    lower = mask(iota((rows, rows), 1) < iota((rows, rows), 0))
    before = jnp.dot(lower, onehot.astype(bf16), preferred_element_type=f32)
    return ids, jnp.sum(before * onehot, axis=1, keepdims=True)


def dispatch_kernel(slices, bias_ref, ids_ref, tok_ref, bcd_ref, *outs):
    pack_ref, out_ref = outs
    rows, width = tok_ref.shape
    depth = width // slices
    ids, slot = route(ids_ref[...])
    pick = mask(ids[:, :1] * CAP + slot == iota((rows, EXPERTS * CAP), 1).astype(f32))
    step = min(512, depth)
    for c in range(0, depth, step):
        got = [
            lax.dot_general(
                pick,
                tok_ref[:, s * depth + c : s * depth + c + step],
                (((0,), (0,)), ((), ())),
                preferred_element_type=f32,
            )
            for s in range(slices)
        ]
        for e in range(EXPERTS):
            piece = jnp.concatenate([g[e * CAP : (e + 1) * CAP] for g in got], axis=0)
            out_ref[e * slices * CAP : (e + 1) * slices * CAP, c : c + step] = piece.astype(bf16)

    across = (((1,), (1,)), ((), ()))
    tok = tok_ref[...]
    pack_ref[:, : 2 * NS] = lax.dot_general(
        tok, bcd_ref[: 2 * NS, :], across, preferred_element_type=f32
    ).astype(bf16)
    steps = bcd_ref[2 * NS : 2 * NS + HEADS, :]
    raw = lax.dot_general(
        tok, jnp.concatenate([steps] * 4, axis=0), across, preferred_element_type=f32
    )
    lane = iota((rows, 128), 1)
    for h in range(HEADS):
        raw = raw + jnp.where(lane % HEADS == h, bias_ref[h], 0.0)
    steps_dt = jnp.maximum(raw, 0.0) + jnp.log1p(jnp.exp(-jnp.abs(raw)))
    coarse = steps_dt.astype(bf16).astype(f32)
    side = jnp.where(lane < HEADS, coarse, steps_dt - coarse)
    side = jnp.where(lane == 2 * HEADS, ids, jnp.where(lane == 2 * HEADS + 1, slot, side))
    pack_ref[:, 2 * NS :] = jnp.where(lane < 2 * HEADS + 2, side, 0.0).astype(bf16)


def dispatch(bias, ids_row, tokens, bcd, slices):
    rows, width = tokens.shape
    vmem = pl.BlockSpec(memory_space=pltpu.VMEM)
    out = jax.ShapeDtypeStruct((EXPERTS * slices * CAP, width // slices), bf16)
    return pl.pallas_call(
        functools.partial(dispatch_kernel, slices),
        out_shape=(jax.ShapeDtypeStruct((rows, PACK), bf16), out),
        in_specs=[pl.BlockSpec(memory_space=pltpu.SMEM), vmem, vmem, vmem],
        compiler_params=params(),
        name="dispatch",
    )(bias, ids_row, tokens, bcd)


def in_kernel(count, shares, turns, place_ref, *refs):
    rows_refs, w_refs, out_refs = refs[:count], refs[count : 2 * count], refs[2 * count :]
    total = None
    for r in range(count):
        part = jnp.dot(rows_refs[r][...], w_refs[r][...], preferred_element_type=f32)
        total = part if total is None else total + part
    for i, q in enumerate(turns):

        @pl.when(pl.program_id(0) == i)
        def _(i=i, q=q):
            units = out_refs[i].shape[1]
            own = total[:, :units]
            for k in range(1, shares):
                at = (place_ref[1] ^ q) % shares
                own = jnp.where(at == k, total[:, k * units : (k + 1) * units], own)
            out_refs[i][...] = own.astype(bf16)


def in_projection(place, pieces, w_in, units, turns):
    slices = len(pieces)
    rows, depth = pieces[0].shape
    tile = max(128, units)
    shares = tile // units

    def w_spec(r):
        def index(i, place_ref):
            q = sum(jnp.where(i == k, t, 0) for k, t in enumerate(turns))
            return (place_ref[0] - r + slices) % slices, (place_ref[1] ^ q) // shares

        return pl.BlockSpec((depth, tile), index)

    return pl.pallas_call(
        functools.partial(in_kernel, slices, shares, turns),
        out_shape=[jax.ShapeDtypeStruct((rows, units), bf16)] * len(turns),
        grid_spec=pltpu.PrefetchScalarGridSpec(
            num_scalar_prefetch=1,
            grid=(len(turns),),
            in_specs=[pl.BlockSpec((rows, depth), lambda i, place_ref: (0, 0))] * slices
            + [w_spec(r) for r in range(slices)],
            out_specs=[pl.BlockSpec((rows, units), lambda i, place_ref: (0, 0))] * len(turns),
        ),
        compiler_params=params(),
        cost_estimate=pl.CostEstimate(
            flops=2 * rows * slices * depth * tile * len(turns),
            bytes_accessed=2 * slices * depth * (tile * len(turns) + rows),
            transcendentals=0,
        ),
        name="in_projection",
    )(place, *pieces, *([w_in] * slices))


def prep_kernel(heads, place_ref, head_ref, rate_ref, skip_ref, pack_ref, w_ref, c_ref, b_ref, a_ref):
    pack = pack_ref[...]
    row = iota((128, PACK), 0)
    lane = iota((128, PACK), 1)
    side = lane - 2 * NS - 2 * HEADS
    choose = ((row == heads) & (side == 0)) | ((row == heads + 1) & (side == 1))
    choose = choose.astype(f32)
    rate = jnp.zeros((128, PAIR), f32)
    for h in range(heads):
        at = lane - 2 * NS - head_ref[h]
        choose = jnp.where((row == h) & ((at == 0) | (at == HEADS)), 1.0, choose)
        rate = jnp.where(iota((128, PAIR), 0) == h, rate_ref[head_ref[h]], rate)
    across = lax.dot_general(
        choose.astype(bf16), pack, (((1,), (1,)), ((), ())), preferred_element_type=f32
    )
    upto = iota((PAIR, PAIR), 0)
    now = iota((PAIR, PAIR), 1)
    running = jnp.dot(
        -across * rate,
        (upto <= now).astype(f32),
        precision=lax.Precision.HIGHEST,
        preferred_element_type=f32,
    )
    second = iota((1, PAIR), 1) >= PAIR // 2
    turn_of = across[heads : heads + 1].astype(jnp.int32) ^ place_ref[1]
    column = turn_of * (2 * CAP) + across[heads + 1 : heads + 2].astype(jnp.int32)
    column = column + jnp.where(second, CAP, 0)
    slots = 2 * CAP * EXPERTS
    place_t = mask(iota((slots, PAIR), 0) == column)
    down = running.T
    b_rows = pack[:, :NS]
    c_rows = pack[:, NS : 2 * NS]
    scores = lax.dot_general(
        c_rows, b_rows, (((1,), (1,)), ((), ())), preferred_element_type=f32
    )
    causal = upto >= now
    diagonal = upto == now
    b_cols = b_rows.astype(f32).T
    c_wide = c_rows.astype(f32)
    for h in range(heads):
        run_row = running[h : h + 1]
        run_col = down[:, h : h + 1]
        dt_row = across[h : h + 1]
        last = run_row[:, PAIR - 1 : PAIR]
        gap = jnp.where(causal, run_col - run_row, 0.0)
        weights = jnp.where(causal, jnp.exp(gap) * scores * dt_row, 0.0)
        weights = weights + jnp.where(diagonal, skip_ref[head_ref[h]], 0.0)
        half = jnp.dot(place_t, weights.astype(bf16), preferred_element_type=f32).astype(bf16)
        w_ref[h, 0] = lax.dot_general(
            half, place_t, (((1,), (1,)), ((), ())), preferred_element_type=f32
        ).astype(bf16)
        c_now = (c_wide * jnp.exp(run_col)).astype(bf16)
        c_ref[h, 0] = jnp.dot(place_t, c_now, preferred_element_type=f32).astype(bf16)
        b_now = (b_cols * (jnp.exp(last - run_row) * dt_row)).astype(bf16)
        b_ref[h, 0] = lax.dot_general(
            b_now, place_t, (((1,), (1,)), ((), ())), preferred_element_type=f32
        ).astype(bf16)
        a_ref[h, 0] = jnp.broadcast_to(jnp.exp(last), (8, 128))


def prepare(place, own_heads, rate, skip, pack):
    heads = own_heads.shape[0]
    pairs = pack.shape[0] // PAIR
    slots = 2 * CAP * EXPERTS
    smem = pl.BlockSpec(memory_space=pltpu.SMEM)

    def block(*dims):
        return pl.BlockSpec((heads, 1, *dims), lambda p: (0, p, 0, 0))

    return pl.pallas_call(
        functools.partial(prep_kernel, heads),
        out_shape=(
            jax.ShapeDtypeStruct((heads, pairs, slots, slots), bf16),
            jax.ShapeDtypeStruct((heads, pairs, slots, NS), bf16),
            jax.ShapeDtypeStruct((heads, pairs, NS, slots), bf16),
            jax.ShapeDtypeStruct((heads, pairs, 8, 128), f32),
        ),
        grid=(pairs,),
        in_specs=[smem, smem, smem, smem, pl.BlockSpec((PAIR, PACK), lambda p: (p, 0))],
        out_specs=(block(slots, slots), block(slots, NS), block(NS, slots), block(8, 128)),
        compiler_params=params(),
        cost_estimate=pl.CostEstimate(
            flops=4 * heads * pairs * slots * slots * PAIR,
            bytes_accessed=2 * heads * pairs * slots * slots,
            transcendentals=heads * pairs * PAIR * PAIR,
        ),
        name="scan_weights",
    )(place, own_heads, rate, skip, pack)


def scan_kernel(*refs):
    x_refs, refs = refs[:EXPERTS], refs[EXPERTS:]
    w_ref, c_ref, b_ref, a_ref, gain_ref = refs[:5]
    out_refs, last_ref, state = refs[5 : 5 + EXPERTS], refs[-2], refs[-1]

    @pl.when(pl.program_id(0) == 0)
    def _():
        state[...] = jnp.zeros_like(state)

    rows = x_refs[0].shape[0]
    x = jnp.concatenate([x_ref[...] for x_ref in x_refs], axis=0)
    before = state[...]
    y = jnp.dot(w_ref[0, 0], x, preferred_element_type=f32) + jnp.dot(
        c_ref[0, 0], before.astype(bf16), preferred_element_type=f32
    )
    after = before * a_ref[0, 0, 0:1, 0:1] + jnp.dot(
        b_ref[0, 0], x, preferred_element_type=f32
    )
    state[...] = after
    last_ref[...] = after
    z = (y * gain_ref[...]).astype(bf16)
    for q in range(EXPERTS):
        out_refs[q][...] = z[q * rows : (q + 1) * rows]


def scan(x, weights, gain, h):
    rows = x[0].shape[0]
    width = gain.shape[1]
    pairs = rows // (2 * CAP)
    slots = 2 * CAP * EXPERTS

    def block(*dims):
        return pl.BlockSpec((1, 1, *dims), lambda p: (h, p, 0, 0))

    *z, state = pl.pallas_call(
        scan_kernel,
        out_shape=[jax.ShapeDtypeStruct((rows, width), bf16)] * EXPERTS
        + [jax.ShapeDtypeStruct((NS, width), f32)],
        grid=(pairs,),
        in_specs=[pl.BlockSpec((2 * CAP, width), lambda p: (p, h))] * EXPERTS
        + [
            block(slots, slots),
            block(slots, NS),
            block(NS, slots),
            block(8, 128),
            pl.BlockSpec((1, width), lambda p: (0, 0)),
        ],
        out_specs=[pl.BlockSpec((2 * CAP, width), lambda p: (p, 0))] * EXPERTS
        + [pl.BlockSpec((NS, width), lambda p: (0, 0))],
        scratch_shapes=[pltpu.VMEM((NS, width), f32)],
        compiler_params=params(),
        cost_estimate=pl.CostEstimate(
            flops=2 * pairs * slots * (slots + 2 * NS) * width,
            bytes_accessed=2 * pairs * slots * slots,
            transcendentals=0,
        ),
        name="scan",
    )(*x, *weights, gain)
    return z, state


def chunk_product(z_refs, w_refs):
    width = z_refs[0].shape[1]
    group = max(1, 256 // width) if width % 128 == 0 else 1
    total = None
    for q in range(0, EXPERTS, group):
        z = [r[...] for r in z_refs[q : q + group]]
        w = [r[...] for r in w_refs[q : q + group]]
        z = jnp.concatenate(z, axis=1) if group > 1 else z[0]
        w = jnp.concatenate(w, axis=0) if group > 1 else w[0]
        part = jnp.dot(z, w, preferred_element_type=f32)
        total = part if total is None else total + part
    return total


def chunk_squares(place_ref, z_refs, inverse_ref, heads, h):
    total = jnp.zeros((z_refs[0].shape[0], 1), f32)
    for q in range(EXPERTS):
        z = z_refs[q][...].astype(f32) * inverse_ref[(place_ref[1] ^ q) * heads + h]
        total = total + jnp.sum(z * z, axis=1, keepdims=True)
    return total


def out_kernel(layout, place_ref, *refs):
    kind, heads, h, counted, others = layout
    refs = list(refs)

    def take(count):
        got = refs[:count]
        del refs[:count]
        return got

    z_refs, w_refs = take(EXPERTS), take(EXPERTS)
    inverse_ref = take(1)[0] if counted else None
    total_ref = take(1)[0] if kind != "begin" and h > 0 else None
    before_ref = take(1)[0] if counted and kind == "send" and h > 0 else None
    squares_refs = take(1 + others) if kind == "finish" else None
    part_refs = take(others) if kind == "finish" else None
    out_ref = take(1)[0]
    if inverse_ref is not None:

        @pl.when(pl.program_id(0) == 0)
        def _():
            squares = chunk_squares(place_ref, z_refs, inverse_ref, heads, h)
            refs[0][...] = squares if before_ref is None else squares + before_ref[...]

    total = chunk_product(z_refs, w_refs)
    if total_ref is not None:
        total = total + total_ref[0]
    if kind == "finish":
        squares = sum(r[...] for r in squares_refs)
        for part in part_refs:
            total = total + part[...].astype(f32)
        total = total * lax.rsqrt(squares / INNER + 1e-05)
        out_ref[...] = total.astype(bf16)
    else:
        out_ref[0] = total.astype(out_ref.dtype)


def out_projection(
    kind, *, place, z, w_out, heads, h, chunk, inverse=None, total=None, squares=(), parts=()
):
    rows, width = z[0].shape
    slices = INNER // w_out.shape[0]
    slice_width = w_out.shape[1] // slices
    part = slice_width if kind == "begin" else slice_width // CHUNKS
    count = {"begin": slices, "send": slices - 1, "finish": 1}[kind]
    first = slices if kind == "finish" else 1
    tile = min(512, part)
    tiles = part // tile
    whole = slice_width // tile
    offset = 0 if kind == "begin" else chunk * tiles

    def w_spec(q):
        return pl.BlockSpec(
            (width, tile),
            lambda n, place_ref: (
                (place_ref[1] ^ q) * heads + h,
                (place_ref[0] + first + n // tiles) % slices * whole + offset + n % tiles,
            ),
        )

    def fixed(*dims):
        return pl.BlockSpec(dims, lambda n, place_ref: (0,) * len(dims))

    operands = [*z, *([w_out] * EXPERTS)]
    specs = [fixed(rows, width)] * EXPERTS + [w_spec(q) for q in range(EXPERTS)]
    if inverse is not None:
        operands.append(inverse)
        specs.append(fixed(*inverse.shape))
    if total is not None:
        operands.append(total)
        specs.append(
            pl.BlockSpec(
                (1, rows, tile),
                lambda n, place_ref: (first - 1 + n // tiles, 0, offset + n % tiles),
            )
        )
    operands += [*squares, *parts]
    specs += [fixed(rows, 1)] * len(squares)
    specs += [pl.BlockSpec((rows, tile), lambda n, place_ref: (0, n))] * len(parts)
    if kind == "finish":
        out_shape = [jax.ShapeDtypeStruct((rows, part), bf16)]
        out_specs = [pl.BlockSpec((rows, tile), lambda n, place_ref: (0, n))]
    else:
        dtype = f32 if kind == "begin" else bf16
        out_shape = [jax.ShapeDtypeStruct((count, rows, part), dtype)]
        out_specs = [
            pl.BlockSpec((1, rows, tile), lambda n, place_ref: (n // tiles, 0, n % tiles))
        ]
    if inverse is not None:
        out_shape.append(jax.ShapeDtypeStruct((rows, 1), f32))
        out_specs.append(fixed(rows, 1))
    return pl.pallas_call(
        functools.partial(out_kernel, (kind, heads, h, inverse is not None, len(parts))),
        out_shape=out_shape,
        grid_spec=pltpu.PrefetchScalarGridSpec(
            num_scalar_prefetch=1, grid=(count * tiles,), in_specs=specs, out_specs=out_specs
        ),
        compiler_params=params(),
        cost_estimate=pl.CostEstimate(
            flops=2 * rows * EXPERTS * width * count * part,
            bytes_accessed=2 * EXPERTS * width * count * part + 4 * rows * count * part,
            transcendentals=0,
        ),
        name="out_" + kind,
    )(place, *operands)


def collect_kernel(slices, ids_ref, *refs):
    chunk_refs, out_ref = refs[:-1], refs[-1]
    count, part = chunk_refs[0].shape
    rows = ids_ref.shape[1]
    depth = part * len(chunk_refs)
    step = min(512, part)
    ids, slot = route(ids_ref[...])
    at = ids[:, :1] * (slices * CAP) + slot
    lane = iota((rows, count), 1).astype(f32)
    for s in range(slices):
        pick = mask(at + s * CAP == lane)
        for k, rows_ref in enumerate(chunk_refs):
            for c in range(0, part, step):
                start = s * depth + k * part + c
                out_ref[:, start : start + step] = jnp.dot(
                    pick, rows_ref[:, c : c + step], preferred_element_type=f32
                ).astype(bf16)


def collect(ids_row, chunks, slices):
    width = sum(c.shape[1] for c in chunks) * slices
    return pl.pallas_call(
        functools.partial(collect_kernel, slices),
        out_shape=jax.ShapeDtypeStruct((ids_row.shape[1], width), bf16),
        compiler_params=params(),
        name="collect",
    )(ids_row, *chunks)


def turn(a, n, slices, r):
    return lax.ppermute(
        a, "expert", [(d, d // slices * slices + (d + r) % slices) for d in range(n)]
    )


def swap(a, groups=None):
    return lax.all_to_all(
        a, "expert", split_axis=0, concat_axis=0, axis_index_groups=groups, tiled=True
    )


def exchange(arrays, n, slices):
    out = list(arrays)
    for q in reversed(range(1, EXPERTS)):
        pairs = [(d, (d // slices ^ q) * slices + d % slices) for d in range(n)]
        out[q] = lax.ppermute(arrays[q], "expert", pairs)
    return out


def shards(
    tokens, w_in, w_out, w_bcd, dt_bias, decay_rate, skip_gain, norm_gain, expert_ids, decode_heads
):
    n = lax.axis_size("expert")
    slices = n // EXPERTS
    in_dev = w_in.shape[2]
    units = in_dev // EXPERTS
    width = min(HEADDIM, units)
    heads = units // width
    me = lax.axis_index("expert")
    chip = (me // slices).astype(jnp.int32)
    place = jnp.stack([(me % slices).astype(jnp.int32), chip])
    start = place[0] * in_dev + chip * units
    ids_row = expert_ids.reshape(1, -1)
    w_in, w_out = w_in[0], w_out[0]

    pack, outgoing = dispatch(dt_bias, ids_row, tokens, w_bcd.T, slices)
    pack = lax.all_gather(pack, "expert", axis=0, tiled=True)
    landed = swap(outgoing)
    pieces = [landed] + [turn(landed, n, slices, r) for r in range(1, slices)]
    own_heads = start // HEADDIM + jnp.arange(heads, dtype=jnp.int32)
    inner = [None] * EXPERTS
    for order in ((7, 6), (5, 4), (3, 2), (1, 0)):
        got = in_projection(place, pieces, w_in, units, order)
        for q, a in zip(order, got):
            inner[q] = a
        if order == (7, 6):
            weights = prepare(place, own_heads, decay_rate, skip_gain, pack)
            pieces, weights = lax.optimization_barrier((pieces, weights))
    x = exchange(inner, n, slices)

    gain = lax.dynamic_slice(norm_gain, (start,), (units,))
    z, states = [], []
    for h in range(heads):
        rows, state = scan(x, weights, gain[h * width : (h + 1) * width].reshape(1, width), h)
        z.append(exchange(rows, n, slices))
        states.append(state)
    states = lax.all_gather(jnp.stack(states), "expert", axis=0, tiled=False)

    inverse = 1.0 / lax.dynamic_slice(norm_gain, (place[0] * in_dev,), (in_dev,))
    inverse = inverse.reshape(in_dev // width, 1, width)
    project = functools.partial(out_projection, place=place, w_out=w_out, heads=heads)
    total = None
    squares = ()
    for h in range(heads - 1):
        total, squares = project("begin", z=z[h], h=h, chunk=0, inverse=inverse)
        squares = (squares,)
    h = heads - 1
    sent = []
    for k in range(CHUNKS):
        first = inverse if k == 0 else None
        got = project(
            "send",
            z=z[h],
            h=h,
            chunk=k,
            inverse=first,
            total=total,
            squares=squares if k == 0 else (),
        )
        if k == 0:
            all_squares = [got[1]] + [turn(got[1], n, slices, r) for r in range(1, slices)]
        sent.append([turn(got[0][r - 1], n, slices, r) for r in range(1, slices)])
    back = []
    for k in range(CHUNKS):
        [done] = project(
            "finish", z=z[h], h=h, chunk=k, total=total, squares=all_squares, parts=sent[k]
        )
        back.append(swap(done))
    mixed = collect(ids_row, back, slices)

    want = decode_heads[0] * HEADDIM
    within = want % in_dev // width
    states = states.reshape(EXPERTS, slices, heads, NS, width)
    chosen = lax.dynamic_slice(
        states,
        (within // heads, want // in_dev, within % heads, 0, 0),
        (HEADDIM // width, 1, 1, NS, width),
    )
    chosen = chosen.reshape(HEADDIM // width, NS, width).transpose(0, 2, 1)
    return (mixed, chosen.reshape(1, HEADDIM * NS))


def solution(mesh):
    in_specs = (
        P(("groups", "expert"), None),
        P("expert", None, None),
        P("expert", None, None),
        P(),
        P(),
        P(),
        P(),
        P(),
        P(("groups", "expert"), None),
        P("expert"),
    )
    out_specs = (P(("groups", "expert"), None), P(("groups", "expert"), None))
    return jax.shard_map(shards, mesh=mesh, in_specs=in_specs, out_specs=out_specs, check_vma=False)
```

time: 272 us -> 267 us (0.982)
  starting transfers between devices: 41.4 us -> 56.8 us
  local copies, waits for them, and re-layouts: 30.1 us -> 19.4 us
  waiting for transfers between devices: 118 us -> 111 us
    all_to_all x8 -> x3, waiting for transfers between devices: 94.2 us -> 36.5 us  [swap(): lax.all_to_all(a, 'expert', split_axis=0, concat_axis=0, axis_index_group...]
    ppermute x0 -> x21, starting transfers between devices: none -> 36.2 us  [exchange(): out[q] = lax.ppermute(arrays[q], 'expert', pairs)]
    ppermute x0 -> x21, waiting for transfers between devices: none -> 31.8 us  [exchange(): out[q] = lax.ppermute(arrays[q], 'expert', pairs)]
    all_to_all x8 -> x3, starting transfers between devices: 39.6 us -> 18.5 us  [swap(): lax.all_to_all(a, 'expert', split_axis=0, concat_axis=0, axis_index_group...]
    all_gather x1, waiting for transfers between devices: 0.01 us -> 15.4 us  [shards(): pack = lax.all_gather(pack, 'expert', axis=0, tiled=True)]
    unnamed x51 -> x34, local copies, waits for them, and re-layouts: 28.5 us -> 17 us
    all_gather x1, waiting for transfers between devices: 19.4 us -> 23.3 us  [shards(): states = lax.all_gather(jnp.stack(states), 'expert', axis=0, tiled=False)]
    pallas_call x10 -> x11, Pallas kernels: 47 us -> 44.4 us  [the longest x5 26 us: out_projection(): pl.pallas_call(functools.partial(out_kernel, (kind, heads, h, inverse is...]
  transfers between devices with their start and end apart: 15 -> 30, of which waited for: 9 -> 10; matrix products, arithmetic and copies ran while one was open for 1% -> 1% of each run, Pallas kernels for 19% -> 15%
where the time goes in v3:
time: 267 us; the launch traced here: 266 us
  waiting for transfers between devices  111 us (42%)
  Pallas kernels  63 us (24%)
  starting transfers between devices  56.8 us (21%)
  local copies, waits for them, and re-layouts  19.4 us (7%)
  between operations  15 us (6%)
    all_to_all x3, waiting for transfers between devices, swap(): lax.all_to_all(a, 'expert', split_axis=0, concat_axis=0, axis_index_group...  36.5 us
    ppermute x21, starting transfers between devices, exchange(): out[q] = lax.ppermute(arrays[q], 'expert', pairs)  36.2 us
    ppermute x21, waiting for transfers between devices, exchange(): out[q] = lax.ppermute(arrays[q], 'expert', pairs)  31.8 us
    pallas_call x5, Pallas kernels, out_projection(): pl.pallas_call(functools.partial(out_kernel, (kind, heads, h, inverse is...  26 us
    all_gather x1, waiting for transfers between devices, shards(): states = lax.all_gather(jnp.stack(states), 'expert', axis=0, tiled=False)  23.3 us
    all_to_all x3, starting transfers between devices, swap(): lax.all_to_all(a, 'expert', split_axis=0, concat_axis=0, axis_index_group...  18.5 us
    unnamed x34, local copies, waits for them, and re-layouts  17 us
    all_gather x1, waiting for transfers between devices, shards(): pack = lax.all_gather(pack, 'expert', axis=0, tiled=True)  15.4 us
  transfers between devices with their start and end apart: 30, of which 10 were waited for; matrix products, arithmetic and copies ran while one was open for 1% of the time, Pallas kernels for 15%

profile of v3, /device:TPU:0, one launch (start us, length us, event | category | flops | bytes accessed | tf_op | source)
XLA Modules:
  0.0 265.9 jit_solution(3431104681665184743)
XLA Ops:
  11.0 3.2 %dispatch.1 = (bf16[128,256]{1,0:T(8,128)(2,1)}, bf16[384,2048]{1,0:T(8,128)(2,1)}) custom-call(f32[32]{0:T(128)S(1)} %copy-done.12, s32[1,128]{1,0:T(1,128)S(1)} %bitcast.48, bf16[128,4096]{1,0:T(8,128)(2,1)S(1)} %copy-done.5, bf16[160,4096]{1,0:T(8,128)(2,1)S(1)} %bitcast.42), custom_call_target="tpu_custom_call" | custom-call | tf_op jit(solution)/shard_map/dispatch/pallas_call | solution.py:90
  14.2 7.5 %all-to-all-start = ((bf16[16,24,2048]{2,1,0:T(8,128)(2,1)}), bf16[16,24,2048]{2,1,0:T(8,128)(2,1)S(1)}, u32[]{:S(2)}, u32[]{:S(2)}) async-start(bf16[16,24,2048]{2,1,0:T(8,128)(2,1)} %bitcast.4), calls=%async_computation | async-start | bytes 3145728 | tf_op jit(solution)/shard_map/all_to_all | solution.py:465
  22.5 33.3 %all-to-all-done = bf16[16,24,2048]{2,1,0:T(8,128)(2,1)S(1)} async-done(((bf16[16,24,2048]{2,1,0:T(8,128)(2,1)}), bf16[16,24,2048]{2,1,0:T(8,128)(2,1)S(1)}, u32[]{:S(2)}, u32[]{:S(2)}) %all-to-all-start) | async-done | bytes 1572896 | tf_op jit(solution)/shard_map/all_to_all | solution.py:465
  57.5 15.4 %all-gather.4.cloned.1.call-done.pack_ref = bf16[2048,256]{1,0:T(8,128)(2,1)} async-done(((bf16[128,256]{1,0:T(8,128)(2,1)}), bf16[2048,256]{1,0:T(8,128)(2,1)}) %all-gather.4.cloned.1.call-update) | async-done | bytes 1048592 | tf_op jit(solution)/shard_map/all_gather | solution.py:495
  74.1 13.3 %scan_weights.1 = (bf16[2,8,384,384]{3,2,1,0:T(8,128)(2,1)S(1)}, bf16[2,8,384,64]{3,2,1,0:T(8,128)(2,1)S(1)}, bf16[2,8,64,384]{3,2,1,0:T(8,128)(2,1)S(1)}, f32[2,8,8,128]{3,2,1,0:T(8,128)S(1)}) custom-call(s32[2]{0:T(128)S(1)} %pad_add_fusion.place_ref, s32[2]{0:T(128)S(1)} %iota_add_fusion.head_ref, f32[32]{0:T(128)S(1)} %copy-done.14, f32[32]{0:T(128)S(1)} %copy-done.15, ...), custom_call_target="tpu_custom_call" | custom-call | flops 2415919104 | bytes 4718592 | tf_op jit(solution)/shard_map/scan_weights/pallas_call | solution.py:219
  87.5 5.8 %copy-done = bf16[1,4096,2048]{2,1,0:T(8,128)(2,1)S(1)} copy-done((bf16[1,4096,2048]{2,1,0:T(8,128)(2,1)S(1)}, bf16[1,4096,2048]{2,1,0:T(8,128)(2,1)}, u32[]{:S(2)}) %copy-start) | copy-done | bytes 16777240
  93.2 3.2 %in_projection.4 = (bf16[384,256]{1,0:T(8,128)(2,1)S(1)}, bf16[384,256]{1,0:T(8,128)(2,1)S(1)}) custom-call(s32[2]{0:T(128)S(1)} %pad_add_fusion.place_ref, bf16[384,2048]{1,0:T(8,128)(2,1)S(1)} %bitcast.36, bf16[384,2048]{1,0:T(8,128)(2,1)S(1)} %collective-permute-done.refs_1_, bf16[4096,2048]{1,0:T(8,128)(2,1)S(1)} %bitcast.27, bf16[4096,2048]{1,0:T(8,128)(2,1)S(1)} %bitcast.28), custom_call_target="tpu_custom_call" | custom-call | flops 1610612736 | bytes 7340032 | tf_op jit(solution)/shard_map/in_projection/pallas_call | solution.py:130
  96.5 3.2 %in_projection.5 = (bf16[384,256]{1,0:T(8,128)(2,1)S(1)}, bf16[384,256]{1,0:T(8,128)(2,1)S(1)}) custom-call(s32[2]{0:T(128)S(1)} %pad_add_fusion.place_ref, bf16[384,2048]{1,0:T(8,128)(2,1)S(1)} %bitcast.37, bf16[384,2048]{1,0:T(8,128)(2,1)S(1)} %collective-permute-done.refs_1_, bf16[4096,2048]{1,0:T(8,128)(2,1)S(1)} %bitcast.29, bf16[4096,2048]{1,0:T(8,128)(2,1)S(1)} %bitcast.30), custom_call_target="tpu_custom_call" | custom-call | flops 1610612736 | bytes 7340032 | tf_op jit(solution)/shard_map/in_projection/pallas_call | solution.py:130
  101.4 3.2 %in_projection.6 = (bf16[384,256]{1,0:T(8,128)(2,1)S(1)}, bf16[384,256]{1,0:T(8,128)(2,1)S(1)}) custom-call(s32[2]{0:T(128)S(1)} %pad_add_fusion.place_ref, bf16[384,2048]{1,0:T(8,128)(2,1)S(1)} %bitcast.38, bf16[384,2048]{1,0:T(8,128)(2,1)S(1)} %collective-permute-done.refs_1_, bf16[4096,2048]{1,0:T(8,128)(2,1)S(1)} %bitcast.31, bf16[4096,2048]{1,0:T(8,128)(2,1)S(1)} %bitcast.32), custom_call_target="tpu_custom_call" | custom-call | flops 1610612736 | bytes 7340032 | tf_op jit(solution)/shard_map/in_projection/pallas_call | solution.py:130
  109.4 3.2 %in_projection.7 = (bf16[384,256]{1,0:T(8,128)(2,1)S(1)}, bf16[384,256]{1,0:T(8,128)(2,1)S(1)}) custom-call(s32[2]{0:T(128)S(1)} %pad_add_fusion.place_ref, bf16[384,2048]{1,0:T(8,128)(2,1)S(1)} %bitcast.39, bf16[384,2048]{1,0:T(8,128)(2,1)S(1)} %collective-permute-done.refs_1_, bf16[4096,2048]{1,0:T(8,128)(2,1)S(1)} %bitcast.33, bf16[4096,2048]{1,0:T(8,128)(2,1)S(1)} %bitcast.34), custom_call_target="tpu_custom_call" | custom-call | flops 1610612736 | bytes 7340032 | tf_op jit(solution)/shard_map/in_projection/pallas_call | solution.py:130
  115.0 2.5 collective-permute-start.7
  117.5 14.6 %collective-permute-done.4.refs_4_ = bf16[384,256]{1,0:T(8,128)(2,1)S(1)} collective-permute-done((bf16[384,256]{1,0:T(8,128)(2,1)S(1)}, bf16[384,256]{1,0:T(8,128)(2,1)S(1)}, u32[]{:S(2)}, u32[]{:S(2)}) %collective-permute-start.4) | collective-permute-done | bytes 196640 | tf_op jit(solution)/shard_map/ppermute | solution.py:474
  132.1 4.1 %collective-permute-done.5.refs_5_ = bf16[384,256]{1,0:T(8,128)(2,1)S(1)} collective-permute-done((bf16[384,256]{1,0:T(8,128)(2,1)S(1)}, bf16[384,256]{1,0:T(8,128)(2,1)S(1)}, u32[]{:S(2)}, u32[]{:S(2)}) %collective-permute-start.5) | collective-permute-done | bytes 196640 | tf_op jit(solution)/shard_map/ppermute | solution.py:474
  136.3 2.8 %scan.2 = (bf16[384,128]{1,0:T(8,128)(2,1)S(1)}, bf16[384,128]{1,0:T(8,128)(2,1)S(1)}, bf16[384,128]{1,0:T(8,128)(2,1)S(1)}, bf16[384,128]{1,0:T(8,128)(2,1)S(1)...) custom-call(bf16[384,256]{1,0:T(8,128)(2,1)S(1)} %get-tuple-element., ...), custom_call_target="tpu_custom_call" | custom-call | flops 402653184 | bytes 2359296 | tf_op jit(solution)/shard_map/scan/pallas_call | solution.py:274
  140.7 7.4 %collective-permute-start.9 = (bf16[384,128]{1,0:T(8,128)(2,1)S(1)}, bf16[384,128]{1,0:T(8,128)(2,1)S(1)}, u32[]{:S(2)}, u32[]{:S(2)}) collective-permute-start(bf16[384,128]{1,0:T(8,128)(2,1)S(1)} %get-tuple-element.66), channel_id=1, source_target_pairs={{0,4},{1,5},{2,6},{3,7},{4,0},{5,1},{6,2},{7,3},{8,12},{9,13},{10,... | collective-permute-start | bytes 294920 | tf_op jit(solution)/shard_map/ppermute | solution.py:474
  148.1 2.8 %scan.3 = (bf16[384,128]{1,0:T(8,128)(2,1)S(1)}, bf16[384,128]{1,0:T(8,128)(2,1)S(1)}, bf16[384,128]{1,0:T(8,128)(2,1)S(1)}, bf16[384,128]{1,0:T(8,128)(2,1)S(1)...) custom-call(bf16[384,256]{1,0:T(8,128)(2,1)S(1)} %get-tuple-element., ...), custom_call_target="tpu_custom_call" | custom-call | flops 402653184 | bytes 2359296 | tf_op jit(solution)/shard_map/scan/pallas_call | solution.py:274
  152.0 3.0 %collective-permute-start.17 = (bf16[384,128]{1,0:T(8,128)(2,1)S(1)}, bf16[384,128]{1,0:T(8,128)(2,1)S(1)}, u32[]{:S(2)}, u32[]{:S(2)}) collective-permute-start(bf16[384,128]{1,0:T(8,128)(2,1)S(1)} %get-tuple-element.75), channel_id=1, source_target_pairs={{0,6},{1,7},{2,4},{3,5},{4,2},{5,3},{6,0},{7,1},{8,14},{9,15},{10,... | collective-permute-start | bytes 294920 | tf_op jit(solution)/shard_map/ppermute | solution.py:474
  160.1 2.5 collective-permute-start.21
  162.7 7.4 %collective-permute-done.18.refs_4_ = bf16[384,128]{1,0:T(8,128)(2,1)S(1)} collective-permute-done((bf16[384,128]{1,0:T(8,128)(2,1)S(1)}, bf16[384,128]{1,0:T(8,128)(2,1)S(1)}, u32[]{:S(2)}, u32[]{:S(2)}) %collective-permute-start.18) | collective-permute-done | bytes 98336 | tf_op jit(solution)/shard_map/ppermute | solution.py:474
  170.1 5.6 %collective-permute-done.19.refs_5_ = bf16[384,128]{1,0:T(8,128)(2,1)S(1)} collective-permute-done((bf16[384,128]{1,0:T(8,128)(2,1)S(1)}, bf16[384,128]{1,0:T(8,128)(2,1)S(1)}, u32[]{:S(2)}, u32[]{:S(2)}) %collective-permute-start.19) | collective-permute-done | bytes 98336 | tf_op jit(solution)/shard_map/ppermute | solution.py:474
  177.7 2.6 collective-permute-start.14
  180.3 9.8 %out_begin.1 = (f32[2,384,2048]{2,1,0:T(8,128)S(1)}, f32[384,1]{1,0:T(8,128)S(1)}) custom-call(s32[2]{0:T(128)S(1)} %pad_add_fusion.place_ref, bf16[384,128]{1,0:T(8,128)(2,1)S(1)} %get-tuple-element.72.refs_0_, bf16[384,128]{1,0:T(8,128)(2,1)S(1)} %collective-permute-done.15.refs_1_, bf16[384,128]{1,0:T(8,128)(2,1)S(1)} %collective-permute-done.16.refs_2_, ...), custom_call_target="tpu_custom_call" | custom-call | flops 3221225472 | bytes 14680064 | tf_op jit(solution)/shard_map/out_begin/pallas_call | solution.py:413
  190.2 4.8 %out_send.2 = (bf16[1,384,1024]{2,1,0:T(8,128)(2,1)S(1)}, f32[384,1]{1,0:T(8,128)S(1)}) custom-call(s32[2]{0:T(128)S(1)} %pad_add_fusion.place_ref, bf16[384,128]{1,0:T(8,128)(2,1)S(1)} %get-tuple-element.64.refs_0_, bf16[384,128]{1,0:T(8,128)(2,1)S(1)} %collective-permute-done.8.refs_1_, bf16[384,128]{1,0:T(8,128)(2,1)S(1)} %collective-permute-done.9.refs_2_, ...), custom_call_target="tpu_custom_call" | custom-call | flops 805306368 | bytes 3670016 | tf_op jit(solution)/shard_map/out_send/pallas_call | solution.py:413
  197.7 4.0 %out_finish.2 = bf16[384,1024]{1,0:T(8,128)(2,1)} custom-call(s32[2]{0:T(128)S(1)} %pad_add_fusion.place_ref, bf16[384,128]{1,0:T(8,128)(2,1)S(1)} %get-tuple-element.64.refs_0_, bf16[384,128]{1,0:T(8,128)(2,1)S(1)} %collective-permute-done.8.refs_1_, bf16[384,128]{1,0:T(8,128)(2,1)S(1)} %collective-permute-done.9.refs_2_, ...), custom_call_target="tpu_custom_call" | custom-call | flops 805306368 | bytes 3670016 | tf_op jit(solution)/shard_map/out_finish/pallas_call | solution.py:413
  201.7 4.8 %all-to-all-start.1 = ((bf16[16,24,1024]{2,1,0:T(8,128)(2,1)}), bf16[16,24,1024]{2,1,0:T(8,128)(2,1)S(1)}, u32[]{:S(2)}, u32[]{:S(2)}) async-start(bf16[16,24,1024]{2,1,0:T(8,128)(2,1)} %bitcast.12), calls=%async_computation.1 | async-start | bytes 1572864 | tf_op jit(solution)/shard_map/all_to_all | solution.py:465
  206.7 2.8 %copy-done.2 = f32[2,384,2048]{2,1,0:T(8,128)S(1)} copy-done((f32[2,384,2048]{2,1,0:T(8,128)S(1)}, f32[2,384,2048]{2,1,0:T(8,128)}, u32[]{:S(2)}) %copy-start.2) | copy-done | bytes 6291480
  209.5 3.3 %out_send.3 = bf16[1,384,1024]{2,1,0:T(8,128)(2,1)S(1)} custom-call(s32[2]{0:T(128)S(1)} %pad_add_fusion.place_ref, bf16[384,128]{1,0:T(8,128)(2,1)S(1)} %get-tuple-element.64.refs_0_, bf16[384,128]{1,0:T(8,128)(2,1)S(1)} %collective-permute-done.8.refs_1_, bf16[384,128]{1,0:T(8,128)(2,1)S(1)} %collective-permute-done.9.refs_2_, ...), custom_call_target="tpu_custom_call" | custom-call | flops 805306368 | bytes 3670016 | tf_op jit(solution)/shard_map/out_send/pallas_call | solution.py:413
  215.3 2.8 %copy-done.3 = f32[2,384,2048]{2,1,0:T(8,128)S(1)} copy-done((f32[2,384,2048]{2,1,0:T(8,128)S(1)}, f32[2,384,2048]{2,1,0:T(8,128)}, u32[]{:S(2)}) %copy-start.3) | copy-done | bytes 6291480
  218.1 4.1 %out_finish.3 = bf16[384,1024]{1,0:T(8,128)(2,1)} custom-call(s32[2]{0:T(128)S(1)} %pad_add_fusion.place_ref, bf16[384,128]{1,0:T(8,128)(2,1)S(1)} %get-tuple-element.64.refs_0_, bf16[384,128]{1,0:T(8,128)(2,1)S(1)} %collective-permute-done.8.refs_1_, bf16[384,128]{1,0:T(8,128)(2,1)S(1)} %collective-permute-done.9.refs_2_, ...), custom_call_target="tpu_custom_call" | custom-call | flops 805306368 | bytes 3670016 | tf_op jit(solution)/shard_map/out_finish/pallas_call | solution.py:413
  222.1 3.1 %all-to-all-done.1 = bf16[16,24,1024]{2,1,0:T(8,128)(2,1)S(1)} async-done(((bf16[16,24,1024]{2,1,0:T(8,128)(2,1)}), bf16[16,24,1024]{2,1,0:T(8,128)(2,1)S(1)}, u32[]{:S(2)}, u32[]{:S(2)}) %all-to-all-start.1) | async-done | bytes 786464 | tf_op jit(solution)/shard_map/all_to_all | solution.py:465
  225.2 6.2 %all-to-all-start.2 = ((bf16[16,24,1024]{2,1,0:T(8,128)(2,1)}), bf16[16,24,1024]{2,1,0:T(8,128)(2,1)S(1)}, u32[]{:S(2)}, u32[]{:S(2)}) async-start(bf16[16,24,1024]{2,1,0:T(8,128)(2,1)} %bitcast.15), calls=%async_computation.2 | async-start | bytes 1572864 | tf_op jit(solution)/shard_map/all_to_all | solution.py:465
  232.1 23.3 %all-gather.6.cloned.1.call-done = f32[32,64,128]{2,1,0:T(8,128)} async-done(((f32[2,64,128]{2,1,0:T(8,128)}), f32[32,64,128]{2,1,0:T(8,128)}) %all-gather.6.cloned.1.call-update) | async-done | bytes 1048592 | tf_op jit(solution)/shard_map/all_gather | solution.py:515
  (87 shorter events, 35.1 us)
Async XLA Ops:
  14.2 58.7 %copy-start.14 = (f32[32]{0:T(128)S(1)}, f32[32]{0:T(128)}, u32[]{:S(2)}) copy-start(f32[32]{0:T(128)} %rate_ref.1) | copy-start | bytes 388
  14.2 58.7 %copy-start.15 = (f32[32]{0:T(128)S(1)}, f32[32]{0:T(128)}, u32[]{:S(2)}) copy-start(f32[32]{0:T(128)} %skip_ref.1) | copy-start | bytes 388
  14.2 41.6 %all-to-all-start = ((bf16[16,24,2048]{2,1,0:T(8,128)(2,1)}), bf16[16,24,2048]{2,1,0:T(8,128)(2,1)S(1)}, u32[]{:S(2)}, u32[]{:S(2)}) async-start(bf16[16,24,2048]{2,1,0:T(8,128)(2,1)} %bitcast.4), calls=%async_computation | async-start | bytes 3145728 | tf_op jit(solution)/shard_map/all_to_all | solution.py:465
  21.8 51.1 %all-gather.4.cloned.1.call-start = ((), (), s32[]{:S(2)}) async-start(), calls=%async_computation.3 | async-start | bytes 1114112 | tf_op jit(solution)/shard_map/all_gather | solution.py:495
  55.9 31.6 %collective-permute-start = (bf16[384,2048]{1,0:T(8,128)(2,1)S(1)}, bf16[384,2048]{1,0:T(8,128)(2,1)S(1)}, u32[]{:S(2)}, u32[]{:S(2)}) collective-permute-start(bf16[384,2048]{1,0:T(8,128)(2,1)S(1)} %bitcast.35), channel_id=1, source_target_pairs={{0,1},{1,0},{2,3},{3,2},{4,5},{5,4},{6,7},{7,6},{8,9},{9,8},{10,11... | collective-permute-start | bytes 4718600 | tf_op jit(solution)/shard_map/ppermute | solution.py:459
  99.7 12.9 %collective-permute-start.1 = (bf16[384,256]{1,0:T(8,128)(2,1)S(1)}, bf16[384,256]{1,0:T(8,128)(2,1)S(1)}, u32[]{:S(2)}, u32[]{:S(2)}) collective-permute-start(bf16[384,256]{1,0:T(8,128)(2,1)S(1)} %get-tuple-element.53), channel_id=1, source_target_pairs={{0,2},{1,3},{2,0},{3,1},{4,6},{5,7},{6,4},{7,5},{8,10},{9,11},{10,... | collective-permute-start | bytes 589832 | tf_op jit(solution)/shard_map/ppermute | solution.py:474
  100.2 14.8 %collective-permute-start.2 = (bf16[384,256]{1,0:T(8,128)(2,1)S(1)}, bf16[384,256]{1,0:T(8,128)(2,1)S(1)}, u32[]{:S(2)}, u32[]{:S(2)}) collective-permute-start(bf16[384,256]{1,0:T(8,128)(2,1)S(1)} %get-tuple-element.54), channel_id=1, source_target_pairs={{0,4},{1,5},{2,6},{3,7},{4,0},{5,1},{6,2},{7,3},{8,12},{9,13},{10,... | collective-permute-start | bytes 589832 | tf_op jit(solution)/shard_map/ppermute | solution.py:474
  104.6 12.9 %collective-permute-start.3 = (bf16[384,256]{1,0:T(8,128)(2,1)S(1)}, bf16[384,256]{1,0:T(8,128)(2,1)S(1)}, u32[]{:S(2)}, u32[]{:S(2)}) collective-permute-start(bf16[384,256]{1,0:T(8,128)(2,1)S(1)} %get-tuple-element.55), channel_id=1, source_target_pairs={{0,6},{1,7},{2,4},{3,5},{4,2},{5,3},{6,0},{7,1},{8,14},{9,15},{10,... | collective-permute-start | bytes 589832 | tf_op jit(solution)/shard_map/ppermute | solution.py:474
  106.5 25.6 %collective-permute-start.4 = (bf16[384,256]{1,0:T(8,128)(2,1)S(1)}, bf16[384,256]{1,0:T(8,128)(2,1)S(1)}, u32[]{:S(2)}, u32[]{:S(2)}) collective-permute-start(bf16[384,256]{1,0:T(8,128)(2,1)S(1)} %get-tuple-element.56), channel_id=1, source_target_pairs={{0,8},{1,9},{2,10},{3,11},{4,12},{5,13},{6,14},{7,15},{8,0},{9,1},... | collective-permute-start | bytes 589832 | tf_op jit(solution)/shard_map/ppermute | solution.py:474
  107.3 29.0 %collective-permute-start.5 = (bf16[384,256]{1,0:T(8,128)(2,1)S(1)}, bf16[384,256]{1,0:T(8,128)(2,1)S(1)}, u32[]{:S(2)}, u32[]{:S(2)}) collective-permute-start(bf16[384,256]{1,0:T(8,128)(2,1)S(1)} %get-tuple-element.57), channel_id=1, source_target_pairs={{0,10},{1,11},{2,8},{3,9},{4,14},{5,15},{6,12},{7,13},{8,2},{9,3},... | collective-permute-start | bytes 589832 | tf_op jit(solution)/shard_map/ppermute | solution.py:474
  112.6 23.6 %collective-permute-start.6 = (bf16[384,256]{1,0:T(8,128)(2,1)S(1)}, bf16[384,256]{1,0:T(8,128)(2,1)S(1)}, u32[]{:S(2)}, u32[]{:S(2)}) collective-permute-start(bf16[384,256]{1,0:T(8,128)(2,1)S(1)} %get-tuple-element.58), channel_id=1, source_target_pairs={{0,12},{1,13},{2,14},{3,15},{4,8},{5,9},{6,10},{7,11},{8,4},{9,5},... | collective-permute-start | bytes 589832 | tf_op jit(solution)/shard_map/ppermute | solution.py:474
  115.0 21.3 %collective-permute-start.7 = (bf16[384,256]{1,0:T(8,128)(2,1)S(1)}, bf16[384,256]{1,0:T(8,128)(2,1)S(1)}, u32[]{:S(2)}, u32[]{:S(2)}) collective-permute-start(bf16[384,256]{1,0:T(8,128)(2,1)S(1)} %get-tuple-element.59), channel_id=1, source_target_pairs={{0,14},{1,15},{2,12},{3,13},{4,10},{5,11},{6,8},{7,9},{8,6},{9,7},... | collective-permute-start | bytes 589832 | tf_op jit(solution)/shard_map/ppermute | solution.py:474
  139.1 15.9 %collective-permute-start.8 = (bf16[384,128]{1,0:T(8,128)(2,1)S(1)}, bf16[384,128]{1,0:T(8,128)(2,1)S(1)}, u32[]{:S(2)}, u32[]{:S(2)}) collective-permute-start(bf16[384,128]{1,0:T(8,128)(2,1)S(1)} %get-tuple-element.65), channel_id=1, source_target_pairs={{0,2},{1,3},{2,0},{3,1},{4,6},{5,7},{6,4},{7,5},{8,10},{9,11},{10,... | collective-permute-start | bytes 294920 | tf_op jit(solution)/shard_map/ppermute | solution.py:474
  140.7 15.1 %collective-permute-start.9 = (bf16[384,128]{1,0:T(8,128)(2,1)S(1)}, bf16[384,128]{1,0:T(8,128)(2,1)S(1)}, u32[]{:S(2)}, u32[]{:S(2)}) collective-permute-start(bf16[384,128]{1,0:T(8,128)(2,1)S(1)} %get-tuple-element.66), channel_id=1, source_target_pairs={{0,4},{1,5},{2,6},{3,7},{4,0},{5,1},{6,2},{7,3},{8,12},{9,13},{10,... | collective-permute-start | bytes 294920 | tf_op jit(solution)/shard_map/ppermute | solution.py:474
  151.5 6.4 %collective-permute-start.15 = (bf16[384,128]{1,0:T(8,128)(2,1)S(1)}, bf16[384,128]{1,0:T(8,128)(2,1)S(1)}, u32[]{:S(2)}, u32[]{:S(2)}) collective-permute-start(bf16[384,128]{1,0:T(8,128)(2,1)S(1)} %get-tuple-element.73), channel_id=1, source_target_pairs={{0,2},{1,3},{2,0},{3,1},{4,6},{5,7},{6,4},{7,5},{8,10},{9,11},{10,... | collective-permute-start | bytes 294920 | tf_op jit(solution)/shard_map/ppermute | solution.py:474
  152.0 8.1 %collective-permute-start.16 = (bf16[384,128]{1,0:T(8,128)(2,1)S(1)}, bf16[384,128]{1,0:T(8,128)(2,1)S(1)}, u32[]{:S(2)}, u32[]{:S(2)}) collective-permute-start(bf16[384,128]{1,0:T(8,128)(2,1)S(1)} %get-tuple-element.74), channel_id=1, source_target_pairs={{0,4},{1,5},{2,6},{3,7},{4,0},{5,1},{6,2},{7,3},{8,12},{9,13},{10,... | collective-permute-start | bytes 294920 | tf_op jit(solution)/shard_map/ppermute | solution.py:474
  152.0 10.6 %collective-permute-start.17 = (bf16[384,128]{1,0:T(8,128)(2,1)S(1)}, bf16[384,128]{1,0:T(8,128)(2,1)S(1)}, u32[]{:S(2)}, u32[]{:S(2)}) collective-permute-start(bf16[384,128]{1,0:T(8,128)(2,1)S(1)} %get-tuple-element.75), channel_id=1, source_target_pairs={{0,6},{1,7},{2,4},{3,5},{4,2},{5,3},{6,0},{7,1},{8,14},{9,15},{10,... | collective-permute-start | bytes 294920 | tf_op jit(solution)/shard_map/ppermute | solution.py:474
  155.0 15.1 %collective-permute-start.18 = (bf16[384,128]{1,0:T(8,128)(2,1)S(1)}, bf16[384,128]{1,0:T(8,128)(2,1)S(1)}, u32[]{:S(2)}, u32[]{:S(2)}) collective-permute-start(bf16[384,128]{1,0:T(8,128)(2,1)S(1)} %get-tuple-element.76), channel_id=1, source_target_pairs={{0,8},{1,9},{2,10},{3,11},{4,12},{5,13},{6,14},{7,15},{8,0},{9,1},... | collective-permute-start | bytes 294920 | tf_op jit(solution)/shard_map/ppermute | solution.py:474
  155.7 20.0 %collective-permute-start.19 = (bf16[384,128]{1,0:T(8,128)(2,1)S(1)}, bf16[384,128]{1,0:T(8,128)(2,1)S(1)}, u32[]{:S(2)}, u32[]{:S(2)}) collective-permute-start(bf16[384,128]{1,0:T(8,128)(2,1)S(1)} %get-tuple-element.77), channel_id=1, source_target_pairs={{0,10},{1,11},{2,8},{3,9},{4,14},{5,15},{6,12},{7,13},{8,2},{9,3},... | collective-permute-start | bytes 294920 | tf_op jit(solution)/shard_map/ppermute | solution.py:474
  157.8 17.9 %collective-permute-start.20 = (bf16[384,128]{1,0:T(8,128)(2,1)S(1)}, bf16[384,128]{1,0:T(8,128)(2,1)S(1)}, u32[]{:S(2)}, u32[]{:S(2)}) collective-permute-start(bf16[384,128]{1,0:T(8,128)(2,1)S(1)} %get-tuple-element.78), channel_id=1, source_target_pairs={{0,12},{1,13},{2,14},{3,15},{4,8},{5,9},{6,10},{7,11},{8,4},{9,5},... | collective-permute-start | bytes 294920 | tf_op jit(solution)/shard_map/ppermute | solution.py:474
  160.1 17.6 %collective-permute-start.21 = (bf16[384,128]{1,0:T(8,128)(2,1)S(1)}, bf16[384,128]{1,0:T(8,128)(2,1)S(1)}, u32[]{:S(2)}, u32[]{:S(2)}) collective-permute-start(bf16[384,128]{1,0:T(8,128)(2,1)S(1)} %get-tuple-element.79), channel_id=1, source_target_pairs={{0,14},{1,15},{2,12},{3,13},{4,10},{5,11},{6,8},{7,9},{8,6},{9,7},... | collective-permute-start | bytes 294920 | tf_op jit(solution)/shard_map/ppermute | solution.py:474
  162.6 27.5 %collective-permute-start.10 = (bf16[384,128]{1,0:T(8,128)(2,1)S(1)}, bf16[384,128]{1,0:T(8,128)(2,1)S(1)}, u32[]{:S(2)}, u32[]{:S(2)}) collective-permute-start(bf16[384,128]{1,0:T(8,128)(2,1)S(1)} %get-tuple-element.67), channel_id=1, source_target_pairs={{0,6},{1,7},{2,4},{3,5},{4,2},{5,3},{6,0},{7,1},{8,14},{9,15},{10,... | collective-permute-start | bytes 294920 | tf_op jit(solution)/shard_map/ppermute | solution.py:474
  170.1 20.1 %collective-permute-start.11 = (bf16[384,128]{1,0:T(8,128)(2,1)S(1)}, bf16[384,128]{1,0:T(8,128)(2,1)S(1)}, u32[]{:S(2)}, u32[]{:S(2)}) collective-permute-start(bf16[384,128]{1,0:T(8,128)(2,1)S(1)} %get-tuple-element.68), channel_id=1, source_target_pairs={{0,8},{1,9},{2,10},{3,11},{4,12},{5,13},{6,14},{7,15},{8,0},{9,1},... | collective-permute-start | bytes 294920 | tf_op jit(solution)/shard_map/ppermute | solution.py:474
  175.7 14.5 %collective-permute-start.12 = (bf16[384,128]{1,0:T(8,128)(2,1)S(1)}, bf16[384,128]{1,0:T(8,128)(2,1)S(1)}, u32[]{:S(2)}, u32[]{:S(2)}) collective-permute-start(bf16[384,128]{1,0:T(8,128)(2,1)S(1)} %get-tuple-element.69), channel_id=1, source_target_pairs={{0,10},{1,11},{2,8},{3,9},{4,14},{5,15},{6,12},{7,13},{8,2},{9,3},... | collective-permute-start | bytes 294920 | tf_op jit(solution)/shard_map/ppermute | solution.py:474
  175.7 14.5 %collective-permute-start.13 = (bf16[384,128]{1,0:T(8,128)(2,1)S(1)}, bf16[384,128]{1,0:T(8,128)(2,1)S(1)}, u32[]{:S(2)}, u32[]{:S(2)}) collective-permute-start(bf16[384,128]{1,0:T(8,128)(2,1)S(1)} %get-tuple-element.70), channel_id=1, source_target_pairs={{0,12},{1,13},{2,14},{3,15},{4,8},{5,9},{6,10},{7,11},{8,4},{9,5},... | collective-permute-start | bytes 294920 | tf_op jit(solution)/shard_map/ppermute | solution.py:474
  177.7 12.5 %collective-permute-start.14 = (bf16[384,128]{1,0:T(8,128)(2,1)S(1)}, bf16[384,128]{1,0:T(8,128)(2,1)S(1)}, u32[]{:S(2)}, u32[]{:S(2)}) collective-permute-start(bf16[384,128]{1,0:T(8,128)(2,1)S(1)} %get-tuple-element.71), channel_id=1, source_target_pairs={{0,14},{1,15},{2,12},{3,13},{4,10},{5,11},{6,8},{7,9},{8,6},{9,7},... | collective-permute-start | bytes 294920 | tf_op jit(solution)/shard_map/ppermute | solution.py:474
  195.0 2.6 collective-permute-start.23
  195.1 2.6 collective-permute-start.22
  201.7 23.6 %all-to-all-start.1 = ((bf16[16,24,1024]{2,1,0:T(8,128)(2,1)}), bf16[16,24,1024]{2,1,0:T(8,128)(2,1)S(1)}, u32[]{:S(2)}, u32[]{:S(2)}) async-start(bf16[16,24,1024]{2,1,0:T(8,128)(2,1)} %bitcast.12), calls=%async_computation.1 | async-start | bytes 1572864 | tf_op jit(solution)/shard_map/all_to_all | solution.py:465
  206.5 48.9 %all-gather.6.cloned.1.call-start = ((), (), s32[]{:S(2)}) async-start(), calls=%async_computation.4 | async-start | bytes 1114112 | tf_op jit(solution)/shard_map/all_gather | solution.py:515
  212.9 2.4 collective-permute-start.24
  225.2 31.8 %all-to-all-start.2 = ((bf16[16,24,1024]{2,1,0:T(8,128)(2,1)}), bf16[16,24,1024]{2,1,0:T(8,128)(2,1)S(1)}, u32[]{:S(2)}, u32[]{:S(2)}) async-start(bf16[16,24,1024]{2,1,0:T(8,128)(2,1)} %bitcast.15), calls=%async_computation.2 | async-start | bytes 1572864 | tf_op jit(solution)/shard_map/all_to_all | solution.py:465
  (15 other events, 93.5 us)
Sparse Core Ops, SparseCore 0:
  25.3 47.5 all-gather.3
  214.1 41.2 all-gather.5

commit v4 on v3

--- a/solution.py
+++ b/solution.py
@@ -43,8 +43,31 @@
     return ids, jnp.sum(before * onehot, axis=1, keepdims=True)
 
 
-def dispatch_kernel(slices, bias_ref, ids_ref, tok_ref, bcd_ref, *outs):
-    pack_ref, out_ref = outs
+def fetched(refs, buffers, sems):
+    copies = [
+        pltpu.make_async_copy(ref, buffer, sems.at[i])
+        for i, (ref, buffer) in enumerate(zip(refs, buffers))
+    ]
+    for copy in copies:
+        copy.start()
+    for copy in copies:
+        copy.wait()
+
+
+def fetching_call(kernel, operands, out_shape, name):
+    buffers = [pltpu.VMEM(a.shape, a.dtype) for a in operands]
+    return pl.pallas_call(
+        kernel,
+        out_shape=out_shape,
+        in_specs=[pl.BlockSpec(memory_space=pl.ANY)] * len(operands),
+        scratch_shapes=[*buffers, pltpu.SemaphoreType.DMA((len(operands),))],
+        compiler_params=params(),
+        name=name,
+    )(*operands)
+
+
+def dispatch_kernel(slices, ids_hbm, tok_hbm, out_ref, ids_ref, tok_ref, sems):
+    fetched((ids_hbm, tok_hbm), (ids_ref, tok_ref), sems)
     rows, width = tok_ref.shape
     depth = width // slices
     ids, slot = route(ids_ref[...])
@@ -64,6 +87,23 @@
             piece = jnp.concatenate([g[e * CAP : (e + 1) * CAP] for g in got], axis=0)
             out_ref[e * slices * CAP : (e + 1) * slices * CAP, c : c + step] = piece.astype(bf16)
 
+
+def dispatch(ids_row, tokens, slices):
+    width = tokens.shape[1]
+    return fetching_call(
+        functools.partial(dispatch_kernel, slices),
+        (ids_row, tokens),
+        jax.ShapeDtypeStruct((EXPERTS * slices * CAP, width // slices), bf16),
+        "dispatch",
+    )
+
+
+def pack_kernel(*refs):
+    pack_ref = refs[4]
+    bias_ref, ids_ref, tok_ref, bcd_ref, sems = refs[5:]
+    fetched(refs[:4], refs[5:9], sems)
+    rows = tok_ref.shape[0]
+    ids, slot = route(ids_ref[...])
     across = (((1,), (1,)), ((), ()))
     tok = tok_ref[...]
     pack_ref[:, : 2 * NS] = lax.dot_general(
@@ -73,27 +113,25 @@
     raw = lax.dot_general(
         tok, jnp.concatenate([steps] * 4, axis=0), across, preferred_element_type=f32
     )
-    lane = iota((rows, 128), 1)
-    for h in range(HEADS):
-        raw = raw + jnp.where(lane % HEADS == h, bias_ref[h], 0.0)
+    spread = (iota((HEADS, 128), 1) % HEADS == iota((HEADS, 128), 0)).astype(f32)
+    raw = raw + jnp.dot(
+        bias_ref[...], spread, precision=lax.Precision.HIGHEST, preferred_element_type=f32
+    )
     steps_dt = jnp.maximum(raw, 0.0) + jnp.log1p(jnp.exp(-jnp.abs(raw)))
     coarse = steps_dt.astype(bf16).astype(f32)
+    lane = iota((rows, 128), 1)
     side = jnp.where(lane < HEADS, coarse, steps_dt - coarse)
     side = jnp.where(lane == 2 * HEADS, ids, jnp.where(lane == 2 * HEADS + 1, slot, side))
     pack_ref[:, 2 * NS :] = jnp.where(lane < 2 * HEADS + 2, side, 0.0).astype(bf16)
 
 
-def dispatch(bias, ids_row, tokens, bcd, slices):
-    rows, width = tokens.shape
-    vmem = pl.BlockSpec(memory_space=pltpu.VMEM)
-    out = jax.ShapeDtypeStruct((EXPERTS * slices * CAP, width // slices), bf16)
-    return pl.pallas_call(
-        functools.partial(dispatch_kernel, slices),
-        out_shape=(jax.ShapeDtypeStruct((rows, PACK), bf16), out),
-        in_specs=[pl.BlockSpec(memory_space=pltpu.SMEM), vmem, vmem, vmem],
-        compiler_params=params(),
-        name="dispatch",
-    )(bias, ids_row, tokens, bcd)
+def scan_operands(bias, ids_row, tokens, bcd):
+    return fetching_call(
+        pack_kernel,
+        (bias.reshape(1, -1), ids_row, tokens, bcd),
+        jax.ShapeDtypeStruct((tokens.shape[0], PACK), bf16),
+        "scan_operands",
+    )
 
 
 def in_kernel(count, shares, turns, place_ref, *refs):
@@ -298,79 +336,63 @@
     return z, state
 
 
-def chunk_product(z_refs, w_refs):
-    width = z_refs[0].shape[1]
+def out_kernel(kind, heads, counted, others, place_ref, *refs):
+    refs = list(refs)
+
+    def take(count):
+        got = refs[:count]
+        del refs[:count]
+        return got
+
+    z_refs, w_refs = take(EXPERTS * heads), take(EXPERTS * heads)
+    inverse_ref = take(1)[0] if counted else None
+    squares_refs = take(1 + others) if kind == "finish" else None
+    part_refs = take(others) if kind == "finish" else None
+    out_ref = take(1)[0]
+    rows, width = z_refs[0].shape
+    if counted:
+
+        @pl.when(pl.program_id(0) == 0)
+        def _():
+            squares = jnp.zeros((rows, 1), f32)
+            for q in range(EXPERTS):
+                for h in range(heads):
+                    z = z_refs[q * heads + h][...].astype(f32)
+                    z = z * inverse_ref[(place_ref[1] ^ q) * heads + h]
+                    squares = squares + jnp.sum(z * z, axis=1, keepdims=True)
+            refs[0][...] = squares
+
     group = max(1, 256 // width) if width % 128 == 0 else 1
     total = None
-    for q in range(0, EXPERTS, group):
-        z = [r[...] for r in z_refs[q : q + group]]
-        w = [r[...] for r in w_refs[q : q + group]]
+    for i in range(0, EXPERTS * heads, group):
+        z = [r[...] for r in z_refs[i : i + group]]
+        w = [r[...] for r in w_refs[i : i + group]]
         z = jnp.concatenate(z, axis=1) if group > 1 else z[0]
         w = jnp.concatenate(w, axis=0) if group > 1 else w[0]
         part = jnp.dot(z, w, preferred_element_type=f32)
         total = part if total is None else total + part
-    return total
-
-
-def chunk_squares(place_ref, z_refs, inverse_ref, heads, h):
-    total = jnp.zeros((z_refs[0].shape[0], 1), f32)
-    for q in range(EXPERTS):
-        z = z_refs[q][...].astype(f32) * inverse_ref[(place_ref[1] ^ q) * heads + h]
-        total = total + jnp.sum(z * z, axis=1, keepdims=True)
-    return total
-
-
-def out_kernel(layout, place_ref, *refs):
-    kind, heads, h, counted, others = layout
-    refs = list(refs)
-
-    def take(count):
-        got = refs[:count]
-        del refs[:count]
-        return got
-
-    z_refs, w_refs = take(EXPERTS), take(EXPERTS)
-    inverse_ref = take(1)[0] if counted else None
-    total_ref = take(1)[0] if kind != "begin" and h > 0 else None
-    before_ref = take(1)[0] if counted and kind == "send" and h > 0 else None
-    squares_refs = take(1 + others) if kind == "finish" else None
-    part_refs = take(others) if kind == "finish" else None
-    out_ref = take(1)[0]
-    if inverse_ref is not None:
-
-        @pl.when(pl.program_id(0) == 0)
-        def _():
-            squares = chunk_squares(place_ref, z_refs, inverse_ref, heads, h)
-            refs[0][...] = squares if before_ref is None else squares + before_ref[...]
-
-    total = chunk_product(z_refs, w_refs)
-    if total_ref is not None:
-        total = total + total_ref[0]
     if kind == "finish":
         squares = sum(r[...] for r in squares_refs)
         for part in part_refs:
             total = total + part[...].astype(f32)
-        total = total * lax.rsqrt(squares / INNER + 1e-05)
-        out_ref[...] = total.astype(bf16)
+        out_ref[...] = (total * lax.rsqrt(squares / INNER + 1e-05)).astype(bf16)
     else:
-        out_ref[0] = total.astype(out_ref.dtype)
-
-
-def out_projection(
-    kind, *, place, z, w_out, heads, h, chunk, inverse=None, total=None, squares=(), parts=()
-):
-    rows, width = z[0].shape
+        out_ref[0] = total.astype(bf16)
+
+
+def out_projection(kind, chunk, *, place, z, w_out, inverse=None, squares=(), parts=()):
+    heads = len(z[0])
+    rows, width = z[0][0].shape
     slices = INNER // w_out.shape[0]
     slice_width = w_out.shape[1] // slices
-    part = slice_width if kind == "begin" else slice_width // CHUNKS
-    count = {"begin": slices, "send": slices - 1, "finish": 1}[kind]
-    first = slices if kind == "finish" else 1
+    part = slice_width // CHUNKS
+    count, first = (slices - 1, 1) if kind == "send" else (1, 0)
     tile = min(512, part)
     tiles = part // tile
     whole = slice_width // tile
-    offset = 0 if kind == "begin" else chunk * tiles
-
-    def w_spec(q):
+    offset = chunk * tiles
+
+    def w_spec(q, h):
         return pl.BlockSpec(
             (width, tile),
             lambda n, place_ref: (
@@ -382,19 +404,12 @@
     def fixed(*dims):
         return pl.BlockSpec(dims, lambda n, place_ref: (0,) * len(dims))
 
-    operands = [*z, *([w_out] * EXPERTS)]
-    specs = [fixed(rows, width)] * EXPERTS + [w_spec(q) for q in range(EXPERTS)]
+    pieces = [(q, h) for q in range(EXPERTS) for h in range(heads)]
+    operands = [z[q][h] for q, h in pieces] + [w_out] * len(pieces)
+    specs = [fixed(rows, width)] * len(pieces) + [w_spec(q, h) for q, h in pieces]
     if inverse is not None:
         operands.append(inverse)
         specs.append(fixed(*inverse.shape))
-    if total is not None:
-        operands.append(total)
-        specs.append(
-            pl.BlockSpec(
-                (1, rows, tile),
-                lambda n, place_ref: (first - 1 + n // tiles, 0, offset + n % tiles),
-            )
-        )
     operands += [*squares, *parts]
     specs += [fixed(rows, 1)] * len(squares)
     specs += [pl.BlockSpec((rows, tile), lambda n, place_ref: (0, n))] * len(parts)
@@ -402,8 +417,7 @@
         out_shape = [jax.ShapeDtypeStruct((rows, part), bf16)]
         out_specs = [pl.BlockSpec((rows, tile), lambda n, place_ref: (0, n))]
     else:
-        dtype = f32 if kind == "begin" else bf16
-        out_shape = [jax.ShapeDtypeStruct((count, rows, part), dtype)]
+        out_shape = [jax.ShapeDtypeStruct((count, rows, part), bf16)]
         out_specs = [
             pl.BlockSpec((1, rows, tile), lambda n, place_ref: (n // tiles, 0, n % tiles))
         ]
@@ -411,15 +425,15 @@
         out_shape.append(jax.ShapeDtypeStruct((rows, 1), f32))
         out_specs.append(fixed(rows, 1))
     return pl.pallas_call(
-        functools.partial(out_kernel, (kind, heads, h, inverse is not None, len(parts))),
+        functools.partial(out_kernel, kind, heads, inverse is not None, len(parts)),
         out_shape=out_shape,
         grid_spec=pltpu.PrefetchScalarGridSpec(
             num_scalar_prefetch=1, grid=(count * tiles,), in_specs=specs, out_specs=out_specs
         ),
         compiler_params=params(),
         cost_estimate=pl.CostEstimate(
-            flops=2 * rows * EXPERTS * width * count * part,
-            bytes_accessed=2 * EXPERTS * width * count * part + 4 * rows * count * part,
+            flops=2 * rows * w_out.shape[0] * count * part,
+            bytes_accessed=2 * w_out.shape[0] * count * part + 2 * rows * count * part,
             transcendentals=0,
         ),
         name="out_" + kind,
@@ -467,12 +481,44 @@
     )
 
 
+def across(a, q, n, slices):
+    pairs = [(d, (d // slices ^ q) * slices + d % slices) for d in range(n)]
+    return lax.ppermute(a, "expert", pairs)
+
+
 def exchange(arrays, n, slices):
     out = list(arrays)
     for q in reversed(range(1, EXPERTS)):
-        pairs = [(d, (d // slices ^ q) * slices + d % slices) for d in range(n)]
-        out[q] = lax.ppermute(arrays[q], "expert", pairs)
+        out[q] = across(arrays[q], q, n, slices)
     return out
+
+
+def decode_state(states, want, chip, place, n, slices):
+    heads, _, width = states.shape
+    held, seats = states[None], []
+    for q in (4, 2, 1):
+        held = jnp.concatenate([held, across(held, q, n, slices)], axis=0)
+        seats.append(q)
+
+    def picked(head):
+        first = head * HEADDIM % (EXPERTS * heads * width) // width
+        pieces = []
+        for i in range(HEADDIM // width):
+            distance = (first + i) // heads ^ chip
+            seat = sum((distance // q % 2) << k for k, q in enumerate(seats))
+            pieces.append(
+                lax.dynamic_slice(held, (seat, (first + i) % heads, 0, 0), (1, 1, NS, width))
+            )
+        return jnp.concatenate(pieces, axis=0) if len(pieces) > 1 else pieces[0]
+
+    chosen = picked(want)
+    lies = want * HEADDIM // (EXPERTS * heads * width)
+    for r in range(1, slices):
+        asked = turn(want, n, slices, slices - r)
+        got = turn(picked(asked), n, slices, r)
+        chosen = jnp.where((place - lies + slices) % slices == r, got, chosen)
+    chosen = chosen.reshape(HEADDIM // width, NS, width).transpose(0, 2, 1)
+    return chosen.astype(f32).reshape(1, HEADDIM * NS)
 
 
 def shards(
@@ -491,19 +537,19 @@
     ids_row = expert_ids.reshape(1, -1)
     w_in, w_out = w_in[0], w_out[0]
 
-    pack, outgoing = dispatch(dt_bias, ids_row, tokens, w_bcd.T, slices)
+    landed = swap(dispatch(ids_row, tokens, slices))
+    pack = scan_operands(dt_bias, ids_row, tokens, w_bcd.T)
     pack = lax.all_gather(pack, "expert", axis=0, tiled=True)
-    landed = swap(outgoing)
+    own_heads = start // HEADDIM + jnp.arange(heads, dtype=jnp.int32)
+    weights = prepare(place, own_heads, decay_rate, skip_gain, pack)
+
     pieces = [landed] + [turn(landed, n, slices, r) for r in range(1, slices)]
-    own_heads = start // HEADDIM + jnp.arange(heads, dtype=jnp.int32)
     inner = [None] * EXPERTS
-    for order in ((7, 6), (5, 4), (3, 2), (1, 0)):
-        got = in_projection(place, pieces, w_in, units, order)
-        for q, a in zip(order, got):
+    for order in ((7, 6), (5, 4), (3, 2, 1), (0,)):
+        if order == (0,):
+            pieces, weights = lax.optimization_barrier((pieces, weights))
+        for q, a in zip(order, in_projection(place, pieces, w_in, units, order)):
             inner[q] = a
-        if order == (7, 6):
-            weights = prepare(place, own_heads, decay_rate, skip_gain, pack)
-            pieces, weights = lax.optimization_barrier((pieces, weights))
     x = exchange(inner, n, slices)
 
     gain = lax.dynamic_slice(norm_gain, (start,), (units,))
@@ -511,51 +557,24 @@
     for h in range(heads):
         rows, state = scan(x, weights, gain[h * width : (h + 1) * width].reshape(1, width), h)
         z.append(exchange(rows, n, slices))
-        states.append(state)
-    states = lax.all_gather(jnp.stack(states), "expert", axis=0, tiled=False)
+        states.append(state.astype(bf16))
+    z = [[z[h][q] for h in range(heads)] for q in range(EXPERTS)]
+    decoded = decode_state(jnp.stack(states), decode_heads[0], chip, place[0], n, slices)
 
     inverse = 1.0 / lax.dynamic_slice(norm_gain, (place[0] * in_dev,), (in_dev,))
     inverse = inverse.reshape(in_dev // width, 1, width)
-    project = functools.partial(out_projection, place=place, w_out=w_out, heads=heads)
-    total = None
-    squares = ()
-    for h in range(heads - 1):
-        total, squares = project("begin", z=z[h], h=h, chunk=0, inverse=inverse)
-        squares = (squares,)
-    h = heads - 1
+    project = functools.partial(out_projection, place=place, z=z, w_out=w_out)
     sent = []
     for k in range(CHUNKS):
-        first = inverse if k == 0 else None
-        got = project(
-            "send",
-            z=z[h],
-            h=h,
-            chunk=k,
-            inverse=first,
-            total=total,
-            squares=squares if k == 0 else (),
-        )
+        got = project("send", k, inverse=inverse if k == 0 else None)
         if k == 0:
-            all_squares = [got[1]] + [turn(got[1], n, slices, r) for r in range(1, slices)]
+            squares = [got[1]] + [turn(got[1], n, slices, r) for r in range(1, slices)]
         sent.append([turn(got[0][r - 1], n, slices, r) for r in range(1, slices)])
     back = []
     for k in range(CHUNKS):
-        [done] = project(
-            "finish", z=z[h], h=h, chunk=k, total=total, squares=all_squares, parts=sent[k]
-        )
+        [done] = project("finish", k, squares=squares, parts=sent[k])
         back.append(swap(done))
-    mixed = collect(ids_row, back, slices)
-
-    want = decode_heads[0] * HEADDIM
-    within = want % in_dev // width
-    states = states.reshape(EXPERTS, slices, heads, NS, width)
-    chosen = lax.dynamic_slice(
-        states,
-        (within // heads, want // in_dev, within % heads, 0, 0),
-        (HEADDIM // width, 1, 1, NS, width),
-    )
-    chosen = chosen.reshape(HEADDIM // width, NS, width).transpose(0, 2, 1)
-    return (mixed, chosen.reshape(1, HEADDIM * NS))
+    return (collect(ids_row, back, slices), decoded)
 
 
 def solution(mesh):

time: 267 us -> 277 us (1.037)
  blocking collectives: 0 us -> 43.4 us
  waiting for transfers between devices: 111 us -> 68.8 us
  local copies, waits for them, and re-layouts: 19.4 us -> 29.1 us
    all_to_all x0 -> x1, blocking collectives: none -> 43.4 us  [swap(): lax.all_to_all(a, 'expert', split_axis=0, concat_axis=0, axis_index_group...]
    all_to_all x3 -> x2, waiting for transfers between devices: 36.5 us -> 2.45 us  [swap(): lax.all_to_all(a, 'expert', split_axis=0, concat_axis=0, axis_index_group...]
    all_gather x1 -> x0, waiting for transfers between devices: 23.3 us -> none  [shards(): states = lax.all_gather(jnp.stack(states), 'expert', axis=0, tiled=False)]
    unnamed x34 -> x28, local copies, waits for them, and re-layouts: 17 us -> 27.5 us
    pallas_call x6, Pallas kernels: 29.3 us -> 20.1 us  [the longest x4 17.3 us: out_projection(): pl.pallas_call(functools.partial(out_kernel, kind, heads, inverse is not...]
    all_gather x1, waiting for transfers between devices: 15.4 us -> 22.7 us  [shards(): pack = lax.all_gather(pack, 'expert', axis=0, tiled=True)]
    ppermute x21 -> x24, waiting for transfers between devices: 31.8 us -> 37.9 us  [across(): return lax.ppermute(a, 'expert', pairs)]
    ppermute x21 -> x24, starting transfers between devices: 36.2 us -> 41.7 us  [across(): return lax.ppermute(a, 'expert', pairs)]
  transfers between devices with their start and end apart: 30 -> 33, of which waited for: 10 -> 14; matrix products, arithmetic and copies ran while one was open for 1% -> 1% of each run, Pallas kernels for 15% -> 15%
where the time goes in v4:
time: 277 us; the launch traced here: 276 us
  waiting for transfers between devices  68.8 us (25%)
  Pallas kernels  60.6 us (22%)
  starting transfers between devices  57.1 us (21%)
  blocking collectives  43.4 us (16%)
  local copies, waits for them, and re-layouts  29.1 us (11%)
  between operations  16 us (6%)
    all_to_all x1, blocking collectives, swap(): lax.all_to_all(a, 'expert', split_axis=0, concat_axis=0, axis_index_group...  43.4 us
    ppermute x24, starting transfers between devices, across(): return lax.ppermute(a, 'expert', pairs)  41.7 us
    ppermute x24, waiting for transfers between devices, across(): return lax.ppermute(a, 'expert', pairs)  37.9 us
    unnamed x28, local copies, waits for them, and re-layouts  27.5 us
    all_gather x1, waiting for transfers between devices, shards(): pack = lax.all_gather(pack, 'expert', axis=0, tiled=True)  22.7 us
    pallas_call x4, Pallas kernels, out_projection(): pl.pallas_call(functools.partial(out_kernel, kind, heads, inverse is not...  17.3 us
    pallas_call x4, Pallas kernels, in_projection(): pl.pallas_call(functools.partial(in_kernel, slices, shares, turns), out_s...  14.7 us
    all_to_all x2, starting transfers between devices, swap(): lax.all_to_all(a, 'expert', split_axis=0, concat_axis=0, axis_index_group...  13.6 us
  transfers between devices with their start and end apart: 33, of which 14 were waited for; matrix products, arithmetic and copies ran while one was open for 1% of the time, Pallas kernels for 15%

profile of v4, /device:TPU:0, one launch (start us, length us, event | category | flops | bytes accessed | tf_op | source)
XLA Modules:
  0.0 275.7 jit_solution(2587197507853841340)
XLA Ops:
  10.2 43.4 %all_to_all.33 = bf16[16,24,2048]{2,1,0:T(8,128)(2,1)S(1)} all-to-all(bf16[16,24,2048]{2,1,0:T(8,128)(2,1)S(1)} %bitcast.110), channel_id=1, replica_groups=mesh['groups'=2,'expert'=16] {'expert'}, dimensions={0} | all-to-all | bytes 3145728 | tf_op jit(solution)/shard_map/all_to_all | solution.py:479
  57.6 5.8 %copy-done.2 = bf16[1,4096,2048]{2,1,0:T(8,128)(2,1)S(1)} copy-done((bf16[1,4096,2048]{2,1,0:T(8,128)(2,1)S(1)}, bf16[1,4096,2048]{2,1,0:T(8,128)(2,1)}, u32[]{:S(2)}) %copy-start.2) | copy-done | bytes 16777240
  63.3 5.2 %in_projection.5 = (bf16[384,256]{1,0:T(8,128)(2,1)}, bf16[384,256]{1,0:T(8,128)(2,1)S(1)}, bf16[384,256]{1,0:T(8,128)(2,1)S(1)}) custom-call(s32[2]{0:T(128)S(1)} %pad_add_fusion.place_ref, bf16[384,2048]{1,0:T(8,128)(2,1)S(1)} %bitcast.106, bf16[384,2048]{1,0:T(8,128)(2,1)S(1)} %collective-permute-done.refs_1_, bf16[4096,2048]{1,0:T(8,128)(2,1)S(1)} %bitcast.97, ...), custom_call_target="tpu_custom_call" | custom-call | flops 2415919104 | bytes 9437184 | tf_op jit(solution)/shard_map/in_projection/pallas_call | solution.py:168
  72.1 4.0 %in_projection.6 = (bf16[384,256]{1,0:T(8,128)(2,1)}, bf16[384,256]{1,0:T(8,128)(2,1)}) custom-call(s32[2]{0:T(128)S(1)} %pad_add_fusion.place_ref, bf16[384,2048]{1,0:T(8,128)(2,1)S(1)} %bitcast.107, bf16[384,2048]{1,0:T(8,128)(2,1)S(1)} %collective-permute-done.refs_1_, bf16[4096,2048]{1,0:T(8,128)(2,1)S(1)} %bitcast.99, bf16[4096,2048]{1,0:T(8,128)(2,1)S(1)} %bitcast.100), custom_call_target="tpu_custom_call" | custom-call | flops 1610612736 | bytes 7340032 | tf_op jit(solution)/shard_map/in_projection/pallas_call | solution.py:168
  76.0 2.6 collective-permute-start.4
  79.7 4.0 %in_projection.7 = (bf16[384,256]{1,0:T(8,128)(2,1)}, bf16[384,256]{1,0:T(8,128)(2,1)}) custom-call(s32[2]{0:T(128)S(1)} %pad_add_fusion.place_ref, bf16[384,2048]{1,0:T(8,128)(2,1)S(1)} %bitcast.108, bf16[384,2048]{1,0:T(8,128)(2,1)S(1)} %collective-permute-done.refs_1_, bf16[4096,2048]{1,0:T(8,128)(2,1)S(1)} %bitcast.101, bf16[4096,2048]{1,0:T(8,128)(2,1)S(1)} %bitcast.102), custom_call_target="tpu_custom_call" | custom-call | flops 1610612736 | bytes 7340032 | tf_op jit(solution)/shard_map/in_projection/pallas_call | solution.py:168
  83.6 2.5 collective-permute-start.6
  87.7 22.7 %all-gather.2.cloned.1.call-done.pack_ref = bf16[2048,256]{1,0:T(8,128)(2,1)} async-done(((bf16[128,256]{1,0:T(8,128)(2,1)}), bf16[2048,256]{1,0:T(8,128)(2,1)}) %all-gather.2.cloned.1.call-update) | async-done | bytes 1048592 | tf_op jit(solution)/shard_map/all_gather | solution.py:542
  112.9 13.3 %scan_weights.1 = (bf16[2,8,384,384]{3,2,1,0:T(8,128)(2,1)S(1)}, bf16[2,8,384,64]{3,2,1,0:T(8,128)(2,1)S(1)}, bf16[2,8,64,384]{3,2,1,0:T(8,128)(2,1)S(1)}, f32[2,8,8,128]{3,2,1,0:T(8,128)S(1)}) custom-call(s32[2]{0:T(128)S(1)} %pad_add_fusion.place_ref, s32[2]{0:T(128)S(1)} %copy-done.12, f32[32]{0:T(128)S(1)} %copy-done.10, f32[32]{0:T(128)S(1)} %copy-done.11, ...), custom_call_target="tpu_custom_call" | custom-call | flops 2415919104 | bytes 4718592 | tf_op jit(solution)/shard_map/scan_weights/pallas_call | solution.py:257
  126.2 5.8 %copy-done.3 = bf16[1,4096,2048]{2,1,0:T(8,128)(2,1)S(1)} copy-done((bf16[1,4096,2048]{2,1,0:T(8,128)(2,1)S(1)}, bf16[1,4096,2048]{2,1,0:T(8,128)(2,1)}, u32[]{:S(2)}) %copy-start.3) | copy-done | bytes 16777240
  133.6 4.7 %scan.2 = (bf16[384,128]{1,0:T(8,128)(2,1)S(1)}, bf16[384,128]{1,0:T(8,128)(2,1)S(1)}, bf16[384,128]{1,0:T(8,128)(2,1)S(1)}, bf16[384,128]{1,0:T(8,128)(2,1)S(1)...) custom-call(bf16[384,256]{1,0:T(8,128)(2,1)S(1)} %in_projection.4.re, ...), custom_call_target="tpu_custom_call" | custom-call | flops 402653184 | bytes 2359296 | tf_op jit(solution)/shard_map/scan/pallas_call | solution.py:312
  139.8 4.7 %scan.3 = (bf16[384,128]{1,0:T(8,128)(2,1)S(1)}, bf16[384,128]{1,0:T(8,128)(2,1)S(1)}, bf16[384,128]{1,0:T(8,128)(2,1)S(1)}, bf16[384,128]{1,0:T(8,128)(2,1)S(1)...) custom-call(bf16[384,256]{1,0:T(8,128)(2,1)S(1)} %in_projection.4.re, ...), custom_call_target="tpu_custom_call" | custom-call | flops 402653184 | bytes 2359296 | tf_op jit(solution)/shard_map/scan/pallas_call | solution.py:312
  150.9 2.1 collective-permute-start.15
  153.0 3.3 %collective-permute-done.11.refs_5_ = bf16[384,128]{1,0:T(8,128)(2,1)S(1)} collective-permute-done((bf16[384,128]{1,0:T(8,128)(2,1)S(1)}, bf16[384,128]{1,0:T(8,128)(2,1)S(1)}, u32[]{:S(2)}, u32[]{:S(2)}) %collective-permute-start.11) | collective-permute-done | bytes 98336 | tf_op jit(solution)/shard_map/ppermute | solution.py:486
  156.5 3.1 %collective-permute-done.12.refs_6_ = bf16[384,128]{1,0:T(8,128)(2,1)S(1)} collective-permute-done((bf16[384,128]{1,0:T(8,128)(2,1)S(1)}, bf16[384,128]{1,0:T(8,128)(2,1)S(1)}, u32[]{:S(2)}, u32[]{:S(2)}) %collective-permute-start.12) | collective-permute-done | bytes 98336 | tf_op jit(solution)/shard_map/ppermute | solution.py:486
  162.4 8.5 %collective-permute-start.19 = (bf16[384,128]{1,0:T(8,128)(2,1)S(1)}, bf16[384,128]{1,0:T(8,128)(2,1)S(1)}, u32[]{:S(2)}, u32[]{:S(2)}) collective-permute-start(bf16[384,128]{1,0:T(8,128)(2,1)S(1)} %get-tuple-element.69), channel_id=1, source_target_pairs={{0,12},{1,13},{2,14},{3,15},{4,8},{5,9},{6,10},{7,11},{8,4},{9,5},... | collective-permute-start | bytes 294920 | tf_op jit(solution)/shard_map/ppermute | solution.py:486
  170.9 3.6 %collective-permute-start.20 = (bf16[384,128]{1,0:T(8,128)(2,1)S(1)}, bf16[384,128]{1,0:T(8,128)(2,1)S(1)}, u32[]{:S(2)}, u32[]{:S(2)}) collective-permute-start(bf16[384,128]{1,0:T(8,128)(2,1)S(1)} %get-tuple-element.70), channel_id=1, source_target_pairs={{0,14},{1,15},{2,12},{3,13},{4,10},{5,11},{6,8},{7,9},{8,6},{9,7},... | collective-permute-start | bytes 294920 | tf_op jit(solution)/shard_map/ppermute | solution.py:486
  176.0 3.7 %collective-permute-done.17.refs_11_ = bf16[384,128]{1,0:T(8,128)(2,1)S(1)} collective-permute-done((bf16[384,128]{1,0:T(8,128)(2,1)S(1)}, bf16[384,128]{1,0:T(8,128)(2,1)S(1)}, u32[]{:S(2)}, u32[]{:S(2)}) %collective-permute-start.17) | collective-permute-done | bytes 98336 | tf_op jit(solution)/shard_map/ppermute | solution.py:486
  179.7 2.2 collective-permute-done.21.refs_15_
  181.9 5.8 %copy-done = bf16[1,2048,4096]{2,1,0:T(8,128)(2,1)S(1)} copy-done((bf16[1,2048,4096]{2,1,0:T(8,128)(2,1)S(1)}, bf16[1,2048,4096]{2,1,0:T(8,128)(2,1)}, u32[]{:S(2)}) %copy-start) | copy-done | bytes 16777240
  187.7 4.7 %out_send.2 = (bf16[1,384,1024]{2,1,0:T(8,128)(2,1)S(1)}, f32[384,1]{1,0:T(8,128)S(1)}) custom-call(s32[2]{0:T(128)S(1)} %pad_add_fusion.place_ref, bf16[384,128]{1,0:T(8,128)(2,1)S(1)} %get-tuple-element.56.refs_0_, bf16[384,128]{1,0:T(8,128)(2,1)S(1)} %get-tuple-element.57.refs_1_, bf16[384,128]{1,0:T(8,128)(2,1)S(1)} %collective-permute-done.8.refs_2_, ...), custom_call_target="tpu_custom_call" | custom-call | flops 1610612736 | bytes 4980736 | tf_op jit(solution)/shard_map/out_send/pallas_call | solution.py:427
  195.0 4.4 %out_finish.2 = bf16[384,1024]{1,0:T(8,128)(2,1)} custom-call(s32[2]{0:T(128)S(1)} %pad_add_fusion.place_ref, bf16[384,128]{1,0:T(8,128)(2,1)S(1)} %get-tuple-element.56.refs_0_, bf16[384,128]{1,0:T(8,128)(2,1)S(1)} %get-tuple-element.57.refs_1_, bf16[384,128]{1,0:T(8,128)(2,1)S(1)} %collective-permute-done.8.refs_2_, ...), custom_call_target="tpu_custom_call" | custom-call | flops 1610612736 | bytes 4980736 | tf_op jit(solution)/shard_map/out_finish/pallas_call | solution.py:427
  199.4 7.8 %all-to-all-start.1 = ((bf16[16,24,1024]{2,1,0:T(8,128)(2,1)}), bf16[16,24,1024]{2,1,0:T(8,128)(2,1)}, u32[]{:S(2)}, u32[]{:S(2)}) async-start(bf16[16,24,1024]{2,1,0:T(8,128)(2,1)} %bitcast.13), calls=%async_computation.1 | async-start | bytes 1572864 | tf_op jit(solution)/shard_map/all_to_all | solution.py:479
  207.3 5.8 %copy-done.1 = bf16[1,2048,4096]{2,1,0:T(8,128)(2,1)S(1)} copy-done((bf16[1,2048,4096]{2,1,0:T(8,128)(2,1)S(1)}, bf16[1,2048,4096]{2,1,0:T(8,128)(2,1)}, u32[]{:S(2)}) %copy-start.1) | copy-done | bytes 16777240
  213.0 3.8 %out_send.3 = bf16[1,384,1024]{2,1,0:T(8,128)(2,1)S(1)} custom-call(s32[2]{0:T(128)S(1)} %pad_add_fusion.place_ref, bf16[384,128]{1,0:T(8,128)(2,1)S(1)} %get-tuple-element.56.refs_0_, bf16[384,128]{1,0:T(8,128)(2,1)S(1)} %get-tuple-element.57.refs_1_, bf16[384,128]{1,0:T(8,128)(2,1)S(1)} %collective-permute-done.8.refs_2_, ...), custom_call_target="tpu_custom_call" | custom-call | flops 1610612736 | bytes 4980736 | tf_op jit(solution)/shard_map/out_send/pallas_call | solution.py:427
  219.1 4.4 %out_finish.3 = bf16[384,1024]{1,0:T(8,128)(2,1)} custom-call(s32[2]{0:T(128)S(1)} %pad_add_fusion.place_ref, bf16[384,128]{1,0:T(8,128)(2,1)S(1)} %get-tuple-element.56.refs_0_, bf16[384,128]{1,0:T(8,128)(2,1)S(1)} %get-tuple-element.57.refs_1_, bf16[384,128]{1,0:T(8,128)(2,1)S(1)} %collective-permute-done.8.refs_2_, ...), custom_call_target="tpu_custom_call" | custom-call | flops 1610612736 | bytes 4980736 | tf_op jit(solution)/shard_map/out_finish/pallas_call | solution.py:427
  223.6 2.4 all-to-all-done.1
  226.0 5.8 %all-to-all-start.2 = ((bf16[16,24,1024]{2,1,0:T(8,128)(2,1)}), bf16[16,24,1024]{2,1,0:T(8,128)(2,1)S(1)}, u32[]{:S(2)}, u32[]{:S(2)}) async-start(bf16[16,24,1024]{2,1,0:T(8,128)(2,1)} %bitcast.16), calls=%async_computation.2 | async-start | bytes 1572864 | tf_op jit(solution)/shard_map/all_to_all | solution.py:479
  231.8 2.9 %collective-permute-start.25 = (bf16[1,2,64,128]{3,2,1,0:T(8,128)(2,1)S(1)}, bf16[1,2,64,128]{3,2,1,0:T(8,128)(2,1)S(1)}, u32[]{:S(2)}, u32[]{:S(2)}) collective-permute-start(bf16[1,2,64,128]{3,2,1,0:T(8,128)(2,1)S(1)} %maximum_bitcast_fusion), channel_id=1, source_target_pairs={{0,8},{1,9},{2,10},{3,11},{4,12},{5,13},{6,14},{7,15},{8,0},{9,1},... | collective-permute-start | bytes 98312 | tf_op jit(solution)/shard_map/ppermute | solution.py:486
  234.7 19.4 %collective-permute-done.25 = bf16[1,2,64,128]{3,2,1,0:T(8,128)(2,1)S(1)} collective-permute-done((bf16[1,2,64,128]{3,2,1,0:T(8,128)(2,1)S(1)}, bf16[1,2,64,128]{3,2,1,0:T(8,128)(2,1)S(1)}, u32[]{:S(2)}, u32[]{:S(2)}) %collective-permute-start.25) | collective-permute-done | bytes 32800 | tf_op jit(solution)/shard_map/ppermute | solution.py:486
  254.2 4.3 %collective-permute-done.26 = bf16[2,2,64,128]{3,2,1,0:T(8,128)(2,1)S(1)} collective-permute-done((bf16[2,2,64,128]{3,2,1,0:T(8,128)(2,1)S(1)}, bf16[2,2,64,128]{3,2,1,0:T(8,128)(2,1)S(1)}, u32[]{:S(2)}, u32[]{:S(2)}) %collective-permute-start.26) | collective-permute-done | bytes 65568 | tf_op jit(solution)/shard_map/ppermute | solution.py:486
  265.6 3.2 %collect.1 = bf16[128,4096]{1,0:T(8,128)(2,1)} custom-call(s32[1,128]{1,0:T(1,128)S(1)} %bitcast.117, bf16[384,1024]{1,0:T(8,128)(2,1)} %bitcast.14.refs_0_, bf16[384,1024]{1,0:T(8,128)(2,1)S(1)} %bitcast.111), custom_call_target="tpu_custom_call" | custom-call | tf_op jit(solution)/shard_map/collect/pallas_call | solution.py:464
  (93 shorter events, 40.2 us)
Async XLA Ops:
  7.2 103.2 %all-gather.2.cloned.1.call-start = ((), (), s32[]{:S(2)}) async-start(), calls=%async_computation.3 | async-start | bytes 1114112 | tf_op jit(solution)/shard_map/all_gather | solution.py:542
  53.6 3.9 %collective-permute-start = (bf16[384,2048]{1,0:T(8,128)(2,1)S(1)}, bf16[384,2048]{1,0:T(8,128)(2,1)S(1)}, u32[]{:S(2)}, u32[]{:S(2)}) collective-permute-start(bf16[384,2048]{1,0:T(8,128)(2,1)S(1)} %bitcast.105), channel_id=1, source_target_pairs={{0,1},{1,0},{2,3},{3,2},{4,5},{5,4},{6,7},{7,6},{8,9},{9,8},{10,11... | collective-permute-start | bytes 4718600 | tf_op jit(solution)/shard_map/ppermute | solution.py:473
  68.6 15.1 %collective-permute-start.1 = (bf16[384,256]{1,0:T(8,128)(2,1)S(1)}, bf16[384,256]{1,0:T(8,128)(2,1)S(1)}, u32[]{:S(2)}, u32[]{:S(2)}) collective-permute-start(bf16[384,256]{1,0:T(8,128)(2,1)S(1)} %get-tuple-element.45), channel_id=1, source_target_pairs={{0,2},{1,3},{2,0},{3,1},{4,6},{5,7},{6,4},{7,5},{8,10},{9,11},{10,... | collective-permute-start | bytes 589832 | tf_op jit(solution)/shard_map/ppermute | solution.py:486
  69.8 16.3 %collective-permute-start.2 = (bf16[384,256]{1,0:T(8,128)(2,1)S(1)}, bf16[384,256]{1,0:T(8,128)(2,1)S(1)}, u32[]{:S(2)}, u32[]{:S(2)}) collective-permute-start(bf16[384,256]{1,0:T(8,128)(2,1)S(1)} %get-tuple-element.46), channel_id=1, source_target_pairs={{0,4},{1,5},{2,6},{3,7},{4,0},{5,1},{6,2},{7,3},{8,12},{9,13},{10,... | collective-permute-start | bytes 589832 | tf_op jit(solution)/shard_map/ppermute | solution.py:486
  71.3 62.2 %collective-permute-start.3 = (bf16[384,256]{1,0:T(8,128)(2,1)}, bf16[384,256]{1,0:T(8,128)(2,1)}, u32[]{:S(2)}, u32[]{:S(2)}) collective-permute-start(bf16[384,256]{1,0:T(8,128)(2,1)} %get-tuple-element.47), channel_id=1, source_target_pairs={{0,6},{1,7},{2,4},{3,5},{4,2},{5,3},{6,0},{7,1},{8,14},{9,15},{10,... | collective-permute-start | bytes 589832 | tf_op jit(solution)/shard_map/ppermute | solution.py:486
  76.0 57.5 %collective-permute-start.4 = (bf16[384,256]{1,0:T(8,128)(2,1)}, bf16[384,256]{1,0:T(8,128)(2,1)}, u32[]{:S(2)}, u32[]{:S(2)}) collective-permute-start(bf16[384,256]{1,0:T(8,128)(2,1)} %get-tuple-element.48), channel_id=1, source_target_pairs={{0,8},{1,9},{2,10},{3,11},{4,12},{5,13},{6,14},{7,15},{8,0},{9,1},... | collective-permute-start | bytes 589832 | tf_op jit(solution)/shard_map/ppermute | solution.py:486
  78.6 55.0 %collective-permute-start.5 = (bf16[384,256]{1,0:T(8,128)(2,1)}, bf16[384,256]{1,0:T(8,128)(2,1)}, u32[]{:S(2)}, u32[]{:S(2)}) collective-permute-start(bf16[384,256]{1,0:T(8,128)(2,1)} %get-tuple-element.49), channel_id=1, source_target_pairs={{0,10},{1,11},{2,8},{3,9},{4,14},{5,15},{6,12},{7,13},{8,2},{9,3},... | collective-permute-start | bytes 589832 | tf_op jit(solution)/shard_map/ppermute | solution.py:486
  83.6 49.9 %collective-permute-start.6 = (bf16[384,256]{1,0:T(8,128)(2,1)}, bf16[384,256]{1,0:T(8,128)(2,1)}, u32[]{:S(2)}, u32[]{:S(2)}) collective-permute-start(bf16[384,256]{1,0:T(8,128)(2,1)} %get-tuple-element.50), channel_id=1, source_target_pairs={{0,12},{1,13},{2,14},{3,15},{4,8},{5,9},{6,10},{7,11},{8,4},{9,5},... | collective-permute-start | bytes 589832 | tf_op jit(solution)/shard_map/ppermute | solution.py:486
  86.1 47.5 %collective-permute-start.7 = (bf16[384,256]{1,0:T(8,128)(2,1)}, bf16[384,256]{1,0:T(8,128)(2,1)}, u32[]{:S(2)}, u32[]{:S(2)}) collective-permute-start(bf16[384,256]{1,0:T(8,128)(2,1)} %get-tuple-element.51), channel_id=1, source_target_pairs={{0,14},{1,15},{2,12},{3,13},{4,10},{5,11},{6,8},{7,9},{8,6},{9,7},... | collective-permute-start | bytes 589832 | tf_op jit(solution)/shard_map/ppermute | solution.py:486
  138.3 9.8 %collective-permute-start.8 = (bf16[384,128]{1,0:T(8,128)(2,1)S(1)}, bf16[384,128]{1,0:T(8,128)(2,1)S(1)}, u32[]{:S(2)}, u32[]{:S(2)}) collective-permute-start(bf16[384,128]{1,0:T(8,128)(2,1)S(1)} %get-tuple-element.58), channel_id=1, source_target_pairs={{0,2},{1,3},{2,0},{3,1},{4,6},{5,7},{6,4},{7,5},{8,10},{9,11},{10,... | collective-permute-start | bytes 294920 | tf_op jit(solution)/shard_map/ppermute | solution.py:486
  144.5 5.6 %collective-permute-start.9 = (bf16[384,128]{1,0:T(8,128)(2,1)S(1)}, bf16[384,128]{1,0:T(8,128)(2,1)S(1)}, u32[]{:S(2)}, u32[]{:S(2)}) collective-permute-start(bf16[384,128]{1,0:T(8,128)(2,1)S(1)} %get-tuple-element.59), channel_id=1, source_target_pairs={{0,2},{1,3},{2,0},{3,1},{4,6},{5,7},{6,4},{7,5},{8,10},{9,11},{10,... | collective-permute-start | bytes 294920 | tf_op jit(solution)/shard_map/ppermute | solution.py:486
  145.1 5.8 %collective-permute-start.10 = (bf16[384,128]{1,0:T(8,128)(2,1)S(1)}, bf16[384,128]{1,0:T(8,128)(2,1)S(1)}, u32[]{:S(2)}, u32[]{:S(2)}) collective-permute-start(bf16[384,128]{1,0:T(8,128)(2,1)S(1)} %get-tuple-element.60), channel_id=1, source_target_pairs={{0,4},{1,5},{2,6},{3,7},{4,0},{5,1},{6,2},{7,3},{8,12},{9,13},{10,... | collective-permute-start | bytes 294920 | tf_op jit(solution)/shard_map/ppermute | solution.py:486
  145.1 11.1 %collective-permute-start.11 = (bf16[384,128]{1,0:T(8,128)(2,1)S(1)}, bf16[384,128]{1,0:T(8,128)(2,1)S(1)}, u32[]{:S(2)}, u32[]{:S(2)}) collective-permute-start(bf16[384,128]{1,0:T(8,128)(2,1)S(1)} %get-tuple-element.61), channel_id=1, source_target_pairs={{0,4},{1,5},{2,6},{3,7},{4,0},{5,1},{6,2},{7,3},{8,12},{9,13},{10,... | collective-permute-start | bytes 294920 | tf_op jit(solution)/shard_map/ppermute | solution.py:486
  147.1 12.5 %collective-permute-start.12 = (bf16[384,128]{1,0:T(8,128)(2,1)S(1)}, bf16[384,128]{1,0:T(8,128)(2,1)S(1)}, u32[]{:S(2)}, u32[]{:S(2)}) collective-permute-start(bf16[384,128]{1,0:T(8,128)(2,1)S(1)} %get-tuple-element.62), channel_id=1, source_target_pairs={{0,6},{1,7},{2,4},{3,5},{4,2},{5,3},{6,0},{7,1},{8,14},{9,15},{10,... | collective-permute-start | bytes 294920 | tf_op jit(solution)/shard_map/ppermute | solution.py:486
  148.1 12.6 %collective-permute-start.13 = (bf16[384,128]{1,0:T(8,128)(2,1)S(1)}, bf16[384,128]{1,0:T(8,128)(2,1)S(1)}, u32[]{:S(2)}, u32[]{:S(2)}) collective-permute-start(bf16[384,128]{1,0:T(8,128)(2,1)S(1)} %get-tuple-element.63), channel_id=1, source_target_pairs={{0,6},{1,7},{2,4},{3,5},{4,2},{5,3},{6,0},{7,1},{8,14},{9,15},{10,... | collective-permute-start | bytes 294920 | tf_op jit(solution)/shard_map/ppermute | solution.py:486
  150.1 12.3 %collective-permute-start.14 = (bf16[384,128]{1,0:T(8,128)(2,1)S(1)}, bf16[384,128]{1,0:T(8,128)(2,1)S(1)}, u32[]{:S(2)}, u32[]{:S(2)}) collective-permute-start(bf16[384,128]{1,0:T(8,128)(2,1)S(1)} %get-tuple-element.64), channel_id=1, source_target_pairs={{0,8},{1,9},{2,10},{3,11},{4,12},{5,13},{6,14},{7,15},{8,0},{9,1},... | collective-permute-start | bytes 294920 | tf_op jit(solution)/shard_map/ppermute | solution.py:486
  150.9 20.0 %collective-permute-start.15 = (bf16[384,128]{1,0:T(8,128)(2,1)S(1)}, bf16[384,128]{1,0:T(8,128)(2,1)S(1)}, u32[]{:S(2)}, u32[]{:S(2)}) collective-permute-start(bf16[384,128]{1,0:T(8,128)(2,1)S(1)} %get-tuple-element.65), channel_id=1, source_target_pairs={{0,8},{1,9},{2,10},{3,11},{4,12},{5,13},{6,14},{7,15},{8,0},{9,1},... | collective-permute-start | bytes 294920 | tf_op jit(solution)/shard_map/ppermute | solution.py:486
  156.2 18.2 %collective-permute-start.16 = (bf16[384,128]{1,0:T(8,128)(2,1)S(1)}, bf16[384,128]{1,0:T(8,128)(2,1)S(1)}, u32[]{:S(2)}, u32[]{:S(2)}) collective-permute-start(bf16[384,128]{1,0:T(8,128)(2,1)S(1)} %get-tuple-element.66), channel_id=1, source_target_pairs={{0,10},{1,11},{2,8},{3,9},{4,14},{5,15},{6,12},{7,13},{8,2},{9,3},... | collective-permute-start | bytes 294920 | tf_op jit(solution)/shard_map/ppermute | solution.py:486
  159.6 20.0 %collective-permute-start.17 = (bf16[384,128]{1,0:T(8,128)(2,1)S(1)}, bf16[384,128]{1,0:T(8,128)(2,1)S(1)}, u32[]{:S(2)}, u32[]{:S(2)}) collective-permute-start(bf16[384,128]{1,0:T(8,128)(2,1)S(1)} %get-tuple-element.67), channel_id=1, source_target_pairs={{0,10},{1,11},{2,8},{3,9},{4,14},{5,15},{6,12},{7,13},{8,2},{9,3},... | collective-permute-start | bytes 294920 | tf_op jit(solution)/shard_map/ppermute | solution.py:486
  160.7 19.0 %collective-permute-start.18 = (bf16[384,128]{1,0:T(8,128)(2,1)S(1)}, bf16[384,128]{1,0:T(8,128)(2,1)S(1)}, u32[]{:S(2)}, u32[]{:S(2)}) collective-permute-start(bf16[384,128]{1,0:T(8,128)(2,1)S(1)} %get-tuple-element.68), channel_id=1, source_target_pairs={{0,12},{1,13},{2,14},{3,15},{4,8},{5,9},{6,10},{7,11},{8,4},{9,5},... | collective-permute-start | bytes 294920 | tf_op jit(solution)/shard_map/ppermute | solution.py:486
  162.4 17.3 %collective-permute-start.19 = (bf16[384,128]{1,0:T(8,128)(2,1)S(1)}, bf16[384,128]{1,0:T(8,128)(2,1)S(1)}, u32[]{:S(2)}, u32[]{:S(2)}) collective-permute-start(bf16[384,128]{1,0:T(8,128)(2,1)S(1)} %get-tuple-element.69), channel_id=1, source_target_pairs={{0,12},{1,13},{2,14},{3,15},{4,8},{5,9},{6,10},{7,11},{8,4},{9,5},... | collective-permute-start | bytes 294920 | tf_op jit(solution)/shard_map/ppermute | solution.py:486
  170.9 8.8 %collective-permute-start.20 = (bf16[384,128]{1,0:T(8,128)(2,1)S(1)}, bf16[384,128]{1,0:T(8,128)(2,1)S(1)}, u32[]{:S(2)}, u32[]{:S(2)}) collective-permute-start(bf16[384,128]{1,0:T(8,128)(2,1)S(1)} %get-tuple-element.70), channel_id=1, source_target_pairs={{0,14},{1,15},{2,12},{3,13},{4,10},{5,11},{6,8},{7,9},{8,6},{9,7},... | collective-permute-start | bytes 294920 | tf_op jit(solution)/shard_map/ppermute | solution.py:486
  174.5 7.4 %collective-permute-start.21 = (bf16[384,128]{1,0:T(8,128)(2,1)S(1)}, bf16[384,128]{1,0:T(8,128)(2,1)S(1)}, u32[]{:S(2)}, u32[]{:S(2)}) collective-permute-start(bf16[384,128]{1,0:T(8,128)(2,1)S(1)} %get-tuple-element.71), channel_id=1, source_target_pairs={{0,14},{1,15},{2,12},{3,13},{4,10},{5,11},{6,8},{7,9},{8,6},{9,7},... | collective-permute-start | bytes 294920 | tf_op jit(solution)/shard_map/ppermute | solution.py:486
  192.4 2.6 collective-permute-start.23
  192.4 2.6 collective-permute-start.22
  199.4 26.6 %all-to-all-start.1 = ((bf16[16,24,1024]{2,1,0:T(8,128)(2,1)}), bf16[16,24,1024]{2,1,0:T(8,128)(2,1)}, u32[]{:S(2)}, u32[]{:S(2)}) async-start(bf16[16,24,1024]{2,1,0:T(8,128)(2,1)} %bitcast.13), calls=%async_computation.1 | async-start | bytes 1572864 | tf_op jit(solution)/shard_map/all_to_all | solution.py:479
  216.8 2.4 collective-permute-start.24
  226.0 39.6 %all-to-all-start.2 = ((bf16[16,24,1024]{2,1,0:T(8,128)(2,1)}), bf16[16,24,1024]{2,1,0:T(8,128)(2,1)S(1)}, u32[]{:S(2)}, u32[]{:S(2)}) async-start(bf16[16,24,1024]{2,1,0:T(8,128)(2,1)} %bitcast.16), calls=%async_computation.2 | async-start | bytes 1572864 | tf_op jit(solution)/shard_map/all_to_all | solution.py:479
  231.8 22.3 %collective-permute-start.25 = (bf16[1,2,64,128]{3,2,1,0:T(8,128)(2,1)S(1)}, bf16[1,2,64,128]{3,2,1,0:T(8,128)(2,1)S(1)}, u32[]{:S(2)}, u32[]{:S(2)}) collective-permute-start(bf16[1,2,64,128]{3,2,1,0:T(8,128)(2,1)S(1)} %maximum_bitcast_fusion), channel_id=1, source_target_pairs={{0,8},{1,9},{2,10},{3,11},{4,12},{5,13},{6,14},{7,15},{8,0},{9,1},... | collective-permute-start | bytes 98312 | tf_op jit(solution)/shard_map/ppermute | solution.py:486
  254.1 4.3 %collective-permute-start.26 = (bf16[2,2,64,128]{3,2,1,0:T(8,128)(2,1)S(1)}, bf16[2,2,64,128]{3,2,1,0:T(8,128)(2,1)S(1)}, u32[]{:S(2)}, u32[]{:S(2)}) collective-permute-start(bf16[2,2,64,128]{3,2,1,0:T(8,128)(2,1)S(1)} %pad_maximum_fusion.2), channel_id=1, source_target_pairs={{0,4},{1,5},{2,6},{3,7},{4,0},{5,1},{6,2},{7,3},{8,12},{9,13},{10,... | collective-permute-start | bytes 196616 | tf_op jit(solution)/shard_map/ppermute | solution.py:486
  258.5 5.0 %collective-permute-start.27 = (bf16[4,2,64,128]{3,2,1,0:T(8,128)(2,1)S(1)}, bf16[4,2,64,128]{3,2,1,0:T(8,128)(2,1)S(1)}, u32[]{:S(2)}, u32[]{:S(2)}) collective-permute-start(bf16[4,2,64,128]{3,2,1,0:T(8,128)(2,1)S(1)} %pad_maximum_fusion.1), channel_id=1, source_target_pairs={{0,2},{1,3},{2,0},{3,1},{4,6},{5,7},{6,4},{7,5},{8,10},{9,11},{10,... | collective-permute-start | bytes 393224 | tf_op jit(solution)/shard_map/ppermute | solution.py:486
  260.0 1.4 collective-permute-start.28
  (15 other events, 224.7 us)
Sparse Core Ops, SparseCore 0:
  56.2 54.0 all-gather.1

commit v5 on v4

--- a/solution.py
+++ b/solution.py
@@ -16,7 +16,7 @@
 PAIR = 256
 PACK = 256
 CHUNKS = 2
-VMEM_BYTES = 32 * 1024 * 1024
+VMEM_BYTES = 48 * 1024 * 1024
 
 f32 = jnp.float32
 bf16 = jnp.bfloat16
@@ -59,15 +59,17 @@
     return pl.pallas_call(
         kernel,
         out_shape=out_shape,
-        in_specs=[pl.BlockSpec(memory_space=pl.ANY)] * len(operands),
+        in_specs=[pl.BlockSpec(memory_space=pltpu.HBM)] * len(operands),
         scratch_shapes=[*buffers, pltpu.SemaphoreType.DMA((len(operands),))],
         compiler_params=params(),
         name=name,
     )(*operands)
 
 
-def dispatch_kernel(slices, ids_hbm, tok_hbm, out_ref, ids_ref, tok_ref, sems):
-    fetched((ids_hbm, tok_hbm), (ids_ref, tok_ref), sems)
+def dispatch_kernel(slices, *refs):
+    pack_ref, out_ref = refs[4:6]
+    bias_ref, ids_ref, tok_ref, bcd_ref, sems = refs[6:]
+    fetched(refs[:4], refs[6:10], sems)
     rows, width = tok_ref.shape
     depth = width // slices
     ids, slot = route(ids_ref[...])
@@ -87,23 +89,6 @@
             piece = jnp.concatenate([g[e * CAP : (e + 1) * CAP] for g in got], axis=0)
             out_ref[e * slices * CAP : (e + 1) * slices * CAP, c : c + step] = piece.astype(bf16)
 
-
-def dispatch(ids_row, tokens, slices):
-    width = tokens.shape[1]
-    return fetching_call(
-        functools.partial(dispatch_kernel, slices),
-        (ids_row, tokens),
-        jax.ShapeDtypeStruct((EXPERTS * slices * CAP, width // slices), bf16),
-        "dispatch",
-    )
-
-
-def pack_kernel(*refs):
-    pack_ref = refs[4]
-    bias_ref, ids_ref, tok_ref, bcd_ref, sems = refs[5:]
-    fetched(refs[:4], refs[5:9], sems)
-    rows = tok_ref.shape[0]
-    ids, slot = route(ids_ref[...])
     across = (((1,), (1,)), ((), ()))
     tok = tok_ref[...]
     pack_ref[:, : 2 * NS] = lax.dot_general(
@@ -125,12 +110,16 @@
     pack_ref[:, 2 * NS :] = jnp.where(lane < 2 * HEADS + 2, side, 0.0).astype(bf16)
 
 
-def scan_operands(bias, ids_row, tokens, bcd):
+def dispatch(bias, ids_row, tokens, bcd, slices):
+    rows, width = tokens.shape
     return fetching_call(
-        pack_kernel,
+        functools.partial(dispatch_kernel, slices),
         (bias.reshape(1, -1), ids_row, tokens, bcd),
-        jax.ShapeDtypeStruct((tokens.shape[0], PACK), bf16),
-        "scan_operands",
+        (
+            jax.ShapeDtypeStruct((rows, PACK), bf16),
+            jax.ShapeDtypeStruct((EXPERTS * slices * CAP, width // slices), bf16),
+        ),
+        "dispatch",
     )
 
 
@@ -493,34 +482,6 @@
     return out
 
 
-def decode_state(states, want, chip, place, n, slices):
-    heads, _, width = states.shape
-    held, seats = states[None], []
-    for q in (4, 2, 1):
-        held = jnp.concatenate([held, across(held, q, n, slices)], axis=0)
-        seats.append(q)
-
-    def picked(head):
-        first = head * HEADDIM % (EXPERTS * heads * width) // width
-        pieces = []
-        for i in range(HEADDIM // width):
-            distance = (first + i) // heads ^ chip
-            seat = sum((distance // q % 2) << k for k, q in enumerate(seats))
-            pieces.append(
-                lax.dynamic_slice(held, (seat, (first + i) % heads, 0, 0), (1, 1, NS, width))
-            )
-        return jnp.concatenate(pieces, axis=0) if len(pieces) > 1 else pieces[0]
-
-    chosen = picked(want)
-    lies = want * HEADDIM // (EXPERTS * heads * width)
-    for r in range(1, slices):
-        asked = turn(want, n, slices, slices - r)
-        got = turn(picked(asked), n, slices, r)
-        chosen = jnp.where((place - lies + slices) % slices == r, got, chosen)
-    chosen = chosen.reshape(HEADDIM // width, NS, width).transpose(0, 2, 1)
-    return chosen.astype(f32).reshape(1, HEADDIM * NS)
-
-
 def shards(
     tokens, w_in, w_out, w_bcd, dt_bias, decay_rate, skip_gain, norm_gain, expert_ids, decode_heads
 ):
@@ -537,15 +498,15 @@
     ids_row = expert_ids.reshape(1, -1)
     w_in, w_out = w_in[0], w_out[0]
 
-    landed = swap(dispatch(ids_row, tokens, slices))
-    pack = scan_operands(dt_bias, ids_row, tokens, w_bcd.T)
+    pack, outgoing = dispatch(dt_bias, ids_row, tokens, w_bcd.T, slices)
+    landed = swap(outgoing)
     pack = lax.all_gather(pack, "expert", axis=0, tiled=True)
     own_heads = start // HEADDIM + jnp.arange(heads, dtype=jnp.int32)
     weights = prepare(place, own_heads, decay_rate, skip_gain, pack)
 
     pieces = [landed] + [turn(landed, n, slices, r) for r in range(1, slices)]
     inner = [None] * EXPERTS
-    for order in ((7, 6), (5, 4), (3, 2, 1), (0,)):
+    for order in ((7,), (6, 5), (4, 3), (2, 1), (0,)):
         if order == (0,):
             pieces, weights = lax.optimization_barrier((pieces, weights))
         for q, a in zip(order, in_projection(place, pieces, w_in, units, order)):
@@ -557,9 +518,9 @@
     for h in range(heads):
         rows, state = scan(x, weights, gain[h * width : (h + 1) * width].reshape(1, width), h)
         z.append(exchange(rows, n, slices))
-        states.append(state.astype(bf16))
+        states.append(state)
     z = [[z[h][q] for h in range(heads)] for q in range(EXPERTS)]
-    decoded = decode_state(jnp.stack(states), decode_heads[0], chip, place[0], n, slices)
+    states = lax.all_gather(jnp.stack(states), "expert", axis=0, tiled=False)
 
     inverse = 1.0 / lax.dynamic_slice(norm_gain, (place[0] * in_dev,), (in_dev,))
     inverse = inverse.reshape(in_dev // width, 1, width)
@@ -574,7 +535,18 @@
     for k in range(CHUNKS):
         [done] = project("finish", k, squares=squares, parts=sent[k])
         back.append(swap(done))
-    return (collect(ids_row, back, slices), decoded)
+    mixed = collect(ids_row, back, slices)
+
+    want = decode_heads[0] * HEADDIM
+    within = want % in_dev // width
+    states = states.reshape(EXPERTS, slices, heads, NS, width)
+    chosen = lax.dynamic_slice(
+        states,
+        (within // heads, want // in_dev, within % heads, 0, 0),
+        (HEADDIM // width, 1, 1, NS, width),
+    )
+    chosen = chosen.reshape(HEADDIM // width, NS, width).transpose(0, 2, 1)
+    return (mixed, chosen.reshape(1, HEADDIM * NS))
 
 
 def solution(mesh):

time: 277 us -> 262 us (0.946)
  local copies, waits for them, and re-layouts: 29.1 us -> 9.38 us
  Pallas kernels: 60.6 us -> 73.2 us
  starting transfers between devices: 57.1 us -> 46.5 us
  waiting for transfers between devices: 68.8 us -> 71.6 us
    all_gather x0 -> x1, waiting for transfers between devices: none -> 21.8 us  [shards(): states = lax.all_gather(jnp.stack(states), 'expert', axis=0, tiled=False)]
    unnamed x28, local copies, waits for them, and re-layouts: 27.5 us -> 7.04 us
    ppermute x24 -> x21, waiting for transfers between devices: 37.9 us -> 19.4 us  [across(): return lax.ppermute(a, 'expert', pairs)]
    ppermute x24 -> x21, starting transfers between devices: 41.7 us -> 30.4 us  [across(): return lax.ppermute(a, 'expert', pairs)]
    pallas_call x4 -> x5, Pallas kernels: 14.7 us -> 20.8 us  [in_projection(): pl.pallas_call(functools.partial(in_kernel, slices, shares, turns), out_s...]
    pallas_call x4, Pallas kernels: 17.3 us -> 21.2 us  [out_projection(): pl.pallas_call(functools.partial(out_kernel, kind, heads, inverse is not...]
    all_to_all x2, waiting for transfers between devices: 2.45 us -> 6.05 us  [swap(): lax.all_to_all(a, 'expert', split_axis=0, concat_axis=0, axis_index_group...]
    all_gather x1, waiting for transfers between devices: 22.7 us -> 19.4 us  [shards(): pack = lax.all_gather(pack, 'expert', axis=0, tiled=True)]
  transfers between devices with their start and end apart: 33 -> 29, of which waited for: 14 -> 13; matrix products, arithmetic and copies ran while one was open for 1% -> 1% of each run, Pallas kernels for 15% -> 19%
where the time goes in v5:
time: 262 us; the launch traced here: 260 us
  Pallas kernels  73.2 us (28%)
  waiting for transfers between devices  71.6 us (27%)
  starting transfers between devices  46.5 us (18%)
  blocking collectives  43.3 us (17%)
  between operations  15 us (6%)
  local copies, waits for them, and re-layouts  9.38 us (4%)
    all_to_all x1, blocking collectives, swap(): lax.all_to_all(a, 'expert', split_axis=0, concat_axis=0, axis_index_group...  43.3 us
    ppermute x21, starting transfers between devices, across(): return lax.ppermute(a, 'expert', pairs)  30.4 us
    all_gather x1, waiting for transfers between devices, shards(): states = lax.all_gather(jnp.stack(states), 'expert', axis=0, tiled=False)  21.8 us
    pallas_call x4, Pallas kernels, out_projection(): pl.pallas_call(functools.partial(out_kernel, kind, heads, inverse is not...  21.2 us
    pallas_call x5, Pallas kernels, in_projection(): pl.pallas_call(functools.partial(in_kernel, slices, shares, turns), out_s...  20.8 us
    ppermute x21, waiting for transfers between devices, across(): return lax.ppermute(a, 'expert', pairs)  19.4 us
    all_gather x1, waiting for transfers between devices, shards(): pack = lax.all_gather(pack, 'expert', axis=0, tiled=True)  19.4 us
    all_to_all x2, starting transfers between devices, swap(): lax.all_to_all(a, 'expert', split_axis=0, concat_axis=0, axis_index_group...  14.1 us
  transfers between devices with their start and end apart: 29, of which 13 were waited for; matrix products, arithmetic and copies ran while one was open for 1% of the time, Pallas kernels for 19%

profile of v5, /device:TPU:0, one launch (start us, length us, event | category | flops | bytes accessed | tf_op | source)
XLA Modules:
  0.0 260.3 jit_solution(599622467193729980)
XLA Ops:
  11.1 2.4 dispatch.1
  13.5 43.3 %all_to_all.33 = bf16[16,24,2048]{2,1,0:T(8,128)(2,1)S(1)} all-to-all(bf16[16,24,2048]{2,1,0:T(8,128)(2,1)S(1)} %bitcast.35), channel_id=1, replica_groups=mesh['groups'=2,'expert'=16] {'expert'}, dimensions={0} | all-to-all | bytes 3145728 | tf_op jit(solution)/shard_map/all_to_all | solution.py:468
  60.6 4.2 %in_projection.6 = (bf16[384,256]{1,0:T(8,128)(2,1)S(1)}, bf16[384,256]{1,0:T(8,128)(2,1)S(1)}) custom-call(s32[2]{0:T(128)S(1)} %pad_add_fusion.place_ref, bf16[384,2048]{1,0:T(8,128)(2,1)S(1)} %bitcast.29, bf16[384,2048]{1,0:T(8,128)(2,1)S(1)} %collective-permute-done.refs_1_, bf16[4096,2048]{1,0:T(8,128)(2,1)} %bitcast.109, bf16[4096,2048]{1,0:T(8,128)(2,1)} %bitcast.110), custom_call_target="tpu_custom_call" | custom-call | flops 1610612736 | bytes 7340032 | tf_op jit(solution)/shard_map/in_projection/pallas_call | solution.py:157
  67.7 4.9 %in_projection.7 = (bf16[384,256]{1,0:T(8,128)(2,1)}, bf16[384,256]{1,0:T(8,128)(2,1)}) custom-call(s32[2]{0:T(128)S(1)} %pad_add_fusion.place_ref, bf16[384,2048]{1,0:T(8,128)(2,1)S(1)} %bitcast.30, bf16[384,2048]{1,0:T(8,128)(2,1)S(1)} %collective-permute-done.refs_1_, bf16[4096,2048]{1,0:T(8,128)(2,1)} %bitcast.111, bf16[4096,2048]{1,0:T(8,128)(2,1)} %bitcast.112), custom_call_target="tpu_custom_call" | custom-call | flops 1610612736 | bytes 7340032 | tf_op jit(solution)/shard_map/in_projection/pallas_call | solution.py:157
  73.2 2.7 %collective-permute-start.4 = (bf16[384,256]{1,0:T(8,128)(2,1)}, bf16[384,256]{1,0:T(8,128)(2,1)}, u32[]{:S(2)}, u32[]{:S(2)}) collective-permute-start(bf16[384,256]{1,0:T(8,128)(2,1)} %get-tuple-element.51), channel_id=1, source_target_pairs={{0,8},{1,9},{2,10},{3,11},{4,12},{5,13},{6,14},{7,15},{8,0},{9,1},... | collective-permute-start | bytes 589832 | tf_op jit(solution)/shard_map/ppermute | solution.py:475
  75.9 4.9 %in_projection.8 = (bf16[384,256]{1,0:T(8,128)(2,1)}, bf16[384,256]{1,0:T(8,128)(2,1)}) custom-call(s32[2]{0:T(128)S(1)} %pad_add_fusion.place_ref, bf16[384,2048]{1,0:T(8,128)(2,1)S(1)} %bitcast.31, bf16[384,2048]{1,0:T(8,128)(2,1)S(1)} %collective-permute-done.refs_1_, bf16[4096,2048]{1,0:T(8,128)(2,1)} %bitcast.113, bf16[4096,2048]{1,0:T(8,128)(2,1)} %bitcast.114), custom_call_target="tpu_custom_call" | custom-call | flops 1610612736 | bytes 7340032 | tf_op jit(solution)/shard_map/in_projection/pallas_call | solution.py:157
  81.8 3.8 %in_projection.9 = bf16[384,256]{1,0:T(8,128)(2,1)} custom-call(s32[2]{0:T(128)S(1)} %pad_add_fusion.place_ref, bf16[384,2048]{1,0:T(8,128)(2,1)S(1)} %bitcast.32, bf16[384,2048]{1,0:T(8,128)(2,1)S(1)} %collective-permute-done.refs_1_, bf16[4096,2048]{1,0:T(8,128)(2,1)} %bitcast.115, bf16[4096,2048]{1,0:T(8,128)(2,1)} %bitcast.116), custom_call_target="tpu_custom_call" | custom-call | flops 805306368 | bytes 5242880 | tf_op jit(solution)/shard_map/in_projection/pallas_call | solution.py:157
  85.5 2.5 collective-permute-start.6
  89.6 19.4 %all-gather.4.cloned.1.call-done.pack_ref = bf16[2048,256]{1,0:T(8,128)(2,1)} async-done(((bf16[128,256]{1,0:T(8,128)(2,1)}), bf16[2048,256]{1,0:T(8,128)(2,1)}) %all-gather.4.cloned.1.call-update) | async-done | bytes 1048592 | tf_op jit(solution)/shard_map/all_gather | solution.py:503
  111.6 13.9 %scan_weights.1 = (bf16[2,8,384,384]{3,2,1,0:T(8,128)(2,1)}, bf16[2,8,384,64]{3,2,1,0:T(8,128)(2,1)S(1)}, bf16[2,8,64,384]{3,2,1,0:T(8,128)(2,1)S(1)}, f32[2,8,8,128]{3,2,1,0:T(8,128)S(1)}) custom-call(s32[2]{0:T(128)S(1)} %pad_add_fusion.place_ref, s32[2]{0:T(128)S(1)} %copy-done.12, f32[32]{0:T(128)S(1)} %copy-done.10, f32[32]{0:T(128)S(1)} %copy-done.11, ...), custom_call_target="tpu_custom_call" | custom-call | flops 2415919104 | bytes 4718592 | tf_op jit(solution)/shard_map/scan_weights/pallas_call | solution.py:246
  125.5 3.1 %in_projection.5.refs_0_ = bf16[384,256]{1,0:T(8,128)(2,1)S(1)} custom-call(s32[2]{0:T(128)S(1)} %pad_add_fusion.place_ref, bf16[384,2048]{1,0:T(8,128)(2,1)S(1)} %bitcast.33, bf16[384,2048]{1,0:T(8,128)(2,1)S(1)} %collective-permute-done.refs_1_, bf16[4096,2048]{1,0:T(8,128)(2,1)} %bitcast.117, bf16[4096,2048]{1,0:T(8,128)(2,1)} %bitcast.118), custom_call_target="tpu_custom_call" | custom-call | flops 805306368 | bytes 5242880 | tf_op jit(solution)/shard_map/in_projection/pallas_call | solution.py:157
  128.6 5.9 %scan.2 = (bf16[384,128]{1,0:T(8,128)(2,1)S(1)}, bf16[384,128]{1,0:T(8,128)(2,1)S(1)}, bf16[384,128]{1,0:T(8,128)(2,1)S(1)}, bf16[384,128]{1,0:T(8,128)(2,1)S(1)...) custom-call(bf16[384,256]{1,0:T(8,128)(2,1)S(1)} %in_projection.5.re, ...), custom_call_target="tpu_custom_call" | custom-call | flops 402653184 | bytes 2359296 | tf_op jit(solution)/shard_map/scan/pallas_call | solution.py:301
  136.0 5.8 %scan.3 = (bf16[384,128]{1,0:T(8,128)(2,1)S(1)}, bf16[384,128]{1,0:T(8,128)(2,1)S(1)}, bf16[384,128]{1,0:T(8,128)(2,1)S(1)}, bf16[384,128]{1,0:T(8,128)(2,1)S(1)...) custom-call(bf16[384,256]{1,0:T(8,128)(2,1)S(1)} %in_projection.5.re, ...), custom_call_target="tpu_custom_call" | custom-call | flops 402653184 | bytes 2359296 | tf_op jit(solution)/shard_map/scan/pallas_call | solution.py:301
  146.0 2.0 collective-permute-start.13
  150.9 3.5 %collective-permute-done.11.refs_5_ = bf16[384,128]{1,0:T(8,128)(2,1)S(1)} collective-permute-done((bf16[384,128]{1,0:T(8,128)(2,1)S(1)}, bf16[384,128]{1,0:T(8,128)(2,1)S(1)}, u32[]{:S(2)}, u32[]{:S(2)}) %collective-permute-start.11) | collective-permute-done | bytes 98336 | tf_op jit(solution)/shard_map/ppermute | solution.py:475
  154.4 3.0 %collective-permute-done.12.refs_6_ = bf16[384,128]{1,0:T(8,128)(2,1)S(1)} collective-permute-done((bf16[384,128]{1,0:T(8,128)(2,1)S(1)}, bf16[384,128]{1,0:T(8,128)(2,1)S(1)}, u32[]{:S(2)}, u32[]{:S(2)}) %collective-permute-start.12) | collective-permute-done | bytes 98336 | tf_op jit(solution)/shard_map/ppermute | solution.py:475
  160.2 2.1 collective-permute-start.19
  162.3 7.3 %collective-permute-done.15.refs_9_ = bf16[384,128]{1,0:T(8,128)(2,1)S(1)} collective-permute-done((bf16[384,128]{1,0:T(8,128)(2,1)S(1)}, bf16[384,128]{1,0:T(8,128)(2,1)S(1)}, u32[]{:S(2)}, u32[]{:S(2)}) %collective-permute-start.15) | collective-permute-done | bytes 98336 | tf_op jit(solution)/shard_map/ppermute | solution.py:475
  169.7 2.1 collective-permute-start.20
  172.2 2.5 collective-permute-start.21
  174.7 2.7 %collective-permute-done.17.refs_11_ = bf16[384,128]{1,0:T(8,128)(2,1)S(1)} collective-permute-done((bf16[384,128]{1,0:T(8,128)(2,1)S(1)}, bf16[384,128]{1,0:T(8,128)(2,1)S(1)}, u32[]{:S(2)}, u32[]{:S(2)}) %collective-permute-start.17) | collective-permute-done | bytes 98336 | tf_op jit(solution)/shard_map/ppermute | solution.py:475
  177.5 2.1 collective-permute-done.21.refs_15_
  179.6 5.7 %out_send.2 = (bf16[1,384,1024]{2,1,0:T(8,128)(2,1)S(1)}, f32[384,1]{1,0:T(8,128)S(1)}) custom-call(s32[2]{0:T(128)S(1)} %pad_add_fusion.place_ref, bf16[384,128]{1,0:T(8,128)(2,1)S(1)} %get-tuple-element.58.refs_0_, bf16[384,128]{1,0:T(8,128)(2,1)S(1)} %get-tuple-element.59.refs_1_, bf16[384,128]{1,0:T(8,128)(2,1)S(1)} %collective-permute-done.8.refs_2_, ...), custom_call_target="tpu_custom_call" | custom-call | flops 1610612736 | bytes 4980736 | tf_op jit(solution)/shard_map/out_send/pallas_call | solution.py:416
  185.9 2.1 collective-permute-done.22.refs_33_
  187.9 5.3 %out_finish.2 = bf16[384,1024]{1,0:T(8,128)(2,1)} custom-call(s32[2]{0:T(128)S(1)} %pad_add_fusion.place_ref, bf16[384,128]{1,0:T(8,128)(2,1)S(1)} %get-tuple-element.58.refs_0_, bf16[384,128]{1,0:T(8,128)(2,1)S(1)} %get-tuple-element.59.refs_1_, bf16[384,128]{1,0:T(8,128)(2,1)S(1)} %collective-permute-done.8.refs_2_, ...), custom_call_target="tpu_custom_call" | custom-call | flops 1610612736 | bytes 4980736 | tf_op jit(solution)/shard_map/out_finish/pallas_call | solution.py:416
  193.3 7.8 %all-to-all-start.1 = ((bf16[16,24,1024]{2,1,0:T(8,128)(2,1)}), bf16[16,24,1024]{2,1,0:T(8,128)(2,1)}, u32[]{:S(2)}, u32[]{:S(2)}) async-start(bf16[16,24,1024]{2,1,0:T(8,128)(2,1)} %bitcast.13), calls=%async_computation.1 | async-start | bytes 1572864 | tf_op jit(solution)/shard_map/all_to_all | solution.py:468
  201.3 4.9 %out_send.3 = bf16[1,384,1024]{2,1,0:T(8,128)(2,1)S(1)} custom-call(s32[2]{0:T(128)S(1)} %pad_add_fusion.place_ref, bf16[384,128]{1,0:T(8,128)(2,1)S(1)} %get-tuple-element.58.refs_0_, bf16[384,128]{1,0:T(8,128)(2,1)S(1)} %get-tuple-element.59.refs_1_, bf16[384,128]{1,0:T(8,128)(2,1)S(1)} %collective-permute-done.8.refs_2_, ...), custom_call_target="tpu_custom_call" | custom-call | flops 1610612736 | bytes 4980736 | tf_op jit(solution)/shard_map/out_send/pallas_call | solution.py:416
  208.5 5.3 %out_finish.3 = bf16[384,1024]{1,0:T(8,128)(2,1)} custom-call(s32[2]{0:T(128)S(1)} %pad_add_fusion.place_ref, bf16[384,128]{1,0:T(8,128)(2,1)S(1)} %get-tuple-element.58.refs_0_, bf16[384,128]{1,0:T(8,128)(2,1)S(1)} %get-tuple-element.59.refs_1_, bf16[384,128]{1,0:T(8,128)(2,1)S(1)} %collective-permute-done.8.refs_2_, ...), custom_call_target="tpu_custom_call" | custom-call | flops 1610612736 | bytes 4980736 | tf_op jit(solution)/shard_map/out_finish/pallas_call | solution.py:416
  213.9 6.1 %all-to-all-done.1 = bf16[16,24,1024]{2,1,0:T(8,128)(2,1)} async-done(((bf16[16,24,1024]{2,1,0:T(8,128)(2,1)}), bf16[16,24,1024]{2,1,0:T(8,128)(2,1)}, u32[]{:S(2)}, u32[]{:S(2)}) %all-to-all-start.1) | async-done | bytes 786464 | tf_op jit(solution)/shard_map/all_to_all | solution.py:468
  219.9 6.3 %all-to-all-start.2 = ((bf16[16,24,1024]{2,1,0:T(8,128)(2,1)}), bf16[16,24,1024]{2,1,0:T(8,128)(2,1)S(1)}, u32[]{:S(2)}, u32[]{:S(2)}) async-start(bf16[16,24,1024]{2,1,0:T(8,128)(2,1)} %bitcast.16), calls=%async_computation.2 | async-start | bytes 1572864 | tf_op jit(solution)/shard_map/all_to_all | solution.py:468
  227.0 21.8 %all-gather.6.cloned.1.call-done = f32[32,64,128]{2,1,0:T(8,128)} async-done(((f32[2,64,128]{2,1,0:T(8,128)}), f32[32,64,128]{2,1,0:T(8,128)}) %all-gather.6.cloned.1.call-update) | async-done | bytes 1048592 | tf_op jit(solution)/shard_map/all_gather | solution.py:523
  250.3 3.2 %collect.1 = bf16[128,4096]{1,0:T(8,128)(2,1)} custom-call(s32[1,128]{1,0:T(1,128)S(1)} %bitcast.42, bf16[384,1024]{1,0:T(8,128)(2,1)} %bitcast.14.refs_0_, bf16[384,1024]{1,0:T(8,128)(2,1)S(1)} %bitcast.34), custom_call_target="tpu_custom_call" | custom-call | tf_op jit(solution)/shard_map/collect/pallas_call | solution.py:453
  (80 shorter events, 32.7 us)
Async XLA Ops:
  7.2 101.8 %all-gather.4.cloned.1.call-start = ((), (), s32[]{:S(2)}) async-start(), calls=%async_computation.3 | async-start | bytes 1114112 | tf_op jit(solution)/shard_map/all_gather | solution.py:503
  56.8 3.8 %collective-permute-start = (bf16[384,2048]{1,0:T(8,128)(2,1)S(1)}, bf16[384,2048]{1,0:T(8,128)(2,1)S(1)}, u32[]{:S(2)}, u32[]{:S(2)}) collective-permute-start(bf16[384,2048]{1,0:T(8,128)(2,1)S(1)} %bitcast.28), channel_id=1, source_target_pairs={{0,1},{1,0},{2,3},{3,2},{4,5},{5,4},{6,7},{7,6},{8,9},{9,8},{10,11... | collective-permute-start | bytes 4718600 | tf_op jit(solution)/shard_map/ppermute | solution.py:462
  64.8 20.8 %collective-permute-start.1 = (bf16[384,256]{1,0:T(8,128)(2,1)S(1)}, bf16[384,256]{1,0:T(8,128)(2,1)S(1)}, u32[]{:S(2)}, u32[]{:S(2)}) collective-permute-start(bf16[384,256]{1,0:T(8,128)(2,1)S(1)} %get-tuple-element.48), channel_id=1, source_target_pairs={{0,2},{1,3},{2,0},{3,1},{4,6},{5,7},{6,4},{7,5},{8,10},{9,11},{10,... | collective-permute-start | bytes 589832 | tf_op jit(solution)/shard_map/ppermute | solution.py:475
  66.1 22.0 %collective-permute-start.2 = (bf16[384,256]{1,0:T(8,128)(2,1)S(1)}, bf16[384,256]{1,0:T(8,128)(2,1)S(1)}, u32[]{:S(2)}, u32[]{:S(2)}) collective-permute-start(bf16[384,256]{1,0:T(8,128)(2,1)S(1)} %get-tuple-element.49), channel_id=1, source_target_pairs={{0,4},{1,5},{2,6},{3,7},{4,0},{5,1},{6,2},{7,3},{8,12},{9,13},{10,... | collective-permute-start | bytes 589832 | tf_op jit(solution)/shard_map/ppermute | solution.py:475
  72.6 56.0 %collective-permute-start.3 = (bf16[384,256]{1,0:T(8,128)(2,1)}, bf16[384,256]{1,0:T(8,128)(2,1)}, u32[]{:S(2)}, u32[]{:S(2)}) collective-permute-start(bf16[384,256]{1,0:T(8,128)(2,1)} %get-tuple-element.50), channel_id=1, source_target_pairs={{0,6},{1,7},{2,4},{3,5},{4,2},{5,3},{6,0},{7,1},{8,14},{9,15},{10,... | collective-permute-start | bytes 589832 | tf_op jit(solution)/shard_map/ppermute | solution.py:475
  73.2 55.4 %collective-permute-start.4 = (bf16[384,256]{1,0:T(8,128)(2,1)}, bf16[384,256]{1,0:T(8,128)(2,1)}, u32[]{:S(2)}, u32[]{:S(2)}) collective-permute-start(bf16[384,256]{1,0:T(8,128)(2,1)} %get-tuple-element.51), channel_id=1, source_target_pairs={{0,8},{1,9},{2,10},{3,11},{4,12},{5,13},{6,14},{7,15},{8,0},{9,1},... | collective-permute-start | bytes 589832 | tf_op jit(solution)/shard_map/ppermute | solution.py:475
  80.8 28.2 %copy-start.10 = (f32[32]{0:T(128)S(1)}, f32[32]{0:T(128)}, u32[]{:S(2)}) copy-start(f32[32]{0:T(128)} %rate_ref.1) | copy-start | bytes 388
  80.8 47.8 %collective-permute-start.5 = (bf16[384,256]{1,0:T(8,128)(2,1)}, bf16[384,256]{1,0:T(8,128)(2,1)}, u32[]{:S(2)}, u32[]{:S(2)}) collective-permute-start(bf16[384,256]{1,0:T(8,128)(2,1)} %get-tuple-element.52), channel_id=1, source_target_pairs={{0,10},{1,11},{2,8},{3,9},{4,14},{5,15},{6,12},{7,13},{8,2},{9,3},... | collective-permute-start | bytes 589832 | tf_op jit(solution)/shard_map/ppermute | solution.py:475
  85.5 43.1 %collective-permute-start.6 = (bf16[384,256]{1,0:T(8,128)(2,1)}, bf16[384,256]{1,0:T(8,128)(2,1)}, u32[]{:S(2)}, u32[]{:S(2)}) collective-permute-start(bf16[384,256]{1,0:T(8,128)(2,1)} %get-tuple-element.53), channel_id=1, source_target_pairs={{0,12},{1,13},{2,14},{3,15},{4,8},{5,9},{6,10},{7,11},{8,4},{9,5},... | collective-permute-start | bytes 589832 | tf_op jit(solution)/shard_map/ppermute | solution.py:475
  88.1 40.6 %collective-permute-start.7 = (bf16[384,256]{1,0:T(8,128)(2,1)}, bf16[384,256]{1,0:T(8,128)(2,1)}, u32[]{:S(2)}, u32[]{:S(2)}) collective-permute-start(bf16[384,256]{1,0:T(8,128)(2,1)} %in_projection.9), channel_id=1, source_target_pairs={{0,14},{1,15},{2,12},{3,13},{4,10},{5,11},{6,8},{7,9},{8,6},{9,7},... | collective-permute-start | bytes 589832 | tf_op jit(solution)/shard_map/ppermute | solution.py:475
  134.5 11.5 %collective-permute-start.8 = (bf16[384,128]{1,0:T(8,128)(2,1)S(1)}, bf16[384,128]{1,0:T(8,128)(2,1)S(1)}, u32[]{:S(2)}, u32[]{:S(2)}) collective-permute-start(bf16[384,128]{1,0:T(8,128)(2,1)S(1)} %get-tuple-element.60), channel_id=1, source_target_pairs={{0,2},{1,3},{2,0},{3,1},{4,6},{5,7},{6,4},{7,5},{8,10},{9,11},{10,... | collective-permute-start | bytes 294920 | tf_op jit(solution)/shard_map/ppermute | solution.py:475
  136.0 38.7 %copy-start.13 = (f32[4096]{0:T(1024)S(1)}, f32[4096]{0:T(1024)}, u32[]{:S(2)}) copy-start(f32[4096]{0:T(1024)} %param.17) | copy-start | bytes 49156
  142.4 5.6 %collective-permute-start.9 = (bf16[384,128]{1,0:T(8,128)(2,1)S(1)}, bf16[384,128]{1,0:T(8,128)(2,1)S(1)}, u32[]{:S(2)}, u32[]{:S(2)}) collective-permute-start(bf16[384,128]{1,0:T(8,128)(2,1)S(1)} %get-tuple-element.61), channel_id=1, source_target_pairs={{0,2},{1,3},{2,0},{3,1},{4,6},{5,7},{6,4},{7,5},{8,10},{9,11},{10,... | collective-permute-start | bytes 294920 | tf_op jit(solution)/shard_map/ppermute | solution.py:475
  143.0 6.6 %collective-permute-start.10 = (bf16[384,128]{1,0:T(8,128)(2,1)S(1)}, bf16[384,128]{1,0:T(8,128)(2,1)S(1)}, u32[]{:S(2)}, u32[]{:S(2)}) collective-permute-start(bf16[384,128]{1,0:T(8,128)(2,1)S(1)} %get-tuple-element.62), channel_id=1, source_target_pairs={{0,4},{1,5},{2,6},{3,7},{4,0},{5,1},{6,2},{7,3},{8,12},{9,13},{10,... | collective-permute-start | bytes 294920 | tf_op jit(solution)/shard_map/ppermute | solution.py:475
  143.9 10.5 %collective-permute-start.11 = (bf16[384,128]{1,0:T(8,128)(2,1)S(1)}, bf16[384,128]{1,0:T(8,128)(2,1)S(1)}, u32[]{:S(2)}, u32[]{:S(2)}) collective-permute-start(bf16[384,128]{1,0:T(8,128)(2,1)S(1)} %get-tuple-element.63), channel_id=1, source_target_pairs={{0,4},{1,5},{2,6},{3,7},{4,0},{5,1},{6,2},{7,3},{8,12},{9,13},{10,... | collective-permute-start | bytes 294920 | tf_op jit(solution)/shard_map/ppermute | solution.py:475
  145.1 12.4 %collective-permute-start.12 = (bf16[384,128]{1,0:T(8,128)(2,1)S(1)}, bf16[384,128]{1,0:T(8,128)(2,1)S(1)}, u32[]{:S(2)}, u32[]{:S(2)}) collective-permute-start(bf16[384,128]{1,0:T(8,128)(2,1)S(1)} %get-tuple-element.64), channel_id=1, source_target_pairs={{0,6},{1,7},{2,4},{3,5},{4,2},{5,3},{6,0},{7,1},{8,14},{9,15},{10,... | collective-permute-start | bytes 294920 | tf_op jit(solution)/shard_map/ppermute | solution.py:475
  146.0 12.5 %collective-permute-start.13 = (bf16[384,128]{1,0:T(8,128)(2,1)S(1)}, bf16[384,128]{1,0:T(8,128)(2,1)S(1)}, u32[]{:S(2)}, u32[]{:S(2)}) collective-permute-start(bf16[384,128]{1,0:T(8,128)(2,1)S(1)} %get-tuple-element.65), channel_id=1, source_target_pairs={{0,6},{1,7},{2,4},{3,5},{4,2},{5,3},{6,0},{7,1},{8,14},{9,15},{10,... | collective-permute-start | bytes 294920 | tf_op jit(solution)/shard_map/ppermute | solution.py:475
  148.0 12.2 %collective-permute-start.14 = (bf16[384,128]{1,0:T(8,128)(2,1)S(1)}, bf16[384,128]{1,0:T(8,128)(2,1)S(1)}, u32[]{:S(2)}, u32[]{:S(2)}) collective-permute-start(bf16[384,128]{1,0:T(8,128)(2,1)S(1)} %get-tuple-element.66), channel_id=1, source_target_pairs={{0,8},{1,9},{2,10},{3,11},{4,12},{5,13},{6,14},{7,15},{8,0},{9,1},... | collective-permute-start | bytes 294920 | tf_op jit(solution)/shard_map/ppermute | solution.py:475
  149.7 20.0 %collective-permute-start.15 = (bf16[384,128]{1,0:T(8,128)(2,1)S(1)}, bf16[384,128]{1,0:T(8,128)(2,1)S(1)}, u32[]{:S(2)}, u32[]{:S(2)}) collective-permute-start(bf16[384,128]{1,0:T(8,128)(2,1)S(1)} %get-tuple-element.67), channel_id=1, source_target_pairs={{0,8},{1,9},{2,10},{3,11},{4,12},{5,13},{6,14},{7,15},{8,0},{9,1},... | collective-permute-start | bytes 294920 | tf_op jit(solution)/shard_map/ppermute | solution.py:475
  154.4 17.8 %collective-permute-start.16 = (bf16[384,128]{1,0:T(8,128)(2,1)S(1)}, bf16[384,128]{1,0:T(8,128)(2,1)S(1)}, u32[]{:S(2)}, u32[]{:S(2)}) collective-permute-start(bf16[384,128]{1,0:T(8,128)(2,1)S(1)} %get-tuple-element.68), channel_id=1, source_target_pairs={{0,10},{1,11},{2,8},{3,9},{4,14},{5,15},{6,12},{7,13},{8,2},{9,3},... | collective-permute-start | bytes 294920 | tf_op jit(solution)/shard_map/ppermute | solution.py:475
  157.5 20.0 %collective-permute-start.17 = (bf16[384,128]{1,0:T(8,128)(2,1)S(1)}, bf16[384,128]{1,0:T(8,128)(2,1)S(1)}, u32[]{:S(2)}, u32[]{:S(2)}) collective-permute-start(bf16[384,128]{1,0:T(8,128)(2,1)S(1)} %get-tuple-element.69), channel_id=1, source_target_pairs={{0,10},{1,11},{2,8},{3,9},{4,14},{5,15},{6,12},{7,13},{8,2},{9,3},... | collective-permute-start | bytes 294920 | tf_op jit(solution)/shard_map/ppermute | solution.py:475
  158.5 19.0 %collective-permute-start.18 = (bf16[384,128]{1,0:T(8,128)(2,1)S(1)}, bf16[384,128]{1,0:T(8,128)(2,1)S(1)}, u32[]{:S(2)}, u32[]{:S(2)}) collective-permute-start(bf16[384,128]{1,0:T(8,128)(2,1)S(1)} %get-tuple-element.70), channel_id=1, source_target_pairs={{0,12},{1,13},{2,14},{3,15},{4,8},{5,9},{6,10},{7,11},{8,4},{9,5},... | collective-permute-start | bytes 294920 | tf_op jit(solution)/shard_map/ppermute | solution.py:475
  160.2 17.2 %collective-permute-start.19 = (bf16[384,128]{1,0:T(8,128)(2,1)S(1)}, bf16[384,128]{1,0:T(8,128)(2,1)S(1)}, u32[]{:S(2)}, u32[]{:S(2)}) collective-permute-start(bf16[384,128]{1,0:T(8,128)(2,1)S(1)} %get-tuple-element.71), channel_id=1, source_target_pairs={{0,12},{1,13},{2,14},{3,15},{4,8},{5,9},{6,10},{7,11},{8,4},{9,5},... | collective-permute-start | bytes 294920 | tf_op jit(solution)/shard_map/ppermute | solution.py:475
  169.7 7.8 %collective-permute-start.20 = (bf16[384,128]{1,0:T(8,128)(2,1)S(1)}, bf16[384,128]{1,0:T(8,128)(2,1)S(1)}, u32[]{:S(2)}, u32[]{:S(2)}) collective-permute-start(bf16[384,128]{1,0:T(8,128)(2,1)S(1)} %get-tuple-element.72), channel_id=1, source_target_pairs={{0,14},{1,15},{2,12},{3,13},{4,10},{5,11},{6,8},{7,9},{8,6},{9,7},... | collective-permute-start | bytes 294920 | tf_op jit(solution)/shard_map/ppermute | solution.py:475
  172.2 7.4 %collective-permute-start.21 = (bf16[384,128]{1,0:T(8,128)(2,1)S(1)}, bf16[384,128]{1,0:T(8,128)(2,1)S(1)}, u32[]{:S(2)}, u32[]{:S(2)}) collective-permute-start(bf16[384,128]{1,0:T(8,128)(2,1)S(1)} %get-tuple-element.73), channel_id=1, source_target_pairs={{0,14},{1,15},{2,12},{3,13},{4,10},{5,11},{6,8},{7,9},{8,6},{9,7},... | collective-permute-start | bytes 294920 | tf_op jit(solution)/shard_map/ppermute | solution.py:475
  185.3 2.6 %collective-permute-start.23 = (bf16[384,1024]{1,0:T(8,128)(2,1)S(1)}, bf16[384,1024]{1,0:T(8,128)(2,1)S(1)}, u32[]{:S(2)}, u32[]{:S(2)}) collective-permute-start(bf16[384,1024]{1,0:T(8,128)(2,1)S(1)} %bitcast.44), channel_id=1, source_target_pairs={{0,1},{1,0},{2,3},{3,2},{4,5},{5,4},{6,7},{7,6},{8,9},{9,8},{10,11... | collective-permute-start | bytes 2359304 | tf_op jit(solution)/shard_map/ppermute | solution.py:462
  185.4 2.6 collective-permute-start.22
  193.3 26.6 %all-to-all-start.1 = ((bf16[16,24,1024]{2,1,0:T(8,128)(2,1)}), bf16[16,24,1024]{2,1,0:T(8,128)(2,1)}, u32[]{:S(2)}, u32[]{:S(2)}) async-start(bf16[16,24,1024]{2,1,0:T(8,128)(2,1)} %bitcast.13), calls=%async_computation.1 | async-start | bytes 1572864 | tf_op jit(solution)/shard_map/all_to_all | solution.py:468
  201.0 47.7 %all-gather.6.cloned.1.call-start = ((), (), s32[]{:S(2)}) async-start(), calls=%async_computation.4 | async-start | bytes 1114112 | tf_op jit(solution)/shard_map/all_gather | solution.py:523
  206.2 2.4 collective-permute-start.24
  213.8 36.5 %copy-start.7 = (s32[128,1]{0,1:T(1,128)S(1)}, s32[128,1]{0,1:T(1,128)}, u32[]{:S(2)}) copy-start(s32[128,1]{0,1:T(1,128)} %param.18) | copy-start | bytes 1540
  219.9 30.4 %all-to-all-start.2 = ((bf16[16,24,1024]{2,1,0:T(8,128)(2,1)}), bf16[16,24,1024]{2,1,0:T(8,128)(2,1)S(1)}, u32[]{:S(2)}, u32[]{:S(2)}) async-start(bf16[16,24,1024]{2,1,0:T(8,128)(2,1)} %bitcast.16), calls=%async_computation.2 | async-start | bytes 1572864 | tf_op jit(solution)/shard_map/all_to_all | solution.py:468
  (11 other events, 25.0 us)
Sparse Core Ops, SparseCore 0:
  57.7 51.2 all-gather.3
  207.4 41.3 all-gather.5

commit v6 on v5

--- a/solution.py
+++ b/solution.py
@@ -273,37 +273,40 @@
     def _():
         state[...] = jnp.zeros_like(state)
 
-    rows = x_refs[0].shape[0]
-    x = jnp.concatenate([x_ref[...] for x_ref in x_refs], axis=0)
-    before = state[...]
-    y = jnp.dot(w_ref[0, 0], x, preferred_element_type=f32) + jnp.dot(
-        c_ref[0, 0], before.astype(bf16), preferred_element_type=f32
-    )
-    after = before * a_ref[0, 0, 0:1, 0:1] + jnp.dot(
-        b_ref[0, 0], x, preferred_element_type=f32
-    )
-    state[...] = after
-    last_ref[...] = after
-    z = (y * gain_ref[...]).astype(bf16)
-    for q in range(EXPERTS):
-        out_refs[q][...] = z[q * rows : (q + 1) * rows]
+    rows = 2 * CAP
+    now = state[...]
+    for i in range(w_ref.shape[1]):
+        at = slice(i * rows, (i + 1) * rows)
+        x = jnp.concatenate([x_ref[at, :] for x_ref in x_refs], axis=0)
+        y = jnp.dot(w_ref[0, i], x, preferred_element_type=f32) + jnp.dot(
+            c_ref[0, i], now.astype(bf16), preferred_element_type=f32
+        )
+        now = now * a_ref[0, i, 0:1, 0:1] + jnp.dot(
+            b_ref[0, i], x, preferred_element_type=f32
+        )
+        z = (y * gain_ref[...]).astype(bf16)
+        for q in range(EXPERTS):
+            out_refs[q][at, :] = z[q * rows : (q + 1) * rows]
+    state[...] = now
+    last_ref[...] = now
 
 
 def scan(x, weights, gain, h):
     rows = x[0].shape[0]
     width = gain.shape[1]
     pairs = rows // (2 * CAP)
+    step = 2
     slots = 2 * CAP * EXPERTS
 
     def block(*dims):
-        return pl.BlockSpec((1, 1, *dims), lambda p: (h, p, 0, 0))
+        return pl.BlockSpec((1, step, *dims), lambda p: (h, p, 0, 0))
 
     *z, state = pl.pallas_call(
         scan_kernel,
         out_shape=[jax.ShapeDtypeStruct((rows, width), bf16)] * EXPERTS
         + [jax.ShapeDtypeStruct((NS, width), f32)],
-        grid=(pairs,),
-        in_specs=[pl.BlockSpec((2 * CAP, width), lambda p: (p, h))] * EXPERTS
+        grid=(pairs // step,),
+        in_specs=[pl.BlockSpec((2 * CAP * step, width), lambda p: (p, h))] * EXPERTS
         + [
             block(slots, slots),
             block(slots, NS),
@@ -311,10 +314,10 @@
             block(8, 128),
             pl.BlockSpec((1, width), lambda p: (0, 0)),
         ],
-        out_specs=[pl.BlockSpec((2 * CAP, width), lambda p: (p, 0))] * EXPERTS
+        out_specs=[pl.BlockSpec((2 * CAP * step, width), lambda p: (p, 0))] * EXPERTS
         + [pl.BlockSpec((NS, width), lambda p: (0, 0))],
         scratch_shapes=[pltpu.VMEM((NS, width), f32)],
-        compiler_params=params(),
+        compiler_params=pltpu.CompilerParams(vmem_limit_bytes=VMEM_BYTES // 2),
         cost_estimate=pl.CostEstimate(
             flops=2 * pairs * slots * (slots + 2 * NS) * width,
             bytes_accessed=2 * pairs * slots * slots,
@@ -333,7 +336,7 @@
         del refs[:count]
         return got
 
-    z_refs, w_refs = take(EXPERTS * heads), take(EXPERTS * heads)
+    z_refs, [w_ref] = take(EXPERTS * heads), take(1)
     inverse_ref = take(1)[0] if counted else None
     squares_refs = take(1 + others) if kind == "finish" else None
     part_refs = take(others) if kind == "finish" else None
@@ -351,13 +354,12 @@
                     squares = squares + jnp.sum(z * z, axis=1, keepdims=True)
             refs[0][...] = squares
 
-    group = max(1, 256 // width) if width % 128 == 0 else 1
+    units = heads * width
     total = None
-    for i in range(0, EXPERTS * heads, group):
-        z = [r[...] for r in z_refs[i : i + group]]
-        w = [r[...] for r in w_refs[i : i + group]]
-        z = jnp.concatenate(z, axis=1) if group > 1 else z[0]
-        w = jnp.concatenate(w, axis=0) if group > 1 else w[0]
+    for q in range(EXPERTS):
+        z = [r[...] for r in z_refs[q * heads : (q + 1) * heads]]
+        z = jnp.concatenate(z, axis=1) if heads > 1 else z[0]
+        w = w_ref[pl.ds(pl.multiple_of((place_ref[1] ^ q) * units, units), units), :]
         part = jnp.dot(z, w, preferred_element_type=f32)
         total = part if total is None else total + part
     if kind == "finish":
@@ -381,21 +383,18 @@
     whole = slice_width // tile
     offset = chunk * tiles
 
-    def w_spec(q, h):
-        return pl.BlockSpec(
-            (width, tile),
-            lambda n, place_ref: (
-                (place_ref[1] ^ q) * heads + h,
-                (place_ref[0] + first + n // tiles) % slices * whole + offset + n % tiles,
-            ),
-        )
+    def column(n, place_ref):
+        return (place_ref[0] + first + n // tiles) % slices * whole + offset + n % tiles
 
     def fixed(*dims):
         return pl.BlockSpec(dims, lambda n, place_ref: (0,) * len(dims))
 
     pieces = [(q, h) for q in range(EXPERTS) for h in range(heads)]
-    operands = [z[q][h] for q, h in pieces] + [w_out] * len(pieces)
-    specs = [fixed(rows, width)] * len(pieces) + [w_spec(q, h) for q, h in pieces]
+    operands = [z[q][h] for q, h in pieces] + [w_out]
+    specs = [fixed(rows, width)] * len(pieces)
+    specs.append(
+        pl.BlockSpec((w_out.shape[0], tile), lambda n, place_ref: (0, column(n, place_ref)))
+    )
     if inverse is not None:
         operands.append(inverse)
         specs.append(fixed(*inverse.shape))
@@ -502,11 +501,13 @@
     landed = swap(outgoing)
     pack = lax.all_gather(pack, "expert", axis=0, tiled=True)
     own_heads = start // HEADDIM + jnp.arange(heads, dtype=jnp.int32)
-    weights = prepare(place, own_heads, decay_rate, skip_gain, pack)
 
     pieces = [landed] + [turn(landed, n, slices, r) for r in range(1, slices)]
     inner = [None] * EXPERTS
     for order in ((7,), (6, 5), (4, 3), (2, 1), (0,)):
+        if order == (4, 3):
+            pieces, pack = lax.optimization_barrier((pieces, pack))
+            weights = prepare(place, own_heads, decay_rate, skip_gain, pack)
         if order == (0,):
             pieces, weights = lax.optimization_barrier((pieces, weights))
         for q, a in zip(order, in_projection(place, pieces, w_in, units, order)):

time: 262 us -> 245 us (0.935)
  blocking collectives: 43.3 us -> 0 us
  waiting for transfers between devices: 71.6 us -> 101 us
  starting transfers between devices: 46.5 us -> 58.2 us
  Pallas kernels: 73.2 us -> 62.4 us
  local copies, waits for them, and re-layouts: 9.38 us -> 6.15 us
    all_to_all x1 -> x0, blocking collectives: 43.3 us -> none  [swap(): lax.all_to_all(a, 'expert', split_axis=0, concat_axis=0, axis_index_group...]
    all_to_all x2 -> x3, waiting for transfers between devices: 6.05 us -> 39.6 us  [swap(): lax.all_to_all(a, 'expert', split_axis=0, concat_axis=0, axis_index_group...]
    pallas_call x2, Pallas kernels: 11.6 us -> 4.88 us  [scan(): pl.pallas_call(scan_kernel, out_shape=[jax.ShapeDtypeStruct((rows, width)...]
    ppermute x21, starting transfers between devices: 30.4 us -> 36.5 us  [across(): return lax.ppermute(a, 'expert', pairs)]
    all_to_all x2 -> x3, starting transfers between devices: 14.1 us -> 19.8 us  [swap(): lax.all_to_all(a, 'expert', split_axis=0, concat_axis=0, axis_index_group...]
    all_gather x1, waiting for transfers between devices: 19.4 us -> 16.1 us  [shards(): pack = lax.all_gather(pack, 'expert', axis=0, tiled=True)]
    unnamed x28 -> x30, local copies, waits for them, and re-layouts: 7.04 us -> 4.5 us
  transfers between devices with their start and end apart: 29 -> 30, of which waited for: 13 -> 13; matrix products, arithmetic and copies ran while one was open for 1% -> 1% of each run, Pallas kernels for 19% -> 15%
where the time goes in v6:
time: 245 us; the launch traced here: 243 us
  waiting for transfers between devices  101 us (41%)
  Pallas kernels  62.4 us (25%)
  starting transfers between devices  58.2 us (24%)
  between operations  15.1 us (6%)
  local copies, waits for them, and re-layouts  6.15 us (3%)
    all_to_all x3, waiting for transfers between devices, swap(): lax.all_to_all(a, 'expert', split_axis=0, concat_axis=0, axis_index_group...  39.6 us
    ppermute x21, starting transfers between devices, across(): return lax.ppermute(a, 'expert', pairs)  36.5 us
    all_gather x1, waiting for transfers between devices, shards(): states = lax.all_gather(jnp.stack(states), 'expert', axis=0, tiled=False)  21.9 us
    pallas_call x4, Pallas kernels, out_projection(): pl.pallas_call(functools.partial(out_kernel, kind, heads, inverse is not...  20 us
    all_to_all x3, starting transfers between devices, swap(): lax.all_to_all(a, 'expert', split_axis=0, concat_axis=0, axis_index_group...  19.8 us
    ppermute x21, waiting for transfers between devices, across(): return lax.ppermute(a, 'expert', pairs)  19.1 us
    pallas_call x5, Pallas kernels, in_projection(): pl.pallas_call(functools.partial(in_kernel, slices, shares, turns), out_s...  19 us
    all_gather x1, waiting for transfers between devices, shards(): pack = lax.all_gather(pack, 'expert', axis=0, tiled=True)  16.1 us
  transfers between devices with their start and end apart: 30, of which 13 were waited for; matrix products, arithmetic and copies ran while one was open for 1% of the time, Pallas kernels for 15%

profile of v6, /device:TPU:0, one launch (start us, length us, event | category | flops | bytes accessed | tf_op | source)
XLA Modules:
  0.0 243.4 jit_solution(8781836236363981175)
XLA Ops:
  11.0 2.5 %dispatch.1 = (bf16[128,256]{1,0:T(8,128)(2,1)}, bf16[384,2048]{1,0:T(8,128)(2,1)}) custom-call(f32[1,32]{1,0:T(1,128)S(1)} %bitcast.44, s32[1,128]{1,0:T(1,128)S(1)} %bitcast.42, bf16[128,4096]{1,0:T(8,128)(2,1)S(1)} %copy-done.1, bf16[160,4096]{1,0:T(8,128)(2,1)S(1)} %bitcast.38), custom_call_target="tpu_custom_call" | custom-call | tf_op jit(solution)/shard_map/dispatch/pallas_call | solution.py:59
  13.5 7.4 %all-to-all-start = ((bf16[16,24,2048]{2,1,0:T(8,128)(2,1)}), bf16[16,24,2048]{2,1,0:T(8,128)(2,1)S(1)}, u32[]{:S(2)}, u32[]{:S(2)}) async-start(bf16[16,24,2048]{2,1,0:T(8,128)(2,1)} %bitcast.5), calls=%async_computation | async-start | bytes 3145728 | tf_op jit(solution)/shard_map/all_to_all | solution.py:467
  21.6 33.3 %all-to-all-done = bf16[16,24,2048]{2,1,0:T(8,128)(2,1)S(1)} async-done(((bf16[16,24,2048]{2,1,0:T(8,128)(2,1)}), bf16[16,24,2048]{2,1,0:T(8,128)(2,1)S(1)}, u32[]{:S(2)}, u32[]{:S(2)}) %all-to-all-start) | async-done | bytes 1572896 | tf_op jit(solution)/shard_map/all_to_all | solution.py:467
  55.9 16.1 %all-gather.4.cloned.1.call-done.pack_ref = bf16[2048,256]{1,0:T(8,128)(2,1)} async-done(((bf16[128,256]{1,0:T(8,128)(2,1)}), bf16[2048,256]{1,0:T(8,128)(2,1)}) %all-gather.4.cloned.1.call-update) | async-done | bytes 1048592 | tf_op jit(solution)/shard_map/all_gather | solution.py:502
  72.0 4.2 %in_projection.6 = (bf16[384,256]{1,0:T(8,128)(2,1)S(1)}, bf16[384,256]{1,0:T(8,128)(2,1)S(1)}) custom-call(s32[2]{0:T(128)S(1)} %pad_add_fusion.place_ref, bf16[384,2048]{1,0:T(8,128)(2,1)S(1)} %bitcast.29, bf16[384,2048]{1,0:T(8,128)(2,1)S(1)} %collective-permute-done.refs_1_, bf16[4096,2048]{1,0:T(8,128)(2,1)} %bitcast.46, bf16[4096,2048]{1,0:T(8,128)(2,1)} %bitcast.47), custom_call_target="tpu_custom_call" | custom-call | flops 1610612736 | bytes 7340032 | tf_op jit(solution)/shard_map/in_projection/pallas_call | solution.py:157
  76.2 4.2 %in_projection.7 = (bf16[384,256]{1,0:T(8,128)(2,1)S(1)}, bf16[384,256]{1,0:T(8,128)(2,1)S(1)}) custom-call(s32[2]{0:T(128)S(1)} %pad_add_fusion.place_ref, bf16[384,2048]{1,0:T(8,128)(2,1)S(1)} %bitcast.30, bf16[384,2048]{1,0:T(8,128)(2,1)S(1)} %collective-permute-done.refs_1_, bf16[4096,2048]{1,0:T(8,128)(2,1)} %bitcast.48, bf16[4096,2048]{1,0:T(8,128)(2,1)} %bitcast.49), custom_call_target="tpu_custom_call" | custom-call | flops 1610612736 | bytes 7340032 | tf_op jit(solution)/shard_map/in_projection/pallas_call | solution.py:157
  84.8 4.2 %in_projection.8 = (bf16[384,256]{1,0:T(8,128)(2,1)S(1)}, bf16[384,256]{1,0:T(8,128)(2,1)S(1)}) custom-call(s32[2]{0:T(128)S(1)} %pad_add_fusion.place_ref, bf16[384,2048]{1,0:T(8,128)(2,1)S(1)} %bitcast.31, bf16[384,2048]{1,0:T(8,128)(2,1)S(1)} %collective-permute-done.refs_1_, bf16[4096,2048]{1,0:T(8,128)(2,1)} %bitcast.50, bf16[4096,2048]{1,0:T(8,128)(2,1)} %bitcast.51), custom_call_target="tpu_custom_call" | custom-call | flops 1610612736 | bytes 7340032 | tf_op jit(solution)/shard_map/in_projection/pallas_call | solution.py:157
  89.0 2.1 collective-permute-start.5
  91.1 3.1 %in_projection.9 = bf16[384,256]{1,0:T(8,128)(2,1)S(1)} custom-call(s32[2]{0:T(128)S(1)} %pad_add_fusion.place_ref, bf16[384,2048]{1,0:T(8,128)(2,1)S(1)} %bitcast.32, bf16[384,2048]{1,0:T(8,128)(2,1)S(1)} %collective-permute-done.refs_1_, bf16[4096,2048]{1,0:T(8,128)(2,1)} %bitcast.52, bf16[4096,2048]{1,0:T(8,128)(2,1)} %bitcast.53), custom_call_target="tpu_custom_call" | custom-call | flops 805306368 | bytes 5242880 | tf_op jit(solution)/shard_map/in_projection/pallas_call | solution.py:157
  94.2 2.4 collective-permute-start.6
  96.6 2.5 %collective-permute-start.7 = (bf16[384,256]{1,0:T(8,128)(2,1)S(1)}, bf16[384,256]{1,0:T(8,128)(2,1)S(1)}, u32[]{:S(2)}, u32[]{:S(2)}) collective-permute-start(bf16[384,256]{1,0:T(8,128)(2,1)S(1)} %in_projection.9), channel_id=1, source_target_pairs={{0,14},{1,15},{2,12},{3,13},{4,10},{5,11},{6,8},{7,9},{8,6},{9,7},... | collective-permute-start | bytes 589832 | tf_op jit(solution)/shard_map/ppermute | solution.py:474
  99.1 14.0 %scan_weights.1 = (bf16[2,8,384,384]{3,2,1,0:T(8,128)(2,1)}, bf16[2,8,384,64]{3,2,1,0:T(8,128)(2,1)S(1)}, bf16[2,8,64,384]{3,2,1,0:T(8,128)(2,1)S(1)}, f32[2,8,8,128]{3,2,1,0:T(8,128)S(1)}) custom-call(s32[2]{0:T(128)S(1)} %pad_add_fusion.place_ref, s32[2]{0:T(128)S(1)} %iota_add_fusion.head_ref, f32[32]{0:T(128)S(1)} %copy-done.10, f32[32]{0:T(128)S(1)} %copy-done.11, ...), custom_call_target="tpu_custom_call" | custom-call | flops 2415919104 | bytes 4718592 | tf_op jit(solution)/shard_map/scan_weights/pallas_call | solution.py:246
  113.1 3.3 %in_projection.5.refs_0_ = bf16[384,256]{1,0:T(8,128)(2,1)S(1)} custom-call(s32[2]{0:T(128)S(1)} %pad_add_fusion.place_ref, bf16[384,2048]{1,0:T(8,128)(2,1)S(1)} %bitcast.33, bf16[384,2048]{1,0:T(8,128)(2,1)S(1)} %collective-permute-done.refs_1_, bf16[4096,2048]{1,0:T(8,128)(2,1)} %bitcast.54, bf16[4096,2048]{1,0:T(8,128)(2,1)} %bitcast.55), custom_call_target="tpu_custom_call" | custom-call | flops 805306368 | bytes 5242880 | tf_op jit(solution)/shard_map/in_projection/pallas_call | solution.py:157
  116.6 2.5 %scan.2 = (bf16[384,128]{1,0:T(8,128)(2,1)S(1)}, bf16[384,128]{1,0:T(8,128)(2,1)S(1)}, bf16[384,128]{1,0:T(8,128)(2,1)S(1)}, bf16[384,128]{1,0:T(8,128)(2,1)S(1)...) custom-call(bf16[384,256]{1,0:T(8,128)(2,1)S(1)} %in_projection.5.re, ...), custom_call_target="tpu_custom_call" | custom-call | flops 402653184 | bytes 2359296 | tf_op jit(solution)/shard_map/scan/pallas_call | solution.py:304
  119.5 2.4 scan.3
  124.2 6.3 %collective-permute-start.10 = (bf16[384,128]{1,0:T(8,128)(2,1)S(1)}, bf16[384,128]{1,0:T(8,128)(2,1)S(1)}, u32[]{:S(2)}, u32[]{:S(2)}) collective-permute-start(bf16[384,128]{1,0:T(8,128)(2,1)S(1)} %get-tuple-element.68), channel_id=1, source_target_pairs={{0,4},{1,5},{2,6},{3,7},{4,0},{5,1},{6,2},{7,3},{8,12},{9,13},{10,... | collective-permute-start | bytes 294920 | tf_op jit(solution)/shard_map/ppermute | solution.py:474
  133.4 2.2 collective-permute-start.14
  136.4 2.6 %collective-permute-done.11.refs_5_ = bf16[384,128]{1,0:T(8,128)(2,1)S(1)} collective-permute-done((bf16[384,128]{1,0:T(8,128)(2,1)S(1)}, bf16[384,128]{1,0:T(8,128)(2,1)S(1)}, u32[]{:S(2)}, u32[]{:S(2)}) %collective-permute-start.11) | collective-permute-done | bytes 98336 | tf_op jit(solution)/shard_map/ppermute | solution.py:474
  139.5 2.1 collective-permute-done.12.refs_6_
  143.2 2.5 %collective-permute-start.18 = (bf16[384,128]{1,0:T(8,128)(2,1)S(1)}, bf16[384,128]{1,0:T(8,128)(2,1)S(1)}, u32[]{:S(2)}, u32[]{:S(2)}) collective-permute-start(bf16[384,128]{1,0:T(8,128)(2,1)S(1)} %get-tuple-element.76), channel_id=1, source_target_pairs={{0,12},{1,13},{2,14},{3,15},{4,8},{5,9},{6,10},{7,11},{8,4},{9,5},... | collective-permute-start | bytes 294920 | tf_op jit(solution)/shard_map/ppermute | solution.py:474
  147.1 9.1 %collective-permute-done.15.refs_9_ = bf16[384,128]{1,0:T(8,128)(2,1)S(1)} collective-permute-done((bf16[384,128]{1,0:T(8,128)(2,1)S(1)}, bf16[384,128]{1,0:T(8,128)(2,1)S(1)}, u32[]{:S(2)}, u32[]{:S(2)}) %collective-permute-start.15) | collective-permute-done | bytes 98336 | tf_op jit(solution)/shard_map/ppermute | solution.py:474
  156.1 2.8 %collective-permute-start.20 = (bf16[384,128]{1,0:T(8,128)(2,1)S(1)}, bf16[384,128]{1,0:T(8,128)(2,1)S(1)}, u32[]{:S(2)}, u32[]{:S(2)}) collective-permute-start(bf16[384,128]{1,0:T(8,128)(2,1)S(1)} %get-tuple-element.78), channel_id=1, source_target_pairs={{0,14},{1,15},{2,12},{3,13},{4,10},{5,11},{6,8},{7,9},{8,6},{9,7},... | collective-permute-start | bytes 294920 | tf_op jit(solution)/shard_map/ppermute | solution.py:474
  159.0 2.6 %collective-permute-start.21 = (bf16[384,128]{1,0:T(8,128)(2,1)S(1)}, bf16[384,128]{1,0:T(8,128)(2,1)S(1)}, u32[]{:S(2)}, u32[]{:S(2)}) collective-permute-start(bf16[384,128]{1,0:T(8,128)(2,1)S(1)} %get-tuple-element.79), channel_id=1, source_target_pairs={{0,14},{1,15},{2,12},{3,13},{4,10},{5,11},{6,8},{7,9},{8,6},{9,7},... | collective-permute-start | bytes 294920 | tf_op jit(solution)/shard_map/ppermute | solution.py:474
  163.5 2.9 %collective-permute-done.21.refs_15_ = bf16[384,128]{1,0:T(8,128)(2,1)S(1)} collective-permute-done((bf16[384,128]{1,0:T(8,128)(2,1)S(1)}, bf16[384,128]{1,0:T(8,128)(2,1)S(1)}, u32[]{:S(2)}, u32[]{:S(2)}) %collective-permute-start.21) | collective-permute-done | bytes 98336 | tf_op jit(solution)/shard_map/ppermute | solution.py:474
  166.4 5.2 %out_send.2 = (bf16[1,384,1024]{2,1,0:T(8,128)(2,1)S(1)}, f32[384,1]{1,0:T(8,128)S(1)}) custom-call(s32[2]{0:T(128)S(1)} %pad_add_fusion.place_ref, bf16[384,128]{1,0:T(8,128)(2,1)S(1)} %get-tuple-element.64.refs_0_, bf16[384,128]{1,0:T(8,128)(2,1)S(1)} %get-tuple-element.65.refs_1_, bf16[384,128]{1,0:T(8,128)(2,1)S(1)} %collective-permute-done.8.refs_2_, ...), custom_call_target="tpu_custom_call" | custom-call | flops 1610612736 | bytes 4980736 | tf_op jit(solution)/shard_map/out_send/pallas_call | solution.py:415
  174.2 4.9 %out_finish.2 = bf16[384,1024]{1,0:T(8,128)(2,1)} custom-call(s32[2]{0:T(128)S(1)} %pad_add_fusion.place_ref, bf16[384,128]{1,0:T(8,128)(2,1)S(1)} %get-tuple-element.64.refs_0_, bf16[384,128]{1,0:T(8,128)(2,1)S(1)} %get-tuple-element.65.refs_1_, bf16[384,128]{1,0:T(8,128)(2,1)S(1)} %collective-permute-done.8.refs_2_, ...), custom_call_target="tpu_custom_call" | custom-call | flops 1610612736 | bytes 4980736 | tf_op jit(solution)/shard_map/out_finish/pallas_call | solution.py:415
  179.1 6.3 %all-to-all-start.1 = ((bf16[16,24,1024]{2,1,0:T(8,128)(2,1)}), bf16[16,24,1024]{2,1,0:T(8,128)(2,1)S(1)}, u32[]{:S(2)}, u32[]{:S(2)}) async-start(bf16[16,24,1024]{2,1,0:T(8,128)(2,1)} %bitcast.13), calls=%async_computation.1 | async-start | bytes 1572864 | tf_op jit(solution)/shard_map/all_to_all | solution.py:467
  185.5 5.0 %out_send.3 = bf16[1,384,1024]{2,1,0:T(8,128)(2,1)} custom-call(s32[2]{0:T(128)S(1)} %pad_add_fusion.place_ref, bf16[384,128]{1,0:T(8,128)(2,1)S(1)} %get-tuple-element.64.refs_0_, bf16[384,128]{1,0:T(8,128)(2,1)S(1)} %get-tuple-element.65.refs_1_, bf16[384,128]{1,0:T(8,128)(2,1)S(1)} %collective-permute-done.8.refs_2_, ...), custom_call_target="tpu_custom_call" | custom-call | flops 1610612736 | bytes 4980736 | tf_op jit(solution)/shard_map/out_send/pallas_call | solution.py:415
  193.0 5.0 %out_finish.3 = bf16[384,1024]{1,0:T(8,128)(2,1)} custom-call(s32[2]{0:T(128)S(1)} %pad_add_fusion.place_ref, bf16[384,128]{1,0:T(8,128)(2,1)S(1)} %get-tuple-element.64.refs_0_, bf16[384,128]{1,0:T(8,128)(2,1)S(1)} %get-tuple-element.65.refs_1_, bf16[384,128]{1,0:T(8,128)(2,1)S(1)} %collective-permute-done.8.refs_2_, ...), custom_call_target="tpu_custom_call" | custom-call | flops 1610612736 | bytes 4980736 | tf_op jit(solution)/shard_map/out_finish/pallas_call | solution.py:415
  198.0 6.2 %all-to-all-done.1 = bf16[16,24,1024]{2,1,0:T(8,128)(2,1)S(1)} async-done(((bf16[16,24,1024]{2,1,0:T(8,128)(2,1)}), bf16[16,24,1024]{2,1,0:T(8,128)(2,1)S(1)}, u32[]{:S(2)}, u32[]{:S(2)}) %all-to-all-start.1) | async-done | bytes 786464 | tf_op jit(solution)/shard_map/all_to_all | solution.py:467
  204.2 6.1 %all-to-all-start.2 = ((bf16[16,24,1024]{2,1,0:T(8,128)(2,1)}), bf16[16,24,1024]{2,1,0:T(8,128)(2,1)S(1)}, u32[]{:S(2)}, u32[]{:S(2)}) async-start(bf16[16,24,1024]{2,1,0:T(8,128)(2,1)} %bitcast.16), calls=%async_computation.2 | async-start | bytes 1572864 | tf_op jit(solution)/shard_map/all_to_all | solution.py:467
  211.1 21.9 %all-gather.6.cloned.1.call-done = f32[32,64,128]{2,1,0:T(8,128)} async-done(((f32[2,64,128]{2,1,0:T(8,128)}), f32[32,64,128]{2,1,0:T(8,128)}) %all-gather.6.cloned.1.call-update) | async-done | bytes 1048592 | tf_op jit(solution)/shard_map/all_gather | solution.py:524
  (84 shorter events, 30.6 us)
Async XLA Ops:
  13.5 42.3 %copy-start.12 = (f32[4096]{0:T(1024)S(1)}, f32[4096]{0:T(1024)}, u32[]{:S(2)}) copy-start(f32[4096]{0:T(1024)} %param.17) | copy-start | bytes 49156
  13.5 41.5 %all-to-all-start = ((bf16[16,24,2048]{2,1,0:T(8,128)(2,1)}), bf16[16,24,2048]{2,1,0:T(8,128)(2,1)S(1)}, u32[]{:S(2)}, u32[]{:S(2)}) async-start(bf16[16,24,2048]{2,1,0:T(8,128)(2,1)} %bitcast.5), calls=%async_computation | async-start | bytes 3145728 | tf_op jit(solution)/shard_map/all_to_all | solution.py:467
  20.9 51.1 %all-gather.4.cloned.1.call-start = ((), (), s32[]{:S(2)}) async-start(), calls=%async_computation.3 | async-start | bytes 1114112 | tf_op jit(solution)/shard_map/all_gather | solution.py:502
  55.0 17.0 %collective-permute-start = (bf16[384,2048]{1,0:T(8,128)(2,1)S(1)}, bf16[384,2048]{1,0:T(8,128)(2,1)S(1)}, u32[]{:S(2)}, u32[]{:S(2)}) collective-permute-start(bf16[384,2048]{1,0:T(8,128)(2,1)S(1)} %bitcast.28), channel_id=1, source_target_pairs={{0,1},{1,0},{2,3},{3,2},{4,5},{5,4},{6,7},{7,6},{8,9},{9,8},{10,11... | collective-permute-start | bytes 4718600 | tf_op jit(solution)/shard_map/ppermute | solution.py:461
  80.4 13.8 %collective-permute-start.1 = (bf16[384,256]{1,0:T(8,128)(2,1)S(1)}, bf16[384,256]{1,0:T(8,128)(2,1)S(1)}, u32[]{:S(2)}, u32[]{:S(2)}) collective-permute-start(bf16[384,256]{1,0:T(8,128)(2,1)S(1)} %get-tuple-element.54), channel_id=1, source_target_pairs={{0,2},{1,3},{2,0},{3,1},{4,6},{5,7},{6,4},{7,5},{8,10},{9,11},{10,... | collective-permute-start | bytes 589832 | tf_op jit(solution)/shard_map/ppermute | solution.py:474
  81.0 15.6 %collective-permute-start.2 = (bf16[384,256]{1,0:T(8,128)(2,1)S(1)}, bf16[384,256]{1,0:T(8,128)(2,1)S(1)}, u32[]{:S(2)}, u32[]{:S(2)}) collective-permute-start(bf16[384,256]{1,0:T(8,128)(2,1)S(1)} %get-tuple-element.55), channel_id=1, source_target_pairs={{0,4},{1,5},{2,6},{3,7},{4,0},{5,1},{6,2},{7,3},{8,12},{9,13},{10,... | collective-permute-start | bytes 589832 | tf_op jit(solution)/shard_map/ppermute | solution.py:474
  82.1 34.4 %collective-permute-start.3 = (bf16[384,256]{1,0:T(8,128)(2,1)S(1)}, bf16[384,256]{1,0:T(8,128)(2,1)S(1)}, u32[]{:S(2)}, u32[]{:S(2)}) collective-permute-start(bf16[384,256]{1,0:T(8,128)(2,1)S(1)} %get-tuple-element.56), channel_id=1, source_target_pairs={{0,6},{1,7},{2,4},{3,5},{4,2},{5,3},{6,0},{7,1},{8,14},{9,15},{10,... | collective-permute-start | bytes 589832 | tf_op jit(solution)/shard_map/ppermute | solution.py:474
  84.0 32.5 %collective-permute-start.4 = (bf16[384,256]{1,0:T(8,128)(2,1)S(1)}, bf16[384,256]{1,0:T(8,128)(2,1)S(1)}, u32[]{:S(2)}, u32[]{:S(2)}) collective-permute-start(bf16[384,256]{1,0:T(8,128)(2,1)S(1)} %get-tuple-element.57), channel_id=1, source_target_pairs={{0,8},{1,9},{2,10},{3,11},{4,12},{5,13},{6,14},{7,15},{8,0},{9,1},... | collective-permute-start | bytes 589832 | tf_op jit(solution)/shard_map/ppermute | solution.py:474
  89.0 27.5 %collective-permute-start.5 = (bf16[384,256]{1,0:T(8,128)(2,1)S(1)}, bf16[384,256]{1,0:T(8,128)(2,1)S(1)}, u32[]{:S(2)}, u32[]{:S(2)}) collective-permute-start(bf16[384,256]{1,0:T(8,128)(2,1)S(1)} %get-tuple-element.58), channel_id=1, source_target_pairs={{0,10},{1,11},{2,8},{3,9},{4,14},{5,15},{6,12},{7,13},{8,2},{9,3},... | collective-permute-start | bytes 589832 | tf_op jit(solution)/shard_map/ppermute | solution.py:474
  94.2 22.3 %collective-permute-start.6 = (bf16[384,256]{1,0:T(8,128)(2,1)S(1)}, bf16[384,256]{1,0:T(8,128)(2,1)S(1)}, u32[]{:S(2)}, u32[]{:S(2)}) collective-permute-start(bf16[384,256]{1,0:T(8,128)(2,1)S(1)} %get-tuple-element.59), channel_id=1, source_target_pairs={{0,12},{1,13},{2,14},{3,15},{4,8},{5,9},{6,10},{7,11},{8,4},{9,5},... | collective-permute-start | bytes 589832 | tf_op jit(solution)/shard_map/ppermute | solution.py:474
  96.6 20.0 %collective-permute-start.7 = (bf16[384,256]{1,0:T(8,128)(2,1)S(1)}, bf16[384,256]{1,0:T(8,128)(2,1)S(1)}, u32[]{:S(2)}, u32[]{:S(2)}) collective-permute-start(bf16[384,256]{1,0:T(8,128)(2,1)S(1)} %in_projection.9), channel_id=1, source_target_pairs={{0,14},{1,15},{2,12},{3,13},{4,10},{5,11},{6,8},{7,9},{8,6},{9,7},... | collective-permute-start | bytes 589832 | tf_op jit(solution)/shard_map/ppermute | solution.py:474
  119.0 13.5 %collective-permute-start.8 = (bf16[384,128]{1,0:T(8,128)(2,1)S(1)}, bf16[384,128]{1,0:T(8,128)(2,1)S(1)}, u32[]{:S(2)}, u32[]{:S(2)}) collective-permute-start(bf16[384,128]{1,0:T(8,128)(2,1)S(1)} %get-tuple-element.66), channel_id=1, source_target_pairs={{0,2},{1,3},{2,0},{3,1},{4,6},{5,7},{6,4},{7,5},{8,10},{9,11},{10,... | collective-permute-start | bytes 294920 | tf_op jit(solution)/shard_map/ppermute | solution.py:474
  122.6 10.8 %collective-permute-start.9 = (bf16[384,128]{1,0:T(8,128)(2,1)S(1)}, bf16[384,128]{1,0:T(8,128)(2,1)S(1)}, u32[]{:S(2)}, u32[]{:S(2)}) collective-permute-start(bf16[384,128]{1,0:T(8,128)(2,1)S(1)} %get-tuple-element.67), channel_id=1, source_target_pairs={{0,2},{1,3},{2,0},{3,1},{4,6},{5,7},{6,4},{7,5},{8,10},{9,11},{10,... | collective-permute-start | bytes 294920 | tf_op jit(solution)/shard_map/ppermute | solution.py:474
  124.2 11.4 %collective-permute-start.10 = (bf16[384,128]{1,0:T(8,128)(2,1)S(1)}, bf16[384,128]{1,0:T(8,128)(2,1)S(1)}, u32[]{:S(2)}, u32[]{:S(2)}) collective-permute-start(bf16[384,128]{1,0:T(8,128)(2,1)S(1)} %get-tuple-element.68), channel_id=1, source_target_pairs={{0,4},{1,5},{2,6},{3,7},{4,0},{5,1},{6,2},{7,3},{8,12},{9,13},{10,... | collective-permute-start | bytes 294920 | tf_op jit(solution)/shard_map/ppermute | solution.py:474
  130.5 8.6 %collective-permute-start.11 = (bf16[384,128]{1,0:T(8,128)(2,1)S(1)}, bf16[384,128]{1,0:T(8,128)(2,1)S(1)}, u32[]{:S(2)}, u32[]{:S(2)}) collective-permute-start(bf16[384,128]{1,0:T(8,128)(2,1)S(1)} %get-tuple-element.69), channel_id=1, source_target_pairs={{0,4},{1,5},{2,6},{3,7},{4,0},{5,1},{6,2},{7,3},{8,12},{9,13},{10,... | collective-permute-start | bytes 294920 | tf_op jit(solution)/shard_map/ppermute | solution.py:474
  130.5 11.1 %collective-permute-start.12 = (bf16[384,128]{1,0:T(8,128)(2,1)S(1)}, bf16[384,128]{1,0:T(8,128)(2,1)S(1)}, u32[]{:S(2)}, u32[]{:S(2)}) collective-permute-start(bf16[384,128]{1,0:T(8,128)(2,1)S(1)} %get-tuple-element.70), channel_id=1, source_target_pairs={{0,6},{1,7},{2,4},{3,5},{4,2},{5,3},{6,0},{7,1},{8,14},{9,15},{10,... | collective-permute-start | bytes 294920 | tf_op jit(solution)/shard_map/ppermute | solution.py:474
  132.5 10.7 %collective-permute-start.13 = (bf16[384,128]{1,0:T(8,128)(2,1)S(1)}, bf16[384,128]{1,0:T(8,128)(2,1)S(1)}, u32[]{:S(2)}, u32[]{:S(2)}) collective-permute-start(bf16[384,128]{1,0:T(8,128)(2,1)S(1)} %get-tuple-element.71), channel_id=1, source_target_pairs={{0,6},{1,7},{2,4},{3,5},{4,2},{5,3},{6,0},{7,1},{8,14},{9,15},{10,... | collective-permute-start | bytes 294920 | tf_op jit(solution)/shard_map/ppermute | solution.py:474
  133.4 12.3 %collective-permute-start.14 = (bf16[384,128]{1,0:T(8,128)(2,1)S(1)}, bf16[384,128]{1,0:T(8,128)(2,1)S(1)}, u32[]{:S(2)}, u32[]{:S(2)}) collective-permute-start(bf16[384,128]{1,0:T(8,128)(2,1)S(1)} %get-tuple-element.72), channel_id=1, source_target_pairs={{0,8},{1,9},{2,10},{3,11},{4,12},{5,13},{6,14},{7,15},{8,0},{9,1},... | collective-permute-start | bytes 294920 | tf_op jit(solution)/shard_map/ppermute | solution.py:474
  135.6 20.5 %collective-permute-start.15 = (bf16[384,128]{1,0:T(8,128)(2,1)S(1)}, bf16[384,128]{1,0:T(8,128)(2,1)S(1)}, u32[]{:S(2)}, u32[]{:S(2)}) collective-permute-start(bf16[384,128]{1,0:T(8,128)(2,1)S(1)} %get-tuple-element.73), channel_id=1, source_target_pairs={{0,8},{1,9},{2,10},{3,11},{4,12},{5,13},{6,14},{7,15},{8,0},{9,1},... | collective-permute-start | bytes 294920 | tf_op jit(solution)/shard_map/ppermute | solution.py:474
  139.0 19.9 %collective-permute-start.16 = (bf16[384,128]{1,0:T(8,128)(2,1)S(1)}, bf16[384,128]{1,0:T(8,128)(2,1)S(1)}, u32[]{:S(2)}, u32[]{:S(2)}) collective-permute-start(bf16[384,128]{1,0:T(8,128)(2,1)S(1)} %get-tuple-element.74), channel_id=1, source_target_pairs={{0,10},{1,11},{2,8},{3,9},{4,14},{5,15},{6,12},{7,13},{8,2},{9,3},... | collective-permute-start | bytes 294920 | tf_op jit(solution)/shard_map/ppermute | solution.py:474
  141.6 19.9 %collective-permute-start.17 = (bf16[384,128]{1,0:T(8,128)(2,1)S(1)}, bf16[384,128]{1,0:T(8,128)(2,1)S(1)}, u32[]{:S(2)}, u32[]{:S(2)}) collective-permute-start(bf16[384,128]{1,0:T(8,128)(2,1)S(1)} %get-tuple-element.75), channel_id=1, source_target_pairs={{0,10},{1,11},{2,8},{3,9},{4,14},{5,15},{6,12},{7,13},{8,2},{9,3},... | collective-permute-start | bytes 294920 | tf_op jit(solution)/shard_map/ppermute | solution.py:474
  143.2 18.3 %collective-permute-start.18 = (bf16[384,128]{1,0:T(8,128)(2,1)S(1)}, bf16[384,128]{1,0:T(8,128)(2,1)S(1)}, u32[]{:S(2)}, u32[]{:S(2)}) collective-permute-start(bf16[384,128]{1,0:T(8,128)(2,1)S(1)} %get-tuple-element.76), channel_id=1, source_target_pairs={{0,12},{1,13},{2,14},{3,15},{4,8},{5,9},{6,10},{7,11},{8,4},{9,5},... | collective-permute-start | bytes 294920 | tf_op jit(solution)/shard_map/ppermute | solution.py:474
  145.7 15.8 %collective-permute-start.19 = (bf16[384,128]{1,0:T(8,128)(2,1)S(1)}, bf16[384,128]{1,0:T(8,128)(2,1)S(1)}, u32[]{:S(2)}, u32[]{:S(2)}) collective-permute-start(bf16[384,128]{1,0:T(8,128)(2,1)S(1)} %get-tuple-element.77), channel_id=1, source_target_pairs={{0,12},{1,13},{2,14},{3,15},{4,8},{5,9},{6,10},{7,11},{8,4},{9,5},... | collective-permute-start | bytes 294920 | tf_op jit(solution)/shard_map/ppermute | solution.py:474
  156.1 7.4 %collective-permute-start.20 = (bf16[384,128]{1,0:T(8,128)(2,1)S(1)}, bf16[384,128]{1,0:T(8,128)(2,1)S(1)}, u32[]{:S(2)}, u32[]{:S(2)}) collective-permute-start(bf16[384,128]{1,0:T(8,128)(2,1)S(1)} %get-tuple-element.78), channel_id=1, source_target_pairs={{0,14},{1,15},{2,12},{3,13},{4,10},{5,11},{6,8},{7,9},{8,6},{9,7},... | collective-permute-start | bytes 294920 | tf_op jit(solution)/shard_map/ppermute | solution.py:474
  159.0 7.4 %collective-permute-start.21 = (bf16[384,128]{1,0:T(8,128)(2,1)S(1)}, bf16[384,128]{1,0:T(8,128)(2,1)S(1)}, u32[]{:S(2)}, u32[]{:S(2)}) collective-permute-start(bf16[384,128]{1,0:T(8,128)(2,1)S(1)} %get-tuple-element.79), channel_id=1, source_target_pairs={{0,14},{1,15},{2,12},{3,13},{4,10},{5,11},{6,8},{7,9},{8,6},{9,7},... | collective-permute-start | bytes 294920 | tf_op jit(solution)/shard_map/ppermute | solution.py:474
  171.6 2.6 %collective-permute-start.23 = (bf16[384,1024]{1,0:T(8,128)(2,1)S(1)}, bf16[384,1024]{1,0:T(8,128)(2,1)S(1)}, u32[]{:S(2)}, u32[]{:S(2)}) collective-permute-start(bf16[384,1024]{1,0:T(8,128)(2,1)S(1)} %bitcast.45), channel_id=1, source_target_pairs={{0,1},{1,0},{2,3},{3,2},{4,5},{5,4},{6,7},{7,6},{8,9},{9,8},{10,11... | collective-permute-start | bytes 2359304 | tf_op jit(solution)/shard_map/ppermute | solution.py:461
  171.6 2.6 %collective-permute-start.22 = (f32[384,1]{1,0:T(8,128)S(1)}, f32[384,1]{1,0:T(8,128)S(1)}, u32[]{:S(2)}, u32[]{:S(2)}) collective-permute-start(f32[384,1]{1,0:T(8,128)S(1)} %get-tuple-element.80.refs_17_), channel_id=1, source_target_pairs={{0,1},{1,0},{2,3},{3,2},{4,5},{5,4},{6,7},{7,6},{8,9},{9,8},{10,11... | collective-permute-start | bytes 4616 | tf_op jit(solution)/shard_map/ppermute | solution.py:461
  179.1 25.1 %all-to-all-start.1 = ((bf16[16,24,1024]{2,1,0:T(8,128)(2,1)}), bf16[16,24,1024]{2,1,0:T(8,128)(2,1)S(1)}, u32[]{:S(2)}, u32[]{:S(2)}) async-start(bf16[16,24,1024]{2,1,0:T(8,128)(2,1)} %bitcast.13), calls=%async_computation.1 | async-start | bytes 1572864 | tf_op jit(solution)/shard_map/all_to_all | solution.py:467
  185.5 47.5 %all-gather.6.cloned.1.call-start = ((), (), s32[]{:S(2)}) async-start(), calls=%async_computation.4 | async-start | bytes 1114112 | tf_op jit(solution)/shard_map/all_gather | solution.py:524
  190.5 2.5 %collective-permute-start.24 = (bf16[384,1024]{1,0:T(8,128)(2,1)}, bf16[384,1024]{1,0:T(8,128)(2,1)S(1)}, u32[]{:S(2)}, u32[]{:S(2)}) collective-permute-start(bf16[384,1024]{1,0:T(8,128)(2,1)} %bitcast.15), channel_id=1, source_target_pairs={{0,1},{1,0},{2,3},{3,2},{4,5},{5,4},{6,7},{7,6},{8,9},{9,8},{10,11... | collective-permute-start | bytes 2359304 | tf_op jit(solution)/shard_map/ppermute | solution.py:461
  198.0 36.6 %copy-start.7 = (s32[128,1]{0,1:T(1,128)S(1)}, s32[128,1]{0,1:T(1,128)}, u32[]{:S(2)}) copy-start(s32[128,1]{0,1:T(1,128)} %param.18) | copy-start | bytes 1540
  204.2 30.3 %all-to-all-start.2 = ((bf16[16,24,1024]{2,1,0:T(8,128)(2,1)}), bf16[16,24,1024]{2,1,0:T(8,128)(2,1)S(1)}, u32[]{:S(2)}, u32[]{:S(2)}) async-start(bf16[16,24,1024]{2,1,0:T(8,128)(2,1)} %bitcast.16), calls=%async_computation.2 | async-start | bytes 1572864 | tf_op jit(solution)/shard_map/all_to_all | solution.py:467
  (13 other events, 55.4 us)
Sparse Core Ops, SparseCore 0:
  24.5 47.5 all-gather.3
  191.7 41.2 all-gather.5

commit v7 on v6

--- a/solution.py
+++ b/solution.py
@@ -15,7 +15,7 @@
 CAP = 24
 PAIR = 256
 PACK = 256
-CHUNKS = 2
+CHUNKS = 1
 VMEM_BYTES = 48 * 1024 * 1024
 
 f32 = jnp.float32
@@ -67,9 +67,9 @@
 
 
 def dispatch_kernel(slices, *refs):
-    pack_ref, out_ref = refs[4:6]
-    bias_ref, ids_ref, tok_ref, bcd_ref, sems = refs[6:]
-    fetched(refs[:4], refs[6:10], sems)
+    pack_ref, out_ref = refs[3:5]
+    ids_ref, tok_ref, bcd_ref, sems = refs[5:]
+    fetched(refs[:3], refs[5:8], sems)
     rows, width = tok_ref.shape
     depth = width // slices
     ids, slot = route(ids_ref[...])
@@ -98,23 +98,18 @@
     raw = lax.dot_general(
         tok, jnp.concatenate([steps] * 4, axis=0), across, preferred_element_type=f32
     )
-    spread = (iota((HEADS, 128), 1) % HEADS == iota((HEADS, 128), 0)).astype(f32)
-    raw = raw + jnp.dot(
-        bias_ref[...], spread, precision=lax.Precision.HIGHEST, preferred_element_type=f32
-    )
-    steps_dt = jnp.maximum(raw, 0.0) + jnp.log1p(jnp.exp(-jnp.abs(raw)))
-    coarse = steps_dt.astype(bf16).astype(f32)
+    coarse = raw.astype(bf16).astype(f32)
     lane = iota((rows, 128), 1)
-    side = jnp.where(lane < HEADS, coarse, steps_dt - coarse)
+    side = jnp.where(lane < HEADS, coarse, raw - coarse)
     side = jnp.where(lane == 2 * HEADS, ids, jnp.where(lane == 2 * HEADS + 1, slot, side))
     pack_ref[:, 2 * NS :] = jnp.where(lane < 2 * HEADS + 2, side, 0.0).astype(bf16)
 
 
-def dispatch(bias, ids_row, tokens, bcd, slices):
+def dispatch(ids_row, tokens, bcd, slices):
     rows, width = tokens.shape
     return fetching_call(
         functools.partial(dispatch_kernel, slices),
-        (bias.reshape(1, -1), ids_row, tokens, bcd),
+        (ids_row, tokens, bcd),
         (
             jax.ShapeDtypeStruct((rows, PACK), bf16),
             jax.ShapeDtypeStruct((EXPERTS * slices * CAP, width // slices), bf16),
@@ -174,25 +169,28 @@
     )(place, *pieces, *([w_in] * slices))
 
 
-def prep_kernel(heads, place_ref, head_ref, rate_ref, skip_ref, pack_ref, w_ref, c_ref, b_ref, a_ref):
+def prep_kernel(heads, place_ref, head_ref, bias_ref, rate_ref, skip_ref, pack_ref, w_ref, c_ref, b_ref, a_ref):
     pack = pack_ref[...]
     row = iota((128, PACK), 0)
     lane = iota((128, PACK), 1)
     side = lane - 2 * NS - 2 * HEADS
     choose = ((row == heads) & (side == 0)) | ((row == heads + 1) & (side == 1))
     choose = choose.astype(f32)
-    rate = jnp.zeros((128, PAIR), f32)
+    rate = bias = jnp.zeros((128, PAIR), f32)
     for h in range(heads):
         at = lane - 2 * NS - head_ref[h]
         choose = jnp.where((row == h) & ((at == 0) | (at == HEADS)), 1.0, choose)
         rate = jnp.where(iota((128, PAIR), 0) == h, rate_ref[head_ref[h]], rate)
+        bias = jnp.where(iota((128, PAIR), 0) == h, bias_ref[head_ref[h]], bias)
     across = lax.dot_general(
         choose.astype(bf16), pack, (((1,), (1,)), ((), ())), preferred_element_type=f32
     )
+    raw = across + bias
+    steps_dt = jnp.maximum(raw, 0.0) + jnp.log1p(jnp.exp(-jnp.abs(raw)))
     upto = iota((PAIR, PAIR), 0)
     now = iota((PAIR, PAIR), 1)
     running = jnp.dot(
-        -across * rate,
+        -steps_dt * rate,
         (upto <= now).astype(f32),
         precision=lax.Precision.HIGHEST,
         preferred_element_type=f32,
@@ -216,7 +214,7 @@
     for h in range(heads):
         run_row = running[h : h + 1]
         run_col = down[:, h : h + 1]
-        dt_row = across[h : h + 1]
+        dt_row = steps_dt[h : h + 1]
         last = run_row[:, PAIR - 1 : PAIR]
         gap = jnp.where(causal, run_col - run_row, 0.0)
         weights = jnp.where(causal, jnp.exp(gap) * scores * dt_row, 0.0)
@@ -234,7 +232,7 @@
         a_ref[h, 0] = jnp.broadcast_to(jnp.exp(last), (8, 128))
 
 
-def prepare(place, own_heads, rate, skip, pack):
+def prepare(place, own_heads, bias, rate, skip, pack):
     heads = own_heads.shape[0]
     pairs = pack.shape[0] // PAIR
     slots = 2 * CAP * EXPERTS
@@ -252,7 +250,7 @@
             jax.ShapeDtypeStruct((heads, pairs, 8, 128), f32),
         ),
         grid=(pairs,),
-        in_specs=[smem, smem, smem, smem, pl.BlockSpec((PAIR, PACK), lambda p: (p, 0))],
+        in_specs=[smem] * 5 + [pl.BlockSpec((PAIR, PACK), lambda p: (p, 0))],
         out_specs=(block(slots, slots), block(slots, NS), block(NS, slots), block(8, 128)),
         compiler_params=params(),
         cost_estimate=pl.CostEstimate(
@@ -261,13 +259,12 @@
             transcendentals=heads * pairs * PAIR * PAIR,
         ),
         name="scan_weights",
-    )(place, own_heads, rate, skip, pack)
-
-
-def scan_kernel(*refs):
+    )(place, own_heads, bias, rate, skip, pack)
+
+
+def scan_kernel(place_ref, *refs):
     x_refs, refs = refs[:EXPERTS], refs[EXPERTS:]
-    w_ref, c_ref, b_ref, a_ref, gain_ref = refs[:5]
-    out_refs, last_ref, state = refs[5 : 5 + EXPERTS], refs[-2], refs[-1]
+    w_ref, c_ref, b_ref, a_ref, gain_ref, out_ref, last_ref, state = refs
 
     @pl.when(pl.program_id(0) == 0)
     def _():
@@ -286,12 +283,12 @@
         )
         z = (y * gain_ref[...]).astype(bf16)
         for q in range(EXPERTS):
-            out_refs[q][at, :] = z[q * rows : (q + 1) * rows]
+            out_ref[place_ref[1] ^ q, at, :] = z[q * rows : (q + 1) * rows]
     state[...] = now
     last_ref[...] = now
 
 
-def scan(x, weights, gain, h):
+def scan(place, x, weights, gain, h):
     rows = x[0].shape[0]
     width = gain.shape[1]
     pairs = rows // (2 * CAP)
@@ -299,24 +296,31 @@
     slots = 2 * CAP * EXPERTS
 
     def block(*dims):
-        return pl.BlockSpec((1, step, *dims), lambda p: (h, p, 0, 0))
-
-    *z, state = pl.pallas_call(
+        return pl.BlockSpec((1, step, *dims), lambda p, place_ref: (h, p, 0, 0))
+
+    return pl.pallas_call(
         scan_kernel,
-        out_shape=[jax.ShapeDtypeStruct((rows, width), bf16)] * EXPERTS
-        + [jax.ShapeDtypeStruct((NS, width), f32)],
-        grid=(pairs // step,),
-        in_specs=[pl.BlockSpec((2 * CAP * step, width), lambda p: (p, h))] * EXPERTS
-        + [
-            block(slots, slots),
-            block(slots, NS),
-            block(NS, slots),
-            block(8, 128),
-            pl.BlockSpec((1, width), lambda p: (0, 0)),
-        ],
-        out_specs=[pl.BlockSpec((2 * CAP * step, width), lambda p: (p, 0))] * EXPERTS
-        + [pl.BlockSpec((NS, width), lambda p: (0, 0))],
-        scratch_shapes=[pltpu.VMEM((NS, width), f32)],
+        out_shape=(
+            jax.ShapeDtypeStruct((EXPERTS, rows, width), bf16),
+            jax.ShapeDtypeStruct((NS, width), f32),
+        ),
+        grid_spec=pltpu.PrefetchScalarGridSpec(
+            num_scalar_prefetch=1,
+            grid=(pairs // step,),
+            in_specs=[pl.BlockSpec((2 * CAP * step, width), lambda p, place_ref: (p, h))] * EXPERTS
+            + [
+                block(slots, slots),
+                block(slots, NS),
+                block(NS, slots),
+                block(8, 128),
+                pl.BlockSpec((1, width), lambda p, place_ref: (0, 0)),
+            ],
+            out_specs=(
+                pl.BlockSpec((EXPERTS, 2 * CAP * step, width), lambda p, place_ref: (0, p, 0)),
+                pl.BlockSpec((NS, width), lambda p, place_ref: (0, 0)),
+            ),
+            scratch_shapes=[pltpu.VMEM((NS, width), f32)],
+        ),
         compiler_params=pltpu.CompilerParams(vmem_limit_bytes=VMEM_BYTES // 2),
         cost_estimate=pl.CostEstimate(
             flops=2 * pairs * slots * (slots + 2 * NS) * width,
@@ -324,8 +328,7 @@
             transcendentals=0,
         ),
         name="scan",
-    )(*x, *weights, gain)
-    return z, state
+    )(place, *x, *weights, gain)
 
 
 def out_kernel(kind, heads, counted, others, place_ref, *refs):
@@ -336,31 +339,29 @@
         del refs[:count]
         return got
 
-    z_refs, [w_ref] = take(EXPERTS * heads), take(1)
+    z_refs, [w_ref] = take(heads), take(1)
     inverse_ref = take(1)[0] if counted else None
     squares_refs = take(1 + others) if kind == "finish" else None
     part_refs = take(others) if kind == "finish" else None
     out_ref = take(1)[0]
-    rows, width = z_refs[0].shape
+    _, rows, width = z_refs[0].shape
     if counted:
 
         @pl.when(pl.program_id(0) == 0)
         def _():
             squares = jnp.zeros((rows, 1), f32)
-            for q in range(EXPERTS):
+            for j in range(EXPERTS):
                 for h in range(heads):
-                    z = z_refs[q * heads + h][...].astype(f32)
-                    z = z * inverse_ref[(place_ref[1] ^ q) * heads + h]
+                    z = z_refs[h][j].astype(f32) * inverse_ref[j * heads + h]
                     squares = squares + jnp.sum(z * z, axis=1, keepdims=True)
             refs[0][...] = squares
 
     units = heads * width
     total = None
-    for q in range(EXPERTS):
-        z = [r[...] for r in z_refs[q * heads : (q + 1) * heads]]
+    for j in range(EXPERTS):
+        z = [r[j] for r in z_refs]
         z = jnp.concatenate(z, axis=1) if heads > 1 else z[0]
-        w = w_ref[pl.ds(pl.multiple_of((place_ref[1] ^ q) * units, units), units), :]
-        part = jnp.dot(z, w, preferred_element_type=f32)
+        part = jnp.dot(z, w_ref[j * units : (j + 1) * units, :], preferred_element_type=f32)
         total = part if total is None else total + part
     if kind == "finish":
         squares = sum(r[...] for r in squares_refs)
@@ -372,8 +373,8 @@
 
 
 def out_projection(kind, chunk, *, place, z, w_out, inverse=None, squares=(), parts=()):
-    heads = len(z[0])
-    rows, width = z[0][0].shape
+    heads = len(z)
+    _, rows, width = z[0].shape
     slices = INNER // w_out.shape[0]
     slice_width = w_out.shape[1] // slices
     part = slice_width // CHUNKS
@@ -389,9 +390,8 @@
     def fixed(*dims):
         return pl.BlockSpec(dims, lambda n, place_ref: (0,) * len(dims))
 
-    pieces = [(q, h) for q in range(EXPERTS) for h in range(heads)]
-    operands = [z[q][h] for q, h in pieces] + [w_out]
-    specs = [fixed(rows, width)] * len(pieces)
+    operands = [*z, w_out]
+    specs = [fixed(*z[0].shape)] * heads
     specs.append(
         pl.BlockSpec((w_out.shape[0], tile), lambda n, place_ref: (0, column(n, place_ref)))
     )
@@ -474,6 +474,14 @@
     return lax.ppermute(a, "expert", pairs)
 
 
+def gathered(a, me, n):
+    other = lax.ppermute(a, "expert", [(d, d ^ 1) for d in range(n)])
+    first = me % 2 == 0
+    pair = jnp.concatenate([jnp.where(first, a, other), jnp.where(first, other, a)], axis=0)
+    groups = [list(range(k, n, 2)) for k in range(2)]
+    return lax.all_gather(pair, "expert", axis=0, axis_index_groups=groups, tiled=True)
+
+
 def exchange(arrays, n, slices):
     out = list(arrays)
     for q in reversed(range(1, EXPERTS)):
@@ -494,12 +502,13 @@
     chip = (me // slices).astype(jnp.int32)
     place = jnp.stack([(me % slices).astype(jnp.int32), chip])
     start = place[0] * in_dev + chip * units
+    same_slice = [[j * slices + k for j in range(EXPERTS)] for k in range(slices)]
     ids_row = expert_ids.reshape(1, -1)
     w_in, w_out = w_in[0], w_out[0]
 
-    pack, outgoing = dispatch(dt_bias, ids_row, tokens, w_bcd.T, slices)
+    pack, outgoing = dispatch(ids_row, tokens, w_bcd.T, slices)
     landed = swap(outgoing)
-    pack = lax.all_gather(pack, "expert", axis=0, tiled=True)
+    pack = gathered(pack, me, n)
     own_heads = start // HEADDIM + jnp.arange(heads, dtype=jnp.int32)
 
     pieces = [landed] + [turn(landed, n, slices, r) for r in range(1, slices)]
@@ -507,7 +516,7 @@
     for order in ((7,), (6, 5), (4, 3), (2, 1), (0,)):
         if order == (4, 3):
             pieces, pack = lax.optimization_barrier((pieces, pack))
-            weights = prepare(place, own_heads, decay_rate, skip_gain, pack)
+            weights = prepare(place, own_heads, dt_bias, decay_rate, skip_gain, pack)
         if order == (0,):
             pieces, weights = lax.optimization_barrier((pieces, weights))
         for q, a in zip(order, in_projection(place, pieces, w_in, units, order)):
@@ -517,11 +526,11 @@
     gain = lax.dynamic_slice(norm_gain, (start,), (units,))
     z, states = [], []
     for h in range(heads):
-        rows, state = scan(x, weights, gain[h * width : (h + 1) * width].reshape(1, width), h)
-        z.append(exchange(rows, n, slices))
+        own_gain = gain[h * width : (h + 1) * width].reshape(1, width)
+        rows, state = scan(place, x, weights, own_gain, h)
+        z.append(swap(rows, same_slice))
         states.append(state)
-    z = [[z[h][q] for h in range(heads)] for q in range(EXPERTS)]
-    states = lax.all_gather(jnp.stack(states), "expert", axis=0, tiled=False)
+    states = gathered(jnp.stack(states), me, n)
 
     inverse = 1.0 / lax.dynamic_slice(norm_gain, (place[0] * in_dev,), (in_dev,))
     inverse = inverse.reshape(in_dev // width, 1, width)

time: 245 us -> 262 us (1.069)
  waiting for transfers between devices: 101 us -> 133 us
  starting transfers between devices: 58.2 us -> 33.9 us
  local copies, waits for them, and re-layouts: 6.15 us -> 15.5 us
    all_gather x2, waiting for transfers between devices: 38 us -> 68.2 us  [gathered(): lax.all_gather(pair, 'expert', axis=0, axis_index_groups=groups, tiled=True)]
    ppermute x21 -> x7, starting transfers between devices: 36.5 us -> 11.3 us  [across(): return lax.ppermute(a, 'expert', pairs)]
    all_to_all x3 -> x4, waiting for transfers between devices: 39.6 us -> 59.5 us  [swap(): lax.all_to_all(a, 'expert', split_axis=0, concat_axis=0, axis_index_group...]
    ppermute x21 -> x7, waiting for transfers between devices: 19.1 us -> 0.02 us  [across(): return lax.ppermute(a, 'expert', pairs)]
    unnamed x30 -> x60, local copies, waits for them, and re-layouts: 4.5 us -> 13.1 us
    pallas_call x4 -> x2, Pallas kernels: 20 us -> 15.8 us  [out_projection(): pl.pallas_call(functools.partial(out_kernel, kind, heads, inverse is not...]
    all_to_all x3 -> x4, starting transfers between devices: 19.8 us -> 20.3 us  [swap(): lax.all_to_all(a, 'expert', split_axis=0, concat_axis=0, axis_index_group...]
  transfers between devices with their start and end apart: 30 -> 18, of which waited for: 13 -> 8; matrix products, arithmetic and copies ran while one was open for 1% -> 1% of each run, Pallas kernels for 15% -> 11%
where the time goes in v7:
time: 262 us; the launch traced here: 261 us
  waiting for transfers between devices  133 us (51%)
  Pallas kernels  62.2 us (24%)
  starting transfers between devices  33.9 us (13%)
  local copies, waits for them, and re-layouts  15.5 us (6%)
  between operations  15.2 us (6%)
    all_gather x2, waiting for transfers between devices, gathered(): lax.all_gather(pair, 'expert', axis=0, axis_index_groups=groups, tiled=True)  68.2 us
    all_to_all x4, waiting for transfers between devices, swap(): lax.all_to_all(a, 'expert', split_axis=0, concat_axis=0, axis_index_group...  59.5 us
    all_to_all x4, starting transfers between devices, swap(): lax.all_to_all(a, 'expert', split_axis=0, concat_axis=0, axis_index_group...  20.3 us
    pallas_call x5, Pallas kernels, in_projection(): pl.pallas_call(functools.partial(in_kernel, slices, shares, turns), out_s...  19.9 us
    pallas_call x2, Pallas kernels, out_projection(): pl.pallas_call(functools.partial(out_kernel, kind, heads, inverse is not...  15.8 us
    pallas_call x1, Pallas kernels, prepare(): pl.pallas_call(functools.partial(prep_kernel, heads), out_shape=(jax.Shap...  14.7 us
    unnamed x60, local copies, waits for them, and re-layouts  13.1 us
    ppermute x7, starting transfers between devices, across(): return lax.ppermute(a, 'expert', pairs)  11.3 us
  transfers between devices with their start and end apart: 18, of which 8 were waited for; matrix products, arithmetic and copies ran while one was open for 1% of the time, Pallas kernels for 11%

profile of v7, /device:TPU:0, one launch (start us, length us, event | category | flops | bytes accessed | tf_op | source)
XLA Modules:
  0.0 261.0 jit_solution(10962168838158804966)
XLA Ops:
  7.2 1.3 copy-done.5
  8.5 1.2 copy-done.6
  10.4 2.3 dispatch.1
  12.7 7.4 %all-to-all-start = ((bf16[16,24,2048]{2,1,0:T(8,128)(2,1)}), bf16[16,24,2048]{2,1,0:T(8,128)(2,1)S(1)}, u32[]{:S(2)}, u32[]{:S(2)}) async-start(bf16[16,24,2048]{2,1,0:T(8,128)(2,1)} %bitcast.4), calls=%async_computation | async-start | bytes 3145728 | tf_op jit(solution)/shard_map/all_to_all | solution.py:467
  22.2 34.1 %all-to-all-done = bf16[16,24,2048]{2,1,0:T(8,128)(2,1)S(1)} async-done(((bf16[16,24,2048]{2,1,0:T(8,128)(2,1)}), bf16[16,24,2048]{2,1,0:T(8,128)(2,1)S(1)}, u32[]{:S(2)}, u32[]{:S(2)}) %all-to-all-start) | async-done | bytes 1572896 | tf_op jit(solution)/shard_map/all_to_all | solution.py:467
  57.9 16.4 %all-gather.3.cloned.1.call-done.pack_ref = bf16[2048,256]{1,0:T(8,128)(2,1)} async-done(((bf16[256,256]{1,0:T(8,128)(2,1)}), bf16[2048,256]{1,0:T(8,128)(2,1)}) %all-gather.3.cloned.1.call-update) | async-done | bytes 1048592 | tf_op jit(solution)/shard_map/all_gather | solution.py:482
  74.3 4.2 %in_projection.6 = (bf16[384,256]{1,0:T(8,128)(2,1)S(1)}, bf16[384,256]{1,0:T(8,128)(2,1)S(1)}) custom-call(s32[2]{0:T(128)S(1)} %pad_add_fusion.place_ref, bf16[384,2048]{1,0:T(8,128)(2,1)S(1)} %bitcast.25, bf16[384,2048]{1,0:T(8,128)(2,1)S(1)} %collective-permute-done.refs_1_, bf16[4096,2048]{1,0:T(8,128)(2,1)} %bitcast.42, bf16[4096,2048]{1,0:T(8,128)(2,1)} %bitcast.43), custom_call_target="tpu_custom_call" | custom-call | flops 1610612736 | bytes 7340032 | tf_op jit(solution)/shard_map/in_projection/pallas_call | solution.py:152
  78.5 4.2 %in_projection.7 = (bf16[384,256]{1,0:T(8,128)(2,1)S(1)}, bf16[384,256]{1,0:T(8,128)(2,1)S(1)}) custom-call(s32[2]{0:T(128)S(1)} %pad_add_fusion.place_ref, bf16[384,2048]{1,0:T(8,128)(2,1)S(1)} %bitcast.26, bf16[384,2048]{1,0:T(8,128)(2,1)S(1)} %collective-permute-done.refs_1_, bf16[4096,2048]{1,0:T(8,128)(2,1)} %bitcast.44, bf16[4096,2048]{1,0:T(8,128)(2,1)} %bitcast.45), custom_call_target="tpu_custom_call" | custom-call | flops 1610612736 | bytes 7340032 | tf_op jit(solution)/shard_map/in_projection/pallas_call | solution.py:152
  84.4 1.9 collective-permute-start.4
  86.9 4.2 %in_projection.8 = (bf16[384,256]{1,0:T(8,128)(2,1)S(1)}, bf16[384,256]{1,0:T(8,128)(2,1)S(1)}) custom-call(s32[2]{0:T(128)S(1)} %pad_add_fusion.place_ref, bf16[384,2048]{1,0:T(8,128)(2,1)S(1)} %bitcast.27, bf16[384,2048]{1,0:T(8,128)(2,1)S(1)} %collective-permute-done.refs_1_, bf16[4096,2048]{1,0:T(8,128)(2,1)} %bitcast.46, bf16[4096,2048]{1,0:T(8,128)(2,1)} %bitcast.47), custom_call_target="tpu_custom_call" | custom-call | flops 1610612736 | bytes 7340032 | tf_op jit(solution)/shard_map/in_projection/pallas_call | solution.py:152
  91.1 2.5 collective-permute-start.6
  93.7 3.1 %in_projection.9 = bf16[384,256]{1,0:T(8,128)(2,1)S(1)} custom-call(s32[2]{0:T(128)S(1)} %pad_add_fusion.place_ref, bf16[384,2048]{1,0:T(8,128)(2,1)S(1)} %bitcast.28, bf16[384,2048]{1,0:T(8,128)(2,1)S(1)} %collective-permute-done.refs_1_, bf16[4096,2048]{1,0:T(8,128)(2,1)} %bitcast.48, bf16[4096,2048]{1,0:T(8,128)(2,1)} %bitcast.49), custom_call_target="tpu_custom_call" | custom-call | flops 805306368 | bytes 5242880 | tf_op jit(solution)/shard_map/in_projection/pallas_call | solution.py:152
  96.8 2.3 collective-permute-start.7
  99.0 2.3 collective-permute-start.8
  101.3 14.7 %scan_weights.1 = (bf16[2,8,384,384]{3,2,1,0:T(8,128)(2,1)}, bf16[2,8,384,64]{3,2,1,0:T(8,128)(2,1)S(1)}, bf16[2,8,64,384]{3,2,1,0:T(8,128)(2,1)S(1)}, f32[2,8,8,128]{3,2,1,0:T(8,128)S(1)}) custom-call(s32[2]{0:T(128)S(1)} %pad_add_fusion.place_ref, s32[2]{0:T(128)S(1)} %iota_add_fusion.head_ref, f32[32]{0:T(128)S(1)} %copy-done.24, f32[32]{0:T(128)S(1)} %copy-done.25, ...), custom_call_target="tpu_custom_call" | custom-call | flops 2415919104 | bytes 4718592 | tf_op jit(solution)/shard_map/scan_weights/pallas_call | solution.py:244
  116.1 4.2 %in_projection.5.refs_0_ = bf16[384,256]{1,0:T(8,128)(2,1)S(1)} custom-call(s32[2]{0:T(128)S(1)} %pad_add_fusion.place_ref, bf16[384,2048]{1,0:T(8,128)(2,1)S(1)} %bitcast.29, bf16[384,2048]{1,0:T(8,128)(2,1)S(1)} %collective-permute-done.refs_1_, bf16[4096,2048]{1,0:T(8,128)(2,1)} %bitcast.50, bf16[4096,2048]{1,0:T(8,128)(2,1)} %bitcast.51), custom_call_target="tpu_custom_call" | custom-call | flops 805306368 | bytes 5242880 | tf_op jit(solution)/shard_map/in_projection/pallas_call | solution.py:152
  120.5 3.7 %scan.2 = (bf16[8,384,128]{2,1,0:T(8,128)(2,1)}, f32[64,128]{1,0:T(8,128)S(1)}) custom-call(s32[2]{0:T(128)S(1)} %pad_add_fusion.place_ref, bf16[384,256]{1,0:T(8,128)(2,1)S(1)} %in_projection.5.refs_0_, bf16[384,256]{1,0:T(8,128)(2,1)S(1)} %collective-permute-done.2.refs_1_, bf16[384,256]{1,0:T(8,128)(2,1)S(1)} %collective-permute-done.3.refs_2_, ...), custom_call_target="tpu_custom_call" | custom-call | flops 402653184 | bytes 2359296 | tf_op jit(solution)/shard_map/scan/pallas_call | solution.py:301
  124.2 5.5 %all-to-all-start.1 = ((bf16[8,384,128]{2,1,0:T(8,128)(2,1)}), bf16[8,384,128]{2,1,0:T(8,128)(2,1)S(1)}, u32[]{:S(2)}, u32[]{:S(2)}) async-start(bf16[8,384,128]{2,1,0:T(8,128)(2,1)} %get-tuple-element.50), calls=%async_computation.1 | async-start | bytes 1572864 | tf_op jit(solution)/shard_map/all_to_all | solution.py:467
  129.8 2.3 copy-done
  132.1 1.1 copy-done.4
  133.2 0.9 copy-done.8
  139.6 3.8 %scan.3 = (bf16[8,384,128]{2,1,0:T(8,128)(2,1)}, f32[64,128]{1,0:T(8,128)S(1)}) custom-call(s32[2]{0:T(128)S(1)} %pad_add_fusion.place_ref, bf16[384,256]{1,0:T(8,128)(2,1)S(1)} %in_projection.5.refs_0_, bf16[384,256]{1,0:T(8,128)(2,1)S(1)} %collective-permute-done.2.refs_1_, bf16[384,256]{1,0:T(8,128)(2,1)S(1)} %copy-done.8, ...), custom_call_target="tpu_custom_call" | custom-call | flops 402653184 | bytes 2359296 | tf_op jit(solution)/shard_map/scan/pallas_call | solution.py:301
  143.4 5.5 %all-to-all-done.1.refs_0_ = bf16[8,384,128]{2,1,0:T(8,128)(2,1)S(1)} async-done(((bf16[8,384,128]{2,1,0:T(8,128)(2,1)}), bf16[8,384,128]{2,1,0:T(8,128)(2,1)S(1)}, u32[]{:S(2)}, u32[]{:S(2)}) %all-to-all-start.1) | async-done | bytes 786464 | tf_op jit(solution)/shard_map/all_to_all | solution.py:467
  148.9 3.5 %all-to-all-start.2 = ((bf16[8,384,128]{2,1,0:T(8,128)(2,1)}), bf16[8,384,128]{2,1,0:T(8,128)(2,1)S(1)}, u32[]{:S(2)}, u32[]{:S(2)}) async-start(bf16[8,384,128]{2,1,0:T(8,128)(2,1)} %get-tuple-element.51), calls=%async_computation.2 | async-start | bytes 1572864 | tf_op jit(solution)/shard_map/all_to_all | solution.py:467
  152.4 20.0 %all-to-all-done.2.refs_1_ = bf16[8,384,128]{2,1,0:T(8,128)(2,1)S(1)} async-done(((bf16[8,384,128]{2,1,0:T(8,128)(2,1)}), bf16[8,384,128]{2,1,0:T(8,128)(2,1)S(1)}, u32[]{:S(2)}, u32[]{:S(2)}) %all-to-all-start.2) | async-done | bytes 786464 | tf_op jit(solution)/shard_map/all_to_all | solution.py:467
  172.5 7.9 %out_send.1 = (bf16[1,384,2048]{2,1,0:T(8,128)(2,1)S(1)}, f32[384,1]{1,0:T(8,128)S(1)}) custom-call(s32[2]{0:T(128)S(1)} %pad_add_fusion.place_ref, bf16[8,384,128]{2,1,0:T(8,128)(2,1)S(1)} %all-to-all-done.1.refs_0_, bf16[8,384,128]{2,1,0:T(8,128)(2,1)S(1)} %all-to-all-done.2.refs_1_, bf16[2048,4096]{1,0:T(8,128)(2,1)} %bitcast.52, f32[16,1,128]{2,1,0:T(1,128)S(1)} %bitcast.38), custom_call_target="tpu_custom_call" | custom-call | flops 3221225472 | bytes 9961472 | tf_op jit(solution)/shard_map/out_send/pallas_call | solution.py:415
  180.9 3.2 %collective-permute-done.9.refs_4_ = f32[384,1]{1,0:T(8,128)S(1)} collective-permute-done((f32[384,1]{1,0:T(8,128)S(1)}, f32[384,1]{1,0:T(8,128)S(1)}, u32[]{:S(2)}, u32[]{:S(2)}) %collective-permute-start.9) | collective-permute-done | bytes 1568 | tf_op jit(solution)/shard_map/ppermute | solution.py:461
  184.1 7.9 %out_finish.1 = bf16[384,2048]{1,0:T(8,128)(2,1)} custom-call(s32[2]{0:T(128)S(1)} %pad_add_fusion.place_ref, bf16[8,384,128]{2,1,0:T(8,128)(2,1)S(1)} %all-to-all-done.1.refs_0_, bf16[8,384,128]{2,1,0:T(8,128)(2,1)S(1)} %all-to-all-done.2.refs_1_, bf16[2048,4096]{1,0:T(8,128)(2,1)} %bitcast.53, f32[384,1]{1,0:T(8,128)S(1)} %get-tuple-element.52.refs_3_, ...), custom_call_target="tpu_custom_call" | custom-call | flops 3221225472 | bytes 9961472 | tf_op jit(solution)/shard_map/out_finish/pallas_call | solution.py:415
  192.1 3.8 %all-to-all-start.3 = ((bf16[16,24,2048]{2,1,0:T(8,128)(2,1)}), bf16[16,24,2048]{2,1,0:T(8,128)(2,1)S(1)}, u32[]{:S(2)}, u32[]{:S(2)}) async-start(bf16[16,24,2048]{2,1,0:T(8,128)(2,1)} %bitcast.12), calls=%async_computation.3 | async-start | bytes 3145728 | tf_op jit(solution)/shard_map/all_to_all | solution.py:467
  196.3 1.0 collective-permute-done.11
  198.7 51.9 %all-gather.5.cloned.1.call-done = f32[32,64,128]{2,1,0:T(8,128)} async-done(((f32[4,64,128]{2,1,0:T(8,128)}), f32[32,64,128]{2,1,0:T(8,128)}) %all-gather.5.cloned.1.call-update) | async-done | bytes 1048592 | tf_op jit(solution)/shard_map/all_gather | solution.py:482
  252.2 2.0 collect.1
  (92 shorter events, 15.6 us)
Async XLA Ops:
  12.7 43.6 %all-to-all-start = ((bf16[16,24,2048]{2,1,0:T(8,128)(2,1)}), bf16[16,24,2048]{2,1,0:T(8,128)(2,1)S(1)}, u32[]{:S(2)}, u32[]{:S(2)}) async-start(bf16[16,24,2048]{2,1,0:T(8,128)(2,1)} %bitcast.4), calls=%async_computation | async-start | bytes 3145728 | tf_op jit(solution)/shard_map/all_to_all | solution.py:467
  20.1 54.2 %all-gather.3.cloned.1.call-start = ((), (), s32[]{:S(2)}) async-start(), calls=%async_computation.4 | async-start | bytes 1179648 | tf_op jit(solution)/shard_map/all_gather | solution.py:482
  20.2 1.4 collective-permute-start.1
  56.3 18.0 %collective-permute-start = (bf16[384,2048]{1,0:T(8,128)(2,1)S(1)}, bf16[384,2048]{1,0:T(8,128)(2,1)S(1)}, u32[]{:S(2)}, u32[]{:S(2)}) collective-permute-start(bf16[384,2048]{1,0:T(8,128)(2,1)S(1)} %bitcast.24), channel_id=1, source_target_pairs={{0,1},{1,0},{2,3},{3,2},{4,5},{5,4},{6,7},{7,6},{8,9},{9,8},{10,11... | collective-permute-start | bytes 4718600 | tf_op jit(solution)/shard_map/ppermute | solution.py:461
  82.7 14.1 %collective-permute-start.2 = (bf16[384,256]{1,0:T(8,128)(2,1)S(1)}, bf16[384,256]{1,0:T(8,128)(2,1)S(1)}, u32[]{:S(2)}, u32[]{:S(2)}) collective-permute-start(bf16[384,256]{1,0:T(8,128)(2,1)S(1)} %get-tuple-element.40), channel_id=1, source_target_pairs={{0,2},{1,3},{2,0},{3,1},{4,6},{5,7},{6,4},{7,5},{8,10},{9,11},{10,... | collective-permute-start | bytes 589832 | tf_op jit(solution)/shard_map/ppermute | solution.py:474
  83.5 15.5 %collective-permute-start.3 = (bf16[384,256]{1,0:T(8,128)(2,1)S(1)}, bf16[384,256]{1,0:T(8,128)(2,1)S(1)}, u32[]{:S(2)}, u32[]{:S(2)}) collective-permute-start(bf16[384,256]{1,0:T(8,128)(2,1)S(1)} %get-tuple-element.41), channel_id=1, source_target_pairs={{0,4},{1,5},{2,6},{3,7},{4,0},{5,1},{6,2},{7,3},{8,12},{9,13},{10,... | collective-permute-start | bytes 589832 | tf_op jit(solution)/shard_map/ppermute | solution.py:474
  84.4 35.9 %collective-permute-start.4 = (bf16[384,256]{1,0:T(8,128)(2,1)S(1)}, bf16[384,256]{1,0:T(8,128)(2,1)S(1)}, u32[]{:S(2)}, u32[]{:S(2)}) collective-permute-start(bf16[384,256]{1,0:T(8,128)(2,1)S(1)} %get-tuple-element.42), channel_id=1, source_target_pairs={{0,6},{1,7},{2,4},{3,5},{4,2},{5,3},{6,0},{7,1},{8,14},{9,15},{10,... | collective-permute-start | bytes 589832 | tf_op jit(solution)/shard_map/ppermute | solution.py:474
  86.2 34.1 %collective-permute-start.5 = (bf16[384,256]{1,0:T(8,128)(2,1)S(1)}, bf16[384,256]{1,0:T(8,128)(2,1)S(1)}, u32[]{:S(2)}, u32[]{:S(2)}) collective-permute-start(bf16[384,256]{1,0:T(8,128)(2,1)S(1)} %get-tuple-element.43), channel_id=1, source_target_pairs={{0,8},{1,9},{2,10},{3,11},{4,12},{5,13},{6,14},{7,15},{8,0},{9,1},... | collective-permute-start | bytes 589832 | tf_op jit(solution)/shard_map/ppermute | solution.py:474
  91.1 10.3 %copy-start.23 = (bf16[2048,256]{1,0:T(8,128)(2,1)S(1)}, bf16[2048,256]{1,0:T(8,128)(2,1)}, u32[]{:S(2)}) copy-start(bf16[2048,256]{1,0:T(8,128)(2,1)} %all-gather.3.cloned.1.call-done.pack_ref) | copy-start | bytes 3145732
  91.1 10.2 %copy-start.24 = (f32[32]{0:T(128)S(1)}, f32[32]{0:T(128)}, u32[]{:S(2)}) copy-start(f32[32]{0:T(128)} %bias_ref.1) | copy-start | bytes 388
  91.1 10.2 %copy-start.25 = (f32[32]{0:T(128)S(1)}, f32[32]{0:T(128)}, u32[]{:S(2)}) copy-start(f32[32]{0:T(128)} %rate_ref.1) | copy-start | bytes 388
  91.1 10.2 %copy-start.26 = (f32[32]{0:T(128)S(1)}, f32[32]{0:T(128)}, u32[]{:S(2)}) copy-start(f32[32]{0:T(128)} %skip_ref.1) | copy-start | bytes 388
  91.1 29.2 %collective-permute-start.6 = (bf16[384,256]{1,0:T(8,128)(2,1)S(1)}, bf16[384,256]{1,0:T(8,128)(2,1)S(1)}, u32[]{:S(2)}, u32[]{:S(2)}) collective-permute-start(bf16[384,256]{1,0:T(8,128)(2,1)S(1)} %get-tuple-element.44), channel_id=1, source_target_pairs={{0,10},{1,11},{2,8},{3,9},{4,14},{5,15},{6,12},{7,13},{8,2},{9,3},... | collective-permute-start | bytes 589832 | tf_op jit(solution)/shard_map/ppermute | solution.py:474
  96.8 23.6 %collective-permute-start.7 = (bf16[384,256]{1,0:T(8,128)(2,1)S(1)}, bf16[384,256]{1,0:T(8,128)(2,1)S(1)}, u32[]{:S(2)}, u32[]{:S(2)}) collective-permute-start(bf16[384,256]{1,0:T(8,128)(2,1)S(1)} %get-tuple-element.45), channel_id=1, source_target_pairs={{0,12},{1,13},{2,14},{3,15},{4,8},{5,9},{6,10},{7,11},{8,4},{9,5},... | collective-permute-start | bytes 589832 | tf_op jit(solution)/shard_map/ppermute | solution.py:474
  99.0 21.4 %copy-start.7 = (bf16[384,256]{1,0:T(8,128)(2,1)}, bf16[384,256]{1,0:T(8,128)(2,1)S(1)}, u32[]{:S(2)}) copy-start(bf16[384,256]{1,0:T(8,128)(2,1)S(1)} %collective-permute-done.3.refs_2_) | copy-start | bytes 589828
  99.0 21.4 %collective-permute-start.8 = (bf16[384,256]{1,0:T(8,128)(2,1)S(1)}, bf16[384,256]{1,0:T(8,128)(2,1)S(1)}, u32[]{:S(2)}, u32[]{:S(2)}) collective-permute-start(bf16[384,256]{1,0:T(8,128)(2,1)S(1)} %in_projection.9), channel_id=1, source_target_pairs={{0,14},{1,15},{2,12},{3,13},{4,10},{5,11},{6,8},{7,9},{8,6},{9,7},... | collective-permute-start | bytes 589832 | tf_op jit(solution)/shard_map/ppermute | solution.py:474
  116.0 4.4 %copy-start.1 = (bf16[2,8,384,64]{3,2,1,0:T(8,128)(2,1)}, bf16[2,8,384,64]{3,2,1,0:T(8,128)(2,1)S(1)}, u32[]{:S(2)}) copy-start(bf16[2,8,384,64]{3,2,1,0:T(8,128)(2,1)S(1)} %get-tuple-element.47.refs_9_) | copy-start | bytes 2359300
  116.0 4.4 %copy-start.3 = (bf16[2,8,64,384]{3,2,1,0:T(8,128)(2,1)}, bf16[2,8,64,384]{3,2,1,0:T(8,128)(2,1)S(1)}, u32[]{:S(2)}) copy-start(bf16[2,8,64,384]{3,2,1,0:T(8,128)(2,1)S(1)} %get-tuple-element.48.refs_10_) | copy-start | bytes 2359300
  116.0 4.4 %copy-start.19 = (f32[2,8,8,128]{3,2,1,0:T(8,128)}, f32[2,8,8,128]{3,2,1,0:T(8,128)S(1)}, u32[]{:S(2)}) copy-start(f32[2,8,8,128]{3,2,1,0:T(8,128)S(1)} %get-tuple-element.49.refs_11_) | copy-start | bytes 196612
  116.0 4.4 %slice-start = ((s8[4718592]{0:T(1024)(128)(4,1)}), s8[4194304]{0:T(1024)(128)(4,1)S(1)}, s32[]{:S(2)}) async-start(s8[4718592]{0:T(1024)(128)(4,1)} %bitcast.30), calls=%async_computation.6 | async-start | bytes 8388608
  116.0 4.4 %slice-start.1 = ((s8[4718592]{0:T(1024)(128)(4,1)}), s8[524288]{0:T(1024)(128)(4,1)S(1)}, s32[]{:S(2)}) async-start(s8[4718592]{0:T(1024)(128)(4,1)} %bitcast.30), calls=%async_computation.7 | async-start | bytes 1048576
  120.3 3.9 %copy-start.9 = (bf16[384,256]{1,0:T(8,128)(2,1)}, bf16[384,256]{1,0:T(8,128)(2,1)S(1)}, u32[]{:S(2)}) copy-start(bf16[384,256]{1,0:T(8,128)(2,1)S(1)} %collective-permute-done.4.refs_3_) | copy-start | bytes 589828
  124.2 5.5 %copy-start.2 = (bf16[2,8,384,64]{3,2,1,0:T(8,128)(2,1)S(1)}, bf16[2,8,384,64]{3,2,1,0:T(8,128)(2,1)}, u32[]{:S(2)}) copy-start(bf16[2,8,384,64]{3,2,1,0:T(8,128)(2,1)} %copy-done.1) | copy-start | bytes 2359300
  124.2 24.6 %all-to-all-start.1 = ((bf16[8,384,128]{2,1,0:T(8,128)(2,1)}), bf16[8,384,128]{2,1,0:T(8,128)(2,1)S(1)}, u32[]{:S(2)}, u32[]{:S(2)}) async-start(bf16[8,384,128]{2,1,0:T(8,128)(2,1)} %get-tuple-element.50), calls=%async_computation.1 | async-start | bytes 1572864 | tf_op jit(solution)/shard_map/all_to_all | solution.py:467
  143.4 9.0 %copy-start.27 = (f32[4096]{0:T(1024)S(1)}, f32[4096]{0:T(1024)}, u32[]{:S(2)}) copy-start(f32[4096]{0:T(1024)} %param.17) | copy-start | bytes 49156
  148.9 23.6 %all-to-all-start.2 = ((bf16[8,384,128]{2,1,0:T(8,128)(2,1)}), bf16[8,384,128]{2,1,0:T(8,128)(2,1)S(1)}, u32[]{:S(2)}, u32[]{:S(2)}) async-start(bf16[8,384,128]{2,1,0:T(8,128)(2,1)} %get-tuple-element.51), calls=%async_computation.2 | async-start | bytes 1572864 | tf_op jit(solution)/shard_map/all_to_all | solution.py:467
  180.4 3.8 %collective-permute-start.10 = (bf16[384,2048]{1,0:T(8,128)(2,1)S(1)}, bf16[384,2048]{1,0:T(8,128)(2,1)S(1)}, u32[]{:S(2)}, u32[]{:S(2)}) collective-permute-start(bf16[384,2048]{1,0:T(8,128)(2,1)S(1)} %bitcast.41), channel_id=1, source_target_pairs={{0,1},{1,0},{2,3},{3,2},{4,5},{5,4},{6,7},{7,6},{8,9},{9,8},{10,11... | collective-permute-start | bytes 4718600 | tf_op jit(solution)/shard_map/ppermute | solution.py:461
  180.4 3.7 %collective-permute-start.9 = (f32[384,1]{1,0:T(8,128)S(1)}, f32[384,1]{1,0:T(8,128)S(1)}, u32[]{:S(2)}, u32[]{:S(2)}) collective-permute-start(f32[384,1]{1,0:T(8,128)S(1)} %get-tuple-element.52.refs_3_), channel_id=1, source_target_pairs={{0,1},{1,0},{2,3},{3,2},{4,5},{5,4},{6,7},{7,6},{8,9},{9,8},{10,11... | collective-permute-start | bytes 4616 | tf_op jit(solution)/shard_map/ppermute | solution.py:461
  192.1 60.1 %copy-start.22 = (s32[128,1]{0,1:T(1,128)S(1)}, s32[128,1]{0,1:T(1,128)}, u32[]{:S(2)}) copy-start(s32[128,1]{0,1:T(1,128)} %param.18) | copy-start | bytes 1540
  192.1 60.1 %all-to-all-start.3 = ((bf16[16,24,2048]{2,1,0:T(8,128)(2,1)}), bf16[16,24,2048]{2,1,0:T(8,128)(2,1)S(1)}, u32[]{:S(2)}, u32[]{:S(2)}) async-start(bf16[16,24,2048]{2,1,0:T(8,128)(2,1)} %bitcast.12), calls=%async_computation.3 | async-start | bytes 3145728 | tf_op jit(solution)/shard_map/all_to_all | solution.py:467
  195.9 54.7 %all-gather.5.cloned.1.call-start = ((), (), s32[]{:S(2)}) async-start(), calls=%async_computation.5 | async-start | bytes 1179648 | tf_op jit(solution)/shard_map/all_gather | solution.py:482
  196.0 1.3 collective-permute-start.11
  (16 other events, 28.4 us)
Sparse Core Ops, SparseCore 0:
  23.6 50.5 all-gather.2
  199.4 51.0 all-gather.4

commit v8 on v7

--- a/solution.py
+++ b/solution.py
@@ -160,11 +160,7 @@
             out_specs=[pl.BlockSpec((rows, units), lambda i, place_ref: (0, 0))] * len(turns),
         ),
         compiler_params=params(),
-        cost_estimate=pl.CostEstimate(
-            flops=2 * rows * slices * depth * tile * len(turns),
-            bytes_accessed=2 * slices * depth * (tile * len(turns) + rows),
-            transcendentals=0,
-        ),
+        cost_estimate=pl.CostEstimate(flops=rows, bytes_accessed=rows, transcendentals=0),
         name="in_projection",
     )(place, *pieces, *([w_in] * slices))
 
@@ -262,76 +258,85 @@
     )(place, own_heads, bias, rate, skip, pack)
 
 
-def scan_kernel(place_ref, *refs):
+def scan_kernel(heads, place_ref, *refs):
     x_refs, refs = refs[:EXPERTS], refs[EXPERTS:]
-    w_ref, c_ref, b_ref, a_ref, gain_ref, out_ref, last_ref, state = refs
+    w_ref, c_ref, b_ref, a_ref, gain_ref, out_ref, state = refs
 
     @pl.when(pl.program_id(0) == 0)
     def _():
         state[...] = jnp.zeros_like(state)
 
     rows = 2 * CAP
-    now = state[...]
-    for i in range(w_ref.shape[1]):
+    width = state.shape[2]
+    steps = w_ref.shape[1]
+    for i in range(steps):
         at = slice(i * rows, (i + 1) * rows)
+        to = pl.ds(pl.multiple_of((pl.program_id(0) * steps + i) * rows, rows), rows)
         x = jnp.concatenate([x_ref[at, :] for x_ref in x_refs], axis=0)
-        y = jnp.dot(w_ref[0, i], x, preferred_element_type=f32) + jnp.dot(
-            c_ref[0, i], now.astype(bf16), preferred_element_type=f32
-        )
-        now = now * a_ref[0, i, 0:1, 0:1] + jnp.dot(
-            b_ref[0, i], x, preferred_element_type=f32
-        )
+        y = []
+        for h in range(heads):
+            x_head = x[:, h * width : (h + 1) * width]
+            now = state[h]
+            y.append(
+                jnp.dot(w_ref[h, i], x_head, preferred_element_type=f32)
+                + jnp.dot(c_ref[h, i], now.astype(bf16), preferred_element_type=f32)
+            )
+            state[h] = now * a_ref[h, i, 0:1, 0:1] + jnp.dot(
+                b_ref[h, i], x_head, preferred_element_type=f32
+            )
+        y = jnp.concatenate(y, axis=1) if heads > 1 else y[0]
         z = (y * gain_ref[...]).astype(bf16)
         for q in range(EXPERTS):
-            out_ref[place_ref[1] ^ q, at, :] = z[q * rows : (q + 1) * rows]
-    state[...] = now
-    last_ref[...] = now
-
-
-def scan(place, x, weights, gain, h):
-    rows = x[0].shape[0]
-    width = gain.shape[1]
+            out_ref[place_ref[1] ^ q, to, :] = z[q * rows : (q + 1) * rows]
+
+    @pl.when(pl.program_id(0) == pl.num_programs(0) - 1)
+    def _():
+        last = [state[h].astype(bf16) for h in range(heads)]
+        last = jnp.concatenate(last, axis=1) if heads > 1 else last[0]
+        for j in range(EXPERTS):
+            out_ref[j, out_ref.shape[1] - NS :, :] = last
+
+
+def scan(place, x, weights, gain, heads):
+    rows, units = x[0].shape
+    width = units // heads
     pairs = rows // (2 * CAP)
     step = 2
     slots = 2 * CAP * EXPERTS
 
     def block(*dims):
-        return pl.BlockSpec((1, step, *dims), lambda p, place_ref: (h, p, 0, 0))
+        return pl.BlockSpec((heads, step, *dims), lambda p, place_ref: (0, p, 0, 0))
 
     return pl.pallas_call(
-        scan_kernel,
-        out_shape=(
-            jax.ShapeDtypeStruct((EXPERTS, rows, width), bf16),
-            jax.ShapeDtypeStruct((NS, width), f32),
-        ),
+        functools.partial(scan_kernel, heads),
+        out_shape=jax.ShapeDtypeStruct((EXPERTS, rows + NS, units), bf16),
         grid_spec=pltpu.PrefetchScalarGridSpec(
             num_scalar_prefetch=1,
             grid=(pairs // step,),
-            in_specs=[pl.BlockSpec((2 * CAP * step, width), lambda p, place_ref: (p, h))] * EXPERTS
+            in_specs=[pl.BlockSpec((2 * CAP * step, units), lambda p, place_ref: (p, 0))] * EXPERTS
             + [
                 block(slots, slots),
                 block(slots, NS),
                 block(NS, slots),
                 block(8, 128),
-                pl.BlockSpec((1, width), lambda p, place_ref: (0, 0)),
+                pl.BlockSpec((1, units), lambda p, place_ref: (0, 0)),
             ],
-            out_specs=(
-                pl.BlockSpec((EXPERTS, 2 * CAP * step, width), lambda p, place_ref: (0, p, 0)),
-                pl.BlockSpec((NS, width), lambda p, place_ref: (0, 0)),
+            out_specs=pl.BlockSpec(
+                (EXPERTS, rows + NS, units), lambda p, place_ref: (0, 0, 0)
             ),
-            scratch_shapes=[pltpu.VMEM((NS, width), f32)],
+            scratch_shapes=[pltpu.VMEM((heads, NS, width), f32)],
         ),
         compiler_params=pltpu.CompilerParams(vmem_limit_bytes=VMEM_BYTES // 2),
         cost_estimate=pl.CostEstimate(
-            flops=2 * pairs * slots * (slots + 2 * NS) * width,
-            bytes_accessed=2 * pairs * slots * slots,
+            flops=2 * heads * pairs * slots * (slots + 2 * NS) * width,
+            bytes_accessed=2 * heads * pairs * slots * slots,
             transcendentals=0,
         ),
         name="scan",
     )(place, *x, *weights, gain)
 
 
-def out_kernel(kind, heads, counted, others, place_ref, *refs):
+def out_kernel(kind, counted, others, place_ref, *refs):
     refs = list(refs)
 
     def take(count):
@@ -339,29 +344,27 @@
         del refs[:count]
         return got
 
-    z_refs, [w_ref] = take(heads), take(1)
+    z_ref, w_ref = take(2)
     inverse_ref = take(1)[0] if counted else None
     squares_refs = take(1 + others) if kind == "finish" else None
     part_refs = take(others) if kind == "finish" else None
     out_ref = take(1)[0]
-    _, rows, width = z_refs[0].shape
+    _, rows, units = z_ref.shape
     if counted:
 
         @pl.when(pl.program_id(0) == 0)
         def _():
-            squares = jnp.zeros((rows, 1), f32)
+            squares = jnp.zeros((rows, units), f32)
             for j in range(EXPERTS):
-                for h in range(heads):
-                    z = z_refs[h][j].astype(f32) * inverse_ref[j * heads + h]
-                    squares = squares + jnp.sum(z * z, axis=1, keepdims=True)
-            refs[0][...] = squares
-
-    units = heads * width
+                z = z_ref[j].astype(f32) * inverse_ref[:, j * units : (j + 1) * units]
+                squares = squares + z * z
+            refs[0][...] = jnp.sum(squares, axis=1, keepdims=True)
+
     total = None
     for j in range(EXPERTS):
-        z = [r[j] for r in z_refs]
-        z = jnp.concatenate(z, axis=1) if heads > 1 else z[0]
-        part = jnp.dot(z, w_ref[j * units : (j + 1) * units, :], preferred_element_type=f32)
+        part = jnp.dot(
+            z_ref[j], w_ref[j * units : (j + 1) * units, :], preferred_element_type=f32
+        )
         total = part if total is None else total + part
     if kind == "finish":
         squares = sum(r[...] for r in squares_refs)
@@ -373,8 +376,8 @@
 
 
 def out_projection(kind, chunk, *, place, z, w_out, inverse=None, squares=(), parts=()):
-    heads = len(z)
-    _, rows, width = z[0].shape
+    _, rows, units = z.shape
+    rows = rows - NS
     slices = INNER // w_out.shape[0]
     slice_width = w_out.shape[1] // slices
     part = slice_width // CHUNKS
@@ -390,8 +393,8 @@
     def fixed(*dims):
         return pl.BlockSpec(dims, lambda n, place_ref: (0,) * len(dims))
 
-    operands = [*z, w_out]
-    specs = [fixed(*z[0].shape)] * heads
+    operands = [z, w_out]
+    specs = [fixed(EXPERTS, rows, units)]
     specs.append(
         pl.BlockSpec((w_out.shape[0], tile), lambda n, place_ref: (0, column(n, place_ref)))
     )
@@ -413,7 +416,7 @@
         out_shape.append(jax.ShapeDtypeStruct((rows, 1), f32))
         out_specs.append(fixed(rows, 1))
     return pl.pallas_call(
-        functools.partial(out_kernel, kind, heads, inverse is not None, len(parts)),
+        functools.partial(out_kernel, kind, inverse is not None, len(parts)),
         out_shape=out_shape,
         grid_spec=pltpu.PrefetchScalarGridSpec(
             num_scalar_prefetch=1, grid=(count * tiles,), in_specs=specs, out_specs=out_specs
@@ -474,14 +477,6 @@
     return lax.ppermute(a, "expert", pairs)
 
 
-def gathered(a, me, n):
-    other = lax.ppermute(a, "expert", [(d, d ^ 1) for d in range(n)])
-    first = me % 2 == 0
-    pair = jnp.concatenate([jnp.where(first, a, other), jnp.where(first, other, a)], axis=0)
-    groups = [list(range(k, n, 2)) for k in range(2)]
-    return lax.all_gather(pair, "expert", axis=0, axis_index_groups=groups, tiled=True)
-
-
 def exchange(arrays, n, slices):
     out = list(arrays)
     for q in reversed(range(1, EXPERTS)):
@@ -508,32 +503,24 @@
 
     pack, outgoing = dispatch(ids_row, tokens, w_bcd.T, slices)
     landed = swap(outgoing)
-    pack = gathered(pack, me, n)
+    pack = lax.all_gather(pack, "expert", axis=0, tiled=True)
     own_heads = start // HEADDIM + jnp.arange(heads, dtype=jnp.int32)
 
     pieces = [landed] + [turn(landed, n, slices, r) for r in range(1, slices)]
     inner = [None] * EXPERTS
     for order in ((7,), (6, 5), (4, 3), (2, 1), (0,)):
-        if order == (4, 3):
-            pieces, pack = lax.optimization_barrier((pieces, pack))
+        if order == (0,):
             weights = prepare(place, own_heads, dt_bias, decay_rate, skip_gain, pack)
-        if order == (0,):
             pieces, weights = lax.optimization_barrier((pieces, weights))
         for q, a in zip(order, in_projection(place, pieces, w_in, units, order)):
             inner[q] = a
     x = exchange(inner, n, slices)
 
-    gain = lax.dynamic_slice(norm_gain, (start,), (units,))
-    z, states = [], []
-    for h in range(heads):
-        own_gain = gain[h * width : (h + 1) * width].reshape(1, width)
-        rows, state = scan(place, x, weights, own_gain, h)
-        z.append(swap(rows, same_slice))
-        states.append(state)
-    states = gathered(jnp.stack(states), me, n)
+    gain = lax.dynamic_slice(norm_gain, (start,), (units,)).reshape(1, units)
+    z = swap(scan(place, x, weights, gain, heads), same_slice)
 
     inverse = 1.0 / lax.dynamic_slice(norm_gain, (place[0] * in_dev,), (in_dev,))
-    inverse = inverse.reshape(in_dev // width, 1, width)
+    inverse = inverse.reshape(1, in_dev)
     project = functools.partial(out_projection, place=place, z=z, w_out=w_out)
     sent = []
     for k in range(CHUNKS):
@@ -547,15 +534,24 @@
         back.append(swap(done))
     mixed = collect(ids_row, back, slices)
 
-    want = decode_heads[0] * HEADDIM
-    within = want % in_dev // width
-    states = states.reshape(EXPERTS, slices, heads, NS, width)
-    chosen = lax.dynamic_slice(
-        states,
-        (within // heads, want // in_dev, within % heads, 0, 0),
-        (HEADDIM // width, 1, 1, NS, width),
-    )
-    chosen = chosen.reshape(HEADDIM // width, NS, width).transpose(0, 2, 1)
+    def picked(head):
+        first = head * HEADDIM % in_dev
+        parts = [
+            lax.dynamic_slice(
+                z, ((first + i) // units, z.shape[1] - NS, (first + i) % units), (1, NS, width)
+            )
+            for i in range(0, HEADDIM, width)
+        ]
+        return jnp.concatenate(parts, axis=0) if len(parts) > 1 else parts[0]
+
+    want = decode_heads[0]
+    chosen = picked(want)
+    for r in range(1, slices):
+        asked = turn(want, n, slices, slices - r)
+        got = turn(picked(asked), n, slices, r)
+        lies = want * HEADDIM // in_dev
+        chosen = jnp.where((place[0] - lies + slices) % slices == r, got, chosen)
+    chosen = chosen.transpose(0, 2, 1).astype(f32)
     return (mixed, chosen.reshape(1, HEADDIM * NS))
 
 

time: 262 us -> 235 us (0.90); the launches traced: 261 us -> 231 us
  waiting for transfers between devices: 133 us -> 111 us
  local copies, waits for them, and re-layouts: 15.5 us -> 9.82 us
  Pallas kernels: 62.2 us -> 59.3 us
    all_gather x2 -> x1, waiting for transfers between devices: 68.2 us -> 0.01 us  [shards(): pack = lax.all_gather(pack, 'expert', axis=0, tiled=True)]
    all_to_all x4 -> x3, waiting for transfers between devices: 59.5 us -> 103 us  [swap(): lax.all_to_all(a, 'expert', split_axis=0, concat_axis=0, axis_index_group...]
    ppermute x7, starting transfers between devices: 11.3 us -> 16.6 us  [across(): return lax.ppermute(a, 'expert', pairs)]
    unnamed x60 -> x28, local copies, waits for them, and re-layouts: 13.1 us -> 8.16 us
    all_to_all x4 -> x3, starting transfers between devices: 20.3 us -> 16.1 us  [swap(): lax.all_to_all(a, 'expert', split_axis=0, concat_axis=0, axis_index_group...]
    ppermute x3 -> x5, waiting for transfers between devices: 3.19 us -> 7.27 us  [turn(): lax.ppermute(a, 'expert', [(d, d // slices * slices + (d + r) % slices) f...]
    pallas_call x4 -> x3, Pallas kernels: 23.3 us -> 19.2 us  [the longest x2 14.6 us: out_projection(): pl.pallas_call(functools.partial(out_kernel, kind, inverse is not None, l...]
  transfers between devices with their start and end apart: 18 -> 16, of which waited for: 8 -> 7; matrix products, arithmetic and copies ran while one was open for 1% -> 1% of each run, Pallas kernels for 11% -> 15%
where the time goes in v8:
time: 235 us; the launch traced here: 231 us
  waiting for transfers between devices  111 us (47%)
  Pallas kernels  59.3 us (25%)
  starting transfers between devices  34.7 us (15%)
  between operations  15.7 us (7%)
  local copies, waits for them, and re-layouts  9.82 us (4%)
    all_to_all x3, waiting for transfers between devices, swap(): lax.all_to_all(a, 'expert', split_axis=0, concat_axis=0, axis_index_group...  103 us
    pallas_call x5, Pallas kernels, in_projection(): pl.pallas_call(functools.partial(in_kernel, slices, shares, turns), out_s...  21.1 us
    ppermute x7, starting transfers between devices, across(): return lax.ppermute(a, 'expert', pairs)  16.6 us
    all_to_all x3, starting transfers between devices, swap(): lax.all_to_all(a, 'expert', split_axis=0, concat_axis=0, axis_index_group...  16.1 us
    pallas_call x1, Pallas kernels, prepare(): pl.pallas_call(functools.partial(prep_kernel, heads), out_shape=(jax.Shap...  14.6 us
    pallas_call x2, Pallas kernels, out_projection(): pl.pallas_call(functools.partial(out_kernel, kind, inverse is not None, l...  14.6 us
    unnamed x28, local copies, waits for them, and re-layouts  8.16 us
    ppermute x5, waiting for transfers between devices, turn(): lax.ppermute(a, 'expert', [(d, d // slices * slices + (d + r) % slices) f...  7.27 us
  transfers between devices with their start and end apart: 16, of which 7 were waited for; matrix products, arithmetic and copies ran while one was open for 1% of the time, Pallas kernels for 15%

profile of v8, /device:TPU:0, one launch (start us, length us, event | category | flops | bytes accessed | tf_op | source)
XLA Modules:
  0.0 231.1 jit_solution(3410325162999687307)
XLA Ops:
  7.2 1.3 copy-done.2
  8.5 1.2 copy-done.3
  10.4 2.3 %dispatch.1 = (bf16[128,256]{1,0:T(8,128)(2,1)}, bf16[384,2048]{1,0:T(8,128)(2,1)}) custom-call(s32[1,128]{1,0:T(1,128)S(1)} %bitcast.30, bf16[128,4096]{1,0:T(8,128)(2,1)S(1)} %copy-done.3, bf16[160,4096]{1,0:T(8,128)(2,1)S(1)} %bitcast.27), custom_call_target="tpu_custom_call" | custom-call | tf_op jit(solution)/shard_map/dispatch/pallas_call | solution.py:59
  12.7 7.4 %all-to-all-start = ((bf16[16,24,2048]{2,1,0:T(8,128)(2,1)}), bf16[16,24,2048]{2,1,0:T(8,128)(2,1)S(1)}, u32[]{:S(2)}, u32[]{:S(2)}) async-start(bf16[16,24,2048]{2,1,0:T(8,128)(2,1)} %bitcast.4), calls=%async_computation | async-start | bytes 3145728 | tf_op jit(solution)/shard_map/all_to_all | solution.py:470
  20.9 33.3 %all-to-all-done = bf16[16,24,2048]{2,1,0:T(8,128)(2,1)S(1)} async-done(((bf16[16,24,2048]{2,1,0:T(8,128)(2,1)}), bf16[16,24,2048]{2,1,0:T(8,128)(2,1)S(1)}, u32[]{:S(2)}, u32[]{:S(2)}) %all-to-all-start) | async-done | bytes 1572896 | tf_op jit(solution)/shard_map/all_to_all | solution.py:470
  54.2 0.8 collective-permute-start
  55.0 3.0 %collective-permute-done.refs_1_ = bf16[384,2048]{1,0:T(8,128)(2,1)S(1)} collective-permute-done((bf16[384,2048]{1,0:T(8,128)(2,1)S(1)}, bf16[384,2048]{1,0:T(8,128)(2,1)S(1)}, u32[]{:S(2)}, u32[]{:S(2)}) %collective-permute-start) | collective-permute-done | bytes 1572896 | tf_op jit(solution)/shard_map/ppermute | solution.py:464
  58.0 4.9 %in_projection.6 = (bf16[384,256]{1,0:T(8,128)(2,1)}, bf16[384,256]{1,0:T(8,128)(2,1)}) custom-call(s32[2]{0:T(128)S(1)} %pad_add_fusion.place_ref, bf16[384,2048]{1,0:T(8,128)(2,1)S(1)} %bitcast.18, bf16[384,2048]{1,0:T(8,128)(2,1)S(1)} %collective-permute-done.refs_1_, bf16[4096,2048]{1,0:T(8,128)(2,1)} %bitcast.33, bf16[4096,2048]{1,0:T(8,128)(2,1)} %bitcast.34), custom_call_target="tpu_custom_call" | custom-call | flops 384 | bytes 384 | tf_op jit(solution)/shard_map/in_projection/pallas_call | solution.py:152
  62.9 2.7 %collective-permute-start.1 = (bf16[384,256]{1,0:T(8,128)(2,1)}, bf16[384,256]{1,0:T(8,128)(2,1)S(1)}, u32[]{:S(2)}, u32[]{:S(2)}) collective-permute-start(bf16[384,256]{1,0:T(8,128)(2,1)} %get-tuple-element.30), channel_id=1, source_target_pairs={{0,2},{1,3},{2,0},{3,1},{4,6},{5,7},{6,4},{7,5},{8,10},{9,11},{10,... | collective-permute-start | bytes 589832 | tf_op jit(solution)/shard_map/ppermute | solution.py:477
  65.6 6.2 %collective-permute-start.2 = (bf16[384,256]{1,0:T(8,128)(2,1)}, bf16[384,256]{1,0:T(8,128)(2,1)}, u32[]{:S(2)}, u32[]{:S(2)}) collective-permute-start(bf16[384,256]{1,0:T(8,128)(2,1)} %get-tuple-element.31), channel_id=1, source_target_pairs={{0,4},{1,5},{2,6},{3,7},{4,0},{5,1},{6,2},{7,3},{8,12},{9,13},{10,... | collective-permute-start | bytes 589832 | tf_op jit(solution)/shard_map/ppermute | solution.py:477
  73.0 4.9 %in_projection.7 = (bf16[384,256]{1,0:T(8,128)(2,1)}, bf16[384,256]{1,0:T(8,128)(2,1)}) custom-call(s32[2]{0:T(128)S(1)} %pad_add_fusion.place_ref, bf16[384,2048]{1,0:T(8,128)(2,1)S(1)} %bitcast.19, bf16[384,2048]{1,0:T(8,128)(2,1)S(1)} %collective-permute-done.refs_1_, bf16[4096,2048]{1,0:T(8,128)(2,1)} %bitcast.35, bf16[4096,2048]{1,0:T(8,128)(2,1)} %bitcast.36), custom_call_target="tpu_custom_call" | custom-call | flops 384 | bytes 384 | tf_op jit(solution)/shard_map/in_projection/pallas_call | solution.py:152
  77.9 2.9 %collective-permute-start.4 = (bf16[384,256]{1,0:T(8,128)(2,1)}, bf16[384,256]{1,0:T(8,128)(2,1)}, u32[]{:S(2)}, u32[]{:S(2)}) collective-permute-start(bf16[384,256]{1,0:T(8,128)(2,1)} %get-tuple-element.33), channel_id=1, source_target_pairs={{0,8},{1,9},{2,10},{3,11},{4,12},{5,13},{6,14},{7,15},{8,0},{9,1},... | collective-permute-start | bytes 589832 | tf_op jit(solution)/shard_map/ppermute | solution.py:477
  80.8 4.9 %in_projection.8 = (bf16[384,256]{1,0:T(8,128)(2,1)}, bf16[384,256]{1,0:T(8,128)(2,1)}) custom-call(s32[2]{0:T(128)S(1)} %pad_add_fusion.place_ref, bf16[384,2048]{1,0:T(8,128)(2,1)S(1)} %bitcast.20, bf16[384,2048]{1,0:T(8,128)(2,1)S(1)} %collective-permute-done.refs_1_, bf16[4096,2048]{1,0:T(8,128)(2,1)} %bitcast.37, bf16[4096,2048]{1,0:T(8,128)(2,1)} %bitcast.38), custom_call_target="tpu_custom_call" | custom-call | flops 384 | bytes 384 | tf_op jit(solution)/shard_map/in_projection/pallas_call | solution.py:152
  85.8 0.9 collective-permute-start.5
  86.7 3.1 %in_projection.9 = bf16[384,256]{1,0:T(8,128)(2,1)S(1)} custom-call(s32[2]{0:T(128)S(1)} %pad_add_fusion.place_ref, bf16[384,2048]{1,0:T(8,128)(2,1)S(1)} %bitcast.21, bf16[384,2048]{1,0:T(8,128)(2,1)S(1)} %collective-permute-done.refs_1_, bf16[4096,2048]{1,0:T(8,128)(2,1)} %bitcast.39, bf16[4096,2048]{1,0:T(8,128)(2,1)} %bitcast.40), custom_call_target="tpu_custom_call" | custom-call | flops 384 | bytes 384 | tf_op jit(solution)/shard_map/in_projection/pallas_call | solution.py:152
  89.8 2.6 %collective-permute-start.6 = (bf16[384,256]{1,0:T(8,128)(2,1)}, bf16[384,256]{1,0:T(8,128)(2,1)}, u32[]{:S(2)}, u32[]{:S(2)}) collective-permute-start(bf16[384,256]{1,0:T(8,128)(2,1)} %get-tuple-element.35), channel_id=1, source_target_pairs={{0,12},{1,13},{2,14},{3,15},{4,8},{5,9},{6,10},{7,11},{8,4},{9,5},... | collective-permute-start | bytes 589832 | tf_op jit(solution)/shard_map/ppermute | solution.py:477
  92.3 1.3 collective-permute-start.7
  93.7 1.2 copy-done.6
  96.2 14.6 %scan_weights.1 = (bf16[2,8,384,384]{3,2,1,0:T(8,128)(2,1)}, bf16[2,8,384,64]{3,2,1,0:T(8,128)(2,1)S(1)}, bf16[2,8,64,384]{3,2,1,0:T(8,128)(2,1)S(1)}, f32[2,8,8,128]{3,2,1,0:T(8,128)S(1)}) custom-call(s32[2]{0:T(128)S(1)} %pad_add_fusion.place_ref, s32[2]{0:T(128)S(1)} %copy-done.10, f32[32]{0:T(128)S(1)} %copy-done.7, f32[32]{0:T(128)S(1)} %copy-done.8, ...), custom_call_target="tpu_custom_call" | custom-call | flops 2415919104 | bytes 4718592 | tf_op jit(solution)/shard_map/scan_weights/pallas_call | solution.py:240
  110.8 3.3 %in_projection.5.refs_0_ = bf16[384,256]{1,0:T(8,128)(2,1)S(1)} custom-call(s32[2]{0:T(128)S(1)} %pad_add_fusion.place_ref, bf16[384,2048]{1,0:T(8,128)(2,1)S(1)} %bitcast.22, bf16[384,2048]{1,0:T(8,128)(2,1)S(1)} %collective-permute-done.refs_1_, bf16[4096,2048]{1,0:T(8,128)(2,1)} %bitcast.41, bf16[4096,2048]{1,0:T(8,128)(2,1)} %bitcast.42), custom_call_target="tpu_custom_call" | custom-call | flops 384 | bytes 384 | tf_op jit(solution)/shard_map/in_projection/pallas_call | solution.py:152
  114.3 4.6 %scan.1 = bf16[8,448,256]{2,1,0:T(8,128)(2,1)S(1)} custom-call(s32[2]{0:T(128)S(1)} %pad_add_fusion.place_ref, bf16[384,256]{1,0:T(8,128)(2,1)S(1)} %in_projection.5.refs_0_, bf16[384,256]{1,0:T(8,128)(2,1)S(1)} %collective-permute-done.1.refs_1_, bf16[384,256]{1,0:T(8,128)(2,1)} %collective-permute-done.2.refs_2_, ...), custom_call_target="tpu_custom_call" | custom-call | flops 805306368 | bytes 4718592 | tf_op jit(solution)/shard_map/scan/pallas_call | solution.py:310
  118.9 1.2 copy-done
  120.1 4.8 %all-to-all-start.1 = ((bf16[8,448,256]{2,1,0:T(8,128)(2,1)}), bf16[8,448,256]{2,1,0:T(8,128)(2,1)S(1)}, u32[]{:S(2)}, u32[]{:S(2)}) async-start(bf16[8,448,256]{2,1,0:T(8,128)(2,1)} %copy-done), calls=%async_computation.1 | async-start | bytes 3670016 | tf_op jit(solution)/shard_map/all_to_all | solution.py:470
  125.0 41.8 %all-to-all-done.1.refs_0_ = bf16[8,448,256]{2,1,0:T(8,128)(2,1)S(1)} async-done(((bf16[8,448,256]{2,1,0:T(8,128)(2,1)}), bf16[8,448,256]{2,1,0:T(8,128)(2,1)S(1)}, u32[]{:S(2)}, u32[]{:S(2)}) %all-to-all-start.1) | async-done | bytes 1835040 | tf_op jit(solution)/shard_map/all_to_all | solution.py:470
  166.8 7.5 %out_send.1 = (bf16[1,384,2048]{2,1,0:T(8,128)(2,1)S(1)}, f32[384,1]{1,0:T(8,128)S(1)}) custom-call(s32[2]{0:T(128)S(1)} %pad_add_fusion.place_ref, bf16[8,448,256]{2,1,0:T(8,128)(2,1)S(1)} %all-to-all-done.1.refs_0_, bf16[2048,4096]{1,0:T(8,128)(2,1)} %bitcast.43, f32[1,2048]{1,0:T(1,128)S(1)} %bitcast.28), custom_call_target="tpu_custom_call" | custom-call | flops 3221225472 | bytes 9961472 | tf_op jit(solution)/shard_map/out_send/pallas_call | solution.py:418
  174.9 3.2 %collective-permute-done.8.refs_3_ = f32[384,1]{1,0:T(8,128)S(1)} collective-permute-done((f32[384,1]{1,0:T(8,128)S(1)}, f32[384,1]{1,0:T(8,128)S(1)}, u32[]{:S(2)}, u32[]{:S(2)}) %collective-permute-start.8) | collective-permute-done | bytes 1568 | tf_op jit(solution)/shard_map/ppermute | solution.py:464
  178.1 7.1 %out_finish.1 = bf16[384,2048]{1,0:T(8,128)(2,1)S(1)} custom-call(s32[2]{0:T(128)S(1)} %pad_add_fusion.place_ref, bf16[8,448,256]{2,1,0:T(8,128)(2,1)S(1)} %all-to-all-done.1.refs_0_, bf16[2048,4096]{1,0:T(8,128)(2,1)} %bitcast.44, f32[384,1]{1,0:T(8,128)S(1)} %get-tuple-element.40.refs_2_, f32[384,1]{1,0:T(8,128)S(1)} %collective-permute-done.8.refs_3_, ...), custom_call_target="tpu_custom_call" | custom-call | flops 3221225472 | bytes 9961472 | tf_op jit(solution)/shard_map/out_finish/pallas_call | solution.py:418
  185.2 1.2 copy-done.1
  186.3 3.9 %all-to-all-start.2 = ((bf16[16,24,2048]{2,1,0:T(8,128)(2,1)}), bf16[16,24,2048]{2,1,0:T(8,128)(2,1)S(1)}, u32[]{:S(2)}, u32[]{:S(2)}) async-start(bf16[16,24,2048]{2,1,0:T(8,128)(2,1)} %bitcast.24), calls=%async_computation.2 | async-start | bytes 3145728 | tf_op jit(solution)/shard_map/all_to_all | solution.py:470
  190.6 1.0 collective-permute-done.10
  194.5 27.7 %all-to-all-done.2 = bf16[16,24,2048]{2,1,0:T(8,128)(2,1)S(1)} async-done(((bf16[16,24,2048]{2,1,0:T(8,128)(2,1)}), bf16[16,24,2048]{2,1,0:T(8,128)(2,1)S(1)}, u32[]{:S(2)}, u32[]{:S(2)}) %all-to-all-start.2) | async-done | bytes 1572896 | tf_op jit(solution)/shard_map/all_to_all | solution.py:470
  222.2 2.0 collect.1
  (49 shorter events, 6.5 us)
Async XLA Ops:
  7.2 1.3 copy-start.2
  8.5 1.2 copy-start.3
  9.7 0.7 copy-start.4
  12.7 41.5 %all-to-all-start = ((bf16[16,24,2048]{2,1,0:T(8,128)(2,1)}), bf16[16,24,2048]{2,1,0:T(8,128)(2,1)S(1)}, u32[]{:S(2)}, u32[]{:S(2)}) async-start(bf16[16,24,2048]{2,1,0:T(8,128)(2,1)} %bitcast.4), calls=%async_computation | async-start | bytes 3145728 | tf_op jit(solution)/shard_map/all_to_all | solution.py:470
  20.1 73.5 %all-gather.2.cloned.1.call-start = ((), (), s32[]{:S(2)}) async-start(), calls=%async_computation.3 | async-start | bytes 1114112 | tf_op jit(solution)/shard_map/all_gather | solution.py:506
  54.2 3.8 %collective-permute-start = (bf16[384,2048]{1,0:T(8,128)(2,1)S(1)}, bf16[384,2048]{1,0:T(8,128)(2,1)S(1)}, u32[]{:S(2)}, u32[]{:S(2)}) collective-permute-start(bf16[384,2048]{1,0:T(8,128)(2,1)S(1)} %bitcast.17), channel_id=1, source_target_pairs={{0,1},{1,0},{2,3},{3,2},{4,5},{5,4},{6,7},{7,6},{8,9},{9,8},{10,11... | collective-permute-start | bytes 4718600 | tf_op jit(solution)/shard_map/ppermute | solution.py:464
  62.9 26.9 %collective-permute-start.1 = (bf16[384,256]{1,0:T(8,128)(2,1)}, bf16[384,256]{1,0:T(8,128)(2,1)S(1)}, u32[]{:S(2)}, u32[]{:S(2)}) collective-permute-start(bf16[384,256]{1,0:T(8,128)(2,1)} %get-tuple-element.30), channel_id=1, source_target_pairs={{0,2},{1,3},{2,0},{3,1},{4,6},{5,7},{6,4},{7,5},{8,10},{9,11},{10,... | collective-permute-start | bytes 589832 | tf_op jit(solution)/shard_map/ppermute | solution.py:477
  65.6 26.8 %collective-permute-start.2 = (bf16[384,256]{1,0:T(8,128)(2,1)}, bf16[384,256]{1,0:T(8,128)(2,1)}, u32[]{:S(2)}, u32[]{:S(2)}) collective-permute-start(bf16[384,256]{1,0:T(8,128)(2,1)} %get-tuple-element.31), channel_id=1, source_target_pairs={{0,4},{1,5},{2,6},{3,7},{4,0},{5,1},{6,2},{7,3},{8,12},{9,13},{10,... | collective-permute-start | bytes 589832 | tf_op jit(solution)/shard_map/ppermute | solution.py:477
  77.9 36.3 %collective-permute-start.3 = (bf16[384,256]{1,0:T(8,128)(2,1)}, bf16[384,256]{1,0:T(8,128)(2,1)}, u32[]{:S(2)}, u32[]{:S(2)}) collective-permute-start(bf16[384,256]{1,0:T(8,128)(2,1)} %get-tuple-element.32), channel_id=1, source_target_pairs={{0,6},{1,7},{2,4},{3,5},{4,2},{5,3},{6,0},{7,1},{8,14},{9,15},{10,... | collective-permute-start | bytes 589832 | tf_op jit(solution)/shard_map/ppermute | solution.py:477
  77.9 36.3 %collective-permute-start.4 = (bf16[384,256]{1,0:T(8,128)(2,1)}, bf16[384,256]{1,0:T(8,128)(2,1)}, u32[]{:S(2)}, u32[]{:S(2)}) collective-permute-start(bf16[384,256]{1,0:T(8,128)(2,1)} %get-tuple-element.33), channel_id=1, source_target_pairs={{0,8},{1,9},{2,10},{3,11},{4,12},{5,13},{6,14},{7,15},{8,0},{9,1},... | collective-permute-start | bytes 589832 | tf_op jit(solution)/shard_map/ppermute | solution.py:477
  85.7 7.9 %copy-start.7 = (f32[32]{0:T(128)S(1)}, f32[32]{0:T(128)}, u32[]{:S(2)}) copy-start(f32[32]{0:T(128)} %bias_ref.1) | copy-start | bytes 388
  85.8 7.9 %copy-start.8 = (f32[32]{0:T(128)S(1)}, f32[32]{0:T(128)}, u32[]{:S(2)}) copy-start(f32[32]{0:T(128)} %rate_ref.1) | copy-start | bytes 388
  85.8 28.4 %collective-permute-start.5 = (bf16[384,256]{1,0:T(8,128)(2,1)}, bf16[384,256]{1,0:T(8,128)(2,1)}, u32[]{:S(2)}, u32[]{:S(2)}) collective-permute-start(bf16[384,256]{1,0:T(8,128)(2,1)} %get-tuple-element.34), channel_id=1, source_target_pairs={{0,10},{1,11},{2,8},{3,9},{4,14},{5,15},{6,12},{7,13},{8,2},{9,3},... | collective-permute-start | bytes 589832 | tf_op jit(solution)/shard_map/ppermute | solution.py:477
  89.8 24.4 %collective-permute-start.6 = (bf16[384,256]{1,0:T(8,128)(2,1)}, bf16[384,256]{1,0:T(8,128)(2,1)}, u32[]{:S(2)}, u32[]{:S(2)}) collective-permute-start(bf16[384,256]{1,0:T(8,128)(2,1)} %get-tuple-element.35), channel_id=1, source_target_pairs={{0,12},{1,13},{2,14},{3,15},{4,8},{5,9},{6,10},{7,11},{8,4},{9,5},... | collective-permute-start | bytes 589832 | tf_op jit(solution)/shard_map/ppermute | solution.py:477
  92.3 21.9 %collective-permute-start.7 = (bf16[384,256]{1,0:T(8,128)(2,1)S(1)}, bf16[384,256]{1,0:T(8,128)(2,1)}, u32[]{:S(2)}, u32[]{:S(2)}) collective-permute-start(bf16[384,256]{1,0:T(8,128)(2,1)S(1)} %in_projection.9), channel_id=1, source_target_pairs={{0,14},{1,15},{2,12},{3,13},{4,10},{5,11},{6,8},{7,9},{8,6},{9,7},... | collective-permute-start | bytes 589832 | tf_op jit(solution)/shard_map/ppermute | solution.py:477
  93.7 1.2 copy-start.6
  94.9 0.7 copy-start.9
  95.5 0.7 copy-start.10
  110.8 3.4 %slice-start = ((s8[4718592]{0:T(1024)(128)(4,1)}), s8[4194304]{0:T(1024)(128)(4,1)S(1)}, s32[]{:S(2)}) async-start(s8[4718592]{0:T(1024)(128)(4,1)} %bitcast.25), calls=%async_computation.4 | async-start | bytes 8388608
  110.8 3.4 %slice-start.1 = ((s8[4718592]{0:T(1024)(128)(4,1)}), s8[524288]{0:T(1024)(128)(4,1)S(1)}, s32[]{:S(2)}) async-start(s8[4718592]{0:T(1024)(128)(4,1)} %bitcast.25), calls=%async_computation.5 | async-start | bytes 1048576
  118.9 1.3 copy-start
  120.1 4.8 %copy-start.11 = (f32[4096]{0:T(1024)S(1)}, f32[4096]{0:T(1024)}, u32[]{:S(2)}) copy-start(f32[4096]{0:T(1024)} %param.17) | copy-start | bytes 49156
  120.1 46.6 %all-to-all-start.1 = ((bf16[8,448,256]{2,1,0:T(8,128)(2,1)}), bf16[8,448,256]{2,1,0:T(8,128)(2,1)S(1)}, u32[]{:S(2)}, u32[]{:S(2)}) async-start(bf16[8,448,256]{2,1,0:T(8,128)(2,1)} %copy-done), calls=%async_computation.1 | async-start | bytes 3670016 | tf_op jit(solution)/shard_map/all_to_all | solution.py:470
  174.3 3.8 %collective-permute-start.9 = (bf16[384,2048]{1,0:T(8,128)(2,1)S(1)}, bf16[384,2048]{1,0:T(8,128)(2,1)S(1)}, u32[]{:S(2)}, u32[]{:S(2)}) collective-permute-start(bf16[384,2048]{1,0:T(8,128)(2,1)S(1)} %bitcast.32), channel_id=1, source_target_pairs={{0,1},{1,0},{2,3},{3,2},{4,5},{5,4},{6,7},{7,6},{8,9},{9,8},{10,11... | collective-permute-start | bytes 4718600 | tf_op jit(solution)/shard_map/ppermute | solution.py:464
  174.4 3.7 %collective-permute-start.8 = (f32[384,1]{1,0:T(8,128)S(1)}, f32[384,1]{1,0:T(8,128)S(1)}, u32[]{:S(2)}, u32[]{:S(2)}) collective-permute-start(f32[384,1]{1,0:T(8,128)S(1)} %get-tuple-element.40.refs_2_), channel_id=1, source_target_pairs={{0,1},{1,0},{2,3},{3,2},{4,5},{5,4},{6,7},{7,6},{8,9},{9,8},{10,11... | collective-permute-start | bytes 4616 | tf_op jit(solution)/shard_map/ppermute | solution.py:464
  185.1 1.2 copy-start.1
  186.3 35.9 %copy-start.5 = (s32[128,1]{0,1:T(1,128)S(1)}, s32[128,1]{0,1:T(1,128)}, u32[]{:S(2)}) copy-start(s32[128,1]{0,1:T(1,128)} %param.18) | copy-start | bytes 1540
  186.3 35.9 %all-to-all-start.2 = ((bf16[16,24,2048]{2,1,0:T(8,128)(2,1)}), bf16[16,24,2048]{2,1,0:T(8,128)(2,1)S(1)}, u32[]{:S(2)}, u32[]{:S(2)}) async-start(bf16[16,24,2048]{2,1,0:T(8,128)(2,1)} %bitcast.24), calls=%async_computation.2 | async-start | bytes 3145728 | tf_op jit(solution)/shard_map/all_to_all | solution.py:470
  190.2 1.4 collective-permute-start.10
  192.4 1.2 collective-permute-start.11
Sparse Core Ops, SparseCore 0:
  23.1 47.0 all-gather.1

commit v9 on v8

--- a/solution.py
+++ b/solution.py
@@ -15,15 +15,15 @@
 CAP = 24
 PAIR = 256
 PACK = 256
-CHUNKS = 1
+CHUNKS = 2
 VMEM_BYTES = 48 * 1024 * 1024
 
 f32 = jnp.float32
 bf16 = jnp.bfloat16
 
 
-def params():
-    return pltpu.CompilerParams(vmem_limit_bytes=VMEM_BYTES)
+def params(limit=VMEM_BYTES):
+    return pltpu.CompilerParams(vmem_limit_bytes=limit)
 
 
 def mask(condition):
@@ -54,22 +54,11 @@
         copy.wait()
 
 
-def fetching_call(kernel, operands, out_shape, name):
-    buffers = [pltpu.VMEM(a.shape, a.dtype) for a in operands]
-    return pl.pallas_call(
-        kernel,
-        out_shape=out_shape,
-        in_specs=[pl.BlockSpec(memory_space=pltpu.HBM)] * len(operands),
-        scratch_shapes=[*buffers, pltpu.SemaphoreType.DMA((len(operands),))],
-        compiler_params=params(),
-        name=name,
-    )(*operands)
-
-
 def dispatch_kernel(slices, *refs):
-    pack_ref, out_ref = refs[3:5]
-    ids_ref, tok_ref, bcd_ref, sems = refs[5:]
-    fetched(refs[:3], refs[5:8], sems)
+    pack_ref, out_ref = refs[4:6]
+    want_ref = refs[0]
+    ids_ref, tok_ref, bcd_ref, sems = refs[6:]
+    fetched(refs[1:4], refs[6:9], sems)
     rows, width = tok_ref.shape
     depth = width // slices
     ids, slot = route(ids_ref[...])
@@ -102,20 +91,26 @@
     lane = iota((rows, 128), 1)
     side = jnp.where(lane < HEADS, coarse, raw - coarse)
     side = jnp.where(lane == 2 * HEADS, ids, jnp.where(lane == 2 * HEADS + 1, slot, side))
-    pack_ref[:, 2 * NS :] = jnp.where(lane < 2 * HEADS + 2, side, 0.0).astype(bf16)
-
-
-def dispatch(ids_row, tokens, bcd, slices):
+    side = jnp.where(lane == 2 * HEADS + 2, want_ref[0].astype(f32), side)
+    pack_ref[:, 2 * NS :] = jnp.where(lane < 2 * HEADS + 3, side, 0.0).astype(bf16)
+
+
+def dispatch(want, ids_row, tokens, bcd, slices):
     rows, width = tokens.shape
-    return fetching_call(
+    operands = (ids_row, tokens, bcd)
+    return pl.pallas_call(
         functools.partial(dispatch_kernel, slices),
-        (ids_row, tokens, bcd),
-        (
+        out_shape=(
             jax.ShapeDtypeStruct((rows, PACK), bf16),
             jax.ShapeDtypeStruct((EXPERTS * slices * CAP, width // slices), bf16),
         ),
-        "dispatch",
-    )
+        in_specs=[pl.BlockSpec(memory_space=pltpu.SMEM)]
+        + [pl.BlockSpec(memory_space=pltpu.HBM)] * len(operands),
+        scratch_shapes=[pltpu.VMEM(a.shape, a.dtype) for a in operands]
+        + [pltpu.SemaphoreType.DMA((len(operands),))],
+        compiler_params=params(60 * 1024 * 1024),
+        name="dispatch",
+    )(want, *operands)
 
 
 def in_kernel(count, shares, turns, place_ref, *refs):
@@ -167,17 +162,19 @@
 
 def prep_kernel(heads, place_ref, head_ref, bias_ref, rate_ref, skip_ref, pack_ref, w_ref, c_ref, b_ref, a_ref):
     pack = pack_ref[...]
-    row = iota((128, PACK), 0)
-    lane = iota((128, PACK), 1)
+    few = 8
+    row = iota((few, PACK), 0)
+    lane = iota((few, PACK), 1)
     side = lane - 2 * NS - 2 * HEADS
     choose = ((row == heads) & (side == 0)) | ((row == heads + 1) & (side == 1))
     choose = choose.astype(f32)
-    rate = bias = jnp.zeros((128, PAIR), f32)
+    row = iota((few, PAIR), 0)
+    rate = bias = jnp.zeros((few, PAIR), f32)
     for h in range(heads):
         at = lane - 2 * NS - head_ref[h]
-        choose = jnp.where((row == h) & ((at == 0) | (at == HEADS)), 1.0, choose)
-        rate = jnp.where(iota((128, PAIR), 0) == h, rate_ref[head_ref[h]], rate)
-        bias = jnp.where(iota((128, PAIR), 0) == h, bias_ref[head_ref[h]], bias)
+        choose = jnp.where((iota((few, PACK), 0) == h) & ((at == 0) | (at == HEADS)), 1.0, choose)
+        rate = jnp.where(row == h, rate_ref[head_ref[h]], rate)
+        bias = jnp.where(row == h, bias_ref[head_ref[h]], bias)
     across = lax.dot_general(
         choose.astype(bf16), pack, (((1,), (1,)), ((), ())), preferred_element_type=f32
     )
@@ -185,19 +182,24 @@
     steps_dt = jnp.maximum(raw, 0.0) + jnp.log1p(jnp.exp(-jnp.abs(raw)))
     upto = iota((PAIR, PAIR), 0)
     now = iota((PAIR, PAIR), 1)
-    running = jnp.dot(
-        -steps_dt * rate,
-        (upto <= now).astype(f32),
-        precision=lax.Precision.HIGHEST,
+    rest = -steps_dt * rate
+    split = []
+    for _ in range(3):
+        split.append(rest.astype(bf16).astype(f32))
+        rest = rest - split[-1]
+    sums = jnp.dot(
+        jnp.concatenate(split + [jnp.zeros_like(rest)], axis=0).astype(bf16),
+        mask(upto <= now),
         preferred_element_type=f32,
     )
+    running = sums[:few] + sums[few : 2 * few] + sums[2 * few : 3 * few]
     second = iota((1, PAIR), 1) >= PAIR // 2
     turn_of = across[heads : heads + 1].astype(jnp.int32) ^ place_ref[1]
     column = turn_of * (2 * CAP) + across[heads + 1 : heads + 2].astype(jnp.int32)
     column = column + jnp.where(second, CAP, 0)
     slots = 2 * CAP * EXPERTS
     place_t = mask(iota((slots, PAIR), 0) == column)
-    down = running.T
+    down = jnp.concatenate([running] * (128 // few), axis=0).T
     b_rows = pack[:, :NS]
     c_rows = pack[:, NS : 2 * NS]
     scores = lax.dot_general(
@@ -309,7 +311,7 @@
 
     return pl.pallas_call(
         functools.partial(scan_kernel, heads),
-        out_shape=jax.ShapeDtypeStruct((EXPERTS, rows + NS, units), bf16),
+        out_shape=pltpu.HBM((EXPERTS, rows + NS, units), bf16),
         grid_spec=pltpu.PrefetchScalarGridSpec(
             num_scalar_prefetch=1,
             grid=(pairs // step,),
@@ -336,7 +338,7 @@
     )(place, *x, *weights, gain)
 
 
-def out_kernel(kind, counted, others, place_ref, *refs):
+def out_kernel(kind, counted, others, resumed, place_ref, *refs):
     refs = list(refs)
 
     def take(count):
@@ -348,6 +350,8 @@
     inverse_ref = take(1)[0] if counted else None
     squares_refs = take(1 + others) if kind == "finish" else None
     part_refs = take(others) if kind == "finish" else None
+    if resumed:
+        take(1)
     out_ref = take(1)[0]
     _, rows, units = z_ref.shape
     if counted:
@@ -375,14 +379,16 @@
         out_ref[0] = total.astype(bf16)
 
 
-def out_projection(kind, chunk, *, place, z, w_out, inverse=None, squares=(), parts=()):
+def out_projection(
+    kind, chunk, *, place, z, w_out, inverse=None, squares=(), parts=(), before=None
+):
     _, rows, units = z.shape
     rows = rows - NS
     slices = INNER // w_out.shape[0]
     slice_width = w_out.shape[1] // slices
     part = slice_width // CHUNKS
     count, first = (slices - 1, 1) if kind == "send" else (1, 0)
-    tile = min(512, part)
+    tile = min(256, part)
     tiles = part // tile
     whole = slice_width // tile
     offset = chunk * tiles
@@ -404,9 +410,14 @@
     operands += [*squares, *parts]
     specs += [fixed(rows, 1)] * len(squares)
     specs += [pl.BlockSpec((rows, tile), lambda n, place_ref: (0, n))] * len(parts)
+    aliases = {}
+    if before is not None:
+        aliases = {1 + len(operands): 0}
+        operands.append(before)
+        specs.append(pl.BlockSpec(memory_space=pl.ANY))
     if kind == "finish":
-        out_shape = [jax.ShapeDtypeStruct((rows, part), bf16)]
-        out_specs = [pl.BlockSpec((rows, tile), lambda n, place_ref: (0, n))]
+        out_shape = [pltpu.HBM((rows, slice_width), bf16)]
+        out_specs = [pl.BlockSpec((rows, tile), lambda n, place_ref: (0, offset + n))]
     else:
         out_shape = [jax.ShapeDtypeStruct((count, rows, part), bf16)]
         out_specs = [
@@ -416,11 +427,12 @@
         out_shape.append(jax.ShapeDtypeStruct((rows, 1), f32))
         out_specs.append(fixed(rows, 1))
     return pl.pallas_call(
-        functools.partial(out_kernel, kind, inverse is not None, len(parts)),
+        functools.partial(out_kernel, kind, inverse is not None, len(parts), before is not None),
         out_shape=out_shape,
         grid_spec=pltpu.PrefetchScalarGridSpec(
             num_scalar_prefetch=1, grid=(count * tiles,), in_specs=specs, out_specs=out_specs
         ),
+        input_output_aliases=aliases,
         compiler_params=params(),
         cost_estimate=pl.CostEstimate(
             flops=2 * rows * w_out.shape[0] * count * part,
@@ -501,14 +513,14 @@
     ids_row = expert_ids.reshape(1, -1)
     w_in, w_out = w_in[0], w_out[0]
 
-    pack, outgoing = dispatch(ids_row, tokens, w_bcd.T, slices)
+    pack, outgoing = dispatch(decode_heads, ids_row, tokens, w_bcd.T, slices)
     landed = swap(outgoing)
     pack = lax.all_gather(pack, "expert", axis=0, tiled=True)
     own_heads = start // HEADDIM + jnp.arange(heads, dtype=jnp.int32)
 
     pieces = [landed] + [turn(landed, n, slices, r) for r in range(1, slices)]
     inner = [None] * EXPERTS
-    for order in ((7,), (6, 5), (4, 3), (2, 1), (0,)):
+    for order in ((7, 6), (5, 4, 3), (2, 1), (0,)):
         if order == (0,):
             weights = prepare(place, own_heads, dt_bias, decay_rate, skip_gain, pack)
             pieces, weights = lax.optimization_barrier((pieces, weights))
@@ -528,11 +540,10 @@
         if k == 0:
             squares = [got[1]] + [turn(got[1], n, slices, r) for r in range(1, slices)]
         sent.append([turn(got[0][r - 1], n, slices, r) for r in range(1, slices)])
-    back = []
+    done = None
     for k in range(CHUNKS):
-        [done] = project("finish", k, squares=squares, parts=sent[k])
-        back.append(swap(done))
-    mixed = collect(ids_row, back, slices)
+        [done] = project("finish", k, squares=squares, parts=sent[k], before=done)
+    mixed = collect(ids_row, [swap(done)], slices)
 
     def picked(head):
         first = head * HEADDIM % in_dev
@@ -547,7 +558,10 @@
     want = decode_heads[0]
     chosen = picked(want)
     for r in range(1, slices):
-        asked = turn(want, n, slices, slices - r)
+        other = chip * slices + (place[0] + r) % slices
+        asked = lax.dynamic_slice(
+            pack, (other * tokens.shape[0], 2 * NS + 2 * HEADS + 2), (1, 1)
+        )[0, 0].astype(jnp.int32)
         got = turn(picked(asked), n, slices, r)
         lies = want * HEADDIM // in_dev
         chosen = jnp.where((place[0] - lies + slices) % slices == r, got, chosen)

time: 235 us -> 237 us (level)
  Pallas kernels: 59.3 us -> 66.4 us
  local copies, waits for them, and re-layouts: 9.82 us -> 4.82 us
    pallas_call x2 -> x4, Pallas kernels: 14.6 us -> 22 us  [out_projection(): pl.pallas_call(functools.partial(out_kernel, kind, inverse is not None, l...]
    unnamed x28 -> x20, local copies, waits for them, and re-layouts: 8.16 us -> 3.15 us
    pallas_call x2, Pallas kernels: 6.97 us -> 9.66 us  [the longest x1 5.81 us: scan(): pl.pallas_call(functools.partial(scan_kernel, heads), out_shape=pltpu.HBM...]
    pallas_call x5 -> x4, Pallas kernels: 21.1 us -> 19.6 us  [in_projection(): pl.pallas_call(functools.partial(in_kernel, slices, shares, turns), out_s...]
  transfers between devices with their start and end apart: 16 -> 16, of which waited for: 7 -> 6; matrix products, arithmetic and copies ran while one was open for 1% -> 2% of each run, Pallas kernels for 15% -> 19%
where the time goes in v9:
time: 237 us; the launch traced here: 232 us
  waiting for transfers between devices  109 us (46%)
  Pallas kernels  66.4 us (28%)
  starting transfers between devices  34.4 us (15%)
  between operations  15.6 us (7%)
  local copies, waits for them, and re-layouts  4.82 us (2%)
    all_to_all x3, waiting for transfers between devices, swap(): lax.all_to_all(a, 'expert', split_axis=0, concat_axis=0, axis_index_group...  102 us
    pallas_call x4, Pallas kernels, out_projection(): pl.pallas_call(functools.partial(out_kernel, kind, inverse is not None, l...  22 us
    pallas_call x4, Pallas kernels, in_projection(): pl.pallas_call(functools.partial(in_kernel, slices, shares, turns), out_s...  19.6 us
    ppermute x7, starting transfers between devices, across(): return lax.ppermute(a, 'expert', pairs)  16.7 us
    all_to_all x3, starting transfers between devices, swap(): lax.all_to_all(a, 'expert', split_axis=0, concat_axis=0, axis_index_group...  15.9 us
    pallas_call x1, Pallas kernels, prepare(): pl.pallas_call(functools.partial(prep_kernel, heads), out_shape=(jax.Shap...  13.1 us
    ppermute x5, waiting for transfers between devices, turn(): lax.ppermute(a, 'expert', [(d, d // slices * slices + (d + r) % slices) f...  5.99 us
    pallas_call x1, Pallas kernels, scan(): pl.pallas_call(functools.partial(scan_kernel, heads), out_shape=pltpu.HBM...  5.81 us
  transfers between devices with their start and end apart: 16, of which 6 were waited for; matrix products, arithmetic and copies ran while one was open for 2% of the time, Pallas kernels for 19%

profile of v9, /device:TPU:0, one launch (start us, length us, event | category | flops | bytes accessed | tf_op | source)
XLA Modules:
  0.0 232.2 jit_solution(15477345159279172807)
XLA Ops:
  7.8 3.8 %dispatch.1 = (bf16[128,256]{1,0:T(8,128)(2,1)}, bf16[384,2048]{1,0:T(8,128)(2,1)}) custom-call(s32[1]{0:T(128)S(6)} %copy.15.refs_0_, s32[1,128]{1,0:T(1,128)} %bitcast.29, bf16[128,4096]{1,0:T(8,128)(2,1)} %refs_2_.1, bf16[160,4096]{1,0:T(8,128)(2,1)} %bitcast.46), custom_call_target="tpu_custom_call" | custom-call | tf_op jit(solution)/shard_map/dispatch/pallas_call | solution.py:101
  11.7 7.4 %all-to-all-start = ((bf16[16,24,2048]{2,1,0:T(8,128)(2,1)}), bf16[16,24,2048]{2,1,0:T(8,128)(2,1)S(1)}, u32[]{:S(2)}, u32[]{:S(2)}) async-start(bf16[16,24,2048]{2,1,0:T(8,128)(2,1)} %bitcast.45), calls=%async_computation | async-start | bytes 3145728 | tf_op jit(solution)/shard_map/all_to_all | solution.py:482
  19.1 0.7 all-gather.2.cloned.1.call-update
  19.8 33.3 %all-to-all-done = bf16[16,24,2048]{2,1,0:T(8,128)(2,1)S(1)} async-done(((bf16[16,24,2048]{2,1,0:T(8,128)(2,1)}), bf16[16,24,2048]{2,1,0:T(8,128)(2,1)S(1)}, u32[]{:S(2)}, u32[]{:S(2)}) %all-to-all-start) | async-done | bytes 1572896 | tf_op jit(solution)/shard_map/all_to_all | solution.py:482
  53.2 0.8 collective-permute-start
  54.0 3.0 %collective-permute-done.refs_1_ = bf16[384,2048]{1,0:T(8,128)(2,1)S(1)} collective-permute-done((bf16[384,2048]{1,0:T(8,128)(2,1)S(1)}, bf16[384,2048]{1,0:T(8,128)(2,1)S(1)}, u32[]{:S(2)}, u32[]{:S(2)}) %collective-permute-start) | collective-permute-done | bytes 1572896 | tf_op jit(solution)/shard_map/ppermute | solution.py:476
  57.0 6.5 %in_projection.6 = (bf16[384,256]{1,0:T(8,128)(2,1)S(1)}, bf16[384,256]{1,0:T(8,128)(2,1)}, bf16[384,256]{1,0:T(8,128)(2,1)}) custom-call(s32[2]{0:T(128)S(1)} %pad_add_fusion.place_ref, bf16[384,2048]{1,0:T(8,128)(2,1)S(1)} %bitcast.19, bf16[384,2048]{1,0:T(8,128)(2,1)S(1)} %collective-permute-done.refs_1_, bf16[4096,2048]{1,0:T(8,128)(2,1)} %bitcast.32, ...), custom_call_target="tpu_custom_call" | custom-call | flops 384 | bytes 384 | tf_op jit(solution)/shard_map/in_projection/pallas_call | solution.py:147
  64.1 8.3 %collective-permute-start.3 = (bf16[384,256]{1,0:T(8,128)(2,1)}, bf16[384,256]{1,0:T(8,128)(2,1)S(1)}, u32[]{:S(2)}, u32[]{:S(2)}) collective-permute-start(bf16[384,256]{1,0:T(8,128)(2,1)} %get-tuple-element.33), channel_id=1, source_target_pairs={{0,6},{1,7},{2,4},{3,5},{4,2},{5,3},{6,0},{7,1},{8,14},{9,15},{10,... | collective-permute-start | bytes 589832 | tf_op jit(solution)/shard_map/ppermute | solution.py:489
  72.4 1.0 collective-permute-start.4
  73.4 0.8 dynamic_slice.15
  74.8 4.9 %in_projection.5 = (bf16[384,256]{1,0:T(8,128)(2,1)}, bf16[384,256]{1,0:T(8,128)(2,1)}) custom-call(s32[2]{0:T(128)S(1)} %pad_add_fusion.place_ref, bf16[384,2048]{1,0:T(8,128)(2,1)S(1)} %bitcast.20, bf16[384,2048]{1,0:T(8,128)(2,1)S(1)} %collective-permute-done.refs_1_, bf16[4096,2048]{1,0:T(8,128)(2,1)} %bitcast.34, bf16[4096,2048]{1,0:T(8,128)(2,1)} %bitcast.35), custom_call_target="tpu_custom_call" | custom-call | flops 384 | bytes 384 | tf_op jit(solution)/shard_map/in_projection/pallas_call | solution.py:147
  79.7 3.3 %collective-permute-start.1 = (bf16[384,256]{1,0:T(8,128)(2,1)}, bf16[384,256]{1,0:T(8,128)(2,1)}, u32[]{:S(2)}, u32[]{:S(2)}) collective-permute-start(bf16[384,256]{1,0:T(8,128)(2,1)} %get-tuple-element.31), channel_id=1, source_target_pairs={{0,2},{1,3},{2,0},{3,1},{4,6},{5,7},{6,4},{7,5},{8,10},{9,11},{10,... | collective-permute-start | bytes 589832 | tf_op jit(solution)/shard_map/ppermute | solution.py:489
  82.9 4.9 %in_projection.7 = (bf16[384,256]{1,0:T(8,128)(2,1)}, bf16[384,256]{1,0:T(8,128)(2,1)}) custom-call(s32[2]{0:T(128)S(1)} %pad_add_fusion.place_ref, bf16[384,2048]{1,0:T(8,128)(2,1)S(1)} %bitcast.21, bf16[384,2048]{1,0:T(8,128)(2,1)S(1)} %collective-permute-done.refs_1_, bf16[4096,2048]{1,0:T(8,128)(2,1)} %bitcast.36, bf16[4096,2048]{1,0:T(8,128)(2,1)} %bitcast.37), custom_call_target="tpu_custom_call" | custom-call | flops 384 | bytes 384 | tf_op jit(solution)/shard_map/in_projection/pallas_call | solution.py:147
  87.8 2.5 %collective-permute-start.6 = (bf16[384,256]{1,0:T(8,128)(2,1)}, bf16[384,256]{1,0:T(8,128)(2,1)}, u32[]{:S(2)}, u32[]{:S(2)}) collective-permute-start(bf16[384,256]{1,0:T(8,128)(2,1)} %get-tuple-element.36), channel_id=1, source_target_pairs={{0,12},{1,13},{2,14},{3,15},{4,8},{5,9},{6,10},{7,11},{8,4},{9,5},... | collective-permute-start | bytes 589832 | tf_op jit(solution)/shard_map/ppermute | solution.py:489
  90.3 1.5 collective-permute-start.7
  91.9 1.2 copy-done.1
  94.3 13.1 %scan_weights.1 = (bf16[2,8,384,384]{3,2,1,0:T(8,128)(2,1)}, bf16[2,8,384,64]{3,2,1,0:T(8,128)(2,1)S(1)}, bf16[2,8,64,384]{3,2,1,0:T(8,128)(2,1)S(1)}, f32[2,8,8,128]{3,2,1,0:T(8,128)S(1)}) custom-call(s32[2]{0:T(128)S(1)} %pad_add_fusion.place_ref, s32[2]{0:T(128)S(1)} %copy-done.6, f32[32]{0:T(128)S(1)} %copy-done.3, f32[32]{0:T(128)S(1)} %copy-done.4, ...), custom_call_target="tpu_custom_call" | custom-call | flops 2415919104 | bytes 4718592 | tf_op jit(solution)/shard_map/scan_weights/pallas_call | solution.py:242
  107.4 3.3 %in_projection.4.refs_0_ = bf16[384,256]{1,0:T(8,128)(2,1)S(1)} custom-call(s32[2]{0:T(128)S(1)} %pad_add_fusion.place_ref, bf16[384,2048]{1,0:T(8,128)(2,1)S(1)} %bitcast.22, bf16[384,2048]{1,0:T(8,128)(2,1)S(1)} %collective-permute-done.refs_1_, bf16[4096,2048]{1,0:T(8,128)(2,1)} %bitcast.38, bf16[4096,2048]{1,0:T(8,128)(2,1)} %bitcast.39), custom_call_target="tpu_custom_call" | custom-call | flops 384 | bytes 384 | tf_op jit(solution)/shard_map/in_projection/pallas_call | solution.py:147
  110.8 5.8 %scan.1 = bf16[8,448,256]{2,1,0:T(8,128)(2,1)} custom-call(s32[2]{0:T(128)S(1)} %pad_add_fusion.place_ref, bf16[384,256]{1,0:T(8,128)(2,1)S(1)} %in_projection.4.refs_0_, bf16[384,256]{1,0:T(8,128)(2,1)} %collective-permute-done.1.refs_1_, bf16[384,256]{1,0:T(8,128)(2,1)} %collective-permute-done.2.refs_2_, ...), custom_call_target="tpu_custom_call" | custom-call | flops 805306368 | bytes 4718592 | tf_op jit(solution)/shard_map/scan/pallas_call | solution.py:312
  116.7 4.6 %all-to-all-start.1 = ((bf16[8,448,256]{2,1,0:T(8,128)(2,1)}), bf16[8,448,256]{2,1,0:T(8,128)(2,1)S(1)}, u32[]{:S(2)}, u32[]{:S(2)}) async-start(bf16[8,448,256]{2,1,0:T(8,128)(2,1)} %scan.1), calls=%async_computation.1 | async-start | bytes 3670016 | tf_op jit(solution)/shard_map/all_to_all | solution.py:482
  121.3 41.3 %all-to-all-done.1.refs_0_ = bf16[8,448,256]{2,1,0:T(8,128)(2,1)S(1)} async-done(((bf16[8,448,256]{2,1,0:T(8,128)(2,1)}), bf16[8,448,256]{2,1,0:T(8,128)(2,1)S(1)}, u32[]{:S(2)}, u32[]{:S(2)}) %all-to-all-start.1) | async-done | bytes 1835040 | tf_op jit(solution)/shard_map/all_to_all | solution.py:482
  162.6 5.5 %out_send.2 = (bf16[1,384,1024]{2,1,0:T(8,128)(2,1)S(1)}, f32[384,1]{1,0:T(8,128)S(1)}) custom-call(s32[2]{0:T(128)S(1)} %pad_add_fusion.place_ref, bf16[8,448,256]{2,1,0:T(8,128)(2,1)S(1)} %all-to-all-done.1.refs_0_, bf16[2048,4096]{1,0:T(8,128)(2,1)} %bitcast.40, f32[1,2048]{1,0:T(1,128)S(1)} %bitcast.27), custom_call_target="tpu_custom_call" | custom-call | flops 1610612736 | bytes 4980736 | tf_op jit(solution)/shard_map/out_send/pallas_call | solution.py:429
  168.2 5.0 %out_send.3 = bf16[1,384,1024]{2,1,0:T(8,128)(2,1)S(1)} custom-call(s32[2]{0:T(128)S(1)} %pad_add_fusion.place_ref, bf16[8,448,256]{2,1,0:T(8,128)(2,1)S(1)} %all-to-all-done.1.refs_0_, bf16[2048,4096]{1,0:T(8,128)(2,1)} %bitcast.41), custom_call_target="tpu_custom_call" | custom-call | flops 1610612736 | bytes 4980736 | tf_op jit(solution)/shard_map/out_send/pallas_call | solution.py:429
  173.9 2.1 collective-permute-done.8.refs_3_
  176.0 5.8 %out_finish.2.refs_5_ = bf16[384,2048]{1,0:T(8,128)(2,1)} custom-call(s32[2]{0:T(128)S(1)} %pad_add_fusion.place_ref, bf16[8,448,256]{2,1,0:T(8,128)(2,1)S(1)} %all-to-all-done.1.refs_0_, bf16[2048,4096]{1,0:T(8,128)(2,1)} %bitcast.42, f32[384,1]{1,0:T(8,128)S(1)} %get-tuple-element.42.refs_2_, f32[384,1]{1,0:T(8,128)S(1)} %collective-permute-done.8.refs_3_, ...), custom_call_target="tpu_custom_call" | custom-call | flops 1610612736 | bytes 4980736 | tf_op jit(solution)/shard_map/out_finish/pallas_call | solution.py:429
  181.8 5.7 %out_finish.3 = bf16[384,2048]{1,0:T(8,128)(2,1)} custom-call(s32[2]{0:T(128)S(1)} %pad_add_fusion.place_ref, bf16[8,448,256]{2,1,0:T(8,128)(2,1)S(1)} %all-to-all-done.1.refs_0_, bf16[2048,4096]{1,0:T(8,128)(2,1)} %bitcast.43, f32[384,1]{1,0:T(8,128)S(1)} %get-tuple-element.42.refs_2_, ...), custom_call_target="tpu_custom_call", output_to_operand_aliasing={{}: (6, {})} | custom-call | flops 1610612736 | bytes 4980736 | tf_op jit(solution)/shard_map/out_finish/pallas_call | solution.py:429
  187.5 3.8 %all-to-all-start.2 = ((bf16[16,24,2048]{2,1,0:T(8,128)(2,1)}), bf16[16,24,2048]{2,1,0:T(8,128)(2,1)S(1)}, u32[]{:S(2)}, u32[]{:S(2)}) async-start(bf16[16,24,2048]{2,1,0:T(8,128)(2,1)} %bitcast.44), calls=%async_computation.2 | async-start | bytes 3145728 | tf_op jit(solution)/shard_map/all_to_all | solution.py:482
  191.4 1.3 fusion
  193.7 0.9 collective-permute-done.11
  194.8 0.7 reshape.34
  195.5 27.7 %all-to-all-done.2 = bf16[16,24,2048]{2,1,0:T(8,128)(2,1)S(1)} async-done(((bf16[16,24,2048]{2,1,0:T(8,128)(2,1)}), bf16[16,24,2048]{2,1,0:T(8,128)(2,1)S(1)}, u32[]{:S(2)}, u32[]{:S(2)}) %all-to-all-start.2) | async-done | bytes 1572896 | tf_op jit(solution)/shard_map/all_to_all | solution.py:482
  223.3 2.0 collect.1
  (43 shorter events, 3.9 us)
Async XLA Ops:
  11.7 41.5 %all-to-all-start = ((bf16[16,24,2048]{2,1,0:T(8,128)(2,1)}), bf16[16,24,2048]{2,1,0:T(8,128)(2,1)S(1)}, u32[]{:S(2)}, u32[]{:S(2)}) async-start(bf16[16,24,2048]{2,1,0:T(8,128)(2,1)} %bitcast.45), calls=%async_computation | async-start | bytes 3145728 | tf_op jit(solution)/shard_map/all_to_all | solution.py:482
  19.1 72.8 %all-gather.2.cloned.1.call-start = ((), (), s32[]{:S(2)}) async-start(), calls=%async_computation.3 | async-start | bytes 1114112 | tf_op jit(solution)/shard_map/all_gather | solution.py:518
  53.2 3.8 %collective-permute-start = (bf16[384,2048]{1,0:T(8,128)(2,1)S(1)}, bf16[384,2048]{1,0:T(8,128)(2,1)S(1)}, u32[]{:S(2)}, u32[]{:S(2)}) collective-permute-start(bf16[384,2048]{1,0:T(8,128)(2,1)S(1)} %bitcast.18), channel_id=1, source_target_pairs={{0,1},{1,0},{2,3},{3,2},{4,5},{5,4},{6,7},{7,6},{8,9},{9,8},{10,11... | collective-permute-start | bytes 4718600 | tf_op jit(solution)/shard_map/ppermute | solution.py:476
  63.4 0.7 copy-start.2
  64.1 23.7 %collective-permute-start.3 = (bf16[384,256]{1,0:T(8,128)(2,1)}, bf16[384,256]{1,0:T(8,128)(2,1)S(1)}, u32[]{:S(2)}, u32[]{:S(2)}) collective-permute-start(bf16[384,256]{1,0:T(8,128)(2,1)} %get-tuple-element.33), channel_id=1, source_target_pairs={{0,6},{1,7},{2,4},{3,5},{4,2},{5,3},{6,0},{7,1},{8,14},{9,15},{10,... | collective-permute-start | bytes 589832 | tf_op jit(solution)/shard_map/ppermute | solution.py:489
  72.4 18.0 %collective-permute-start.4 = (bf16[384,256]{1,0:T(8,128)(2,1)}, bf16[384,256]{1,0:T(8,128)(2,1)S(1)}, u32[]{:S(2)}, u32[]{:S(2)}) collective-permute-start(bf16[384,256]{1,0:T(8,128)(2,1)} %get-tuple-element.34), channel_id=1, source_target_pairs={{0,8},{1,9},{2,10},{3,11},{4,12},{5,13},{6,14},{7,15},{8,0},{9,1},... | collective-permute-start | bytes 589832 | tf_op jit(solution)/shard_map/ppermute | solution.py:489
  74.7 36.1 %collective-permute-start.5 = (bf16[384,256]{1,0:T(8,128)(2,1)}, bf16[384,256]{1,0:T(8,128)(2,1)}, u32[]{:S(2)}, u32[]{:S(2)}) collective-permute-start(bf16[384,256]{1,0:T(8,128)(2,1)} %copy-done.2), channel_id=1, source_target_pairs={{0,10},{1,11},{2,8},{3,9},{4,14},{5,15},{6,12},{7,13},{8,2},{9,3},... | collective-permute-start | bytes 589832 | tf_op jit(solution)/shard_map/ppermute | solution.py:489
  79.7 31.1 %collective-permute-start.1 = (bf16[384,256]{1,0:T(8,128)(2,1)}, bf16[384,256]{1,0:T(8,128)(2,1)}, u32[]{:S(2)}, u32[]{:S(2)}) collective-permute-start(bf16[384,256]{1,0:T(8,128)(2,1)} %get-tuple-element.31), channel_id=1, source_target_pairs={{0,2},{1,3},{2,0},{3,1},{4,6},{5,7},{6,4},{7,5},{8,10},{9,11},{10,... | collective-permute-start | bytes 589832 | tf_op jit(solution)/shard_map/ppermute | solution.py:489
  82.9 8.9 %copy-start.3 = (f32[32]{0:T(128)S(1)}, f32[32]{0:T(128)}, u32[]{:S(2)}) copy-start(f32[32]{0:T(128)} %bias_ref.1) | copy-start | bytes 388
  82.9 8.9 %copy-start.4 = (f32[32]{0:T(128)S(1)}, f32[32]{0:T(128)}, u32[]{:S(2)}) copy-start(f32[32]{0:T(128)} %rate_ref.1) | copy-start | bytes 388
  82.9 27.8 %collective-permute-start.2 = (bf16[384,256]{1,0:T(8,128)(2,1)}, bf16[384,256]{1,0:T(8,128)(2,1)}, u32[]{:S(2)}, u32[]{:S(2)}) collective-permute-start(bf16[384,256]{1,0:T(8,128)(2,1)} %get-tuple-element.32), channel_id=1, source_target_pairs={{0,4},{1,5},{2,6},{3,7},{4,0},{5,1},{6,2},{7,3},{8,12},{9,13},{10,... | collective-permute-start | bytes 589832 | tf_op jit(solution)/shard_map/ppermute | solution.py:489
  87.8 22.9 %collective-permute-start.6 = (bf16[384,256]{1,0:T(8,128)(2,1)}, bf16[384,256]{1,0:T(8,128)(2,1)}, u32[]{:S(2)}, u32[]{:S(2)}) collective-permute-start(bf16[384,256]{1,0:T(8,128)(2,1)} %get-tuple-element.36), channel_id=1, source_target_pairs={{0,12},{1,13},{2,14},{3,15},{4,8},{5,9},{6,10},{7,11},{8,4},{9,5},... | collective-permute-start | bytes 589832 | tf_op jit(solution)/shard_map/ppermute | solution.py:489
  90.3 20.5 %collective-permute-start.7 = (bf16[384,256]{1,0:T(8,128)(2,1)}, bf16[384,256]{1,0:T(8,128)(2,1)}, u32[]{:S(2)}, u32[]{:S(2)}) collective-permute-start(bf16[384,256]{1,0:T(8,128)(2,1)} %get-tuple-element.37), channel_id=1, source_target_pairs={{0,14},{1,15},{2,12},{3,13},{4,10},{5,11},{6,8},{7,9},{8,6},{9,7},... | collective-permute-start | bytes 589832 | tf_op jit(solution)/shard_map/ppermute | solution.py:489
  91.9 1.2 copy-start.1
  93.1 0.7 copy-start.5
  93.7 0.6 copy-start.6
  107.4 3.4 %slice-start = ((s8[4718592]{0:T(1024)(128)(4,1)}), s8[4194304]{0:T(1024)(128)(4,1)S(1)}, s32[]{:S(2)}) async-start(s8[4718592]{0:T(1024)(128)(4,1)} %bitcast.24), calls=%async_computation.4 | async-start | bytes 8388608
  107.4 3.4 %slice-start.1 = ((s8[4718592]{0:T(1024)(128)(4,1)}), s8[524288]{0:T(1024)(128)(4,1)S(1)}, s32[]{:S(2)}) async-start(s8[4718592]{0:T(1024)(128)(4,1)} %bitcast.24), calls=%async_computation.5 | async-start | bytes 1048576
  116.7 4.6 %copy-start.7 = (f32[4096]{0:T(1024)S(1)}, f32[4096]{0:T(1024)}, u32[]{:S(2)}) copy-start(f32[4096]{0:T(1024)} %param.17) | copy-start | bytes 49156
  116.7 46.0 %all-to-all-start.1 = ((bf16[8,448,256]{2,1,0:T(8,128)(2,1)}), bf16[8,448,256]{2,1,0:T(8,128)(2,1)S(1)}, u32[]{:S(2)}, u32[]{:S(2)}) async-start(bf16[8,448,256]{2,1,0:T(8,128)(2,1)} %scan.1), calls=%async_computation.1 | async-start | bytes 3670016 | tf_op jit(solution)/shard_map/all_to_all | solution.py:482
  168.2 7.9 %collective-permute-start.10 = (bf16[384,1024]{1,0:T(8,128)(2,1)S(1)}, bf16[384,1024]{1,0:T(8,128)(2,1)S(1)}, u32[]{:S(2)}, u32[]{:S(2)}) collective-permute-start(bf16[384,1024]{1,0:T(8,128)(2,1)S(1)} %bitcast.31), channel_id=1, source_target_pairs={{0,1},{1,0},{2,3},{3,2},{4,5},{5,4},{6,7},{7,6},{8,9},{9,8},{10,11... | collective-permute-start | bytes 2359304 | tf_op jit(solution)/shard_map/ppermute | solution.py:476
  173.3 8.5 %collective-permute-start.9 = (bf16[384,1024]{1,0:T(8,128)(2,1)S(1)}, bf16[384,1024]{1,0:T(8,128)(2,1)S(1)}, u32[]{:S(2)}, u32[]{:S(2)}) collective-permute-start(bf16[384,1024]{1,0:T(8,128)(2,1)S(1)} %bitcast.26), channel_id=1, source_target_pairs={{0,1},{1,0},{2,3},{3,2},{4,5},{5,4},{6,7},{7,6},{8,9},{9,8},{10,11... | collective-permute-start | bytes 2359304 | tf_op jit(solution)/shard_map/ppermute | solution.py:476
  173.9 2.2 collective-permute-start.8
  187.5 35.8 %copy-start = (s32[128,1]{0,1:T(1,128)S(1)}, s32[128,1]{0,1:T(1,128)}, u32[]{:S(2)}) copy-start(s32[128,1]{0,1:T(1,128)} %param.18) | copy-start | bytes 1540
  187.5 35.8 %all-to-all-start.2 = ((bf16[16,24,2048]{2,1,0:T(8,128)(2,1)}), bf16[16,24,2048]{2,1,0:T(8,128)(2,1)S(1)}, u32[]{:S(2)}, u32[]{:S(2)}) async-start(bf16[16,24,2048]{2,1,0:T(8,128)(2,1)} %bitcast.44), calls=%async_computation.2 | async-start | bytes 3145728 | tf_op jit(solution)/shard_map/all_to_all | solution.py:482
  193.5 1.2 collective-permute-start.11
Sparse Core Ops, SparseCore 0:
  22.1 47.0 all-gather.1

commit v10 on v9

--- a/solution.py
+++ b/solution.py
@@ -15,7 +15,7 @@
 CAP = 24
 PAIR = 256
 PACK = 256
-CHUNKS = 2
+CHUNKS = 1
 VMEM_BYTES = 48 * 1024 * 1024
 
 f32 = jnp.float32
@@ -209,6 +209,7 @@
     diagonal = upto == now
     b_cols = b_rows.astype(f32).T
     c_wide = c_rows.astype(f32)
+    to_place, b_now = [], []
     for h in range(heads):
         run_row = running[h : h + 1]
         run_col = down[:, h : h + 1]
@@ -217,17 +218,24 @@
         gap = jnp.where(causal, run_col - run_row, 0.0)
         weights = jnp.where(causal, jnp.exp(gap) * scores * dt_row, 0.0)
         weights = weights + jnp.where(diagonal, skip_ref[head_ref[h]], 0.0)
-        half = jnp.dot(place_t, weights.astype(bf16), preferred_element_type=f32).astype(bf16)
-        w_ref[h, 0] = lax.dot_general(
-            half, place_t, (((1,), (1,)), ((), ())), preferred_element_type=f32
-        ).astype(bf16)
+        to_place.append(weights.astype(bf16))
+        b_now.append((b_cols * (jnp.exp(last - run_row) * dt_row)).astype(bf16))
         c_now = (c_wide * jnp.exp(run_col)).astype(bf16)
         c_ref[h, 0] = jnp.dot(place_t, c_now, preferred_element_type=f32).astype(bf16)
-        b_now = (b_cols * (jnp.exp(last - run_row) * dt_row)).astype(bf16)
-        b_ref[h, 0] = lax.dot_general(
-            b_now, place_t, (((1,), (1,)), ((), ())), preferred_element_type=f32
-        ).astype(bf16)
         a_ref[h, 0] = jnp.broadcast_to(jnp.exp(last), (8, 128))
+    together = jnp.concatenate(to_place, axis=1) if heads > 1 else to_place[0]
+    half = jnp.dot(place_t, together, preferred_element_type=f32).astype(bf16)
+    rows = [half[:, h * PAIR : (h + 1) * PAIR] for h in range(heads)] + b_now
+    placed = lax.dot_general(
+        jnp.concatenate(rows, axis=0),
+        place_t,
+        (((1,), (1,)), ((), ())),
+        preferred_element_type=f32,
+    ).astype(bf16)
+    for h in range(heads):
+        w_ref[h, 0] = placed[h * slots : (h + 1) * slots]
+        below = heads * slots + h * NS
+        b_ref[h, 0] = placed[below : below + NS]
 
 
 def prepare(place, own_heads, bias, rate, skip, pack):
@@ -388,7 +396,7 @@
     slice_width = w_out.shape[1] // slices
     part = slice_width // CHUNKS
     count, first = (slices - 1, 1) if kind == "send" else (1, 0)
-    tile = min(256, part)
+    tile = min(512, part)
     tiles = part // tile
     whole = slice_width // tile
     offset = chunk * tiles
@@ -520,7 +528,7 @@
 
     pieces = [landed] + [turn(landed, n, slices, r) for r in range(1, slices)]
     inner = [None] * EXPERTS
-    for order in ((7, 6), (5, 4, 3), (2, 1), (0,)):
+    for order in ((7, 6, 5, 4), (3, 2, 1), (0,)):
         if order == (0,):
             weights = prepare(place, own_heads, dt_bias, decay_rate, skip_gain, pack)
             pieces, weights = lax.optimization_barrier((pieces, weights))

time: 237 us -> 240 us (1.013)
  waiting for transfers between devices: 109 us -> 124 us
  Pallas kernels: 66.4 us -> 56.9 us
    ppermute x7, waiting for transfers between devices: 0.02 us -> 12.9 us  [across(): return lax.ppermute(a, 'expert', pairs)]
    pallas_call x4 -> x2, Pallas kernels: 22 us -> 15.4 us  [out_projection(): pl.pallas_call(functools.partial(out_kernel, kind, inverse is not None, l...]
    ppermute x7, starting transfers between devices: 16.7 us -> 14.1 us  [across(): return lax.ppermute(a, 'expert', pairs)]
    pallas_call x4 -> x3, Pallas kernels: 19.6 us -> 17.5 us  [in_projection(): pl.pallas_call(functools.partial(in_kernel, slices, shares, turns), out_s...]
    ppermute x5 -> x4, waiting for transfers between devices: 5.99 us -> 6.98 us  [turn(): lax.ppermute(a, 'expert', [(d, d // slices * slices + (d + r) % slices) f...]
  transfers between devices with their start and end apart: 16 -> 15, of which waited for: 6 -> 8; matrix products, arithmetic and copies ran while one was open for 2% -> 2% of each run, Pallas kernels for 19% -> 13%
where the time goes in v10:
time: 240 us; the launch traced here: 236 us
  waiting for transfers between devices  124 us (52%)
  Pallas kernels  56.9 us (24%)
  starting transfers between devices  32.8 us (14%)
  between operations  15.5 us (6%)
  local copies, waits for them, and re-layouts  4.9 us (2%)
    all_to_all x3, waiting for transfers between devices, swap(): lax.all_to_all(a, 'expert', split_axis=0, concat_axis=0, axis_index_group...  104 us
    pallas_call x3, Pallas kernels, in_projection(): pl.pallas_call(functools.partial(in_kernel, slices, shares, turns), out_s...  17.5 us
    all_to_all x3, starting transfers between devices, swap(): lax.all_to_all(a, 'expert', split_axis=0, concat_axis=0, axis_index_group...  16.9 us
    pallas_call x2, Pallas kernels, out_projection(): pl.pallas_call(functools.partial(out_kernel, kind, inverse is not None, l...  15.4 us
    ppermute x7, starting transfers between devices, across(): return lax.ppermute(a, 'expert', pairs)  14.1 us
    ppermute x7, waiting for transfers between devices, across(): return lax.ppermute(a, 'expert', pairs)  12.9 us
    pallas_call x1, Pallas kernels, prepare(): pl.pallas_call(functools.partial(prep_kernel, heads), out_shape=(jax.Shap...  12.2 us
    ppermute x4, waiting for transfers between devices, turn(): lax.ppermute(a, 'expert', [(d, d // slices * slices + (d + r) % slices) f...  6.98 us
  transfers between devices with their start and end apart: 15, of which 8 were waited for; matrix products, arithmetic and copies ran while one was open for 2% of the time, Pallas kernels for 13%

profile of v10, /device:TPU:0, one launch (start us, length us, event | category | flops | bytes accessed | tf_op | source)
XLA Modules:
  0.0 236.2 jit_solution(8273044230725191451)
XLA Ops:
  7.8 3.9 %dispatch.1 = (bf16[128,256]{1,0:T(8,128)(2,1)}, bf16[384,2048]{1,0:T(8,128)(2,1)}) custom-call(s32[1]{0:T(128)S(6)} %copy.13.refs_0_, s32[1,128]{1,0:T(1,128)} %bitcast.26, bf16[128,4096]{1,0:T(8,128)(2,1)} %refs_2_.1, bf16[160,4096]{1,0:T(8,128)(2,1)} %bitcast.39), custom_call_target="tpu_custom_call" | custom-call | tf_op jit(solution)/shard_map/dispatch/pallas_call | solution.py:101
  11.7 7.4 %all-to-all-start = ((bf16[16,24,2048]{2,1,0:T(8,128)(2,1)}), bf16[16,24,2048]{2,1,0:T(8,128)(2,1)S(1)}, u32[]{:S(2)}, u32[]{:S(2)}) async-start(bf16[16,24,2048]{2,1,0:T(8,128)(2,1)} %bitcast.38), calls=%async_computation | async-start | bytes 3145728 | tf_op jit(solution)/shard_map/all_to_all | solution.py:490
  19.1 0.7 all-gather.2.cloned.1.call-update
  19.8 33.3 %all-to-all-done = bf16[16,24,2048]{2,1,0:T(8,128)(2,1)S(1)} async-done(((bf16[16,24,2048]{2,1,0:T(8,128)(2,1)}), bf16[16,24,2048]{2,1,0:T(8,128)(2,1)S(1)}, u32[]{:S(2)}, u32[]{:S(2)}) %all-to-all-start) | async-done | bytes 1572896 | tf_op jit(solution)/shard_map/all_to_all | solution.py:490
  53.2 0.8 collective-permute-start
  54.0 3.0 %collective-permute-done.refs_1_ = bf16[384,2048]{1,0:T(8,128)(2,1)S(1)} collective-permute-done((bf16[384,2048]{1,0:T(8,128)(2,1)S(1)}, bf16[384,2048]{1,0:T(8,128)(2,1)S(1)}, u32[]{:S(2)}, u32[]{:S(2)}) %collective-permute-start) | collective-permute-done | bytes 1572896 | tf_op jit(solution)/shard_map/ppermute | solution.py:484
  57.0 7.6 %in_projection.5 = (bf16[384,256]{1,0:T(8,128)(2,1)S(1)}, bf16[384,256]{1,0:T(8,128)(2,1)S(1)}, bf16[384,256]{1,0:T(8,128)(2,1)}, bf16[384,256]{1,0:T(8,128)(2,1)}) custom-call(s32[2]{0:T(128)S(1)} %pad_add_fusion.place_ref, bf16[384,2048]{1,0:T(8,128)(2,1)S(1)} %bitcast.18, bf16[384,2048]{1,0:T(8,128)(2,1)S(1)} %collective-permute-done.refs_1_, ...), custom_call_target="tpu_custom_call" | custom-call | flops 384 | bytes 384 | tf_op jit(solution)/shard_map/in_projection/pallas_call | solution.py:147
  64.6 0.7 copy-done.2
  65.3 8.3 %collective-permute-start.4 = (bf16[384,256]{1,0:T(8,128)(2,1)}, bf16[384,256]{1,0:T(8,128)(2,1)S(1)}, u32[]{:S(2)}, u32[]{:S(2)}) collective-permute-start(bf16[384,256]{1,0:T(8,128)(2,1)} %get-tuple-element.34), channel_id=1, source_target_pairs={{0,8},{1,9},{2,10},{3,11},{4,12},{5,13},{6,14},{7,15},{8,0},{9,1},... | collective-permute-start | bytes 589832 | tf_op jit(solution)/shard_map/ppermute | solution.py:497
  73.6 0.8 dynamic_slice.15
  75.0 3.4 %collective-permute-start.6 = (bf16[384,256]{1,0:T(8,128)(2,1)}, bf16[384,256]{1,0:T(8,128)(2,1)}, u32[]{:S(2)}, u32[]{:S(2)}) collective-permute-start(bf16[384,256]{1,0:T(8,128)(2,1)} %copy-done.3), channel_id=1, source_target_pairs={{0,12},{1,13},{2,14},{3,15},{4,8},{5,9},{6,10},{7,11},{8,4},{9,5},... | collective-permute-start | bytes 589832 | tf_op jit(solution)/shard_map/ppermute | solution.py:497
  78.3 2.0 collective-permute-start.7
  80.3 6.5 %in_projection.4 = (bf16[384,256]{1,0:T(8,128)(2,1)}, bf16[384,256]{1,0:T(8,128)(2,1)}, bf16[384,256]{1,0:T(8,128)(2,1)}) custom-call(s32[2]{0:T(128)S(1)} %pad_add_fusion.place_ref, bf16[384,2048]{1,0:T(8,128)(2,1)S(1)} %bitcast.19, bf16[384,2048]{1,0:T(8,128)(2,1)S(1)} %collective-permute-done.refs_1_, bf16[4096,2048]{1,0:T(8,128)(2,1)} %bitcast.31, ...), custom_call_target="tpu_custom_call" | custom-call | flops 384 | bytes 384 | tf_op jit(solution)/shard_map/in_projection/pallas_call | solution.py:147
  86.9 8.5 %collective-permute-done.4.refs_4_ = bf16[384,256]{1,0:T(8,128)(2,1)S(1)} collective-permute-done((bf16[384,256]{1,0:T(8,128)(2,1)}, bf16[384,256]{1,0:T(8,128)(2,1)S(1)}, u32[]{:S(2)}, u32[]{:S(2)}) %collective-permute-start.4) | collective-permute-done | bytes 196640 | tf_op jit(solution)/shard_map/ppermute | solution.py:497
  95.3 4.4 %collective-permute-done.5.refs_5_ = bf16[384,256]{1,0:T(8,128)(2,1)S(1)} collective-permute-done((bf16[384,256]{1,0:T(8,128)(2,1)}, bf16[384,256]{1,0:T(8,128)(2,1)S(1)}, u32[]{:S(2)}, u32[]{:S(2)}) %collective-permute-start.5) | collective-permute-done | bytes 196640 | tf_op jit(solution)/shard_map/ppermute | solution.py:497
  100.2 1.2 copy-done.1
  101.4 0.7 copy-done.6
  102.0 0.7 copy-done.7
  102.7 12.2 %scan_weights.1 = (bf16[2,8,384,384]{3,2,1,0:T(8,128)(2,1)}, bf16[2,8,384,64]{3,2,1,0:T(8,128)(2,1)S(1)}, bf16[2,8,64,384]{3,2,1,0:T(8,128)(2,1)S(1)}, f32[2,8,8,128]{3,2,1,0:T(8,128)S(1)}) custom-call(s32[2]{0:T(128)S(1)} %pad_add_fusion.place_ref, s32[2]{0:T(128)S(1)} %copy-done.7, f32[32]{0:T(128)S(1)} %copy-done.4, f32[32]{0:T(128)S(1)} %copy-done.5, ...), custom_call_target="tpu_custom_call" | custom-call | flops 2415919104 | bytes 4718592 | tf_op jit(solution)/shard_map/scan_weights/pallas_call | solution.py:250
  114.9 3.3 %in_projection.3.refs_0_ = bf16[384,256]{1,0:T(8,128)(2,1)S(1)} custom-call(s32[2]{0:T(128)S(1)} %pad_add_fusion.place_ref, bf16[384,2048]{1,0:T(8,128)(2,1)S(1)} %bitcast.20, bf16[384,2048]{1,0:T(8,128)(2,1)S(1)} %collective-permute-done.refs_1_, bf16[4096,2048]{1,0:T(8,128)(2,1)} %bitcast.33, bf16[4096,2048]{1,0:T(8,128)(2,1)} %bitcast.34), custom_call_target="tpu_custom_call" | custom-call | flops 384 | bytes 384 | tf_op jit(solution)/shard_map/in_projection/pallas_call | solution.py:147
  118.4 5.8 %scan.1 = bf16[8,448,256]{2,1,0:T(8,128)(2,1)} custom-call(s32[2]{0:T(128)S(1)} %pad_add_fusion.place_ref, bf16[384,256]{1,0:T(8,128)(2,1)S(1)} %in_projection.3.refs_0_, bf16[384,256]{1,0:T(8,128)(2,1)} %collective-permute-done.1.refs_1_, bf16[384,256]{1,0:T(8,128)(2,1)} %collective-permute-done.2.refs_2_, bf16[384,256]{1,0:T(8,128)(2,1)} %collective-permute-done.3.refs_3_, ...), custom_call_target="tpu_custom_call" | custom-call | flops 805306368 | bytes 4718592 | tf_op jit(solution)/shard_map/scan/pallas_call | solution.py:320
  124.2 5.6 %all-to-all-start.1 = ((bf16[8,448,256]{2,1,0:T(8,128)(2,1)}), bf16[8,448,256]{2,1,0:T(8,128)(2,1)S(1)}, u32[]{:S(2)}, u32[]{:S(2)}) async-start(bf16[8,448,256]{2,1,0:T(8,128)(2,1)} %scan.1), calls=%async_computation.1 | async-start | bytes 3670016 | tf_op jit(solution)/shard_map/all_to_all | solution.py:490
  129.9 42.4 %all-to-all-done.1.refs_0_ = bf16[8,448,256]{2,1,0:T(8,128)(2,1)S(1)} async-done(((bf16[8,448,256]{2,1,0:T(8,128)(2,1)}), bf16[8,448,256]{2,1,0:T(8,128)(2,1)S(1)}, u32[]{:S(2)}, u32[]{:S(2)}) %all-to-all-start.1) | async-done | bytes 1835040 | tf_op jit(solution)/shard_map/all_to_all | solution.py:490
  172.3 7.5 %out_send.1 = (bf16[1,384,2048]{2,1,0:T(8,128)(2,1)S(1)}, f32[384,1]{1,0:T(8,128)S(1)}) custom-call(s32[2]{0:T(128)S(1)} %pad_add_fusion.place_ref, bf16[8,448,256]{2,1,0:T(8,128)(2,1)S(1)} %all-to-all-done.1.refs_0_, bf16[2048,4096]{1,0:T(8,128)(2,1)} %bitcast.35, f32[1,2048]{1,0:T(1,128)S(1)} %bitcast.24), custom_call_target="tpu_custom_call" | custom-call | flops 3221225472 | bytes 9961472 | tf_op jit(solution)/shard_map/out_send/pallas_call | solution.py:437
  180.4 3.2 %collective-permute-done.8.refs_3_ = f32[384,1]{1,0:T(8,128)S(1)} collective-permute-done((f32[384,1]{1,0:T(8,128)S(1)}, f32[384,1]{1,0:T(8,128)S(1)}, u32[]{:S(2)}, u32[]{:S(2)}) %collective-permute-start.8) | collective-permute-done | bytes 1568 | tf_op jit(solution)/shard_map/ppermute | solution.py:484
  183.6 7.9 %out_finish.1 = bf16[384,2048]{1,0:T(8,128)(2,1)} custom-call(s32[2]{0:T(128)S(1)} %pad_add_fusion.place_ref, bf16[8,448,256]{2,1,0:T(8,128)(2,1)S(1)} %all-to-all-done.1.refs_0_, bf16[2048,4096]{1,0:T(8,128)(2,1)} %bitcast.36, f32[384,1]{1,0:T(8,128)S(1)} %get-tuple-element.42.refs_2_, f32[384,1]{1,0:T(8,128)S(1)} %collective-permute-done.8.refs_3_, ...), custom_call_target="tpu_custom_call" | custom-call | flops 3221225472 | bytes 9961472 | tf_op jit(solution)/shard_map/out_finish/pallas_call | solution.py:437
  191.5 3.9 %all-to-all-start.2 = ((bf16[16,24,2048]{2,1,0:T(8,128)(2,1)}), bf16[16,24,2048]{2,1,0:T(8,128)(2,1)S(1)}, u32[]{:S(2)}, u32[]{:S(2)}) async-start(bf16[16,24,2048]{2,1,0:T(8,128)(2,1)} %bitcast.37), calls=%async_computation.2 | async-start | bytes 3145728 | tf_op jit(solution)/shard_map/all_to_all | solution.py:490
  195.4 1.3 fusion
  197.8 0.8 collective-permute-done.10
  198.8 0.7 reshape.34
  199.6 27.8 %all-to-all-done.2 = bf16[16,24,2048]{2,1,0:T(8,128)(2,1)S(1)} async-done(((bf16[16,24,2048]{2,1,0:T(8,128)(2,1)}), bf16[16,24,2048]{2,1,0:T(8,128)(2,1)S(1)}, u32[]{:S(2)}, u32[]{:S(2)}) %all-to-all-start.2) | async-done | bytes 1572896 | tf_op jit(solution)/shard_map/all_to_all | solution.py:490
  227.4 2.0 collect.1
  (40 shorter events, 2.3 us)
Async XLA Ops:
  11.7 41.5 %all-to-all-start = ((bf16[16,24,2048]{2,1,0:T(8,128)(2,1)}), bf16[16,24,2048]{2,1,0:T(8,128)(2,1)S(1)}, u32[]{:S(2)}, u32[]{:S(2)}) async-start(bf16[16,24,2048]{2,1,0:T(8,128)(2,1)} %bitcast.38), calls=%async_computation | async-start | bytes 3145728 | tf_op jit(solution)/shard_map/all_to_all | solution.py:490
  19.1 81.1 %all-gather.2.cloned.1.call-start = ((), (), s32[]{:S(2)}) async-start(), calls=%async_computation.3 | async-start | bytes 1114112 | tf_op jit(solution)/shard_map/all_gather | solution.py:526
  53.2 3.8 %collective-permute-start = (bf16[384,2048]{1,0:T(8,128)(2,1)S(1)}, bf16[384,2048]{1,0:T(8,128)(2,1)S(1)}, u32[]{:S(2)}, u32[]{:S(2)}) collective-permute-start(bf16[384,2048]{1,0:T(8,128)(2,1)S(1)} %bitcast.17), channel_id=1, source_target_pairs={{0,1},{1,0},{2,3},{3,2},{4,5},{5,4},{6,7},{7,6},{8,9},{9,8},{10,11... | collective-permute-start | bytes 4718600 | tf_op jit(solution)/shard_map/ppermute | solution.py:484
  64.6 0.7 copy-start.2
  65.3 8.3 %copy-start.3 = (bf16[384,256]{1,0:T(8,128)(2,1)}, bf16[384,256]{1,0:T(8,128)(2,1)S(1)}, u32[]{:S(2)}) copy-start(bf16[384,256]{1,0:T(8,128)(2,1)S(1)} %get-tuple-element.36) | copy-start | bytes 589828
  65.3 30.0 %collective-permute-start.4 = (bf16[384,256]{1,0:T(8,128)(2,1)}, bf16[384,256]{1,0:T(8,128)(2,1)S(1)}, u32[]{:S(2)}, u32[]{:S(2)}) collective-permute-start(bf16[384,256]{1,0:T(8,128)(2,1)} %get-tuple-element.34), channel_id=1, source_target_pairs={{0,8},{1,9},{2,10},{3,11},{4,12},{5,13},{6,14},{7,15},{8,0},{9,1},... | collective-permute-start | bytes 589832 | tf_op jit(solution)/shard_map/ppermute | solution.py:497
  73.6 26.2 %collective-permute-start.5 = (bf16[384,256]{1,0:T(8,128)(2,1)}, bf16[384,256]{1,0:T(8,128)(2,1)S(1)}, u32[]{:S(2)}, u32[]{:S(2)}) collective-permute-start(bf16[384,256]{1,0:T(8,128)(2,1)} %get-tuple-element.35), channel_id=1, source_target_pairs={{0,10},{1,11},{2,8},{3,9},{4,14},{5,15},{6,12},{7,13},{8,2},{9,3},... | collective-permute-start | bytes 589832 | tf_op jit(solution)/shard_map/ppermute | solution.py:497
  75.0 43.3 %collective-permute-start.6 = (bf16[384,256]{1,0:T(8,128)(2,1)}, bf16[384,256]{1,0:T(8,128)(2,1)}, u32[]{:S(2)}, u32[]{:S(2)}) collective-permute-start(bf16[384,256]{1,0:T(8,128)(2,1)} %copy-done.3), channel_id=1, source_target_pairs={{0,12},{1,13},{2,14},{3,15},{4,8},{5,9},{6,10},{7,11},{8,4},{9,5},... | collective-permute-start | bytes 589832 | tf_op jit(solution)/shard_map/ppermute | solution.py:497
  78.3 21.8 %copy-start.4 = (f32[32]{0:T(128)S(1)}, f32[32]{0:T(128)}, u32[]{:S(2)}) copy-start(f32[32]{0:T(128)} %bias_ref.1) | copy-start | bytes 388
  78.3 21.8 %copy-start.5 = (f32[32]{0:T(128)S(1)}, f32[32]{0:T(128)}, u32[]{:S(2)}) copy-start(f32[32]{0:T(128)} %rate_ref.1) | copy-start | bytes 388
  78.3 40.0 %collective-permute-start.7 = (bf16[384,256]{1,0:T(8,128)(2,1)}, bf16[384,256]{1,0:T(8,128)(2,1)}, u32[]{:S(2)}, u32[]{:S(2)}) collective-permute-start(bf16[384,256]{1,0:T(8,128)(2,1)} %copy-done.2), channel_id=1, source_target_pairs={{0,14},{1,15},{2,12},{3,13},{4,10},{5,11},{6,8},{7,9},{8,6},{9,7},... | collective-permute-start | bytes 589832 | tf_op jit(solution)/shard_map/ppermute | solution.py:497
  86.9 31.4 %collective-permute-start.1 = (bf16[384,256]{1,0:T(8,128)(2,1)}, bf16[384,256]{1,0:T(8,128)(2,1)}, u32[]{:S(2)}, u32[]{:S(2)}) collective-permute-start(bf16[384,256]{1,0:T(8,128)(2,1)} %get-tuple-element.31), channel_id=1, source_target_pairs={{0,2},{1,3},{2,0},{3,1},{4,6},{5,7},{6,4},{7,5},{8,10},{9,11},{10,... | collective-permute-start | bytes 589832 | tf_op jit(solution)/shard_map/ppermute | solution.py:497
  95.3 23.0 %collective-permute-start.2 = (bf16[384,256]{1,0:T(8,128)(2,1)}, bf16[384,256]{1,0:T(8,128)(2,1)}, u32[]{:S(2)}, u32[]{:S(2)}) collective-permute-start(bf16[384,256]{1,0:T(8,128)(2,1)} %get-tuple-element.32), channel_id=1, source_target_pairs={{0,4},{1,5},{2,6},{3,7},{4,0},{5,1},{6,2},{7,3},{8,12},{9,13},{10,... | collective-permute-start | bytes 589832 | tf_op jit(solution)/shard_map/ppermute | solution.py:497
  99.8 18.6 %collective-permute-start.3 = (bf16[384,256]{1,0:T(8,128)(2,1)}, bf16[384,256]{1,0:T(8,128)(2,1)}, u32[]{:S(2)}, u32[]{:S(2)}) collective-permute-start(bf16[384,256]{1,0:T(8,128)(2,1)} %get-tuple-element.33), channel_id=1, source_target_pairs={{0,6},{1,7},{2,4},{3,5},{4,2},{5,3},{6,0},{7,1},{8,14},{9,15},{10,... | collective-permute-start | bytes 589832 | tf_op jit(solution)/shard_map/ppermute | solution.py:497
  100.2 1.2 copy-start.1
  101.4 0.7 copy-start.6
  102.0 0.7 copy-start.7
  114.9 3.4 %slice-start = ((s8[4718592]{0:T(1024)(128)(4,1)}), s8[4194304]{0:T(1024)(128)(4,1)S(1)}, s32[]{:S(2)}) async-start(s8[4718592]{0:T(1024)(128)(4,1)} %bitcast.22), calls=%async_computation.4 | async-start | bytes 8388608
  114.9 3.4 %slice-start.1 = ((s8[4718592]{0:T(1024)(128)(4,1)}), s8[524288]{0:T(1024)(128)(4,1)S(1)}, s32[]{:S(2)}) async-start(s8[4718592]{0:T(1024)(128)(4,1)} %bitcast.22), calls=%async_computation.5 | async-start | bytes 1048576
  124.2 5.7 %copy-start.8 = (f32[4096]{0:T(1024)S(1)}, f32[4096]{0:T(1024)}, u32[]{:S(2)}) copy-start(f32[4096]{0:T(1024)} %param.17) | copy-start | bytes 49156
  124.2 48.1 %all-to-all-start.1 = ((bf16[8,448,256]{2,1,0:T(8,128)(2,1)}), bf16[8,448,256]{2,1,0:T(8,128)(2,1)S(1)}, u32[]{:S(2)}, u32[]{:S(2)}) async-start(bf16[8,448,256]{2,1,0:T(8,128)(2,1)} %scan.1), calls=%async_computation.1 | async-start | bytes 3670016 | tf_op jit(solution)/shard_map/all_to_all | solution.py:490
  179.8 3.8 %collective-permute-start.9 = (bf16[384,2048]{1,0:T(8,128)(2,1)S(1)}, bf16[384,2048]{1,0:T(8,128)(2,1)S(1)}, u32[]{:S(2)}, u32[]{:S(2)}) collective-permute-start(bf16[384,2048]{1,0:T(8,128)(2,1)S(1)} %bitcast.28), channel_id=1, source_target_pairs={{0,1},{1,0},{2,3},{3,2},{4,5},{5,4},{6,7},{7,6},{8,9},{9,8},{10,11... | collective-permute-start | bytes 4718600 | tf_op jit(solution)/shard_map/ppermute | solution.py:484
  179.9 3.7 %collective-permute-start.8 = (f32[384,1]{1,0:T(8,128)S(1)}, f32[384,1]{1,0:T(8,128)S(1)}, u32[]{:S(2)}, u32[]{:S(2)}) collective-permute-start(f32[384,1]{1,0:T(8,128)S(1)} %get-tuple-element.42.refs_2_), channel_id=1, source_target_pairs={{0,1},{1,0},{2,3},{3,2},{4,5},{5,4},{6,7},{7,6},{8,9},{9,8},{10,11... | collective-permute-start | bytes 4616 | tf_op jit(solution)/shard_map/ppermute | solution.py:484
  191.5 35.9 %copy-start = (s32[128,1]{0,1:T(1,128)S(1)}, s32[128,1]{0,1:T(1,128)}, u32[]{:S(2)}) copy-start(s32[128,1]{0,1:T(1,128)} %param.18) | copy-start | bytes 1540
  191.5 35.9 %all-to-all-start.2 = ((bf16[16,24,2048]{2,1,0:T(8,128)(2,1)}), bf16[16,24,2048]{2,1,0:T(8,128)(2,1)S(1)}, u32[]{:S(2)}, u32[]{:S(2)}) async-start(bf16[16,24,2048]{2,1,0:T(8,128)(2,1)} %bitcast.37), calls=%async_computation.2 | async-start | bytes 3145728 | tf_op jit(solution)/shard_map/all_to_all | solution.py:490
  197.4 1.2 collective-permute-start.10
Sparse Core Ops, SparseCore 0:
  22.1 47.0 all-gather.1

commit v11 on v10

--- a/solution.py
+++ b/solution.py
@@ -528,7 +528,7 @@
 
     pieces = [landed] + [turn(landed, n, slices, r) for r in range(1, slices)]
     inner = [None] * EXPERTS
-    for order in ((7, 6, 5, 4), (3, 2, 1), (0,)):
+    for order in ((7, 6), (5, 4, 3), (2, 1), (0,)):
         if order == (0,):
             weights = prepare(place, own_heads, dt_bias, decay_rate, skip_gain, pack)
             pieces, weights = lax.optimization_barrier((pieces, weights))

time: 240 us -> 230 us (0.958)
  waiting for transfers between devices: 124 us -> 110 us
    ppermute x7, waiting for transfers between devices: 12.9 us -> 0.02 us  [across(): return lax.ppermute(a, 'expert', pairs)]
    ppermute x7, starting transfers between devices: 14.1 us -> 16.6 us  [across(): return lax.ppermute(a, 'expert', pairs)]
    pallas_call x3 -> x4, Pallas kernels: 17.5 us -> 19.6 us  [in_projection(): pl.pallas_call(functools.partial(in_kernel, slices, shares, turns), out_s...]
  transfers between devices with their start and end apart: 15 -> 15, of which waited for: 8 -> 6; matrix products, arithmetic and copies ran while one was open for 2% -> 2% of each run, Pallas kernels for 13% -> 14%
where the time goes in v11:
time: 230 us; the launch traced here: 226 us
  waiting for transfers between devices  110 us (48%)
  Pallas kernels  59 us (26%)
  starting transfers between devices  34.2 us (15%)
  between operations  15.5 us (7%)
  local copies, waits for them, and re-layouts  4.89 us (2%)
    all_to_all x3, waiting for transfers between devices, swap(): lax.all_to_all(a, 'expert', split_axis=0, concat_axis=0, axis_index_group...  102 us
    pallas_call x4, Pallas kernels, in_projection(): pl.pallas_call(functools.partial(in_kernel, slices, shares, turns), out_s...  19.6 us
    ppermute x7, starting transfers between devices, across(): return lax.ppermute(a, 'expert', pairs)  16.6 us
    all_to_all x3, starting transfers between devices, swap(): lax.all_to_all(a, 'expert', split_axis=0, concat_axis=0, axis_index_group...  15.9 us
    pallas_call x2, Pallas kernels, out_projection(): pl.pallas_call(functools.partial(out_kernel, kind, inverse is not None, l...  15.4 us
    pallas_call x1, Pallas kernels, prepare(): pl.pallas_call(functools.partial(prep_kernel, heads), out_shape=(jax.Shap...  12.2 us
    ppermute x4, waiting for transfers between devices, turn(): lax.ppermute(a, 'expert', [(d, d // slices * slices + (d + r) % slices) f...  7.08 us
    pallas_call x1, Pallas kernels, scan(): pl.pallas_call(functools.partial(scan_kernel, heads), out_shape=pltpu.HBM...  5.82 us
  transfers between devices with their start and end apart: 15, of which 6 were waited for; matrix products, arithmetic and copies ran while one was open for 2% of the time, Pallas kernels for 14%

profile of v11, /device:TPU:0, one launch (start us, length us, event | category | flops | bytes accessed | tf_op | source)
XLA Modules:
  0.0 225.8 jit_solution(6922385054043804251)
XLA Ops:
  7.8 3.9 %dispatch.1 = (bf16[128,256]{1,0:T(8,128)(2,1)}, bf16[384,2048]{1,0:T(8,128)(2,1)}) custom-call(s32[1]{0:T(128)S(6)} %copy.13.refs_0_, s32[1,128]{1,0:T(1,128)} %bitcast.27, bf16[128,4096]{1,0:T(8,128)(2,1)} %refs_2_.1, bf16[160,4096]{1,0:T(8,128)(2,1)} %bitcast.42), custom_call_target="tpu_custom_call" | custom-call | tf_op jit(solution)/shard_map/dispatch/pallas_call | solution.py:101
  11.7 7.4 %all-to-all-start = ((bf16[16,24,2048]{2,1,0:T(8,128)(2,1)}), bf16[16,24,2048]{2,1,0:T(8,128)(2,1)S(1)}, u32[]{:S(2)}, u32[]{:S(2)}) async-start(bf16[16,24,2048]{2,1,0:T(8,128)(2,1)} %bitcast.41), calls=%async_computation | async-start | bytes 3145728 | tf_op jit(solution)/shard_map/all_to_all | solution.py:490
  19.1 0.7 all-gather.2.cloned.1.call-update
  19.8 33.3 %all-to-all-done = bf16[16,24,2048]{2,1,0:T(8,128)(2,1)S(1)} async-done(((bf16[16,24,2048]{2,1,0:T(8,128)(2,1)}), bf16[16,24,2048]{2,1,0:T(8,128)(2,1)S(1)}, u32[]{:S(2)}, u32[]{:S(2)}) %all-to-all-start) | async-done | bytes 1572896 | tf_op jit(solution)/shard_map/all_to_all | solution.py:490
  53.2 0.8 collective-permute-start
  54.0 3.0 %collective-permute-done.refs_1_ = bf16[384,2048]{1,0:T(8,128)(2,1)S(1)} collective-permute-done((bf16[384,2048]{1,0:T(8,128)(2,1)S(1)}, bf16[384,2048]{1,0:T(8,128)(2,1)S(1)}, u32[]{:S(2)}, u32[]{:S(2)}) %collective-permute-start) | collective-permute-done | bytes 1572896 | tf_op jit(solution)/shard_map/ppermute | solution.py:484
  57.0 6.5 %in_projection.6 = (bf16[384,256]{1,0:T(8,128)(2,1)S(1)}, bf16[384,256]{1,0:T(8,128)(2,1)}, bf16[384,256]{1,0:T(8,128)(2,1)}) custom-call(s32[2]{0:T(128)S(1)} %pad_add_fusion.place_ref, bf16[384,2048]{1,0:T(8,128)(2,1)S(1)} %bitcast.18, bf16[384,2048]{1,0:T(8,128)(2,1)S(1)} %collective-permute-done.refs_1_, bf16[4096,2048]{1,0:T(8,128)(2,1)} %bitcast.30, ...), custom_call_target="tpu_custom_call" | custom-call | flops 384 | bytes 384 | tf_op jit(solution)/shard_map/in_projection/pallas_call | solution.py:147
  63.4 0.7 copy-done.2
  64.1 8.3 %collective-permute-start.3 = (bf16[384,256]{1,0:T(8,128)(2,1)}, bf16[384,256]{1,0:T(8,128)(2,1)S(1)}, u32[]{:S(2)}, u32[]{:S(2)}) collective-permute-start(bf16[384,256]{1,0:T(8,128)(2,1)} %get-tuple-element.33), channel_id=1, source_target_pairs={{0,6},{1,7},{2,4},{3,5},{4,2},{5,3},{6,0},{7,1},{8,14},{9,15},{10,... | collective-permute-start | bytes 589832 | tf_op jit(solution)/shard_map/ppermute | solution.py:497
  72.4 1.0 collective-permute-start.4
  73.5 0.8 dynamic_slice.15
  74.9 4.9 %in_projection.5 = (bf16[384,256]{1,0:T(8,128)(2,1)}, bf16[384,256]{1,0:T(8,128)(2,1)}) custom-call(s32[2]{0:T(128)S(1)} %pad_add_fusion.place_ref, bf16[384,2048]{1,0:T(8,128)(2,1)S(1)} %bitcast.19, bf16[384,2048]{1,0:T(8,128)(2,1)S(1)} %collective-permute-done.refs_1_, bf16[4096,2048]{1,0:T(8,128)(2,1)} %bitcast.32, bf16[4096,2048]{1,0:T(8,128)(2,1)} %bitcast.33), custom_call_target="tpu_custom_call" | custom-call | flops 384 | bytes 384 | tf_op jit(solution)/shard_map/in_projection/pallas_call | solution.py:147
  79.8 3.2 %collective-permute-start.1 = (bf16[384,256]{1,0:T(8,128)(2,1)}, bf16[384,256]{1,0:T(8,128)(2,1)}, u32[]{:S(2)}, u32[]{:S(2)}) collective-permute-start(bf16[384,256]{1,0:T(8,128)(2,1)} %get-tuple-element.31), channel_id=1, source_target_pairs={{0,2},{1,3},{2,0},{3,1},{4,6},{5,7},{6,4},{7,5},{8,10},{9,11},{10,... | collective-permute-start | bytes 589832 | tf_op jit(solution)/shard_map/ppermute | solution.py:497
  83.0 4.9 %in_projection.7 = (bf16[384,256]{1,0:T(8,128)(2,1)}, bf16[384,256]{1,0:T(8,128)(2,1)}) custom-call(s32[2]{0:T(128)S(1)} %pad_add_fusion.place_ref, bf16[384,2048]{1,0:T(8,128)(2,1)S(1)} %bitcast.20, bf16[384,2048]{1,0:T(8,128)(2,1)S(1)} %collective-permute-done.refs_1_, bf16[4096,2048]{1,0:T(8,128)(2,1)} %bitcast.34, bf16[4096,2048]{1,0:T(8,128)(2,1)} %bitcast.35), custom_call_target="tpu_custom_call" | custom-call | flops 384 | bytes 384 | tf_op jit(solution)/shard_map/in_projection/pallas_call | solution.py:147
  87.9 2.5 %collective-permute-start.6 = (bf16[384,256]{1,0:T(8,128)(2,1)}, bf16[384,256]{1,0:T(8,128)(2,1)}, u32[]{:S(2)}, u32[]{:S(2)}) collective-permute-start(bf16[384,256]{1,0:T(8,128)(2,1)} %get-tuple-element.36), channel_id=1, source_target_pairs={{0,12},{1,13},{2,14},{3,15},{4,8},{5,9},{6,10},{7,11},{8,4},{9,5},... | collective-permute-start | bytes 589832 | tf_op jit(solution)/shard_map/ppermute | solution.py:497
  90.4 1.4 collective-permute-start.7
  91.9 1.2 copy-done.1
  93.7 0.7 copy-done.6
  94.4 12.2 %scan_weights.1 = (bf16[2,8,384,384]{3,2,1,0:T(8,128)(2,1)}, bf16[2,8,384,64]{3,2,1,0:T(8,128)(2,1)S(1)}, bf16[2,8,64,384]{3,2,1,0:T(8,128)(2,1)S(1)}, f32[2,8,8,128]{3,2,1,0:T(8,128)S(1)}) custom-call(s32[2]{0:T(128)S(1)} %pad_add_fusion.place_ref, s32[2]{0:T(128)S(1)} %copy-done.6, f32[32]{0:T(128)S(1)} %copy-done.3, f32[32]{0:T(128)S(1)} %copy-done.4, ...), custom_call_target="tpu_custom_call" | custom-call | flops 2415919104 | bytes 4718592 | tf_op jit(solution)/shard_map/scan_weights/pallas_call | solution.py:250
  106.6 3.3 %in_projection.4.refs_0_ = bf16[384,256]{1,0:T(8,128)(2,1)S(1)} custom-call(s32[2]{0:T(128)S(1)} %pad_add_fusion.place_ref, bf16[384,2048]{1,0:T(8,128)(2,1)S(1)} %bitcast.21, bf16[384,2048]{1,0:T(8,128)(2,1)S(1)} %collective-permute-done.refs_1_, bf16[4096,2048]{1,0:T(8,128)(2,1)} %bitcast.36, bf16[4096,2048]{1,0:T(8,128)(2,1)} %bitcast.37), custom_call_target="tpu_custom_call" | custom-call | flops 384 | bytes 384 | tf_op jit(solution)/shard_map/in_projection/pallas_call | solution.py:147
  110.1 5.8 %scan.1 = bf16[8,448,256]{2,1,0:T(8,128)(2,1)} custom-call(s32[2]{0:T(128)S(1)} %pad_add_fusion.place_ref, bf16[384,256]{1,0:T(8,128)(2,1)S(1)} %in_projection.4.refs_0_, bf16[384,256]{1,0:T(8,128)(2,1)} %collective-permute-done.1.refs_1_, bf16[384,256]{1,0:T(8,128)(2,1)} %collective-permute-done.2.refs_2_, ...), custom_call_target="tpu_custom_call" | custom-call | flops 805306368 | bytes 4718592 | tf_op jit(solution)/shard_map/scan/pallas_call | solution.py:320
  115.9 4.7 %all-to-all-start.1 = ((bf16[8,448,256]{2,1,0:T(8,128)(2,1)}), bf16[8,448,256]{2,1,0:T(8,128)(2,1)S(1)}, u32[]{:S(2)}, u32[]{:S(2)}) async-start(bf16[8,448,256]{2,1,0:T(8,128)(2,1)} %scan.1), calls=%async_computation.1 | async-start | bytes 3670016 | tf_op jit(solution)/shard_map/all_to_all | solution.py:490
  120.6 41.3 %all-to-all-done.1.refs_0_ = bf16[8,448,256]{2,1,0:T(8,128)(2,1)S(1)} async-done(((bf16[8,448,256]{2,1,0:T(8,128)(2,1)}), bf16[8,448,256]{2,1,0:T(8,128)(2,1)S(1)}, u32[]{:S(2)}, u32[]{:S(2)}) %all-to-all-start.1) | async-done | bytes 1835040 | tf_op jit(solution)/shard_map/all_to_all | solution.py:490
  161.9 7.5 %out_send.1 = (bf16[1,384,2048]{2,1,0:T(8,128)(2,1)S(1)}, f32[384,1]{1,0:T(8,128)S(1)}) custom-call(s32[2]{0:T(128)S(1)} %pad_add_fusion.place_ref, bf16[8,448,256]{2,1,0:T(8,128)(2,1)S(1)} %all-to-all-done.1.refs_0_, bf16[2048,4096]{1,0:T(8,128)(2,1)} %bitcast.38, f32[1,2048]{1,0:T(1,128)S(1)} %bitcast.25), custom_call_target="tpu_custom_call" | custom-call | flops 3221225472 | bytes 9961472 | tf_op jit(solution)/shard_map/out_send/pallas_call | solution.py:437
  170.1 3.2 %collective-permute-done.8.refs_3_ = f32[384,1]{1,0:T(8,128)S(1)} collective-permute-done((f32[384,1]{1,0:T(8,128)S(1)}, f32[384,1]{1,0:T(8,128)S(1)}, u32[]{:S(2)}, u32[]{:S(2)}) %collective-permute-start.8) | collective-permute-done | bytes 1568 | tf_op jit(solution)/shard_map/ppermute | solution.py:484
  173.2 7.9 %out_finish.1 = bf16[384,2048]{1,0:T(8,128)(2,1)} custom-call(s32[2]{0:T(128)S(1)} %pad_add_fusion.place_ref, bf16[8,448,256]{2,1,0:T(8,128)(2,1)S(1)} %all-to-all-done.1.refs_0_, bf16[2048,4096]{1,0:T(8,128)(2,1)} %bitcast.39, f32[384,1]{1,0:T(8,128)S(1)} %get-tuple-element.42.refs_2_, f32[384,1]{1,0:T(8,128)S(1)} %collective-permute-done.8.refs_3_, ...), custom_call_target="tpu_custom_call" | custom-call | flops 3221225472 | bytes 9961472 | tf_op jit(solution)/shard_map/out_finish/pallas_call | solution.py:437
  181.2 3.8 %all-to-all-start.2 = ((bf16[16,24,2048]{2,1,0:T(8,128)(2,1)}), bf16[16,24,2048]{2,1,0:T(8,128)(2,1)S(1)}, u32[]{:S(2)}, u32[]{:S(2)}) async-start(bf16[16,24,2048]{2,1,0:T(8,128)(2,1)} %bitcast.40), calls=%async_computation.2 | async-start | bytes 3145728 | tf_op jit(solution)/shard_map/all_to_all | solution.py:490
  185.0 1.3 fusion
  187.3 0.9 collective-permute-done.10
  188.5 0.7 reshape.34
  189.2 27.7 %all-to-all-done.2 = bf16[16,24,2048]{2,1,0:T(8,128)(2,1)S(1)} async-done(((bf16[16,24,2048]{2,1,0:T(8,128)(2,1)}), bf16[16,24,2048]{2,1,0:T(8,128)(2,1)S(1)}, u32[]{:S(2)}, u32[]{:S(2)}) %all-to-all-start.2) | async-done | bytes 1572896 | tf_op jit(solution)/shard_map/all_to_all | solution.py:490
  216.9 2.0 collect.1
  (39 shorter events, 2.6 us)
Async XLA Ops:
  11.7 41.5 %all-to-all-start = ((bf16[16,24,2048]{2,1,0:T(8,128)(2,1)}), bf16[16,24,2048]{2,1,0:T(8,128)(2,1)S(1)}, u32[]{:S(2)}, u32[]{:S(2)}) async-start(bf16[16,24,2048]{2,1,0:T(8,128)(2,1)} %bitcast.41), calls=%async_computation | async-start | bytes 3145728 | tf_op jit(solution)/shard_map/all_to_all | solution.py:490
  19.1 72.8 %all-gather.2.cloned.1.call-start = ((), (), s32[]{:S(2)}) async-start(), calls=%async_computation.3 | async-start | bytes 1114112 | tf_op jit(solution)/shard_map/all_gather | solution.py:526
  53.2 3.8 %collective-permute-start = (bf16[384,2048]{1,0:T(8,128)(2,1)S(1)}, bf16[384,2048]{1,0:T(8,128)(2,1)S(1)}, u32[]{:S(2)}, u32[]{:S(2)}) collective-permute-start(bf16[384,2048]{1,0:T(8,128)(2,1)S(1)} %bitcast.17), channel_id=1, source_target_pairs={{0,1},{1,0},{2,3},{3,2},{4,5},{5,4},{6,7},{7,6},{8,9},{9,8},{10,11... | collective-permute-start | bytes 4718600 | tf_op jit(solution)/shard_map/ppermute | solution.py:484
  63.4 0.7 copy-start.2
  64.1 23.8 %collective-permute-start.3 = (bf16[384,256]{1,0:T(8,128)(2,1)}, bf16[384,256]{1,0:T(8,128)(2,1)S(1)}, u32[]{:S(2)}, u32[]{:S(2)}) collective-permute-start(bf16[384,256]{1,0:T(8,128)(2,1)} %get-tuple-element.33), channel_id=1, source_target_pairs={{0,6},{1,7},{2,4},{3,5},{4,2},{5,3},{6,0},{7,1},{8,14},{9,15},{10,... | collective-permute-start | bytes 589832 | tf_op jit(solution)/shard_map/ppermute | solution.py:497
  72.4 18.0 %collective-permute-start.4 = (bf16[384,256]{1,0:T(8,128)(2,1)}, bf16[384,256]{1,0:T(8,128)(2,1)S(1)}, u32[]{:S(2)}, u32[]{:S(2)}) collective-permute-start(bf16[384,256]{1,0:T(8,128)(2,1)} %get-tuple-element.34), channel_id=1, source_target_pairs={{0,8},{1,9},{2,10},{3,11},{4,12},{5,13},{6,14},{7,15},{8,0},{9,1},... | collective-permute-start | bytes 589832 | tf_op jit(solution)/shard_map/ppermute | solution.py:497
  74.8 35.2 %collective-permute-start.5 = (bf16[384,256]{1,0:T(8,128)(2,1)}, bf16[384,256]{1,0:T(8,128)(2,1)}, u32[]{:S(2)}, u32[]{:S(2)}) collective-permute-start(bf16[384,256]{1,0:T(8,128)(2,1)} %copy-done.2), channel_id=1, source_target_pairs={{0,10},{1,11},{2,8},{3,9},{4,14},{5,15},{6,12},{7,13},{8,2},{9,3},... | collective-permute-start | bytes 589832 | tf_op jit(solution)/shard_map/ppermute | solution.py:497
  79.8 30.2 %collective-permute-start.1 = (bf16[384,256]{1,0:T(8,128)(2,1)}, bf16[384,256]{1,0:T(8,128)(2,1)}, u32[]{:S(2)}, u32[]{:S(2)}) collective-permute-start(bf16[384,256]{1,0:T(8,128)(2,1)} %get-tuple-element.31), channel_id=1, source_target_pairs={{0,2},{1,3},{2,0},{3,1},{4,6},{5,7},{6,4},{7,5},{8,10},{9,11},{10,... | collective-permute-start | bytes 589832 | tf_op jit(solution)/shard_map/ppermute | solution.py:497
  83.0 8.8 %copy-start.3 = (f32[32]{0:T(128)S(1)}, f32[32]{0:T(128)}, u32[]{:S(2)}) copy-start(f32[32]{0:T(128)} %bias_ref.1) | copy-start | bytes 388
  83.0 8.8 %copy-start.4 = (f32[32]{0:T(128)S(1)}, f32[32]{0:T(128)}, u32[]{:S(2)}) copy-start(f32[32]{0:T(128)} %rate_ref.1) | copy-start | bytes 388
  83.0 27.0 %collective-permute-start.2 = (bf16[384,256]{1,0:T(8,128)(2,1)}, bf16[384,256]{1,0:T(8,128)(2,1)}, u32[]{:S(2)}, u32[]{:S(2)}) collective-permute-start(bf16[384,256]{1,0:T(8,128)(2,1)} %get-tuple-element.32), channel_id=1, source_target_pairs={{0,4},{1,5},{2,6},{3,7},{4,0},{5,1},{6,2},{7,3},{8,12},{9,13},{10,... | collective-permute-start | bytes 589832 | tf_op jit(solution)/shard_map/ppermute | solution.py:497
  87.9 22.1 %collective-permute-start.6 = (bf16[384,256]{1,0:T(8,128)(2,1)}, bf16[384,256]{1,0:T(8,128)(2,1)}, u32[]{:S(2)}, u32[]{:S(2)}) collective-permute-start(bf16[384,256]{1,0:T(8,128)(2,1)} %get-tuple-element.36), channel_id=1, source_target_pairs={{0,12},{1,13},{2,14},{3,15},{4,8},{5,9},{6,10},{7,11},{8,4},{9,5},... | collective-permute-start | bytes 589832 | tf_op jit(solution)/shard_map/ppermute | solution.py:497
  90.4 19.6 %collective-permute-start.7 = (bf16[384,256]{1,0:T(8,128)(2,1)}, bf16[384,256]{1,0:T(8,128)(2,1)}, u32[]{:S(2)}, u32[]{:S(2)}) collective-permute-start(bf16[384,256]{1,0:T(8,128)(2,1)} %get-tuple-element.37), channel_id=1, source_target_pairs={{0,14},{1,15},{2,12},{3,13},{4,10},{5,11},{6,8},{7,9},{8,6},{9,7},... | collective-permute-start | bytes 589832 | tf_op jit(solution)/shard_map/ppermute | solution.py:497
  91.9 1.2 copy-start.1
  93.1 0.7 copy-start.5
  93.7 0.7 copy-start.6
  106.6 3.4 %slice-start = ((s8[4718592]{0:T(1024)(128)(4,1)}), s8[4194304]{0:T(1024)(128)(4,1)S(1)}, s32[]{:S(2)}) async-start(s8[4718592]{0:T(1024)(128)(4,1)} %bitcast.23), calls=%async_computation.4 | async-start | bytes 8388608
  106.6 3.4 %slice-start.1 = ((s8[4718592]{0:T(1024)(128)(4,1)}), s8[524288]{0:T(1024)(128)(4,1)S(1)}, s32[]{:S(2)}) async-start(s8[4718592]{0:T(1024)(128)(4,1)} %bitcast.23), calls=%async_computation.5 | async-start | bytes 1048576
  115.9 4.7 %copy-start.7 = (f32[4096]{0:T(1024)S(1)}, f32[4096]{0:T(1024)}, u32[]{:S(2)}) copy-start(f32[4096]{0:T(1024)} %param.17) | copy-start | bytes 49156
  115.9 46.0 %all-to-all-start.1 = ((bf16[8,448,256]{2,1,0:T(8,128)(2,1)}), bf16[8,448,256]{2,1,0:T(8,128)(2,1)S(1)}, u32[]{:S(2)}, u32[]{:S(2)}) async-start(bf16[8,448,256]{2,1,0:T(8,128)(2,1)} %scan.1), calls=%async_computation.1 | async-start | bytes 3670016 | tf_op jit(solution)/shard_map/all_to_all | solution.py:490
  169.5 3.8 %collective-permute-start.9 = (bf16[384,2048]{1,0:T(8,128)(2,1)S(1)}, bf16[384,2048]{1,0:T(8,128)(2,1)S(1)}, u32[]{:S(2)}, u32[]{:S(2)}) collective-permute-start(bf16[384,2048]{1,0:T(8,128)(2,1)S(1)} %bitcast.29), channel_id=1, source_target_pairs={{0,1},{1,0},{2,3},{3,2},{4,5},{5,4},{6,7},{7,6},{8,9},{9,8},{10,11... | collective-permute-start | bytes 4718600 | tf_op jit(solution)/shard_map/ppermute | solution.py:484
  169.6 3.7 %collective-permute-start.8 = (f32[384,1]{1,0:T(8,128)S(1)}, f32[384,1]{1,0:T(8,128)S(1)}, u32[]{:S(2)}, u32[]{:S(2)}) collective-permute-start(f32[384,1]{1,0:T(8,128)S(1)} %get-tuple-element.42.refs_2_), channel_id=1, source_target_pairs={{0,1},{1,0},{2,3},{3,2},{4,5},{5,4},{6,7},{7,6},{8,9},{9,8},{10,11... | collective-permute-start | bytes 4616 | tf_op jit(solution)/shard_map/ppermute | solution.py:484
  181.2 35.8 %copy-start = (s32[128,1]{0,1:T(1,128)S(1)}, s32[128,1]{0,1:T(1,128)}, u32[]{:S(2)}) copy-start(s32[128,1]{0,1:T(1,128)} %param.18) | copy-start | bytes 1540
  181.2 35.8 %all-to-all-start.2 = ((bf16[16,24,2048]{2,1,0:T(8,128)(2,1)}), bf16[16,24,2048]{2,1,0:T(8,128)(2,1)S(1)}, u32[]{:S(2)}, u32[]{:S(2)}) async-start(bf16[16,24,2048]{2,1,0:T(8,128)(2,1)} %bitcast.40), calls=%async_computation.2 | async-start | bytes 3145728 | tf_op jit(solution)/shard_map/all_to_all | solution.py:490
  187.1 1.2 collective-permute-start.10
Sparse Core Ops, SparseCore 0:
  22.1 47.0 all-gather.1

commit v12 on v11

--- a/solution.py
+++ b/solution.py
@@ -258,7 +258,7 @@
         grid=(pairs,),
         in_specs=[smem] * 5 + [pl.BlockSpec((PAIR, PACK), lambda p: (p, 0))],
         out_specs=(block(slots, slots), block(slots, NS), block(NS, slots), block(8, 128)),
-        compiler_params=params(),
+        compiler_params=params(56 * 1024 * 1024),
         cost_estimate=pl.CostEstimate(
             flops=4 * heads * pairs * slots * slots * PAIR,
             bytes_accessed=2 * heads * pairs * slots * slots,

time: 230 us -> 229 us (level)
  local copies, waits for them, and re-layouts: 4.89 us -> 2.53 us
    unnamed x20, local copies, waits for them, and re-layouts: 3.23 us -> 0.86 us
where the time goes in v12:
time: 229 us; the launch traced here: 225 us
  waiting for transfers between devices  111 us (48%)
  Pallas kernels  59.4 us (26%)
  starting transfers between devices  34.4 us (15%)
  between operations  15.6 us (7%)
  local copies, waits for them, and re-layouts  2.53 us (1%)
    all_to_all x3, waiting for transfers between devices, swap(): lax.all_to_all(a, 'expert', split_axis=0, concat_axis=0, axis_index_group...  103 us
    pallas_call x4, Pallas kernels, in_projection(): pl.pallas_call(functools.partial(in_kernel, slices, shares, turns), out_s...  19.7 us
    ppermute x7, starting transfers between devices, across(): return lax.ppermute(a, 'expert', pairs)  16.6 us
    all_to_all x3, starting transfers between devices, swap(): lax.all_to_all(a, 'expert', split_axis=0, concat_axis=0, axis_index_group...  16.1 us
    pallas_call x2, Pallas kernels, out_projection(): pl.pallas_call(functools.partial(out_kernel, kind, inverse is not None, l...  15.4 us
    pallas_call x1, Pallas kernels, prepare(): pl.pallas_call(functools.partial(prep_kernel, heads), out_shape=(jax.Shap...  12.6 us
    ppermute x4, waiting for transfers between devices, turn(): lax.ppermute(a, 'expert', [(d, d // slices * slices + (d + r) % slices) f...  6.98 us
    pallas_call x1, Pallas kernels, scan(): pl.pallas_call(functools.partial(scan_kernel, heads), out_shape=pltpu.HBM...  5.8 us
  transfers between devices with their start and end apart: 15, of which 6 were waited for; matrix products, arithmetic and copies ran while one was open for 2% of the time, Pallas kernels for 14%

profile of v12, /device:TPU:0, one launch (start us, length us, event | category | flops | bytes accessed | tf_op | source)
XLA Modules:
  0.0 224.7 jit_solution(564981354446422815)
XLA Ops:
  7.8 3.9 %dispatch.1 = (bf16[128,256]{1,0:T(8,128)(2,1)}, bf16[384,2048]{1,0:T(8,128)(2,1)}) custom-call(s32[1]{0:T(128)S(6)} %copy.13.refs_0_, s32[1,128]{1,0:T(1,128)} %bitcast.27, bf16[128,4096]{1,0:T(8,128)(2,1)} %refs_2_.1, bf16[160,4096]{1,0:T(8,128)(2,1)} %bitcast.42), custom_call_target="tpu_custom_call" | custom-call | tf_op jit(solution)/shard_map/dispatch/pallas_call | solution.py:101
  11.7 7.4 %all-to-all-start = ((bf16[16,24,2048]{2,1,0:T(8,128)(2,1)}), bf16[16,24,2048]{2,1,0:T(8,128)(2,1)S(1)}, u32[]{:S(2)}, u32[]{:S(2)}) async-start(bf16[16,24,2048]{2,1,0:T(8,128)(2,1)} %bitcast.41), calls=%async_computation | async-start | bytes 3145728 | tf_op jit(solution)/shard_map/all_to_all | solution.py:490
  19.1 0.7 all-gather.2.cloned.1.call-update
  19.8 33.3 %all-to-all-done = bf16[16,24,2048]{2,1,0:T(8,128)(2,1)S(1)} async-done(((bf16[16,24,2048]{2,1,0:T(8,128)(2,1)}), bf16[16,24,2048]{2,1,0:T(8,128)(2,1)S(1)}, u32[]{:S(2)}, u32[]{:S(2)}) %all-to-all-start) | async-done | bytes 1572896 | tf_op jit(solution)/shard_map/all_to_all | solution.py:490
  53.2 0.8 collective-permute-start
  54.0 3.0 %collective-permute-done.refs_1_ = bf16[384,2048]{1,0:T(8,128)(2,1)S(1)} collective-permute-done((bf16[384,2048]{1,0:T(8,128)(2,1)S(1)}, bf16[384,2048]{1,0:T(8,128)(2,1)S(1)}, u32[]{:S(2)}, u32[]{:S(2)}) %collective-permute-start) | collective-permute-done | bytes 1572896 | tf_op jit(solution)/shard_map/ppermute | solution.py:484
  57.0 6.5 %in_projection.6 = (bf16[384,256]{1,0:T(8,128)(2,1)S(1)}, bf16[384,256]{1,0:T(8,128)(2,1)}, bf16[384,256]{1,0:T(8,128)(2,1)}) custom-call(s32[2]{0:T(128)S(1)} %pad_add_fusion.place_ref, bf16[384,2048]{1,0:T(8,128)(2,1)S(1)} %bitcast.18, bf16[384,2048]{1,0:T(8,128)(2,1)S(1)} %collective-permute-done.refs_1_, bf16[4096,2048]{1,0:T(8,128)(2,1)} %bitcast.30, ...), custom_call_target="tpu_custom_call" | custom-call | flops 384 | bytes 384 | tf_op jit(solution)/shard_map/in_projection/pallas_call | solution.py:147
  63.5 0.7 copy-done.6
  64.1 8.3 %collective-permute-start.3 = (bf16[384,256]{1,0:T(8,128)(2,1)}, bf16[384,256]{1,0:T(8,128)(2,1)S(1)}, u32[]{:S(2)}, u32[]{:S(2)}) collective-permute-start(bf16[384,256]{1,0:T(8,128)(2,1)} %get-tuple-element.33), channel_id=1, source_target_pairs={{0,6},{1,7},{2,4},{3,5},{4,2},{5,3},{6,0},{7,1},{8,14},{9,15},{10,... | collective-permute-start | bytes 589832 | tf_op jit(solution)/shard_map/ppermute | solution.py:497
  72.4 1.0 collective-permute-start.4
  73.5 0.8 dynamic_slice.15
  74.2 0.6 iota_add_fusion.head_ref
  74.9 4.9 %in_projection.5 = (bf16[384,256]{1,0:T(8,128)(2,1)}, bf16[384,256]{1,0:T(8,128)(2,1)}) custom-call(s32[2]{0:T(128)S(1)} %pad_add_fusion.place_ref, bf16[384,2048]{1,0:T(8,128)(2,1)S(1)} %bitcast.19, bf16[384,2048]{1,0:T(8,128)(2,1)S(1)} %collective-permute-done.refs_1_, bf16[4096,2048]{1,0:T(8,128)(2,1)} %bitcast.32, bf16[4096,2048]{1,0:T(8,128)(2,1)} %bitcast.33), custom_call_target="tpu_custom_call" | custom-call | flops 384 | bytes 384 | tf_op jit(solution)/shard_map/in_projection/pallas_call | solution.py:147
  79.8 3.3 %collective-permute-start.1 = (bf16[384,256]{1,0:T(8,128)(2,1)}, bf16[384,256]{1,0:T(8,128)(2,1)}, u32[]{:S(2)}, u32[]{:S(2)}) collective-permute-start(bf16[384,256]{1,0:T(8,128)(2,1)} %get-tuple-element.31), channel_id=1, source_target_pairs={{0,2},{1,3},{2,0},{3,1},{4,6},{5,7},{6,4},{7,5},{8,10},{9,11},{10,... | collective-permute-start | bytes 589832 | tf_op jit(solution)/shard_map/ppermute | solution.py:497
  83.1 4.9 %in_projection.7 = (bf16[384,256]{1,0:T(8,128)(2,1)}, bf16[384,256]{1,0:T(8,128)(2,1)}) custom-call(s32[2]{0:T(128)S(1)} %pad_add_fusion.place_ref, bf16[384,2048]{1,0:T(8,128)(2,1)S(1)} %bitcast.20, bf16[384,2048]{1,0:T(8,128)(2,1)S(1)} %collective-permute-done.refs_1_, bf16[4096,2048]{1,0:T(8,128)(2,1)} %bitcast.34, bf16[4096,2048]{1,0:T(8,128)(2,1)} %bitcast.35), custom_call_target="tpu_custom_call" | custom-call | flops 384 | bytes 384 | tf_op jit(solution)/shard_map/in_projection/pallas_call | solution.py:147
  88.0 2.5 %collective-permute-start.6 = (bf16[384,256]{1,0:T(8,128)(2,1)}, bf16[384,256]{1,0:T(8,128)(2,1)}, u32[]{:S(2)}, u32[]{:S(2)}) collective-permute-start(bf16[384,256]{1,0:T(8,128)(2,1)} %get-tuple-element.36), channel_id=1, source_target_pairs={{0,12},{1,13},{2,14},{3,15},{4,8},{5,9},{6,10},{7,11},{8,4},{9,5},... | collective-permute-start | bytes 589832 | tf_op jit(solution)/shard_map/ppermute | solution.py:497
  90.5 1.4 collective-permute-start.7
  91.9 12.6 %scan_weights.1 = (bf16[2,8,384,384]{3,2,1,0:T(8,128)(2,1)}, bf16[2,8,384,64]{3,2,1,0:T(8,128)(2,1)}, bf16[2,8,64,384]{3,2,1,0:T(8,128)(2,1)}, f32[2,8,8,128]{3,2,1,0:T(8,128)}) custom-call(s32[2]{0:T(128)} %copy-done.3, s32[2]{0:T(128)} %iota_add_fusion.head_ref, f32[32]{0:T(128)} %bias_ref.1, f32[32]{0:T(128)} %rate_ref.1, f32[32]{0:T(128)} %skip_ref.1, ...), custom_call_target="tpu_custom_call" | custom-call | flops 2415919104 | bytes 4718592 | tf_op jit(solution)/shard_map/scan_weights/pallas_call | solution.py:250
  104.6 3.4 %in_projection.4.refs_0_ = bf16[384,256]{1,0:T(8,128)(2,1)S(1)} custom-call(s32[2]{0:T(128)S(1)} %copy-done.4, bf16[384,2048]{1,0:T(8,128)(2,1)S(1)} %bitcast.21, bf16[384,2048]{1,0:T(8,128)(2,1)S(1)} %collective-permute-done.refs_1_, bf16[4096,2048]{1,0:T(8,128)(2,1)} %bitcast.36, bf16[4096,2048]{1,0:T(8,128)(2,1)} %bitcast.37), custom_call_target="tpu_custom_call" | custom-call | flops 384 | bytes 384 | tf_op jit(solution)/shard_map/in_projection/pallas_call | solution.py:147
  108.2 5.8 %scan.1 = bf16[8,448,256]{2,1,0:T(8,128)(2,1)} custom-call(s32[2]{0:T(128)S(1)} %copy-done.4, bf16[384,256]{1,0:T(8,128)(2,1)S(1)} %in_projection.4.refs_0_, bf16[384,256]{1,0:T(8,128)(2,1)} %collective-permute-done.1.refs_1_, bf16[384,256]{1,0:T(8,128)(2,1)} %collective-permute-done.2.refs_2_, bf16[384,256]{1,0:T(8,128)(2,1)S(1)} %collective-permute-done.3.refs_3_, ...), custom_call_target="tpu_custom_call" | custom-call | flops 805306368 | bytes 4718592 | tf_op jit(solution)/shard_map/scan/pallas_call | solution.py:320
  114.0 4.8 %all-to-all-start.1 = ((bf16[8,448,256]{2,1,0:T(8,128)(2,1)}), bf16[8,448,256]{2,1,0:T(8,128)(2,1)S(1)}, u32[]{:S(2)}, u32[]{:S(2)}) async-start(bf16[8,448,256]{2,1,0:T(8,128)(2,1)} %scan.1), calls=%async_computation.1 | async-start | bytes 3670016 | tf_op jit(solution)/shard_map/all_to_all | solution.py:490
  118.8 42.0 %all-to-all-done.1.refs_0_ = bf16[8,448,256]{2,1,0:T(8,128)(2,1)S(1)} async-done(((bf16[8,448,256]{2,1,0:T(8,128)(2,1)}), bf16[8,448,256]{2,1,0:T(8,128)(2,1)S(1)}, u32[]{:S(2)}, u32[]{:S(2)}) %all-to-all-start.1) | async-done | bytes 1835040 | tf_op jit(solution)/shard_map/all_to_all | solution.py:490
  160.8 7.5 %out_send.1 = (bf16[1,384,2048]{2,1,0:T(8,128)(2,1)S(1)}, f32[384,1]{1,0:T(8,128)S(1)}) custom-call(s32[2]{0:T(128)S(1)} %copy-done.4, bf16[8,448,256]{2,1,0:T(8,128)(2,1)S(1)} %all-to-all-done.1.refs_0_, bf16[2048,4096]{1,0:T(8,128)(2,1)} %bitcast.38, f32[1,2048]{1,0:T(1,128)S(1)} %bitcast.25), custom_call_target="tpu_custom_call" | custom-call | flops 3221225472 | bytes 9961472 | tf_op jit(solution)/shard_map/out_send/pallas_call | solution.py:437
  168.4 0.5 collective-permute-start.8
  168.9 3.2 %collective-permute-done.8.refs_3_ = f32[384,1]{1,0:T(8,128)S(1)} collective-permute-done((f32[384,1]{1,0:T(8,128)S(1)}, f32[384,1]{1,0:T(8,128)S(1)}, u32[]{:S(2)}, u32[]{:S(2)}) %collective-permute-start.8) | collective-permute-done | bytes 1568 | tf_op jit(solution)/shard_map/ppermute | solution.py:484
  172.1 7.9 %out_finish.1 = bf16[384,2048]{1,0:T(8,128)(2,1)} custom-call(s32[2]{0:T(128)S(1)} %copy-done.4, bf16[8,448,256]{2,1,0:T(8,128)(2,1)S(1)} %all-to-all-done.1.refs_0_, bf16[2048,4096]{1,0:T(8,128)(2,1)} %bitcast.39, f32[384,1]{1,0:T(8,128)S(1)} %get-tuple-element.42.refs_2_, f32[384,1]{1,0:T(8,128)S(1)} %collective-permute-done.8.refs_3_, ...), custom_call_target="tpu_custom_call" | custom-call | flops 3221225472 | bytes 9961472 | tf_op jit(solution)/shard_map/out_finish/pallas_call | solution.py:437
  180.0 3.9 %all-to-all-start.2 = ((bf16[16,24,2048]{2,1,0:T(8,128)(2,1)}), bf16[16,24,2048]{2,1,0:T(8,128)(2,1)S(1)}, u32[]{:S(2)}, u32[]{:S(2)}) async-start(bf16[16,24,2048]{2,1,0:T(8,128)(2,1)} %bitcast.40), calls=%async_computation.2 | async-start | bytes 3145728 | tf_op jit(solution)/shard_map/all_to_all | solution.py:490
  183.9 1.3 fusion
  186.3 0.8 collective-permute-done.10
  187.3 0.7 reshape.34
  188.1 27.8 %all-to-all-done.2 = bf16[16,24,2048]{2,1,0:T(8,128)(2,1)S(1)} async-done(((bf16[16,24,2048]{2,1,0:T(8,128)(2,1)}), bf16[16,24,2048]{2,1,0:T(8,128)(2,1)S(1)}, u32[]{:S(2)}, u32[]{:S(2)}) %all-to-all-start.2) | async-done | bytes 1572896 | tf_op jit(solution)/shard_map/all_to_all | solution.py:490
  215.8 2.0 collect.1
  (39 shorter events, 1.1 us)
Async XLA Ops:
  11.7 41.5 %all-to-all-start = ((bf16[16,24,2048]{2,1,0:T(8,128)(2,1)}), bf16[16,24,2048]{2,1,0:T(8,128)(2,1)S(1)}, u32[]{:S(2)}, u32[]{:S(2)}) async-start(bf16[16,24,2048]{2,1,0:T(8,128)(2,1)} %bitcast.41), calls=%async_computation | async-start | bytes 3145728 | tf_op jit(solution)/shard_map/all_to_all | solution.py:490
  19.1 72.8 %all-gather.2.cloned.1.call-start = ((), (), s32[]{:S(2)}) async-start(), calls=%async_computation.3 | async-start | bytes 1114112 | tf_op jit(solution)/shard_map/all_gather | solution.py:526
  53.2 3.8 %collective-permute-start = (bf16[384,2048]{1,0:T(8,128)(2,1)S(1)}, bf16[384,2048]{1,0:T(8,128)(2,1)S(1)}, u32[]{:S(2)}, u32[]{:S(2)}) collective-permute-start(bf16[384,2048]{1,0:T(8,128)(2,1)S(1)} %bitcast.17), channel_id=1, source_target_pairs={{0,1},{1,0},{2,3},{3,2},{4,5},{5,4},{6,7},{7,6},{8,9},{9,8},{10,11... | collective-permute-start | bytes 4718600 | tf_op jit(solution)/shard_map/ppermute | solution.py:484
  54.0 29.1 %copy-start.3 = (s32[2]{0:T(128)}, s32[2]{0:T(128)S(1)}, u32[]{:S(2)}) copy-start(s32[2]{0:T(128)S(1)} %pad_add_fusion.place_ref) | copy-start | bytes 28
  63.5 0.7 copy-start.6
  64.1 23.8 %collective-permute-start.3 = (bf16[384,256]{1,0:T(8,128)(2,1)}, bf16[384,256]{1,0:T(8,128)(2,1)S(1)}, u32[]{:S(2)}, u32[]{:S(2)}) collective-permute-start(bf16[384,256]{1,0:T(8,128)(2,1)} %get-tuple-element.33), channel_id=1, source_target_pairs={{0,6},{1,7},{2,4},{3,5},{4,2},{5,3},{6,0},{7,1},{8,14},{9,15},{10,... | collective-permute-start | bytes 589832 | tf_op jit(solution)/shard_map/ppermute | solution.py:497
  72.4 18.0 %collective-permute-start.4 = (bf16[384,256]{1,0:T(8,128)(2,1)}, bf16[384,256]{1,0:T(8,128)(2,1)S(1)}, u32[]{:S(2)}, u32[]{:S(2)}) collective-permute-start(bf16[384,256]{1,0:T(8,128)(2,1)} %get-tuple-element.34), channel_id=1, source_target_pairs={{0,8},{1,9},{2,10},{3,11},{4,12},{5,13},{6,14},{7,15},{8,0},{9,1},... | collective-permute-start | bytes 589832 | tf_op jit(solution)/shard_map/ppermute | solution.py:497
  74.8 33.1 %collective-permute-start.5 = (bf16[384,256]{1,0:T(8,128)(2,1)}, bf16[384,256]{1,0:T(8,128)(2,1)}, u32[]{:S(2)}, u32[]{:S(2)}) collective-permute-start(bf16[384,256]{1,0:T(8,128)(2,1)} %copy-done.6), channel_id=1, source_target_pairs={{0,10},{1,11},{2,8},{3,9},{4,14},{5,15},{6,12},{7,13},{8,2},{9,3},... | collective-permute-start | bytes 589832 | tf_op jit(solution)/shard_map/ppermute | solution.py:497
  79.8 28.1 %collective-permute-start.1 = (bf16[384,256]{1,0:T(8,128)(2,1)}, bf16[384,256]{1,0:T(8,128)(2,1)}, u32[]{:S(2)}, u32[]{:S(2)}) collective-permute-start(bf16[384,256]{1,0:T(8,128)(2,1)} %get-tuple-element.31), channel_id=1, source_target_pairs={{0,2},{1,3},{2,0},{3,1},{4,6},{5,7},{6,4},{7,5},{8,10},{9,11},{10,... | collective-permute-start | bytes 589832 | tf_op jit(solution)/shard_map/ppermute | solution.py:497
  83.1 24.9 %collective-permute-start.2 = (bf16[384,256]{1,0:T(8,128)(2,1)}, bf16[384,256]{1,0:T(8,128)(2,1)}, u32[]{:S(2)}, u32[]{:S(2)}) collective-permute-start(bf16[384,256]{1,0:T(8,128)(2,1)} %get-tuple-element.32), channel_id=1, source_target_pairs={{0,4},{1,5},{2,6},{3,7},{4,0},{5,1},{6,2},{7,3},{8,12},{9,13},{10,... | collective-permute-start | bytes 589832 | tf_op jit(solution)/shard_map/ppermute | solution.py:497
  88.0 20.0 %collective-permute-start.6 = (bf16[384,256]{1,0:T(8,128)(2,1)}, bf16[384,256]{1,0:T(8,128)(2,1)}, u32[]{:S(2)}, u32[]{:S(2)}) collective-permute-start(bf16[384,256]{1,0:T(8,128)(2,1)} %get-tuple-element.36), channel_id=1, source_target_pairs={{0,12},{1,13},{2,14},{3,15},{4,8},{5,9},{6,10},{7,11},{8,4},{9,5},... | collective-permute-start | bytes 589832 | tf_op jit(solution)/shard_map/ppermute | solution.py:497
  90.5 14.0 %copy-start.4 = (s32[2]{0:T(128)S(1)}, s32[2]{0:T(128)}, u32[]{:S(2)}) copy-start(s32[2]{0:T(128)} %copy-done.3) | copy-start | bytes 28
  90.5 17.5 %collective-permute-start.7 = (bf16[384,256]{1,0:T(8,128)(2,1)}, bf16[384,256]{1,0:T(8,128)(2,1)}, u32[]{:S(2)}, u32[]{:S(2)}) collective-permute-start(bf16[384,256]{1,0:T(8,128)(2,1)} %get-tuple-element.37), channel_id=1, source_target_pairs={{0,14},{1,15},{2,12},{3,13},{4,10},{5,11},{6,8},{7,9},{8,6},{9,7},... | collective-permute-start | bytes 589832 | tf_op jit(solution)/shard_map/ppermute | solution.py:497
  104.5 3.5 %slice-start = ((s8[4718592]{0:T(1024)(128)(4,1)}), s8[4194304]{0:T(1024)(128)(4,1)S(1)}, s32[]{:S(2)}) async-start(s8[4718592]{0:T(1024)(128)(4,1)} %bitcast.23), calls=%async_computation.4 | async-start | bytes 8388608
  104.5 3.5 %slice-start.1 = ((s8[4718592]{0:T(1024)(128)(4,1)}), s8[524288]{0:T(1024)(128)(4,1)S(1)}, s32[]{:S(2)}) async-start(s8[4718592]{0:T(1024)(128)(4,1)} %bitcast.23), calls=%async_computation.5 | async-start | bytes 1048576
  104.5 3.5 %copy-start = (bf16[2,8,384,64]{3,2,1,0:T(8,128)(2,1)S(1)}, bf16[2,8,384,64]{3,2,1,0:T(8,128)(2,1)}, u32[]{:S(2)}) copy-start(bf16[2,8,384,64]{3,2,1,0:T(8,128)(2,1)} %get-tuple-element.39.refs_9_) | copy-start | bytes 2359300
  104.5 3.6 %copy-start.1 = (bf16[2,8,64,384]{3,2,1,0:T(8,128)(2,1)S(1)}, bf16[2,8,64,384]{3,2,1,0:T(8,128)(2,1)}, u32[]{:S(2)}) copy-start(bf16[2,8,64,384]{3,2,1,0:T(8,128)(2,1)} %get-tuple-element.40.refs_10_) | copy-start | bytes 2359300
  104.5 3.6 %copy-start.2 = (f32[2,8,8,128]{3,2,1,0:T(8,128)S(1)}, f32[2,8,8,128]{3,2,1,0:T(8,128)}, u32[]{:S(2)}) copy-start(f32[2,8,8,128]{3,2,1,0:T(8,128)} %get-tuple-element.41.refs_11_) | copy-start | bytes 196612
  114.0 4.8 %copy-start.7 = (f32[4096]{0:T(1024)S(1)}, f32[4096]{0:T(1024)}, u32[]{:S(2)}) copy-start(f32[4096]{0:T(1024)} %param.17) | copy-start | bytes 49156
  114.0 46.8 %all-to-all-start.1 = ((bf16[8,448,256]{2,1,0:T(8,128)(2,1)}), bf16[8,448,256]{2,1,0:T(8,128)(2,1)S(1)}, u32[]{:S(2)}, u32[]{:S(2)}) async-start(bf16[8,448,256]{2,1,0:T(8,128)(2,1)} %scan.1), calls=%async_computation.1 | async-start | bytes 3670016 | tf_op jit(solution)/shard_map/all_to_all | solution.py:490
  168.3 3.8 %collective-permute-start.9 = (bf16[384,2048]{1,0:T(8,128)(2,1)S(1)}, bf16[384,2048]{1,0:T(8,128)(2,1)S(1)}, u32[]{:S(2)}, u32[]{:S(2)}) collective-permute-start(bf16[384,2048]{1,0:T(8,128)(2,1)S(1)} %bitcast.29), channel_id=1, source_target_pairs={{0,1},{1,0},{2,3},{3,2},{4,5},{5,4},{6,7},{7,6},{8,9},{9,8},{10,11... | collective-permute-start | bytes 4718600 | tf_op jit(solution)/shard_map/ppermute | solution.py:484
  168.4 3.7 %collective-permute-start.8 = (f32[384,1]{1,0:T(8,128)S(1)}, f32[384,1]{1,0:T(8,128)S(1)}, u32[]{:S(2)}, u32[]{:S(2)}) collective-permute-start(f32[384,1]{1,0:T(8,128)S(1)} %get-tuple-element.42.refs_2_), channel_id=1, source_target_pairs={{0,1},{1,0},{2,3},{3,2},{4,5},{5,4},{6,7},{7,6},{8,9},{9,8},{10,11... | collective-permute-start | bytes 4616 | tf_op jit(solution)/shard_map/ppermute | solution.py:484
  180.0 35.9 %copy-start.5 = (s32[128,1]{0,1:T(1,128)S(1)}, s32[128,1]{0,1:T(1,128)}, u32[]{:S(2)}) copy-start(s32[128,1]{0,1:T(1,128)} %param.18) | copy-start | bytes 1540
  180.0 35.9 %all-to-all-start.2 = ((bf16[16,24,2048]{2,1,0:T(8,128)(2,1)}), bf16[16,24,2048]{2,1,0:T(8,128)(2,1)S(1)}, u32[]{:S(2)}, u32[]{:S(2)}) async-start(bf16[16,24,2048]{2,1,0:T(8,128)(2,1)} %bitcast.40), calls=%async_computation.2 | async-start | bytes 3145728 | tf_op jit(solution)/shard_map/all_to_all | solution.py:490
  185.9 1.2 collective-permute-start.10
Sparse Core Ops, SparseCore 0:
  22.1 47.0 all-gather.1

commit v13 on v12

--- a/solution.py
+++ b/solution.py
@@ -311,7 +311,7 @@
     rows, units = x[0].shape
     width = units // heads
     pairs = rows // (2 * CAP)
-    step = 2
+    step = 4
     slots = 2 * CAP * EXPERTS
 
     def block(*dims):

time: 229 us -> 228 us (level)
  no operation moved by 1% of the time
where the time goes in v13:
time: 228 us; the launch traced here: 224 us
  waiting for transfers between devices  111 us (49%)
  Pallas kernels  58.8 us (26%)
  starting transfers between devices  34.4 us (15%)
  between operations  15.6 us (7%)
  local copies, waits for them, and re-layouts  2.53 us (1%)
    all_to_all x3, waiting for transfers between devices, swap(): lax.all_to_all(a, 'expert', split_axis=0, concat_axis=0, axis_index_group...  103 us
    pallas_call x4, Pallas kernels, in_projection(): pl.pallas_call(functools.partial(in_kernel, slices, shares, turns), out_s...  19.7 us
    ppermute x7, starting transfers between devices, across(): return lax.ppermute(a, 'expert', pairs)  16.6 us
    all_to_all x3, starting transfers between devices, swap(): lax.all_to_all(a, 'expert', split_axis=0, concat_axis=0, axis_index_group...  16.1 us
    pallas_call x2, Pallas kernels, out_projection(): pl.pallas_call(functools.partial(out_kernel, kind, inverse is not None, l...  15.4 us
    pallas_call x1, Pallas kernels, prepare(): pl.pallas_call(functools.partial(prep_kernel, heads), out_shape=(jax.Shap...  12.6 us
    ppermute x4, waiting for transfers between devices, turn(): lax.ppermute(a, 'expert', [(d, d // slices * slices + (d + r) % slices) f...  6.98 us
    pallas_call x1, Pallas kernels, scan(): pl.pallas_call(functools.partial(scan_kernel, heads), out_shape=pltpu.HBM...  5.22 us
  transfers between devices with their start and end apart: 15, of which 6 were waited for; matrix products, arithmetic and copies ran while one was open for 2% of the time, Pallas kernels for 14%

profile of v13, /device:TPU:0, one launch (start us, length us, event | category | flops | bytes accessed | tf_op | source)
XLA Modules:
  0.0 224.2 jit_solution(6573394945429721258)
XLA Ops:
  7.8 3.9 %dispatch.1 = (bf16[128,256]{1,0:T(8,128)(2,1)}, bf16[384,2048]{1,0:T(8,128)(2,1)}) custom-call(s32[1]{0:T(128)S(6)} %copy.13.refs_0_, s32[1,128]{1,0:T(1,128)} %bitcast.27, bf16[128,4096]{1,0:T(8,128)(2,1)} %refs_2_.1, bf16[160,4096]{1,0:T(8,128)(2,1)} %bitcast.42), custom_call_target="tpu_custom_call" | custom-call | tf_op jit(solution)/shard_map/dispatch/pallas_call | solution.py:101
  11.7 7.4 %all-to-all-start = ((bf16[16,24,2048]{2,1,0:T(8,128)(2,1)}), bf16[16,24,2048]{2,1,0:T(8,128)(2,1)S(1)}, u32[]{:S(2)}, u32[]{:S(2)}) async-start(bf16[16,24,2048]{2,1,0:T(8,128)(2,1)} %bitcast.41), calls=%async_computation | async-start | bytes 3145728 | tf_op jit(solution)/shard_map/all_to_all | solution.py:490
  19.1 0.7 all-gather.2.cloned.1.call-update
  19.8 33.3 %all-to-all-done = bf16[16,24,2048]{2,1,0:T(8,128)(2,1)S(1)} async-done(((bf16[16,24,2048]{2,1,0:T(8,128)(2,1)}), bf16[16,24,2048]{2,1,0:T(8,128)(2,1)S(1)}, u32[]{:S(2)}, u32[]{:S(2)}) %all-to-all-start) | async-done | bytes 1572896 | tf_op jit(solution)/shard_map/all_to_all | solution.py:490
  53.2 0.8 collective-permute-start
  54.0 3.0 %collective-permute-done.refs_1_ = bf16[384,2048]{1,0:T(8,128)(2,1)S(1)} collective-permute-done((bf16[384,2048]{1,0:T(8,128)(2,1)S(1)}, bf16[384,2048]{1,0:T(8,128)(2,1)S(1)}, u32[]{:S(2)}, u32[]{:S(2)}) %collective-permute-start) | collective-permute-done | bytes 1572896 | tf_op jit(solution)/shard_map/ppermute | solution.py:484
  57.0 6.5 %in_projection.6 = (bf16[384,256]{1,0:T(8,128)(2,1)S(1)}, bf16[384,256]{1,0:T(8,128)(2,1)}, bf16[384,256]{1,0:T(8,128)(2,1)}) custom-call(s32[2]{0:T(128)S(1)} %pad_add_fusion.place_ref, bf16[384,2048]{1,0:T(8,128)(2,1)S(1)} %bitcast.18, bf16[384,2048]{1,0:T(8,128)(2,1)S(1)} %collective-permute-done.refs_1_, bf16[4096,2048]{1,0:T(8,128)(2,1)} %bitcast.30, ...), custom_call_target="tpu_custom_call" | custom-call | flops 384 | bytes 384 | tf_op jit(solution)/shard_map/in_projection/pallas_call | solution.py:147
  63.5 0.7 copy-done.6
  64.1 8.3 %collective-permute-start.3 = (bf16[384,256]{1,0:T(8,128)(2,1)}, bf16[384,256]{1,0:T(8,128)(2,1)S(1)}, u32[]{:S(2)}, u32[]{:S(2)}) collective-permute-start(bf16[384,256]{1,0:T(8,128)(2,1)} %get-tuple-element.33), channel_id=1, source_target_pairs={{0,6},{1,7},{2,4},{3,5},{4,2},{5,3},{6,0},{7,1},{8,14},{9,15},{10,... | collective-permute-start | bytes 589832 | tf_op jit(solution)/shard_map/ppermute | solution.py:497
  72.4 1.0 collective-permute-start.4
  73.5 0.8 dynamic_slice.15
  74.2 0.6 iota_add_fusion.head_ref
  74.9 4.9 %in_projection.5 = (bf16[384,256]{1,0:T(8,128)(2,1)}, bf16[384,256]{1,0:T(8,128)(2,1)}) custom-call(s32[2]{0:T(128)S(1)} %pad_add_fusion.place_ref, bf16[384,2048]{1,0:T(8,128)(2,1)S(1)} %bitcast.19, bf16[384,2048]{1,0:T(8,128)(2,1)S(1)} %collective-permute-done.refs_1_, bf16[4096,2048]{1,0:T(8,128)(2,1)} %bitcast.32, bf16[4096,2048]{1,0:T(8,128)(2,1)} %bitcast.33), custom_call_target="tpu_custom_call" | custom-call | flops 384 | bytes 384 | tf_op jit(solution)/shard_map/in_projection/pallas_call | solution.py:147
  79.8 3.3 %collective-permute-start.1 = (bf16[384,256]{1,0:T(8,128)(2,1)}, bf16[384,256]{1,0:T(8,128)(2,1)}, u32[]{:S(2)}, u32[]{:S(2)}) collective-permute-start(bf16[384,256]{1,0:T(8,128)(2,1)} %get-tuple-element.31), channel_id=1, source_target_pairs={{0,2},{1,3},{2,0},{3,1},{4,6},{5,7},{6,4},{7,5},{8,10},{9,11},{10,... | collective-permute-start | bytes 589832 | tf_op jit(solution)/shard_map/ppermute | solution.py:497
  83.1 4.9 %in_projection.7 = (bf16[384,256]{1,0:T(8,128)(2,1)}, bf16[384,256]{1,0:T(8,128)(2,1)}) custom-call(s32[2]{0:T(128)S(1)} %pad_add_fusion.place_ref, bf16[384,2048]{1,0:T(8,128)(2,1)S(1)} %bitcast.20, bf16[384,2048]{1,0:T(8,128)(2,1)S(1)} %collective-permute-done.refs_1_, bf16[4096,2048]{1,0:T(8,128)(2,1)} %bitcast.34, bf16[4096,2048]{1,0:T(8,128)(2,1)} %bitcast.35), custom_call_target="tpu_custom_call" | custom-call | flops 384 | bytes 384 | tf_op jit(solution)/shard_map/in_projection/pallas_call | solution.py:147
  88.0 2.5 %collective-permute-start.6 = (bf16[384,256]{1,0:T(8,128)(2,1)}, bf16[384,256]{1,0:T(8,128)(2,1)}, u32[]{:S(2)}, u32[]{:S(2)}) collective-permute-start(bf16[384,256]{1,0:T(8,128)(2,1)} %get-tuple-element.36), channel_id=1, source_target_pairs={{0,12},{1,13},{2,14},{3,15},{4,8},{5,9},{6,10},{7,11},{8,4},{9,5},... | collective-permute-start | bytes 589832 | tf_op jit(solution)/shard_map/ppermute | solution.py:497
  90.5 1.4 collective-permute-start.7
  91.9 12.6 %scan_weights.1 = (bf16[2,8,384,384]{3,2,1,0:T(8,128)(2,1)}, bf16[2,8,384,64]{3,2,1,0:T(8,128)(2,1)}, bf16[2,8,64,384]{3,2,1,0:T(8,128)(2,1)}, f32[2,8,8,128]{3,2,1,0:T(8,128)}) custom-call(s32[2]{0:T(128)} %copy-done.3, s32[2]{0:T(128)} %iota_add_fusion.head_ref, f32[32]{0:T(128)} %bias_ref.1, f32[32]{0:T(128)} %rate_ref.1, f32[32]{0:T(128)} %skip_ref.1, ...), custom_call_target="tpu_custom_call" | custom-call | flops 2415919104 | bytes 4718592 | tf_op jit(solution)/shard_map/scan_weights/pallas_call | solution.py:250
  104.6 3.4 %in_projection.4.refs_0_ = bf16[384,256]{1,0:T(8,128)(2,1)S(1)} custom-call(s32[2]{0:T(128)S(1)} %copy-done.4, bf16[384,2048]{1,0:T(8,128)(2,1)S(1)} %bitcast.21, bf16[384,2048]{1,0:T(8,128)(2,1)S(1)} %collective-permute-done.refs_1_, bf16[4096,2048]{1,0:T(8,128)(2,1)} %bitcast.36, bf16[4096,2048]{1,0:T(8,128)(2,1)} %bitcast.37), custom_call_target="tpu_custom_call" | custom-call | flops 384 | bytes 384 | tf_op jit(solution)/shard_map/in_projection/pallas_call | solution.py:147
  108.2 5.2 %scan.1 = bf16[8,448,256]{2,1,0:T(8,128)(2,1)} custom-call(s32[2]{0:T(128)S(1)} %copy-done.4, bf16[384,256]{1,0:T(8,128)(2,1)S(1)} %in_projection.4.refs_0_, bf16[384,256]{1,0:T(8,128)(2,1)} %collective-permute-done.1.refs_1_, bf16[384,256]{1,0:T(8,128)(2,1)} %collective-permute-done.2.refs_2_, bf16[384,256]{1,0:T(8,128)(2,1)S(1)} %collective-permute-done.3.refs_3_, ...), custom_call_target="tpu_custom_call" | custom-call | flops 805306368 | bytes 4718592 | tf_op jit(solution)/shard_map/scan/pallas_call | solution.py:320
  113.4 4.8 %all-to-all-start.1 = ((bf16[8,448,256]{2,1,0:T(8,128)(2,1)}), bf16[8,448,256]{2,1,0:T(8,128)(2,1)S(1)}, u32[]{:S(2)}, u32[]{:S(2)}) async-start(bf16[8,448,256]{2,1,0:T(8,128)(2,1)} %scan.1), calls=%async_computation.1 | async-start | bytes 3670016 | tf_op jit(solution)/shard_map/all_to_all | solution.py:490
  118.2 42.0 %all-to-all-done.1.refs_0_ = bf16[8,448,256]{2,1,0:T(8,128)(2,1)S(1)} async-done(((bf16[8,448,256]{2,1,0:T(8,128)(2,1)}), bf16[8,448,256]{2,1,0:T(8,128)(2,1)S(1)}, u32[]{:S(2)}, u32[]{:S(2)}) %all-to-all-start.1) | async-done | bytes 1835040 | tf_op jit(solution)/shard_map/all_to_all | solution.py:490
  160.2 7.5 %out_send.1 = (bf16[1,384,2048]{2,1,0:T(8,128)(2,1)S(1)}, f32[384,1]{1,0:T(8,128)S(1)}) custom-call(s32[2]{0:T(128)S(1)} %copy-done.4, bf16[8,448,256]{2,1,0:T(8,128)(2,1)S(1)} %all-to-all-done.1.refs_0_, bf16[2048,4096]{1,0:T(8,128)(2,1)} %bitcast.38, f32[1,2048]{1,0:T(1,128)S(1)} %bitcast.25), custom_call_target="tpu_custom_call" | custom-call | flops 3221225472 | bytes 9961472 | tf_op jit(solution)/shard_map/out_send/pallas_call | solution.py:437
  167.8 0.5 collective-permute-start.8
  168.3 3.2 %collective-permute-done.8.refs_3_ = f32[384,1]{1,0:T(8,128)S(1)} collective-permute-done((f32[384,1]{1,0:T(8,128)S(1)}, f32[384,1]{1,0:T(8,128)S(1)}, u32[]{:S(2)}, u32[]{:S(2)}) %collective-permute-start.8) | collective-permute-done | bytes 1568 | tf_op jit(solution)/shard_map/ppermute | solution.py:484
  171.5 7.9 %out_finish.1 = bf16[384,2048]{1,0:T(8,128)(2,1)} custom-call(s32[2]{0:T(128)S(1)} %copy-done.4, bf16[8,448,256]{2,1,0:T(8,128)(2,1)S(1)} %all-to-all-done.1.refs_0_, bf16[2048,4096]{1,0:T(8,128)(2,1)} %bitcast.39, f32[384,1]{1,0:T(8,128)S(1)} %get-tuple-element.42.refs_2_, f32[384,1]{1,0:T(8,128)S(1)} %collective-permute-done.8.refs_3_, ...), custom_call_target="tpu_custom_call" | custom-call | flops 3221225472 | bytes 9961472 | tf_op jit(solution)/shard_map/out_finish/pallas_call | solution.py:437
  179.4 3.9 %all-to-all-start.2 = ((bf16[16,24,2048]{2,1,0:T(8,128)(2,1)}), bf16[16,24,2048]{2,1,0:T(8,128)(2,1)S(1)}, u32[]{:S(2)}, u32[]{:S(2)}) async-start(bf16[16,24,2048]{2,1,0:T(8,128)(2,1)} %bitcast.40), calls=%async_computation.2 | async-start | bytes 3145728 | tf_op jit(solution)/shard_map/all_to_all | solution.py:490
  183.3 1.3 fusion
  185.7 0.8 collective-permute-done.10
  186.8 0.7 reshape.34
  187.5 27.8 %all-to-all-done.2 = bf16[16,24,2048]{2,1,0:T(8,128)(2,1)S(1)} async-done(((bf16[16,24,2048]{2,1,0:T(8,128)(2,1)}), bf16[16,24,2048]{2,1,0:T(8,128)(2,1)S(1)}, u32[]{:S(2)}, u32[]{:S(2)}) %all-to-all-start.2) | async-done | bytes 1572896 | tf_op jit(solution)/shard_map/all_to_all | solution.py:490
  215.3 2.0 collect.1
  (39 shorter events, 1.1 us)
Async XLA Ops:
  11.7 41.5 %all-to-all-start = ((bf16[16,24,2048]{2,1,0:T(8,128)(2,1)}), bf16[16,24,2048]{2,1,0:T(8,128)(2,1)S(1)}, u32[]{:S(2)}, u32[]{:S(2)}) async-start(bf16[16,24,2048]{2,1,0:T(8,128)(2,1)} %bitcast.41), calls=%async_computation | async-start | bytes 3145728 | tf_op jit(solution)/shard_map/all_to_all | solution.py:490
  19.1 72.8 %all-gather.2.cloned.1.call-start = ((), (), s32[]{:S(2)}) async-start(), calls=%async_computation.3 | async-start | bytes 1114112 | tf_op jit(solution)/shard_map/all_gather | solution.py:526
  53.2 3.8 %collective-permute-start = (bf16[384,2048]{1,0:T(8,128)(2,1)S(1)}, bf16[384,2048]{1,0:T(8,128)(2,1)S(1)}, u32[]{:S(2)}, u32[]{:S(2)}) collective-permute-start(bf16[384,2048]{1,0:T(8,128)(2,1)S(1)} %bitcast.17), channel_id=1, source_target_pairs={{0,1},{1,0},{2,3},{3,2},{4,5},{5,4},{6,7},{7,6},{8,9},{9,8},{10,11... | collective-permute-start | bytes 4718600 | tf_op jit(solution)/shard_map/ppermute | solution.py:484
  54.0 29.1 %copy-start.3 = (s32[2]{0:T(128)}, s32[2]{0:T(128)S(1)}, u32[]{:S(2)}) copy-start(s32[2]{0:T(128)S(1)} %pad_add_fusion.place_ref) | copy-start | bytes 28
  63.5 0.7 copy-start.6
  64.1 23.8 %collective-permute-start.3 = (bf16[384,256]{1,0:T(8,128)(2,1)}, bf16[384,256]{1,0:T(8,128)(2,1)S(1)}, u32[]{:S(2)}, u32[]{:S(2)}) collective-permute-start(bf16[384,256]{1,0:T(8,128)(2,1)} %get-tuple-element.33), channel_id=1, source_target_pairs={{0,6},{1,7},{2,4},{3,5},{4,2},{5,3},{6,0},{7,1},{8,14},{9,15},{10,... | collective-permute-start | bytes 589832 | tf_op jit(solution)/shard_map/ppermute | solution.py:497
  72.4 18.0 %collective-permute-start.4 = (bf16[384,256]{1,0:T(8,128)(2,1)}, bf16[384,256]{1,0:T(8,128)(2,1)S(1)}, u32[]{:S(2)}, u32[]{:S(2)}) collective-permute-start(bf16[384,256]{1,0:T(8,128)(2,1)} %get-tuple-element.34), channel_id=1, source_target_pairs={{0,8},{1,9},{2,10},{3,11},{4,12},{5,13},{6,14},{7,15},{8,0},{9,1},... | collective-permute-start | bytes 589832 | tf_op jit(solution)/shard_map/ppermute | solution.py:497
  74.8 33.1 %collective-permute-start.5 = (bf16[384,256]{1,0:T(8,128)(2,1)}, bf16[384,256]{1,0:T(8,128)(2,1)}, u32[]{:S(2)}, u32[]{:S(2)}) collective-permute-start(bf16[384,256]{1,0:T(8,128)(2,1)} %copy-done.6), channel_id=1, source_target_pairs={{0,10},{1,11},{2,8},{3,9},{4,14},{5,15},{6,12},{7,13},{8,2},{9,3},... | collective-permute-start | bytes 589832 | tf_op jit(solution)/shard_map/ppermute | solution.py:497
  79.8 28.1 %collective-permute-start.1 = (bf16[384,256]{1,0:T(8,128)(2,1)}, bf16[384,256]{1,0:T(8,128)(2,1)}, u32[]{:S(2)}, u32[]{:S(2)}) collective-permute-start(bf16[384,256]{1,0:T(8,128)(2,1)} %get-tuple-element.31), channel_id=1, source_target_pairs={{0,2},{1,3},{2,0},{3,1},{4,6},{5,7},{6,4},{7,5},{8,10},{9,11},{10,... | collective-permute-start | bytes 589832 | tf_op jit(solution)/shard_map/ppermute | solution.py:497
  83.1 24.9 %collective-permute-start.2 = (bf16[384,256]{1,0:T(8,128)(2,1)}, bf16[384,256]{1,0:T(8,128)(2,1)}, u32[]{:S(2)}, u32[]{:S(2)}) collective-permute-start(bf16[384,256]{1,0:T(8,128)(2,1)} %get-tuple-element.32), channel_id=1, source_target_pairs={{0,4},{1,5},{2,6},{3,7},{4,0},{5,1},{6,2},{7,3},{8,12},{9,13},{10,... | collective-permute-start | bytes 589832 | tf_op jit(solution)/shard_map/ppermute | solution.py:497
  88.0 20.0 %collective-permute-start.6 = (bf16[384,256]{1,0:T(8,128)(2,1)}, bf16[384,256]{1,0:T(8,128)(2,1)}, u32[]{:S(2)}, u32[]{:S(2)}) collective-permute-start(bf16[384,256]{1,0:T(8,128)(2,1)} %get-tuple-element.36), channel_id=1, source_target_pairs={{0,12},{1,13},{2,14},{3,15},{4,8},{5,9},{6,10},{7,11},{8,4},{9,5},... | collective-permute-start | bytes 589832 | tf_op jit(solution)/shard_map/ppermute | solution.py:497
  90.5 14.0 %copy-start.4 = (s32[2]{0:T(128)S(1)}, s32[2]{0:T(128)}, u32[]{:S(2)}) copy-start(s32[2]{0:T(128)} %copy-done.3) | copy-start | bytes 28
  90.5 17.5 %collective-permute-start.7 = (bf16[384,256]{1,0:T(8,128)(2,1)}, bf16[384,256]{1,0:T(8,128)(2,1)}, u32[]{:S(2)}, u32[]{:S(2)}) collective-permute-start(bf16[384,256]{1,0:T(8,128)(2,1)} %get-tuple-element.37), channel_id=1, source_target_pairs={{0,14},{1,15},{2,12},{3,13},{4,10},{5,11},{6,8},{7,9},{8,6},{9,7},... | collective-permute-start | bytes 589832 | tf_op jit(solution)/shard_map/ppermute | solution.py:497
  104.5 3.5 %slice-start = ((s8[4718592]{0:T(1024)(128)(4,1)}), s8[4194304]{0:T(1024)(128)(4,1)S(1)}, s32[]{:S(2)}) async-start(s8[4718592]{0:T(1024)(128)(4,1)} %bitcast.23), calls=%async_computation.4 | async-start | bytes 8388608
  104.5 3.5 %slice-start.1 = ((s8[4718592]{0:T(1024)(128)(4,1)}), s8[524288]{0:T(1024)(128)(4,1)S(1)}, s32[]{:S(2)}) async-start(s8[4718592]{0:T(1024)(128)(4,1)} %bitcast.23), calls=%async_computation.5 | async-start | bytes 1048576
  104.5 3.5 %copy-start = (bf16[2,8,384,64]{3,2,1,0:T(8,128)(2,1)S(1)}, bf16[2,8,384,64]{3,2,1,0:T(8,128)(2,1)}, u32[]{:S(2)}) copy-start(bf16[2,8,384,64]{3,2,1,0:T(8,128)(2,1)} %get-tuple-element.39.refs_9_) | copy-start | bytes 2359300
  104.5 3.6 %copy-start.1 = (bf16[2,8,64,384]{3,2,1,0:T(8,128)(2,1)S(1)}, bf16[2,8,64,384]{3,2,1,0:T(8,128)(2,1)}, u32[]{:S(2)}) copy-start(bf16[2,8,64,384]{3,2,1,0:T(8,128)(2,1)} %get-tuple-element.40.refs_10_) | copy-start | bytes 2359300
  104.5 3.6 %copy-start.2 = (f32[2,8,8,128]{3,2,1,0:T(8,128)S(1)}, f32[2,8,8,128]{3,2,1,0:T(8,128)}, u32[]{:S(2)}) copy-start(f32[2,8,8,128]{3,2,1,0:T(8,128)} %get-tuple-element.41.refs_11_) | copy-start | bytes 196612
  113.4 4.8 %copy-start.7 = (f32[4096]{0:T(1024)S(1)}, f32[4096]{0:T(1024)}, u32[]{:S(2)}) copy-start(f32[4096]{0:T(1024)} %param.17) | copy-start | bytes 49156
  113.4 46.8 %all-to-all-start.1 = ((bf16[8,448,256]{2,1,0:T(8,128)(2,1)}), bf16[8,448,256]{2,1,0:T(8,128)(2,1)S(1)}, u32[]{:S(2)}, u32[]{:S(2)}) async-start(bf16[8,448,256]{2,1,0:T(8,128)(2,1)} %scan.1), calls=%async_computation.1 | async-start | bytes 3670016 | tf_op jit(solution)/shard_map/all_to_all | solution.py:490
  167.7 3.8 %collective-permute-start.9 = (bf16[384,2048]{1,0:T(8,128)(2,1)S(1)}, bf16[384,2048]{1,0:T(8,128)(2,1)S(1)}, u32[]{:S(2)}, u32[]{:S(2)}) collective-permute-start(bf16[384,2048]{1,0:T(8,128)(2,1)S(1)} %bitcast.29), channel_id=1, source_target_pairs={{0,1},{1,0},{2,3},{3,2},{4,5},{5,4},{6,7},{7,6},{8,9},{9,8},{10,11... | collective-permute-start | bytes 4718600 | tf_op jit(solution)/shard_map/ppermute | solution.py:484
  167.8 3.7 %collective-permute-start.8 = (f32[384,1]{1,0:T(8,128)S(1)}, f32[384,1]{1,0:T(8,128)S(1)}, u32[]{:S(2)}, u32[]{:S(2)}) collective-permute-start(f32[384,1]{1,0:T(8,128)S(1)} %get-tuple-element.42.refs_2_), channel_id=1, source_target_pairs={{0,1},{1,0},{2,3},{3,2},{4,5},{5,4},{6,7},{7,6},{8,9},{9,8},{10,11... | collective-permute-start | bytes 4616 | tf_op jit(solution)/shard_map/ppermute | solution.py:484
  179.4 35.9 %copy-start.5 = (s32[128,1]{0,1:T(1,128)S(1)}, s32[128,1]{0,1:T(1,128)}, u32[]{:S(2)}) copy-start(s32[128,1]{0,1:T(1,128)} %param.18) | copy-start | bytes 1540
  179.4 35.9 %all-to-all-start.2 = ((bf16[16,24,2048]{2,1,0:T(8,128)(2,1)}), bf16[16,24,2048]{2,1,0:T(8,128)(2,1)S(1)}, u32[]{:S(2)}, u32[]{:S(2)}) async-start(bf16[16,24,2048]{2,1,0:T(8,128)(2,1)} %bitcast.40), calls=%async_computation.2 | async-start | bytes 3145728 | tf_op jit(solution)/shard_map/all_to_all | solution.py:490
  185.4 1.2 collective-permute-start.10
Sparse Core Ops, SparseCore 0:
  22.1 47.0 all-gather.1
